TPU v7x, 128 devices: a whole 4x4x4 slice. The times are simulated.
128 devices in a mesh: seq: 8 (over z_lo, y), fsdp: 16 (over z_hi, x, core).
Axes of the slice: x: 4, y: 4, z: 4 (z_hi: 2, z_lo: 2; z = z_hi * 2 + z_lo), core: 2. Of those that a mesh axis runs over, the one named last changes fastest.
Arguments:
- layer_input: bfloat16 [16, 1024, 2048], P('fsdp', 'seq'), may hold values from -6 to 6
- positions: int32 [16, 1024], P('fsdp', 'seq'), may hold values from 0 to 1023, as said below
- attn_gain: float32 [2048], P('fsdp'), may hold values from 0.1 to 1.9
- w_query: bfloat16 [2048, 2048], P('fsdp'), may hold values from -0.125 to 0.125
- w_key: bfloat16 [2048, 256], P('fsdp'), may hold values from -0.125 to 0.125
- w_value: bfloat16 [2048, 256], P('fsdp'), may hold values from -0.125 to 0.125
- w_output: bfloat16 [2048, 2048], P('fsdp'), may hold values from -3 to 3
- mlp_gain: float32 [2048], P('fsdp'), may hold values from 0.1 to 1.9
- w_gate: bfloat16 [2048, 5632], P('fsdp'), may hold values from -0.125 to 0.125
- w_up: bfloat16 [2048, 5632], P('fsdp'), may hold values from -0.125 to 0.125
- w_down: bfloat16 [5632, 2048], P('fsdp'), may hold values from -0.109375 to 0.109375
- out_grad: bfloat16 [16, 1024, 2048], P('fsdp', 'seq'), may hold values from -6 to 6
Outputs:
- layer_output: bfloat16 [16, 1024, 2048], P('fsdp', 'seq')
- input_grad: bfloat16 [16, 1024, 2048], P('fsdp', 'seq')
- attn_gain_grad: float32 [2048], P('fsdp')
- w_query_grad: float32 [2048, 2048], P('fsdp')
- w_key_grad: float32 [2048, 256], P('fsdp')
- w_value_grad: float32 [2048, 256], P('fsdp')
- w_output_grad: float32 [2048, 2048], P('fsdp')
- mlp_gain_grad: float32 [2048], P('fsdp')
- w_gate_grad: float32 [2048, 5632], P('fsdp')
- w_up_grad: float32 [2048, 5632], P('fsdp')
- w_down_grad: float32 [5632, 2048], P('fsdp')
Inputs may be any that keep to these rules, and one draw needn't show every extreme that they name: In each sequence the positions rise by one from token to token and fall back to 0 at some tokens; each sequence's first token has position 0; in one sequence they never fall back and run from 0 to 1023.
All inputs are finite; a program needn't handle non-finite values.
Results may differ from a plain program's by a relative error of at most 0.04.
Values may be sent and summed in bfloat16 or wider, within the bound.
No kernel may reach another device: no remote copies, remote signals or barrier semaphores. Data moves between devices by JAX's collectives and lax.ppermute only.
A program may use at most 320 MiB of HBM per device.

v0:
```python
import jax
import jax.numpy as jnp
from jax import lax
from jax.sharding import PartitionSpec as P

H = 32
KV = 4
HD = 64


eps = 1e-05
theta = 10000.0


def rms_scale(values):
    return lax.rsqrt(jnp.mean(values * values, axis=-1, keepdims=True) + eps)


def norm_apply(values, gain_row):
    return values * rms_scale(values) * gain_row


def gated(gate_pre, upward):
    return jax.nn.silu(gate_pre) * upward


def rotate(values, cosine, sine_part):
    half_dim = values.shape[-1] // 2
    turned = jnp.concatenate([-values[..., half_dim:], values[..., :half_dim]], axis=-1)
    return values * cosine + turned * sine_part


def rope_tables(places):
    frequency = theta ** (-jnp.arange(0, HD, 2).astype(jnp.float32) / HD)
    angles = places.astype(jnp.float32)[..., None] * frequency
    angles = jnp.concatenate([angles, angles], axis=-1)
    return (jnp.cos(angles)[..., None, :], jnp.sin(angles)[..., None, :])


def matmul(left, right):
    return jnp.dot(left, right, preferred_element_type=jnp.float32)


def times_transposed(left, right):
    return lax.dot_general(
        left, right, (((1,), (1,)), ((), ())), preferred_element_type=jnp.float32
    )


def outer_sum(left, right):
    return lax.dot_general(
        left, right, (((0,), (0,)), ((), ())), preferred_element_type=jnp.float32
    )


def causal_scores(query_part, key_grid, first_row, score_scale):
    scores = (
        jnp.einsum("qcgd,kcd->cgqk", query_part, key_grid, preferred_element_type=jnp.float32)
        * score_scale
    )
    rows_at = first_row + jnp.arange(query_part.shape[0], dtype=jnp.int32)
    cols_at = jnp.arange(key_grid.shape[0], dtype=jnp.int32)
    return jnp.where(rows_at[:, None] >= cols_at[None, :], scores, -1e30)


def on_device(
    layer_input,
    positions,
    attn_gain,
    w_query,
    w_key,
    w_value,
    w_output,
    mlp_gain,
    w_gate,
    w_up,
    w_down,
    out_grad,
):
    seq_count = lax.axis_size("seq")
    fsdp_count = lax.axis_size("fsdp")
    tokens = layer_input.shape[1]
    seq_len = tokens * seq_count
    block_rows = min(512, seq_len)
    block_count = seq_len // block_rows
    copies_all = max(KV, seq_count)
    repeat_by = copies_all // KV
    local_copies = copies_all // seq_count
    per_copy = H // copies_all
    score_scale = HD ** (-0.5)
    gain_one, query_full, key_full, value_full, output_full = (
        lax.all_gather(attn_gain.astype(jnp.bfloat16), "fsdp", axis=0, tiled=True).astype(
            attn_gain.dtype
        ),
        lax.all_gather(w_query, "fsdp", axis=0, tiled=True),
        lax.all_gather(w_key, "fsdp", axis=0, tiled=True),
        lax.all_gather(w_value, "fsdp", axis=0, tiled=True),
        lax.all_gather(w_output, "fsdp", axis=0, tiled=True),
    )
    inputs = layer_input[0].astype(jnp.float32)
    cosine, sine_part = rope_tables(positions[0])
    normed = norm_apply(inputs, gain_one).astype(jnp.bfloat16)
    query_pre = matmul(normed, query_full).reshape(tokens, H, HD)
    key_pre = matmul(normed, key_full).reshape(tokens, KV, HD)
    query_rot = rotate(query_pre, cosine, sine_part).astype(jnp.bfloat16).reshape(tokens, H * HD)
    key_rot = rotate(key_pre, cosine, sine_part).astype(jnp.bfloat16)
    key_copies = jnp.repeat(key_rot, repeat_by, axis=1).reshape(tokens, copies_all * HD)
    value_low = matmul(normed, value_full).astype(jnp.bfloat16).reshape(tokens, KV, HD)
    value_copies = jnp.repeat(value_low, repeat_by, axis=1).reshape(tokens, copies_all * HD)
    query_heads, key_heads, value_heads = (
        lax.all_to_all(query_rot, "seq", split_axis=1, concat_axis=0, tiled=True),
        lax.all_to_all(key_copies, "seq", split_axis=1, concat_axis=0, tiled=True),
        lax.all_to_all(value_copies, "seq", split_axis=1, concat_axis=0, tiled=True),
    )
    query_grid = query_heads.reshape(seq_len, local_copies, per_copy, HD)
    key_grid = key_heads.reshape(seq_len, local_copies, HD)
    value_grid = value_heads.reshape(seq_len, local_copies, HD)

    def forward_block(block_index, carry_in):
        mixed_all, log_all = carry_in
        first_row = block_index * block_rows
        query_part = lax.dynamic_slice_in_dim(query_grid, first_row, block_rows, 0)
        scores = causal_scores(query_part, key_grid, first_row, score_scale)
        row_top = jnp.max(scores, axis=-1, keepdims=True)
        weights = jnp.exp(scores - row_top)
        row_total = jnp.sum(weights, axis=-1, keepdims=True)
        weights_low = (weights / row_total).astype(jnp.bfloat16)
        mixed_rows = jnp.einsum(
            "cgqk,kcd->qcgd", weights_low, value_grid, preferred_element_type=jnp.float32
        )
        mixed_all = lax.dynamic_update_slice_in_dim(
            mixed_all, mixed_rows.reshape(block_rows, -1).astype(jnp.bfloat16), first_row, 0
        )
        log_all = lax.dynamic_update_slice_in_dim(
            log_all, (row_top + jnp.log(row_total))[..., 0], first_row, 2
        )
        return (mixed_all, log_all)

    mixed_start = jnp.zeros((seq_len, local_copies * per_copy * HD), jnp.bfloat16)
    log_start = jnp.zeros((local_copies, per_copy, seq_len), jnp.float32)
    mixed_heads, log_totals = lax.fori_loop(0, block_count, forward_block, (mixed_start, log_start))
    mixed_seq = lax.all_to_all(mixed_heads, "seq", split_axis=0, concat_axis=1, tiled=True)
    hidden = inputs + matmul(mixed_seq, output_full)
    gain_two, gate_full, up_full, down_full = (
        lax.all_gather(mlp_gain.astype(jnp.bfloat16), "fsdp", axis=0, tiled=True).astype(
            mlp_gain.dtype
        ),
        lax.all_gather(w_gate, "fsdp", axis=0, tiled=True),
        lax.all_gather(w_up, "fsdp", axis=0, tiled=True),
        lax.all_gather(w_down, "fsdp", axis=0, tiled=True),
    )
    normed_two = norm_apply(hidden, gain_two).astype(jnp.bfloat16)
    gate_pre = matmul(normed_two, gate_full)
    upward = matmul(normed_two, up_full)
    activation = gated(gate_pre, upward).astype(jnp.bfloat16)
    result = hidden + matmul(activation, down_full)
    grad_out = out_grad[0]
    grad_act = times_transposed(grad_out, down_full)
    _, gated_pull = jax.vjp(gated, gate_pre, upward)
    grad_gate, grad_up = gated_pull(grad_act)
    grad_gate = grad_gate.astype(jnp.bfloat16)
    grad_up = grad_up.astype(jnp.bfloat16)
    grad_normed_two = times_transposed(grad_gate, gate_full) + times_transposed(grad_up, up_full)
    _, norm_pull_two = jax.vjp(norm_apply, hidden, gain_two)
    grad_hidden_norm, gain_two_term = norm_pull_two(grad_normed_two)
    grad_hidden = grad_out.astype(jnp.float32) + grad_hidden_norm
    gain_two_grid = gain_two_term.reshape(fsdp_count, -1)
    down_term = outer_sum(activation, grad_out)
    gate_term = outer_sum(normed_two, grad_gate)
    up_term = outer_sum(normed_two, grad_up)
    mlp_parts = (
        lax.psum_scatter(
            gain_two_grid.astype(jnp.bfloat16), "fsdp", scatter_dimension=0, tiled=True
        ).astype(jnp.float32),
        lax.psum_scatter(
            gate_term.astype(jnp.bfloat16), "fsdp", scatter_dimension=0, tiled=True
        ).astype(jnp.float32),
        lax.psum_scatter(
            up_term.astype(jnp.bfloat16), "fsdp", scatter_dimension=0, tiled=True
        ).astype(jnp.float32),
        lax.psum_scatter(
            down_term.astype(jnp.bfloat16), "fsdp", scatter_dimension=0, tiled=True
        ).astype(jnp.float32),
    )
    grad_hidden_low = grad_hidden.astype(jnp.bfloat16)
    grad_mixed = times_transposed(grad_hidden_low, output_full).astype(jnp.bfloat16)
    grad_heads = lax.all_to_all(grad_mixed, "seq", split_axis=1, concat_axis=0, tiled=True)
    grad_grid = grad_heads.reshape(seq_len, local_copies, per_copy, HD)

    def backward_block(block_index, carry_in):
        query_grads, key_grads, value_grads = carry_in
        first_row = block_index * block_rows
        query_part = lax.dynamic_slice_in_dim(query_grid, first_row, block_rows, 0)
        grad_part = lax.dynamic_slice_in_dim(grad_grid, first_row, block_rows, 0)
        log_part = lax.dynamic_slice_in_dim(log_totals, first_row, block_rows, 2)
        scores = causal_scores(query_part, key_grid, first_row, score_scale)
        weights = jnp.exp(scores - log_part[..., None])
        weights_low = weights.astype(jnp.bfloat16)
        value_grads = value_grads + jnp.einsum(
            "cgqk,qcgd->kcd", weights_low, grad_part, preferred_element_type=jnp.float32
        )
        grad_weights = jnp.einsum(
            "qcgd,kcd->cgqk", grad_part, value_grid, preferred_element_type=jnp.float32
        )
        row_delta = jnp.sum(weights * grad_weights, axis=-1, keepdims=True)
        grad_scores = (weights * (grad_weights - row_delta) * score_scale).astype(jnp.bfloat16)
        grad_query = jnp.einsum(
            "cgqk,kcd->qcgd", grad_scores, key_grid, preferred_element_type=jnp.float32
        )
        key_grads = key_grads + jnp.einsum(
            "cgqk,qcgd->kcd", grad_scores, query_part, preferred_element_type=jnp.float32
        )
        query_grads = lax.dynamic_update_slice_in_dim(
            query_grads, grad_query.reshape(block_rows, -1).astype(jnp.bfloat16), first_row, 0
        )
        return (query_grads, key_grads, value_grads)

    query_start = jnp.zeros((seq_len, local_copies * per_copy * HD), jnp.bfloat16)
    copy_start = jnp.zeros((seq_len, local_copies, HD), jnp.float32)
    query_grads, key_grads, value_grads = lax.fori_loop(
        0, block_count, backward_block, (query_start, copy_start, copy_start)
    )
    key_grads_low = key_grads.reshape(seq_len, local_copies * HD).astype(jnp.bfloat16)
    value_grads_low = value_grads.reshape(seq_len, local_copies * HD).astype(jnp.bfloat16)
    grad_query_seq, grad_key_seq, grad_value_seq = (
        lax.all_to_all(query_grads, "seq", split_axis=0, concat_axis=1, tiled=True),
        lax.all_to_all(key_grads_low, "seq", split_axis=0, concat_axis=1, tiled=True),
        lax.all_to_all(value_grads_low, "seq", split_axis=0, concat_axis=1, tiled=True),
    )
    grad_key_rot = jnp.sum(
        grad_key_seq.reshape(tokens, KV, repeat_by, HD).astype(jnp.float32), axis=2
    )
    grad_value_pre = jnp.sum(
        grad_value_seq.reshape(tokens, KV, repeat_by, HD).astype(jnp.float32), axis=2
    )
    grad_value_low = grad_value_pre.astype(jnp.bfloat16).reshape(tokens, KV * HD)

    def rotate_local(values):
        return rotate(values, cosine, sine_part)

    _, query_pull = jax.vjp(rotate_local, query_pre)
    grad_query_pre = query_pull(grad_query_seq.reshape(tokens, H, HD).astype(jnp.float32))[0]
    grad_query_pre = grad_query_pre.astype(jnp.bfloat16).reshape(tokens, H * HD)
    _, key_pull = jax.vjp(rotate_local, key_pre)
    grad_key_pre = key_pull(grad_key_rot)[0].astype(jnp.bfloat16).reshape(tokens, KV * HD)
    grad_normed = (
        times_transposed(grad_query_pre, query_full)
        + times_transposed(grad_key_pre, key_full)
        + times_transposed(grad_value_low, value_full)
    )
    _, norm_pull_one = jax.vjp(norm_apply, inputs, gain_one)
    grad_inputs_norm, gain_one_term = norm_pull_one(grad_normed)
    input_grad = (grad_hidden + grad_inputs_norm).astype(jnp.bfloat16)
    gain_one_grid = gain_one_term.reshape(fsdp_count, -1)
    output_term = outer_sum(mixed_seq, grad_hidden_low)
    query_term = outer_sum(normed, grad_query_pre)
    key_term = outer_sum(normed, grad_key_pre)
    value_term = outer_sum(normed, grad_value_low)
    attn_parts = (
        lax.psum_scatter(
            gain_one_grid.astype(jnp.bfloat16), "fsdp", scatter_dimension=0, tiled=True
        ).astype(jnp.float32),
        lax.psum_scatter(
            query_term.astype(jnp.bfloat16), "fsdp", scatter_dimension=0, tiled=True
        ).astype(jnp.float32),
        lax.psum_scatter(
            key_term.astype(jnp.bfloat16), "fsdp", scatter_dimension=0, tiled=True
        ).astype(jnp.float32),
        lax.psum_scatter(
            value_term.astype(jnp.bfloat16), "fsdp", scatter_dimension=0, tiled=True
        ).astype(jnp.float32),
        lax.psum_scatter(
            output_term.astype(jnp.bfloat16), "fsdp", scatter_dimension=0, tiled=True
        ).astype(jnp.float32),
    )
    finals = (
        lax.psum(attn_parts[0].astype(jnp.bfloat16), "seq").astype(jnp.float32),
        lax.psum(attn_parts[1].astype(jnp.bfloat16), "seq").astype(jnp.float32),
        lax.psum(attn_parts[2].astype(jnp.bfloat16), "seq").astype(jnp.float32),
        lax.psum(attn_parts[3].astype(jnp.bfloat16), "seq").astype(jnp.float32),
        lax.psum(attn_parts[4].astype(jnp.bfloat16), "seq").astype(jnp.float32),
        lax.psum(mlp_parts[0].astype(jnp.bfloat16), "seq").astype(jnp.float32),
        lax.psum(mlp_parts[1].astype(jnp.bfloat16), "seq").astype(jnp.float32),
        lax.psum(mlp_parts[2].astype(jnp.bfloat16), "seq").astype(jnp.float32),
        lax.psum(mlp_parts[3].astype(jnp.bfloat16), "seq").astype(jnp.float32),
    )
    return (
        result.astype(jnp.bfloat16)[None],
        input_grad[None],
        finals[0].reshape(-1),
        finals[1],
        finals[2],
        finals[3],
        finals[4],
        finals[5].reshape(-1),
        finals[6],
        finals[7],
        finals[8],
    )


def solution(mesh):
    in_specs = (
        P("fsdp", "seq", None),
        P("fsdp", "seq"),
        P("fsdp"),
        P("fsdp", None),
        P("fsdp", None),
        P("fsdp", None),
        P("fsdp", None),
        P("fsdp"),
        P("fsdp", None),
        P("fsdp", None),
        P("fsdp", None),
        P("fsdp", "seq", None),
    )
    out_specs = (
        P("fsdp", "seq", None),
        P("fsdp", "seq", None),
        P("fsdp"),
        P("fsdp", None),
        P("fsdp", None),
        P("fsdp", None),
        P("fsdp", None),
        P("fsdp"),
        P("fsdp", None),
        P("fsdp", None),
        P("fsdp", None),
    )
    return jax.shard_map(
        on_device, mesh=mesh, in_specs=in_specs, out_specs=out_specs, check_vma=False
    )
```

profile of v0, /device:TPU:1, one launch (start us, length us, event | category | flops | bytes accessed | tf_op | source)
XLA Modules:
  0.0 1835.0 jit_solution(12003018412729658993)
XLA Ops:
  12.6 26.2 %all-gather = bf16[16,1,128]{2,1,0:T(2,128)(2,1)S(1)} all-gather(bf16[1,1,128]{2,1,0:T(2,128)(2,1)S(1)} %convert_bitcast_fusion.7), channel_id=1, replica_groups=mesh['seq'=8,'fsdp'=16] {'fsdp'}, dimensions={0}, use_global_device_ids=true | all-gather | bytes 4352 | tf_op jit(solution)/shard_map/all_gather | solution.py:92
  40.9 18.4 %all-gather.12.cloned.1.call-done = bf16[2048,256]{1,0:T(8,128)(2,1)} async-done(((bf16[128,256]{1,0:T(8,128)(2,1)}), bf16[2048,256]{1,0:T(8,128)(2,1)}) %all-gather.12.cloned.1.call-update) | async-done | bytes 1048592 | tf_op jit(solution)/shard_map/all_gather | solution.py:96
  67.1 38.3 %all-gather.14.cloned.1.call-done = bf16[2048,256]{1,0:T(8,128)(2,1)} async-done(((bf16[128,256]{1,0:T(8,128)(2,1)}), bf16[2048,256]{1,0:T(8,128)(2,1)}) %all-gather.14.cloned.1.call-update) | async-done | bytes 1048592 | tf_op jit(solution)/shard_map/all_gather | solution.py:97
  107.1 72.1 %all-gather.10.cloned.1.call-done = bf16[2048,2048]{1,0:T(8,128)(2,1)} async-done(((bf16[128,2048]{1,0:T(8,128)(2,1)}), bf16[2048,2048]{1,0:T(8,128)(2,1)}) %all-gather.10.cloned.1.call-update) | async-done | bytes 8388624 | tf_op jit(solution)/shard_map/all_gather | solution.py:95
  179.3 12.4 copy.62
  211.6 9.5 all-to-all-done
  222.6 16.8 while.33
  242.9 22.5 %all-gather.1 = bf16[16,1,128]{2,1,0:T(2,128)(2,1)S(1)} all-gather(bf16[1,1,128]{2,1,0:T(2,128)(2,1)S(1)} %convert_bitcast_fusion.5), channel_id=1, replica_groups=mesh['seq'=8,'fsdp'=16] {'fsdp'}, dimensions={0}, use_global_device_ids=true | all-gather | bytes 4352 | tf_op jit(solution)/shard_map/all_gather | solution.py:145
  271.6 123.4 %all-gather.18.cloned.1.call-done = bf16[2048,5632]{1,0:T(8,128)(2,1)} async-done(((bf16[128,5632]{1,0:T(8,128)(2,1)}), bf16[2048,5632]{1,0:T(8,128)(2,1)}) %all-gather.18.cloned.1.call-update) | async-done | bytes 23068688 | tf_op jit(solution)/shard_map/all_gather | solution.py:148
  395.0 12.3 fusion.107
  407.3 126.8 %all-gather.20.cloned.1.call-done = bf16[2048,5632]{1,0:T(8,128)(2,1)} async-done(((bf16[128,5632]{1,0:T(8,128)(2,1)}), bf16[2048,5632]{1,0:T(8,128)(2,1)}) %all-gather.20.cloned.1.call-update) | async-done | bytes 23068688 | tf_op jit(solution)/shard_map/all_gather | solution.py:149
  534.1 12.3 fusion.108
  546.5 127.0 %all-gather.22.cloned.1.call-done = bf16[5632,2048]{1,0:T(8,128)(2,1)} async-done(((bf16[352,2048]{1,0:T(8,128)(2,1)}), bf16[5632,2048]{1,0:T(8,128)(2,1)}) %all-gather.22.cloned.1.call-update) | async-done | bytes 23068688 | tf_op jit(solution)/shard_map/all_gather | solution.py:150
  673.4 15.3 multiply_convert_fusion
  688.7 12.3 fusion.109
  701.0 13.7 multiply_reduce_fusion
  728.5 10.2 all-to-all-done.4
  740.1 38.8 %while.34 = (s32[]{:T(128)}, bf16[1024,256]{0,1:T(8,128)(2,1)}, f32[1024,1,64]{0,2,1:T(8,128)S(1)}, f32[1024,1,64]{0,2,1:T(8,128)S(1)}, bf16[1024,1,4,64]{0,3,2,...) while((s32[]{:T(128)}, bf16[1024,256]{0,1:T(8,128)(2,1)}, ...), condition=%wide.region_9.10_spmd.clone, body=%wide.region_7.9_spmd.clone.sunk | while | flops 1376647680 | bytes 118681872 | solution.py:220
  805.3 10.0 all_to_all.121
  822.4 12.2 convolution_convert_fusion.3
  834.7 12.2 convolution_convert_fusion.2
  848.0 12.3 convolution_convert_fusion.1
  860.3 62.0 %reduce-scatter.12.cloned.1.call-done = bf16[128,256]{1,0:T(8,128)(2,1)} async-done(((bf16[2048,256]{1,0:T(8,128)(2,1)}), bf16[128,256]{1,0:T(8,128)(2,1)}) %reduce-scatter.12.cloned.1.call-update) | async-done | bytes 65552 | tf_op jit(solution)/shard_map/reduce_scatter | solution.py:269
  922.3 106.6 %reduce-scatter.14.cloned.1.call-done = bf16[128,2048]{1,0:T(8,128)(2,1)} async-done(((bf16[2048,2048]{1,0:T(8,128)(2,1)}), bf16[128,2048]{1,0:T(8,128)(2,1)}) %reduce-scatter.14.cloned.1.call-update) | async-done | bytes 524304 | tf_op jit(solution)/shard_map/reduce_scatter | solution.py:272
  1029.0 105.6 %reduce-scatter.8.cloned.1.call-done = bf16[128,2048]{1,0:T(8,128)(2,1)} async-done(((bf16[2048,2048]{1,0:T(8,128)(2,1)}), bf16[128,2048]{1,0:T(8,128)(2,1)}) %reduce-scatter.8.cloned.1.call-update) | async-done | bytes 524304 | tf_op jit(solution)/shard_map/reduce_scatter | solution.py:263
  1134.6 182.5 %reduce-scatter.16.cloned.1.call-done = bf16[128,5632]{1,0:T(8,128)(2,1)} async-done(((bf16[2048,5632]{1,0:T(8,128)(2,1)}), bf16[128,5632]{1,0:T(8,128)(2,1)}) %reduce-scatter.16.cloned.1.call-update) | async-done | bytes 1441808 | tf_op jit(solution)/shard_map/reduce_scatter | solution.py:175
  1317.1 181.6 %reduce-scatter.18.cloned.1.call-done = bf16[128,5632]{1,0:T(8,128)(2,1)} async-done(((bf16[2048,5632]{1,0:T(8,128)(2,1)}), bf16[128,5632]{1,0:T(8,128)(2,1)}) %reduce-scatter.18.cloned.1.call-update) | async-done | bytes 1441808 | tf_op jit(solution)/shard_map/reduce_scatter | solution.py:178
  1498.7 180.8 %reduce-scatter.20.cloned.1.call-done = bf16[352,2048]{1,0:T(8,128)(2,1)} async-done(((bf16[5632,2048]{1,0:T(8,128)(2,1)}), bf16[352,2048]{1,0:T(8,128)(2,1)}) %reduce-scatter.20.cloned.1.call-update) | async-done | bytes 1441808 | tf_op jit(solution)/shard_map/reduce_scatter | solution.py:181
  1680.1 12.0 fusion.58
  1700.7 35.2 %all-reduce.6 = (bf16[16,128]{1,0:T(8,128)(2,1)S(1)}, bf16[16,128]{1,0:T(8,128)(2,1)S(1)}) all-reduce(bf16[16,128]{1,0:T(8,128)(2,1)S(1)} %bitcast.406, bf16[16,128]{1,0:T(8,128)(2,1)S(1)} %bitcast.407), channel_id=2, replica_groups=mesh['seq'=8,'fsdp'=16] {'fsdp'}, use_global_device_ids=true, to_apply=%region_14.15.clone | all-reduce | flops 4096 | bytes 16384
  1737.1 15.8 all-reduce.7
  1756.4 57.2 %all-reduce.11.cloned.1.call-done = (bf16[128,2048]{1,0:T(8,128)(2,1)}, bf16[128,256]{1,0:T(8,128)(2,1)}, bf16[128,256]{1,0:T(8,128)(2,1)}, bf16[128,2048]{1,0:T...) async-done(((bf16[128,2048]{1,0:T(8,128)(2,1)}, bf16[128,256]{1,0:T(8,128)(2,1)}, bf16[128,256]{1,0:T(8,128)(2,1)}, ...) | async-done | bytes 5505040 | tf_op jit(solution)/shard_map/psum | solution.py:278
  (228 shorter events, 180.7 us)
Async XLA Ops:
  7.2 98.3 %copy-start.2 = (bf16[1,128,2048]{2,1,0:T(8,128)(2,1)S(1)}, bf16[1,128,2048]{2,1,0:T(8,128)(2,1)}, u32[]{:S(2)}) copy-start(bf16[1,128,2048]{2,1,0:T(8,128)(2,1)} %param.16) | copy-start | bytes 1572868
  7.2 52.1 %all-gather.12.cloned.1.call-start = ((), (), s32[]{:S(2)}) async-start(), calls=%async_computation.16 | async-start | bytes 1114112 | tf_op jit(solution)/shard_map/all_gather | solution.py:96
  7.9 97.5 %all-gather.14.cloned.1.call-start = ((), (), s32[]{:S(2)}) async-start(), calls=%async_computation.17 | async-start | bytes 1114112 | tf_op jit(solution)/shard_map/all_gather | solution.py:97
  8.7 170.6 %all-gather.10.cloned.1.call-start = ((), (), s32[]{:S(2)}) async-start(), calls=%async_computation.15 | async-start | bytes 8912896 | tf_op jit(solution)/shard_map/all_gather | solution.py:95
  9.4 256.4 %all-gather.16.cloned.1.call-start = ((), (), s32[]{:S(2)}) async-start(), calls=%async_computation.18 | async-start | bytes 8912896 | tf_op jit(solution)/shard_map/all_gather | solution.py:98
  10.0 385.0 %all-gather.18.cloned.1.call-start = ((), (), s32[]{:S(2)}) async-start(), calls=%async_computation.19 | async-start | bytes 24510464 | tf_op jit(solution)/shard_map/all_gather | solution.py:148
  10.6 523.6 %all-gather.20.cloned.1.call-start = ((), (), s32[]{:S(2)}) async-start(), calls=%async_computation.20 | async-start | bytes 24510464 | tf_op jit(solution)/shard_map/all_gather | solution.py:149
  11.1 662.3 %all-gather.22.cloned.1.call-start = ((), (), s32[]{:S(2)}) async-start(), calls=%async_computation.21 | async-start | bytes 24510464 | tf_op jit(solution)/shard_map/all_gather | solution.py:150
  38.7 152.9 %copy-start.25 = (f32[16,1,128]{2,1,0:T(1,128)}, f32[16,1,128]{2,1,0:T(1,128)S(1)}, u32[]{:S(2)}) copy-start(f32[16,1,128]{2,1,0:T(1,128)S(1)} %convert_element_type.323) | copy-start | bytes 24580
  39.6 162.8 %copy-start.21 = (f32[128,64]{0,1:T(8,128)}, f32[128,64]{0,1:T(8,128)S(1)}, u32[]{:S(2)}) copy-start(f32[128,64]{0,1:T(8,128)S(1)} %get-tuple-element.382) | copy-start | bytes 98308
  39.6 162.8 %copy-start.23 = (f32[128,64]{0,1:T(8,128)}, f32[128,64]{0,1:T(8,128)S(1)}, u32[]{:S(2)}) copy-start(f32[128,64]{0,1:T(8,128)S(1)} %get-tuple-element.381) | copy-start | bytes 98308
  40.8 150.8 %copy-start.30 = (f32[128]{0:T(128)}, f32[128]{0:T(128)S(1)}, u32[]{:S(2)}) copy-start(f32[128]{0:T(128)S(1)} %fusion.67) | copy-start | bytes 1540
  40.9 150.8 %copy-start.27 = (f32[128]{0:T(128)}, f32[128]{0:T(128)S(1)}, u32[]{:S(2)}) copy-start(f32[128]{0:T(128)S(1)} %fusion.98) | copy-start | bytes 1540
  63.0 134.6 %all-to-all-start.1 = ((bf16[128,8,64]{0,2,1:T(8,128)(2,1)}), bf16[128,8,64]{0,2,1:T(8,128)(2,1)S(1)}, u32[]{:S(2)}, u32[]{:S(2)}) async-start(bf16[128,8,64]{0,2,1:T(8,128)(2,1)} %bitcast.26), calls=%async_computation.1 | async-start | bytes 262144 | tf_op jit(solution)/shard_map/all_to_all | solution.py:112
  198.3 9.5 all-to-all-start.2
  207.8 13.4 all-to-all-start
  239.4 26.1 %all-to-all-start.3 = ((bf16[8,128,256]{2,1,0:T(8,128)(2,1)}), bf16[8,128,256]{2,1,0:T(8,128)(2,1)S(1)}, u32[]{:S(2)}, u32[]{:S(2)}) async-start(bf16[8,128,256]{2,1,0:T(8,128)(2,1)} %bitcast.31), calls=%async_computation.3 | async-start | bytes 1048576 | tf_op jit(solution)/shard_map/all_to_all | solution.py:142
  271.4 443.3 %copy-start.4 = (f32[128,2048]{1,0:T(8,128)}, f32[128,2048]{1,0:T(8,128)S(1)}, u32[]{:S(2)}) copy-start(f32[128,2048]{1,0:T(8,128)S(1)} %get-tuple-element.384) | copy-start | bytes 3145732
  271.6 262.5 %copy-start.8 = (bf16[128,2048]{1,0:T(8,128)(2,1)}, bf16[128,2048]{1,0:T(8,128)(2,1)S(1)}, u32[]{:S(2)}) copy-start(bf16[128,2048]{1,0:T(8,128)(2,1)S(1)} %multiply_convert_fusion.2) | copy-start | bytes 1572868
  407.3 266.1 %copy-start.16 = (bf16[1,128,2048]{2,1,0:T(8,128)(2,1)S(1)}, bf16[1,128,2048]{2,1,0:T(8,128)(2,1)}, u32[]{:S(2)}) copy-start(bf16[1,128,2048]{2,1,0:T(8,128)(2,1)} %param.27) | copy-start | bytes 1572868
  724.4 14.4 all-to-all-start.4
  728.5 131.9 %reduce-scatter.10.cloned.1.call-start = ((), (), s32[]{:S(2)}) async-start(), calls=%async_computation.23 | async-start | bytes 1114112 | tf_op jit(solution)/shard_map/reduce_scatter | solution.py:266
  788.7 133.6 %reduce-scatter.12.cloned.1.call-start = ((), (), s32[]{:S(2)}) async-start(), calls=%async_computation.24 | async-start | bytes 1114112 | tf_op jit(solution)/shard_map/reduce_scatter | solution.py:269
  798.2 230.8 %reduce-scatter.14.cloned.1.call-start = ((), (), s32[]{:S(2)}) async-start(), calls=%async_computation.25 | async-start | bytes 8912896 | tf_op jit(solution)/shard_map/reduce_scatter | solution.py:272
  804.1 330.4 %reduce-scatter.8.cloned.1.call-start = ((), (), s32[]{:S(2)}) async-start(), calls=%async_computation.22 | async-start | bytes 8912896 | tf_op jit(solution)/shard_map/reduce_scatter | solution.py:263
  822.3 494.7 %reduce-scatter.16.cloned.1.call-start = ((), (), s32[]{:S(2)}) async-start(), calls=%async_computation.26 | async-start | bytes 24510464 | tf_op jit(solution)/shard_map/reduce_scatter | solution.py:175
  834.6 664.0 %reduce-scatter.18.cloned.1.call-start = ((), (), s32[]{:S(2)}) async-start(), calls=%async_computation.27 | async-start | bytes 24510464 | tf_op jit(solution)/shard_map/reduce_scatter | solution.py:178
  847.0 832.5 %reduce-scatter.20.cloned.1.call-start = ((), (), s32[]{:S(2)}) async-start(), calls=%async_computation.28 | async-start | bytes 24510464 | tf_op jit(solution)/shard_map/reduce_scatter | solution.py:181
  860.2 819.2 %copy-start.33 = (u32[128]{0:T(128)S(1)}, u32[128]{0:T(128)}, u32[]{:S(2)}) copy-start(u32[128]{0:T(128)} %constant.142) | copy-start | bytes 1540
  860.2 819.8 %copy-start.5 = (f32[128,2048]{1,0:T(8,128)S(1)}, f32[128,2048]{1,0:T(8,128)}, u32[]{:S(2)}) copy-start(f32[128,2048]{1,0:T(8,128)} %copy-done.4) | copy-start | bytes 3145732
  860.3 953.3 %all-reduce.11.cloned.1.call-start = ((), (), s32[]{:S(2)}) async-start(), calls=%async_computation.29 | async-start | bytes 11010048 | tf_op jit(solution)/shard_map/psum | solution.py:278
  1692.1 61.9 %copy-start.31 = (f32[128]{0:T(128)S(1)}, f32[128]{0:T(128)}, u32[]{:S(2)}) copy-start(f32[128]{0:T(128)} %copy-done.30) | copy-start | bytes 1540
  (24 other events, 388.8 us)
Sparse Core Ops, SparseCore 0:
  10.5 48.7 all-gather.11
  61.7 43.7 all-gather.13
  107.9 71.3 all-gather.9
  181.6 73.4 all-gather.15
  257.3 137.6 all-gather.17
  397.3 136.7 all-gather.19
  536.6 136.7 all-gather.21
  788.8 62.7 reduce-scatter.9
  856.5 65.7 reduce-scatter.11
  926.5 102.4 reduce-scatter.13
  1033.3 101.2 reduce-scatter.7
  1138.9 178.1 reduce-scatter.15
  1322.1 176.5 reduce-scatter.17
  1502.9 176.4 reduce-scatter.19
  1682.7 130.8 all-reduce.10
where the time goes:
time: 1840 us; the launch traced here: 1830 us
  waiting for transfers between devices  1410 us (77%)
  matrix products  195 us (11%)
  blocking collectives  126 us (7%)
  other arithmetic  35.6 us (2%)
  local copies, waits for them, and re-layouts  32.4 us (2%)
  starting transfers between devices  20.4 us (1%)
    reduce_scatter x1, waiting for transfers between devices, on_device(): lax.psum_scatter(gate_term.astype(jnp.bfloat16), 'fsdp', scatter_dimensio...  182 us
    reduce_scatter x1, waiting for transfers between devices, on_device(): lax.psum_scatter(up_term.astype(jnp.bfloat16), 'fsdp', scatter_dimension=...  182 us
    reduce_scatter x1, waiting for transfers between devices, on_device(): lax.psum_scatter(down_term.astype(jnp.bfloat16), 'fsdp', scatter_dimensio...  181 us
    all_gather x1, waiting for transfers between devices, on_device(): lax.all_gather(w_down, 'fsdp', axis=0, tiled=True)  127 us
    all_gather x1, waiting for transfers between devices, on_device(): lax.all_gather(w_up, 'fsdp', axis=0, tiled=True)  127 us
    all_gather x1, waiting for transfers between devices, on_device(): lax.all_gather(w_gate, 'fsdp', axis=0, tiled=True)  123 us
    reduce_scatter x1, waiting for transfers between devices, on_device(): lax.psum_scatter(output_term.astype(jnp.bfloat16), 'fsdp', scatter_dimens...  107 us
    reduce_scatter x1, waiting for transfers between devices, on_device(): lax.psum_scatter(query_term.astype(jnp.bfloat16), 'fsdp', scatter_dimensi...  106 us
  transfers between devices with their start and end apart: 20, of which 16 were waited for; matrix products, arithmetic and copies ran while one was open for 8% of the time, Pallas kernels for 0%

commit v1 on v0

v1 whole, which is shorter than its diff:
```python
import jax
import jax.numpy as jnp
from jax import lax
from jax.sharding import Mesh
from jax.sharding import PartitionSpec as P

H = 32
KV = 4
HD = 64
D = 2048
FF = 5632
B = 128
HALF = 512
HEADS = 4
FFL = 704
PIECE = 88

eps = 1e-05
theta = 10000.0
F32 = jnp.float32
BF16 = jnp.bfloat16
AXES = ("zlo", "y", "zhi", "x", "core")
FSDP = ("zhi", "x", "core")
SEQ = ("zlo", "y")


def matmul(left, right):
    return jnp.dot(left, right, preferred_element_type=F32)


def times_transposed(left, right):
    return lax.dot_general(left, right, (((1,), (1,)), ((), ())), preferred_element_type=F32)


def outer_sum(left, right):
    return lax.dot_general(left, right, (((0,), (0,)), ((), ())), preferred_element_type=F32)


def shift(value, axis, by):
    size = lax.axis_size(axis)
    return lax.ppermute(value, axis, [(i, (i + by) % size) for i in range(size)])


def swap_core(value):
    return shift(value, "core", 1)


def ring_gather(block, axis):
    half = block.shape[0] // 2
    before = shift(block, axis, 1)
    after = shift(block, axis, -1)
    far_low = shift(before[:half], axis, 1)
    far_high = shift(after[half:], axis, -1)
    return block, after, jnp.concatenate([far_low, far_high], axis=0), before


def small_gather(block, axis):
    return block, shift(block, axis, -1), shift(block, axis, 2), shift(block, axis, 1)


def ring_scatter(parts, axis):
    half = parts[2].shape[0] // 2
    far = parts[2].astype(BF16)
    low = shift(far[:half], axis, 1)
    high = shift(far[half:], axis, -1)
    after = jnp.concatenate([parts[1][:half] + low.astype(F32), parts[1][half:]], axis=0)
    before = jnp.concatenate([parts[3][:half], parts[3][half:] + high.astype(F32)], axis=0)
    from_before = shift(after.astype(BF16), axis, 1)
    from_after = shift(before.astype(BF16), axis, -1)
    return parts[0] + from_before.astype(F32) + from_after.astype(F32)


def gather_tokens(block):
    own = jnp.concatenate(ring_gather(block, "y"), axis=0)
    return jnp.concatenate([own, swap_core(own)], axis=0)


def scatter_tokens(partial):
    other = swap_core(partial[HALF:].astype(BF16))
    total = partial[:HALF] + other.astype(F32)
    return ring_scatter([total[i * B : (i + 1) * B] for i in range(4)], "y")


def turn(values):
    first, second = values[..., : HD // 2], values[..., HD // 2 :]
    return jnp.concatenate([-second, first], axis=-1)


def turn_back(values):
    first, second = values[..., : HD // 2], values[..., HD // 2 :]
    return jnp.concatenate([second, -first], axis=-1)


def own_rows(rows_all, y, core, per):
    return lax.dynamic_slice_in_dim(rows_all, (2 * y + core) * per, per, 0)


def on_device(
    layer_input,
    positions,
    attn_gain,
    w_query,
    w_key,
    w_value,
    w_output,
    mlp_gain,
    w_gate,
    w_up,
    w_down,
    out_grad,
):
    zlo = lax.axis_index("zlo")
    y = lax.axis_index("y")
    core = lax.axis_index("core")

    x_low = layer_input[0]
    inputs = x_low.astype(F32)
    scale_one = lax.rsqrt(jnp.mean(inputs * inputs, axis=-1, keepdims=True) + eps)
    x_all = gather_tokens(x_low)
    meta = jnp.concatenate([positions.astype(F32), scale_one.reshape(1, B)], axis=0)
    meta_own = jnp.concatenate(small_gather(meta, "y"), axis=1)
    meta_all = jnp.concatenate([meta_own, swap_core(meta_own)], axis=1)
    scale_all = meta_all[1][:, None]
    frequency = theta ** (-jnp.arange(0, HD, 2).astype(F32) / HD)
    angles = meta_all[0][:, None] * frequency
    angles = jnp.concatenate([angles, angles], axis=-1)
    cosine, sine = jnp.cos(angles)[:, None, :], jnp.sin(angles)[:, None, :]

    qkv_rows = jnp.concatenate([w_query, w_key, w_value], axis=1).astype(F32) * attn_gain[:, None]
    qkv_rows = qkv_rows.astype(BF16).T

    def qkv_of(core_index):
        return jnp.concatenate(
            [
                own_rows(qkv_rows, y, core_index, HEADS * HD),
                lax.dynamic_slice_in_dim(qkv_rows, H * HD + y * HD, HD, 0),
                lax.dynamic_slice_in_dim(qkv_rows, (H + KV) * HD + y * HD, HD, 0),
            ],
            axis=0,
        )

    def both_blocks(mine, for_other):
        got = swap_core(for_other)
        return jnp.where(core == 0, jnp.stack([mine, got]), jnp.stack([got, mine]))

    def gather_blocks(pair):
        got = shift(pair, "zhi", 1)
        zhi = lax.axis_index("zhi")
        column = jnp.where(zhi == 0, jnp.stack([pair, got]), jnp.stack([got, pair]))
        ring = jnp.stack(ring_gather(column, "x"))
        ring = jnp.roll(ring, lax.axis_index("x"), axis=0)
        return ring.transpose(3, 1, 0, 2, 4).reshape(pair.shape[1], D)

    qkv_full = gather_blocks(both_blocks(qkv_of(core), qkv_of(1 - core)))
    o_rows = lax.all_to_all(
        w_output.reshape(B, 16, B).transpose(1, 0, 2), FSDP, 0, 0, tiled=True
    ).reshape(D, B)
    o_full = gather_blocks(
        both_blocks(own_rows(o_rows, y, core, HEADS * HD), own_rows(o_rows, y, 1 - core, HEADS * HD))
    )

    def hidden_rows(weight):
        return (weight.astype(F32) * mlp_gain[:, None]).astype(BF16).T

    picked = jnp.where(zlo == 0, w_gate, w_up)
    picked = hidden_rows(picked).reshape(8, 2, 4, PIECE, B)
    picked = lax.dynamic_index_in_dim(picked, y, 2, keepdims=False)
    mine = lax.dynamic_index_in_dim(picked, core, 1, keepdims=False).reshape(FFL, B)
    for_other = lax.dynamic_index_in_dim(picked, 1 - core, 1, keepdims=False).reshape(FFL, B)
    pair = both_blocks(mine, for_other).reshape(2 * FFL, B)
    down_piece = lax.dynamic_slice(w_down, (y * PIECE, zlo * (D // 2)), (PIECE, D // 2))
    down_piece = down_piece.reshape(PIECE, 8, B).transpose(1, 0, 2).reshape(FFL, B)
    ff_piece = jnp.concatenate([pair, down_piece], axis=0)
    ff_all = lax.all_gather(ff_piece, ("zlo", "zhi", "x"), axis=0, tiled=False)
    ff_all = ff_all.reshape(2, 8, 3 * FFL, B)

    def column_blocks(blocks):
        return blocks.reshape(8, 2, FFL, B).transpose(2, 0, 1, 3).reshape(FFL, D)

    gate_full = column_blocks(ff_all[0, :, : 2 * FFL])
    up_full = column_blocks(ff_all[1, :, : 2 * FFL])
    down_full = ff_all[:, :, 2 * FFL :].reshape(2, 8, 8, PIECE, B)
    down_full = down_full.transpose(1, 3, 0, 2, 4).reshape(FFL, D)

    pre = times_transposed(x_all, qkv_full) * scale_all
    query_pre = pre[:, : HEADS * HD].reshape(2 * HALF, HEADS, HD)
    key_pre = pre[:, HEADS * HD : (HEADS + 1) * HD].reshape(2 * HALF, 1, HD)
    query = (query_pre * cosine + turn(query_pre) * sine).astype(BF16)
    key = (key_pre * cosine + turn(key_pre) * sine).astype(BF16)
    value = pre[:, (HEADS + 1) * HD :].astype(BF16).reshape(2 * HALF, 1, HD)
    key_value = jnp.concatenate([key, value], axis=1).reshape(2, HALF, 2, HD)
    earlier = lax.ppermute(key_value, "zlo", [(0, 1)])
    kv_all = jnp.concatenate([earlier, key_value], axis=1)
    key_all, value_all = kv_all[:, :, 0], kv_all[:, :, 1]
    query = query.reshape(2, HALF, HEADS, HD)

    at = jnp.arange(HALF, dtype=jnp.int32)
    at = ((at // B + y) % 4) * B + at % B
    allowed = jnp.concatenate(
        [jnp.broadcast_to(zlo == 1, (HALF, HALF)), at[:, None] >= at[None, :]], axis=1
    )
    score_scale = HD ** (-0.5)

    def scores_of(query_part, key_part):
        scores = jnp.einsum("qhd,kd->hqk", query_part, key_part, preferred_element_type=F32)
        return jnp.where(allowed, scores * score_scale, -1e30)

    def attend(query_part, key_part, value_part):
        scores = scores_of(query_part, key_part)
        top = jnp.max(scores, axis=-1, keepdims=True)
        weights = jnp.exp(scores - top)
        total = jnp.sum(weights, axis=-1, keepdims=True)
        low = (weights / total).astype(BF16)
        mixed = jnp.einsum("hqk,kd->qhd", low, value_part, preferred_element_type=F32)
        return mixed.reshape(HALF, HEADS * HD).astype(BF16), top + jnp.log(total)

    mixed_parts = [attend(query[s], key_all[s], value_all[s]) for s in range(2)]
    mixed = jnp.concatenate([m for m, _ in mixed_parts], axis=0)

    hidden = inputs + scatter_tokens(matmul(mixed, o_full))
    scale_two = lax.rsqrt(jnp.mean(hidden * hidden, axis=-1, keepdims=True) + eps)
    normed_all = gather_tokens((hidden * scale_two).astype(BF16))
    grad_all = gather_tokens(out_grad[0])

    gate_pre = times_transposed(normed_all, gate_full)
    upward = times_transposed(normed_all, up_full)
    sigmoid = 1.0 / (1.0 + jnp.exp(-gate_pre))
    silu = gate_pre * sigmoid
    activation = (silu * upward).astype(BF16)
    grad_act = times_transposed(grad_all, down_full)
    grad_up = (grad_act * silu).astype(BF16)
    grad_gate = (grad_act * upward * (sigmoid * (1.0 + gate_pre * (1.0 - sigmoid)))).astype(BF16)
    grad_normed_two = scatter_tokens(matmul(grad_gate, gate_full) + matmul(grad_up, up_full))
    result = hidden + scatter_tokens(matmul(activation, down_full))

    gate_term = outer_sum(grad_gate, normed_all).astype(BF16)
    up_term = outer_sum(grad_up, normed_all).astype(BF16)
    down_term = outer_sum(activation, grad_all).astype(BF16)

    def blocks_of(term):
        return term.reshape(FFL, 8, 2, B).transpose(1, 2, 0, 3).reshape(8, 2 * FFL, B)

    ff_terms = jnp.stack([blocks_of(gate_term), blocks_of(up_term)])
    down_blocks = down_term.reshape(8, PIECE, 2, 8, B).transpose(2, 0, 3, 1, 4)
    ff_terms = jnp.concatenate([ff_terms, down_blocks.reshape(2, 8, FFL, B)], axis=2)
    ff_sum = lax.psum_scatter(
        ff_terms.reshape(16, 3 * FFL, B), ("zlo", "zhi", "x"), scatter_dimension=0, tiled=True
    ).reshape(3 * FFL, B)

    mean_two = jnp.mean(grad_normed_two * hidden, axis=-1, keepdims=True)
    grad_hidden = (
        out_grad[0].astype(F32)
        + scale_two * grad_normed_two
        - hidden * (scale_two * scale_two * scale_two) * mean_two
    )
    hidden_grad_all = gather_tokens(grad_hidden.astype(BF16))
    grad_mixed = times_transposed(hidden_grad_all, o_full).astype(BF16)
    output_term = outer_sum(mixed, hidden_grad_all).astype(BF16)
    grad_mixed = grad_mixed.reshape(2, HALF, HEADS, HD)

    def attend_back(query_part, key_part, value_part, grad_part, log_total):
        weights = jnp.exp(scores_of(query_part, key_part) - log_total)
        low = weights.astype(BF16)
        grad_value = jnp.einsum("hqk,qhd->kd", low, grad_part, preferred_element_type=F32)
        grad_weights = jnp.einsum("qhd,kd->hqk", grad_part, value_part, preferred_element_type=F32)
        delta = jnp.sum(weights * grad_weights, axis=-1, keepdims=True)
        grad_scores = (weights * (grad_weights - delta) * score_scale).astype(BF16)
        grad_query = jnp.einsum("hqk,kd->qhd", grad_scores, key_part, preferred_element_type=F32)
        grad_key = jnp.einsum("hqk,qhd->kd", grad_scores, query_part, preferred_element_type=F32)
        return grad_query, grad_key, grad_value

    backs = [
        attend_back(query[s], key_all[s], value_all[s], grad_mixed[s], mixed_parts[s][1])
        for s in range(2)
    ]
    grad_query = jnp.concatenate([b[0] for b in backs], axis=0)
    grad_kv = jnp.stack([jnp.stack([b[1], b[2]], axis=1) for b in backs])
    later = lax.ppermute(grad_kv[:, :HALF].astype(BF16), "zlo", [(1, 0)])
    grad_kv = (grad_kv[:, HALF:] + later.astype(F32)).reshape(2 * HALF, 2, HD)
    grad_key, grad_value = grad_kv[:, :1], grad_kv[:, 1]
    grad_query = grad_query * cosine + turn_back(grad_query * sine)
    grad_key = grad_key * cosine + turn_back(grad_key * sine)
    grad_pre = jnp.concatenate(
        [grad_query.reshape(2 * HALF, HEADS * HD), grad_key.reshape(2 * HALF, HD), grad_value], axis=1
    )
    grad_normed = scatter_tokens(matmul(grad_pre.astype(BF16), qkv_full))
    mean_one = jnp.mean(grad_normed * inputs, axis=-1, keepdims=True)
    input_grad = (
        grad_hidden
        + scale_one * grad_normed
        - inputs * (scale_one * scale_one * scale_one) * mean_one
    )
    qkv_term = outer_sum((grad_pre * scale_all).astype(BF16), x_all).astype(BF16)

    attn_terms = jnp.concatenate([qkv_term, output_term], axis=0)
    rows = attn_terms.shape[0]
    attn_terms = attn_terms.reshape(2, rows // 2, 8, 2, B).transpose(0, 2, 3, 1, 4)
    attn_sum = lax.psum_scatter(
        attn_terms.reshape(16, rows, B), ("zlo", "zhi", "x"), scatter_dimension=0, tiled=True
    ).reshape(2, rows // 2, B)

    def own_block(pair):
        keep = lax.dynamic_index_in_dim(pair, core, 0, keepdims=False)
        got = swap_core(lax.dynamic_index_in_dim(pair, 1 - core, 0, keepdims=False))
        return jnp.where(core == 0, jnp.stack([keep, got]), jnp.stack([got, keep]))

    def both_zlo(part):
        got = shift(part, "zlo", 1)
        return jnp.where(zlo == 0, jnp.stack([part, got]), jnp.stack([got, part]))

    def all_y(part):
        ring = jnp.stack(ring_gather(part, "y"))
        return jnp.roll(ring, y, axis=0)

    attn_own = both_zlo(own_block(attn_sum))
    attn_own = attn_own.transpose(1, 0, 2, 3).reshape(2, rows, B)
    attn_own = all_y(attn_own)
    query_grad = attn_own[:, :, : HEADS * HD].reshape(D, B).T.astype(F32)
    key_grad = jnp.sum(attn_own[:, :, HEADS * HD : (HEADS + 1) * HD].astype(F32), axis=1)
    key_grad = key_grad.reshape(KV * HD, B).T
    value_grad = jnp.sum(attn_own[:, :, (HEADS + 1) * HD : (HEADS + 2) * HD].astype(F32), axis=1)
    value_grad = value_grad.reshape(KV * HD, B).T
    output_rows = attn_own[:, :, (HEADS + 2) * HD :].reshape(16, B, B)
    output_grad = lax.all_to_all(output_rows, FSDP, 0, 0, tiled=True)
    output_grad = output_grad.transpose(1, 0, 2).reshape(B, D).astype(F32)

    gu_own = both_zlo(
        jnp.concatenate(
            [own_block(ff_sum[: 2 * FFL].reshape(2, FFL, B)).reshape(2 * FFL, B), ff_sum[2 * FFL :]], axis=0
        )
    )
    ff_own = all_y(gu_own)
    gate_up = ff_own[:, :, : 2 * FFL].reshape(4, 2, 2, 8, PIECE, B)
    gate_up = gate_up.transpose(1, 3, 2, 0, 4, 5).reshape(2, FF, B)
    gate_grad = gate_up[0].T.astype(F32)
    up_grad = gate_up[1].T.astype(F32)
    down_grad = ff_own[:, :, 2 * FFL :].reshape(4, 2, 8, PIECE, B)
    down_grad = down_grad.transpose(0, 3, 1, 2, 4).reshape(4 * PIECE, D).astype(F32)

    attn_gain_grad = (
        jnp.sum(query_grad * w_query.astype(F32), axis=1)
        + jnp.sum(key_grad * w_key.astype(F32), axis=1)
        + jnp.sum(value_grad * w_value.astype(F32), axis=1)
    )
    mlp_gain_grad = jnp.sum(gate_grad * w_gate.astype(F32) + up_grad * w_up.astype(F32), axis=1)
    one, two = attn_gain[:, None], mlp_gain[:, None]
    return (
        result.astype(BF16)[None],
        input_grad.astype(BF16)[None],
        attn_gain_grad,
        query_grad * one,
        key_grad * one,
        value_grad * one,
        output_grad,
        mlp_gain_grad,
        gate_grad * two,
        up_grad * two,
        down_grad,
    )


def solution(mesh):
    split = Mesh(mesh.devices.reshape(2, 4, 2, 4, 2), AXES)
    tokens = P(FSDP, SEQ, None)
    rows = P(FSDP, None)
    gain = P(FSDP)
    in_specs = (
        tokens, P(FSDP, SEQ), gain, rows, rows, rows, rows, gain, rows, rows, rows, tokens,
    )
    out_specs = (tokens, tokens, gain, rows, rows, rows, rows, gain, rows, rows, rows)
    return jax.shard_map(
        on_device, mesh=split, in_specs=in_specs, out_specs=out_specs, check_vma=False
    )
```

time: 1840 us -> 824 us (0.45)
  waiting for transfers between devices: 1410 us -> 275 us
  starting transfers between devices: 20.4 us -> 168 us
  local copies, waits for them, and re-layouts: 32.4 us -> 165 us
  blocking collectives: 126 us -> 0 us
  matrix products: 195 us -> 132 us
  other arithmetic: 35.6 us -> 56.6 us
    reduce_scatter x7 -> x2, waiting for transfers between devices: 819 us -> 76.6 us  [the longest x1 76.5 us: on_device(): lax.psum_scatter(ff_terms.reshape(16, 3 * FFL, B), ('zlo', 'zhi', 'x'), s...]
    all_gather x7 -> x1, waiting for transfers between devices: 506 us -> 0.01 us  [on_device(): ff_all = lax.all_gather(ff_piece, ('zlo', 'zhi', 'x'), axis=0, tiled=False)]
    ppermute x0 -> x71, waiting for transfers between devices: none -> 197 us  [the longest x69 163 us: shift(): lax.ppermute(value, axis, [(i, (i + by) % size) for i in range(size)])]
    ppermute x0 -> x71, starting transfers between devices: none -> 140 us  [the longest x69 134 us: shift(): lax.ppermute(value, axis, [(i, (i + by) % size) for i in range(size)])]
    psum x1 -> x0, waiting for transfers between devices: 57.2 us -> none  [on_device(): lax.psum(attn_parts[1].astype(jnp.bfloat16), 'seq').astype(jnp.float32)]
    reshape x6 -> x12, local copies, waits for them, and re-layouts: 1.88 us -> 54.8 us  [the longest x4 22.4 us: blocks_of(): term.reshape(FFL, 8, 2, B).transpose(1, 2, 0, 3).reshape(8, 2 * FFL, B)]
    all_gather x2 -> x0, blocking collectives: 48.7 us -> none  [the longest x1 26.2 us: on_device(): lax.all_gather(attn_gain.astype(jnp.bfloat16), 'fsdp', axis=0, tiled=True)]
    unnamed x67 -> x193, local copies, waits for them, and re-layouts: 3.22 us -> 49.7 us
  transfers between devices with their start and end apart: 20 -> 76, of which waited for: 16 -> 33; matrix products, arithmetic and copies ran while one was open for 8% -> 21% of each run, Pallas kernels for 0% -> 0%
where the time goes in v1:
time: 824 us; the launch traced here: 813 us
  waiting for transfers between devices  275 us (33%)
  starting transfers between devices  168 us (20%)
  local copies, waits for them, and re-layouts  165 us (20%)
  matrix products  132 us (16%)
  other arithmetic  56.6 us (7%)
  between operations  16.1 us (2%)
    ppermute x69, waiting for transfers between devices, shift(): lax.ppermute(value, axis, [(i, (i + by) % size) for i in range(size)])  163 us
    ppermute x69, starting transfers between devices, shift(): lax.ppermute(value, axis, [(i, (i + by) % size) for i in range(size)])  134 us
    reduce_scatter x1, waiting for transfers between devices, on_device(): lax.psum_scatter(ff_terms.reshape(16, 3 * FFL, B), ('zlo', 'zhi', 'x'), s...  76.5 us
    unnamed x193, local copies, waits for them, and re-layouts  49.7 us
    ppermute x1, waiting for transfers between devices, on_device(): earlier = lax.ppermute(key_value, 'zlo', [(0, 1)])  33.4 us
    dot_general x2, matrix products, attend_back(): jnp.einsum('hqk,kd->qhd', grad_scores, key_part, preferred_element_type=F32)  26.1 us
    dot_general x2, matrix products, attend_back(): jnp.einsum('hqk,qhd->kd', grad_scores, query_part, preferred_element_type...  26 us
    reshape x4, local copies, waits for them, and re-layouts, blocks_of(): term.reshape(FFL, 8, 2, B).transpose(1, 2, 0, 3).reshape(8, 2 * FFL, B)  22.4 us
  transfers between devices with their start and end apart: 76, of which 33 were waited for; matrix products, arithmetic and copies ran while one was open for 21% of the time, Pallas kernels for 0%

profile of v1, /device:TPU:1, one launch (start us, length us, event | category | flops | bytes accessed | tf_op | source)
XLA Modules:
  0.0 813.1 jit_solution(8556096693885530242)
XLA Ops:
  19.6 9.4 %all-to-all-start = ((bf16[16,128,128]{1,2,0:T(8,128)(2,1)}), bf16[16,128,128]{1,2,0:T(8,128)(2,1)}, u32[]{:S(2)}, u32[]{:S(2)}) async-start(bf16[16,128,128]{1,2,0:T(8,128)(2,1)} %bitcast.45), calls=%async_computation | async-start | bytes 1048576 | tf_op jit(solution)/shard_map/all_to_all | solution.py:155
  73.9 20.0 %collective-permute-done.17 = bf16[2,256,128]{2,1,0:T(8,128)(2,1)S(1)} collective-permute-done((bf16[2,256,128]{2,1,0:T(8,128)(2,1)S(1)}, bf16[2,256,128]{2,1,0:T(8,128)(2,1)S(1)}, u32[]{:S(2)}, u32[]{:S(2)}) %collective-permute-start.17) | collective-permute-done | bytes 131104 | tf_op jit(solution)/shard_map/ppermute | solution.py:41
  105.4 11.1 %collective-permute-done.9 = bf16[1,2,384,128]{2,3,1,0:T(8,128)(2,1)S(1)} collective-permute-done((bf16[1,2,384,128]{2,3,1,0:T(8,128)(2,1)S(1)}, bf16[1,2,384,128]{2,3,1,0:T(8,128)(2,1)S(1)}, u32[]{:S(2)}, u32[]{:S(2)}) %collective-permute-start.9) | collective-permute-done | bytes 196640 | tf_op jit(solution)/shard_map/ppermute | solution.py:41
  120.2 6.1 collective-permute-done.20
  144.0 33.4 %collective-permute-done.15 = bf16[2,512,2,64]{1,3,2,0:T(8,128)(2,1)S(1)} collective-permute-done((bf16[2,512,2,64]{1,3,2,0:T(8,128)(2,1)S(1)}, bf16[2,512,2,64]{1,3,2,0:T(8,128)(2,1)S(1)}, u32[]{:S(2)}, u32[]{:S(2)}) %collective-permute-start.15) | collective-permute-done | bytes 262176 | tf_op jit(solution)/shard_map/ppermute | solution.py:192
  197.6 22.5 %collective-permute-start.38 = (bf16[128,2048]{1,0:T(8,128)(2,1)S(1)}, bf16[128,2048]{1,0:T(8,128)(2,1)S(1)}, u32[]{:S(2)}, u32[]{:S(2)}) collective-permute-start(bf16[128,2048]{1,0:T(8,128)(2,1)S(1)} %bitcast.436), channel_id=1, source_target_pairs={{0,48},{16,0},{32,16},{48,32},{1,49},{17,1},{33,17},{49,33},{2,50}... | collective-permute-start | bytes 1572872 | tf_op jit(solution)/shard_map/ppermute | solution.py:41
  227.1 9.4 %collective-permute-done.38 = bf16[128,2048]{1,0:T(8,128)(2,1)S(1)} collective-permute-done((bf16[128,2048]{1,0:T(8,128)(2,1)S(1)}, bf16[128,2048]{1,0:T(8,128)(2,1)S(1)}, u32[]{:S(2)}, u32[]{:S(2)}) %collective-permute-start.38) | collective-permute-done | bytes 524320 | tf_op jit(solution)/shard_map/ppermute | solution.py:41
  238.1 9.5 %collective-permute-done.26 = bf16[128,2048]{1,0:T(8,128)(2,1)S(1)} collective-permute-done((bf16[128,2048]{1,0:T(8,128)(2,1)S(1)}, bf16[128,2048]{1,0:T(8,128)(2,1)S(1)}, u32[]{:S(2)}, u32[]{:S(2)}) %collective-permute-start.26) | collective-permute-done | bytes 524320 | tf_op jit(solution)/shard_map/ppermute | solution.py:41
  293.9 7.6 reshape.959
  301.5 6.4 copy.94
  307.9 7.4 reshape.960
  319.2 5.6 reshape.962
  324.7 6.0 fusion.160
  336.0 5.5 multiply_convert_fusion
  376.0 7.4 collective-permute-done.47
  383.4 11.2 %collective-permute-done.37 = bf16[128,2048]{1,0:T(8,128)(2,1)S(1)} collective-permute-done((bf16[128,2048]{1,0:T(8,128)(2,1)S(1)}, bf16[128,2048]{1,0:T(8,128)(2,1)S(1)}, u32[]{:S(2)}, u32[]{:S(2)}) %collective-permute-start.37) | collective-permute-done | bytes 524320 | tf_op jit(solution)/shard_map/ppermute | solution.py:41
  400.8 10.2 %collective-permute-done.49 = bf16[128,2048]{1,0:T(8,128)(2,1)S(1)} collective-permute-done((bf16[128,2048]{1,0:T(8,128)(2,1)S(1)}, bf16[128,2048]{1,0:T(8,128)(2,1)S(1)}, u32[]{:S(2)}, u32[]{:S(2)}) %collective-permute-start.49) | collective-permute-done | bytes 524320 | tf_op jit(solution)/shard_map/ppermute | solution.py:41
  436.7 13.6 %fusion.38 = f32[1024,1,64]{0,2,1:T(8,128)S(1)} fusion(f32[1024,512,4]{1,0,2:T(8,128)} %fusion.139, f32[4,512,1024]{1,2,0:T(8,128)} %copy-done.3, f32[4,512]{1,0:T(4,128)S(1)} %log_add_fusion, bf16[1024,4,64]{0,2,1:T(8,128)(2,1)S(1)} %copy-done.35), kind=kOutput, calls=%fused_computation.82 | convolution fusion | flops 283118592 | bytes 34095104 | tf_op jit(solution)/shard_map/hqk,qhd->kd/dot_general | solution.py:269
  450.3 13.6 %fusion.28 = f32[64,4,512]{2,0,1:T(8,128)S(1)} fusion(bf16[1024,64,1]{0,1,2:T(8,128)(2,1)S(1)} %fusion.104, f32[1024,512,4]{1,0,2:T(8,128)} %fusion.139, f32[4,512,1024]{1,2,0:T(8,128)} %copy-done.3, f32[4,512]{1,0:T(4,128)S(1)} %log_add_fusion), kind=kOutput, calls=%fused_computation.63 | convolution fusion | flops 283118592 | bytes 17440768 | tf_op jit(solution)/shard_map/hqk,kd->qhd/dot_general | solution.py:268
  473.3 12.4 %fusion.39 = f32[1024,1,64]{0,2,1:T(8,128)S(1)} fusion(f32[1024,512,4]{1,0,2:T(8,128)} %fusion.136, f32[4,512,1024]{1,2,0:T(8,128)} %copy-done.2, f32[4,512]{1,0:T(4,128)S(1)} %log_add_fusion.1, bf16[1024,4,64]{0,2,1:T(8,128)(2,1)S(1)} %copy-done.35), kind=kOutput, calls=%fused_computation.83 | convolution fusion | flops 283118592 | bytes 34095104 | tf_op jit(solution)/shard_map/hqk,qhd->kd/dot_general | solution.py:269
  488.2 12.5 %fusion.25 = f32[64,4,512]{2,0,1:T(8,128)S(1)} fusion(f32[1024,512,4]{1,0,2:T(8,128)} %fusion.136, f32[4,512,1024]{1,2,0:T(8,128)} %copy-done.2, f32[4,512]{1,0:T(4,128)S(1)} %log_add_fusion.1, bf16[2,512,2,64]{1,3,2,0:T(8,128)(2,1)S(1)} %collective-permute-done.15, bf16[2,512,2,64]{1,3,2,0:T(8,128)(2,1)S(1)} %constant_dynamic-update-slice_fusion.18), kind=kOutput, calls=%fused_computation.60 | convolution fusion | flops 283380736 | bytes 34619392 | tf_op jit(solution)/shard_map/hqk,kd->qhd/dot_general | solution.py:268
  520.4 5.5 fusion.29
  529.2 6.6 convolution_convert_fusion.2
  535.8 7.7 reshape.972
  547.8 6.7 convolution_convert_fusion.1
  554.5 7.7 reshape.973
  583.8 6.4 collective-permute-done.55
  596.6 10.6 %collective-permute-start.59 = (bf16[320,128]{1,0:T(8,128)(2,1)S(1)}, bf16[320,128]{1,0:T(8,128)(2,1)S(1)}, u32[]{:S(2)}, u32[]{:S(2)}) collective-permute-start(bf16[320,128]{1,0:T(8,128)(2,1)S(1)} %get-tuple-element.155), channel_id=1, source_target_pairs={{0,1},{1,0},{2,3},{3,2},{4,5},{5,4},{6,7},{7,6},{8,9},{9,8},{10,11... | collective-permute-start | bytes 245768 | tf_op jit(solution)/shard_map/ppermute | solution.py:41
  631.0 76.5 %reduce-scatter.5.cloned.1.call-done = bf16[1,2112,128]{2,1,0:T(8,128)(2,1)} async-done(((bf16[16,2112,128]{2,1,0:T(8,128)(2,1)}), bf16[1,2112,128]{2,1,0:T(8,128)(2,1)}) %reduce-scatter.5.cloned.1.call-update) | async-done | bytes 540688 | tf_op jit(solution)/shard_map/reduce_scatter | solution.py:246
  716.7 18.9 %all-to-all-start.1 = ((bf16[16,128,128]{2,1,0:T(8,128)(2,1)}), bf16[16,128,128]{2,1,0:T(8,128)(2,1)}, u32[]{:S(2)}, u32[]{:S(2)}) async-start(bf16[16,128,128]{2,1,0:T(8,128)(2,1)} %bitcast.128), calls=%async_computation.2 | async-start | bytes 1048576 | tf_op jit(solution)/shard_map/all_to_all | solution.py:324
  755.7 11.5 %collective-permute-done.68 = bf16[2,2112,128]{2,1,0:T(8,128)(2,1)S(1)} collective-permute-done((bf16[2,2112,128]{2,1,0:T(8,128)(2,1)}, bf16[2,2112,128]{2,1,0:T(8,128)(2,1)S(1)}, u32[]{:S(2)}, u32[]{:S(2)}) %collective-permute-start.68) | collective-permute-done | bytes 1081376 | tf_op jit(solution)/shard_map/ppermute | solution.py:41
  770.3 11.3 %collective-permute-done.69 = bf16[1,2112,128]{2,1,0:T(8,128)(2,1)S(1)} collective-permute-done((bf16[1,2112,128]{2,1,0:T(8,128)(2,1)S(1)}, bf16[1,2112,128]{2,1,0:T(8,128)(2,1)S(1)}, u32[]{:S(2)}, u32[]{:S(2)}) %collective-permute-start.69) | collective-permute-done | bytes 540704 | tf_op jit(solution)/shard_map/ppermute | solution.py:41
  (527 shorter events, 386.7 us)
Async XLA Ops:
  10.3 33.3 %collective-permute-start.12 = (f32[2,128]{1,0:T(2,128)}, f32[2,128]{1,0:T(2,128)}, u32[]{:S(2)}, u32[]{:S(2)}) collective-permute-start(f32[2,128]{1,0:T(2,128)} %get-tuple-element.170), channel_id=1, source_target_pairs={{0,32},{16,48},{32,0},{48,16},{1,33},{17,49},{33,1},{49,17},{2,34}... | collective-permute-start | bytes 3080 | tf_op jit(solution)/shard_map/ppermute | solution.py:41
  14.1 29.7 %collective-permute-start.11 = (f32[2,128]{1,0:T(2,128)}, f32[2,128]{1,0:T(2,128)}, u32[]{:S(2)}, u32[]{:S(2)}) collective-permute-start(f32[2,128]{1,0:T(2,128)} %get-tuple-element.170), channel_id=1, source_target_pairs={{0,48},{16,0},{32,16},{48,32},{1,49},{17,1},{33,17},{49,33},{2,50}... | collective-permute-start | bytes 3080 | tf_op jit(solution)/shard_map/ppermute | solution.py:41
  14.9 29.3 %collective-permute-start.13 = (f32[2,128]{1,0:T(2,128)}, f32[2,128]{1,0:T(2,128)}, u32[]{:S(2)}, u32[]{:S(2)}) collective-permute-start(f32[2,128]{1,0:T(2,128)} %get-tuple-element.170), channel_id=1, source_target_pairs={{0,16},{16,32},{32,48},{48,0},{1,17},{17,33},{33,49},{49,1},{2,18}... | collective-permute-start | bytes 3080 | tf_op jit(solution)/shard_map/ppermute | solution.py:41
  15.5 48.1 %collective-permute-start = (bf16[128,2048]{1,0:T(8,128)(2,1)}, bf16[128,2048]{1,0:T(8,128)(2,1)}, u32[]{:S(2)}, u32[]{:S(2)}) collective-permute-start(bf16[128,2048]{1,0:T(8,128)(2,1)} %bitcast.401), channel_id=1, source_target_pairs={{0,48},{16,0},{32,16},{48,32},{1,49},{17,1},{33,17},{49,33},{2,50}... | collective-permute-start | bytes 1572872 | tf_op jit(solution)/shard_map/ppermute | solution.py:41
  17.5 50.1 %collective-permute-start.1 = (bf16[128,2048]{1,0:T(8,128)(2,1)}, bf16[128,2048]{1,0:T(8,128)(2,1)}, u32[]{:S(2)}, u32[]{:S(2)}) collective-permute-start(bf16[128,2048]{1,0:T(8,128)(2,1)} %bitcast.402), channel_id=1, source_target_pairs={{0,16},{16,32},{32,48},{48,0},{1,17},{17,33},{33,49},{49,1},{2,18}... | collective-permute-start | bytes 1572872 | tf_op jit(solution)/shard_map/ppermute | solution.py:41
  19.6 41.1 %all-to-all-start = ((bf16[16,128,128]{1,2,0:T(8,128)(2,1)}), bf16[16,128,128]{1,2,0:T(8,128)(2,1)}, u32[]{:S(2)}, u32[]{:S(2)}) async-start(bf16[16,128,128]{1,2,0:T(8,128)(2,1)} %bitcast.45), calls=%async_computation | async-start | bytes 1048576 | tf_op jit(solution)/shard_map/all_to_all | solution.py:155
  29.0 252.1 %all-gather.3.cloned.1.call-start = ((), (), s32[]{:S(2)}) async-start(), calls=%async_computation.6 | async-start | bytes 9191424 | tf_op jit(solution)/shard_map/all_gather | solution.py:174
  53.1 542.6 %reduce-scatter.3.cloned.1.call-start = ((), (), s32[]{:S(2)}) async-start(), calls=%async_computation.4 | async-start | bytes 2785280 | tf_op jit(solution)/shard_map/reduce_scatter | solution.py:298
  57.0 37.0 %collective-permute-start.8 = (bf16[2,2,384,128]{2,3,1,0:T(8,128)(2,1)S(1)}, bf16[2,2,384,128]{2,3,1,0:T(8,128)(2,1)S(1)}, u32[]{:S(2)}, u32[]{:S(2)}) collective-permute-start(bf16[2,2,384,128]{2,3,1,0:T(8,128)(2,1)S(1)} %maximum_select_fusion.3), channel_id=1, source_target_pairs={{0,2},{2,4},{4,6},{6,0},{1,3},{3,5},{5,7},{7,1},{8,10},{10,12},{12... | collective-permute-start | bytes 1179656 | tf_op jit(solution)/shard_map/ppermute | solution.py:41
  58.6 38.1 %collective-permute-start.7 = (bf16[2,2,384,128]{2,3,1,0:T(8,128)(2,1)S(1)}, bf16[2,2,384,128]{2,3,1,0:T(8,128)(2,1)S(1)}, u32[]{:S(2)}, u32[]{:S(2)}) collective-permute-start(bf16[2,2,384,128]{2,3,1,0:T(8,128)(2,1)S(1)} %maximum_select_fusion.3), channel_id=1, source_target_pairs={{0,6},{2,0},{4,2},{6,4},{1,7},{3,1},{5,3},{7,5},{8,14},{10,8},{12,... | collective-permute-start | bytes 1179656 | tf_op jit(solution)/shard_map/ppermute | solution.py:41
  64.6 36.0 %collective-permute-start.3 = (bf16[64,2048]{1,0:T(8,128)(2,1)S(1)}, bf16[64,2048]{1,0:T(8,128)(2,1)S(1)}, u32[]{:S(2)}, u32[]{:S(2)}) collective-permute-start(bf16[64,2048]{1,0:T(8,128)(2,1)S(1)} %slice.442), channel_id=1, source_target_pairs={{0,48},{16,0},{32,16},{48,32},{1,49},{17,1},{33,17},{49,33},{2,50}... | collective-permute-start | bytes 786440 | tf_op jit(solution)/shard_map/ppermute | solution.py:41
  68.6 28.4 %collective-permute-start.2 = (bf16[64,2048]{1,0:T(8,128)(2,1)S(1)}, bf16[64,2048]{1,0:T(8,128)(2,1)S(1)}, u32[]{:S(2)}, u32[]{:S(2)}) collective-permute-start(bf16[64,2048]{1,0:T(8,128)(2,1)S(1)} %slice.441), channel_id=1, source_target_pairs={{0,16},{16,32},{32,48},{48,0},{1,17},{17,33},{33,49},{49,1},{2,18}... | collective-permute-start | bytes 786440 | tf_op jit(solution)/shard_map/ppermute | solution.py:41
  70.8 23.1 %collective-permute-start.17 = (bf16[2,256,128]{2,1,0:T(8,128)(2,1)S(1)}, bf16[2,256,128]{2,1,0:T(8,128)(2,1)S(1)}, u32[]{:S(2)}, u32[]{:S(2)}) collective-permute-start(bf16[2,256,128]{2,1,0:T(8,128)(2,1)S(1)} %maximum_select_fusion.14), channel_id=1, source_target_pairs={{0,8},{8,0},{1,9},{9,1},{2,10},{10,2},{3,11},{11,3},{4,12},{12,4},... | collective-permute-start | bytes 393224 | tf_op jit(solution)/shard_map/ppermute | solution.py:41
  93.9 23.2 %collective-permute-start.19 = (bf16[2,2,256,128]{3,2,1,0:T(8,128)(2,1)S(1)}, bf16[2,2,256,128]{3,2,1,0:T(8,128)(2,1)S(1)}, u32[]{:S(2)}, u32[]{:S(2)}) collective-permute-start(bf16[2,2,256,128]{3,2,1,0:T(8,128)(2,1)S(1)} %maximum_select_fusion.8), channel_id=1, source_target_pairs={{0,2},{2,4},{4,6},{6,0},{1,3},{3,5},{5,7},{7,1},{8,10},{10,12},{12... | collective-permute-start | bytes 786440 | tf_op jit(solution)/shard_map/ppermute | solution.py:41
  94.0 23.4 %collective-permute-start.18 = (bf16[2,2,256,128]{3,2,1,0:T(8,128)(2,1)S(1)}, bf16[2,2,256,128]{3,2,1,0:T(8,128)(2,1)S(1)}, u32[]{:S(2)}, u32[]{:S(2)}) collective-permute-start(bf16[2,2,256,128]{3,2,1,0:T(8,128)(2,1)S(1)} %maximum_select_fusion.8), channel_id=1, source_target_pairs={{0,6},{2,0},{4,2},{6,4},{1,7},{3,1},{5,3},{7,5},{8,14},{10,8},{12,... | collective-permute-start | bytes 786440 | tf_op jit(solution)/shard_map/ppermute | solution.py:41
  96.7 19.7 %collective-permute-start.9 = (bf16[1,2,384,128]{2,3,1,0:T(8,128)(2,1)S(1)}, bf16[1,2,384,128]{2,3,1,0:T(8,128)(2,1)S(1)}, u32[]{:S(2)}, u32[]{:S(2)}) collective-permute-start(bf16[1,2,384,128]{2,3,1,0:T(8,128)(2,1)S(1)} %slice.443), channel_id=1, source_target_pairs={{0,2},{2,4},{4,6},{6,0},{1,3},{3,5},{5,7},{7,1},{8,10},{10,12},{12... | collective-permute-start | bytes 589832 | tf_op jit(solution)/shard_map/ppermute | solution.py:41
  97.0 19.5 %collective-permute-start.10 = (bf16[1,2,384,128]{2,3,1,0:T(8,128)(2,1)S(1)}, bf16[1,2,384,128]{2,3,1,0:T(8,128)(2,1)S(1)}, u32[]{:S(2)}, u32[]{:S(2)}) collective-permute-start(bf16[1,2,384,128]{2,3,1,0:T(8,128)(2,1)S(1)} %slice.444), channel_id=1, source_target_pairs={{0,6},{2,0},{4,2},{6,4},{1,7},{3,1},{5,3},{7,5},{8,14},{10,8},{12,... | collective-permute-start | bytes 589832 | tf_op jit(solution)/shard_map/ppermute | solution.py:41
  103.5 24.5 %collective-permute-start.4 = (bf16[512,2048]{1,0:T(8,128)(2,1)}, bf16[512,2048]{1,0:T(8,128)(2,1)}, u32[]{:S(2)}, u32[]{:S(2)}) collective-permute-start(bf16[512,2048]{1,0:T(8,128)(2,1)} %get-tuple-element.123), channel_id=1, source_target_pairs={{0,1},{1,0},{2,3},{3,2},{4,5},{5,4},{6,7},{7,6},{8,9},{9,8},{10,11... | collective-permute-start | bytes 6291464 | tf_op jit(solution)/shard_map/ppermute | solution.py:41
  140.1 37.3 %collective-permute-start.15 = (bf16[2,512,2,64]{1,3,2,0:T(8,128)(2,1)S(1)}, bf16[2,512,2,64]{1,3,2,0:T(8,128)(2,1)S(1)}, u32[]{:S(2)}, u32[]{:S(2)}) collective-permute-start(bf16[2,512,2,64]{1,3,2,0:T(8,128)(2,1)S(1)} %constant_dynamic-update-slice_fusion.18), channel_id=1, source_target_pairs={{0,64},{1,65},{2,66},{3,67},{4,68},{5,69},{6,70},{7,71},{8,72},{9,... | collective-permute-start | bytes 786440 | tf_op jit(solution)/shard_map/ppermute | solution.py:192
  194.9 25.3 %collective-permute-start.23 = (bf16[64,2048]{1,0:T(8,128)(2,1)S(1)}, bf16[64,2048]{1,0:T(8,128)(2,1)S(1)}, u32[]{:S(2)}, u32[]{:S(2)}) collective-permute-start(bf16[64,2048]{1,0:T(8,128)(2,1)S(1)} %get-tuple-element.84), channel_id=1, source_target_pairs={{0,16},{16,32},{32,48},{48,0},{1,17},{17,33},{33,49},{49,1},{2,18}... | collective-permute-start | bytes 786440 | tf_op jit(solution)/shard_map/ppermute | solution.py:41
  195.0 30.2 %collective-permute-start.25 = (bf16[64,2048]{1,0:T(8,128)(2,1)S(1)}, bf16[64,2048]{1,0:T(8,128)(2,1)S(1)}, u32[]{:S(2)}, u32[]{:S(2)}) collective-permute-start(bf16[64,2048]{1,0:T(8,128)(2,1)S(1)} %get-tuple-element.85), channel_id=1, source_target_pairs={{0,48},{16,0},{32,16},{48,32},{1,49},{17,1},{33,17},{49,33},{2,50}... | collective-permute-start | bytes 786440 | tf_op jit(solution)/shard_map/ppermute | solution.py:41
  197.6 38.8 %collective-permute-start.38 = (bf16[128,2048]{1,0:T(8,128)(2,1)S(1)}, bf16[128,2048]{1,0:T(8,128)(2,1)S(1)}, u32[]{:S(2)}, u32[]{:S(2)}) collective-permute-start(bf16[128,2048]{1,0:T(8,128)(2,1)S(1)} %bitcast.436), channel_id=1, source_target_pairs={{0,48},{16,0},{32,16},{48,32},{1,49},{17,1},{33,17},{49,33},{2,50}... | collective-permute-start | bytes 1572872 | tf_op jit(solution)/shard_map/ppermute | solution.py:41
  225.3 22.3 %collective-permute-start.26 = (bf16[128,2048]{1,0:T(8,128)(2,1)S(1)}, bf16[128,2048]{1,0:T(8,128)(2,1)S(1)}, u32[]{:S(2)}, u32[]{:S(2)}) collective-permute-start(bf16[128,2048]{1,0:T(8,128)(2,1)S(1)} %pad_maximum_fusion.10), channel_id=1, source_target_pairs={{0,48},{16,0},{32,16},{48,32},{1,49},{17,1},{33,17},{49,33},{2,50}... | collective-permute-start | bytes 1572872 | tf_op jit(solution)/shard_map/ppermute | solution.py:41
  226.4 21.3 %collective-permute-start.24 = (bf16[128,2048]{1,0:T(8,128)(2,1)S(1)}, bf16[128,2048]{1,0:T(8,128)(2,1)S(1)}, u32[]{:S(2)}, u32[]{:S(2)}) collective-permute-start(bf16[128,2048]{1,0:T(8,128)(2,1)S(1)} %pad_maximum_fusion.9), channel_id=1, source_target_pairs={{0,16},{16,32},{32,48},{48,0},{1,17},{17,33},{33,49},{49,1},{2,18}... | collective-permute-start | bytes 1572872 | tf_op jit(solution)/shard_map/ppermute | solution.py:41
  254.4 21.4 %collective-permute-start.42 = (bf16[512,2048]{1,0:T(8,128)(2,1)S(1)}, bf16[512,2048]{1,0:T(8,128)(2,1)S(1)}, u32[]{:S(2)}, u32[]{:S(2)}) collective-permute-start(bf16[512,2048]{1,0:T(8,128)(2,1)S(1)} %get-tuple-element.113), channel_id=1, source_target_pairs={{0,1},{1,0},{2,3},{3,2},{4,5},{5,4},{6,7},{7,6},{8,9},{9,8},{10,11... | collective-permute-start | bytes 6291464 | tf_op jit(solution)/shard_map/ppermute | solution.py:41
  372.9 21.8 %collective-permute-start.37 = (bf16[128,2048]{1,0:T(8,128)(2,1)S(1)}, bf16[128,2048]{1,0:T(8,128)(2,1)S(1)}, u32[]{:S(2)}, u32[]{:S(2)}) collective-permute-start(bf16[128,2048]{1,0:T(8,128)(2,1)S(1)} %pad_maximum_fusion.12), channel_id=1, source_target_pairs={{0,48},{16,0},{32,16},{48,32},{1,49},{17,1},{33,17},{49,33},{2,50}... | collective-permute-start | bytes 1572872 | tf_op jit(solution)/shard_map/ppermute | solution.py:41
  375.9 18.8 %collective-permute-start.35 = (bf16[128,2048]{1,0:T(8,128)(2,1)S(1)}, bf16[128,2048]{1,0:T(8,128)(2,1)S(1)}, u32[]{:S(2)}, u32[]{:S(2)}) collective-permute-start(bf16[128,2048]{1,0:T(8,128)(2,1)S(1)} %pad_maximum_fusion.11), channel_id=1, source_target_pairs={{0,16},{16,32},{32,48},{48,0},{1,17},{17,33},{33,49},{49,1},{2,18}... | collective-permute-start | bytes 1572872 | tf_op jit(solution)/shard_map/ppermute | solution.py:41
  519.9 187.5 %reduce-scatter.5.cloned.1.call-start = ((), (), s32[]{:S(2)}) async-start(), calls=%async_computation.5 | async-start | bytes 9191424 | tf_op jit(solution)/shard_map/reduce_scatter | solution.py:246
  713.6 25.1 %collective-permute-start.66 = (bf16[2112,128]{1,0:T(8,128)(2,1)}, bf16[2112,128]{1,0:T(8,128)(2,1)S(1)}, u32[]{:S(2)}, u32[]{:S(2)}) collective-permute-start(bf16[2112,128]{1,0:T(8,128)(2,1)} %get-tuple-element.104), channel_id=1, source_target_pairs={{0,64},{64,0},{1,65},{65,1},{2,66},{66,2},{3,67},{67,3},{4,68},{68... | collective-permute-start | bytes 1622024 | tf_op jit(solution)/shard_map/ppermute | solution.py:41
  716.7 30.4 %all-to-all-start.1 = ((bf16[16,128,128]{2,1,0:T(8,128)(2,1)}), bf16[16,128,128]{2,1,0:T(8,128)(2,1)}, u32[]{:S(2)}, u32[]{:S(2)}) async-start(bf16[16,128,128]{2,1,0:T(8,128)(2,1)} %bitcast.128), calls=%async_computation.2 | async-start | bytes 1048576 | tf_op jit(solution)/shard_map/all_to_all | solution.py:324
  739.9 27.3 %collective-permute-start.68 = (bf16[2,2112,128]{2,1,0:T(8,128)(2,1)}, bf16[2,2112,128]{2,1,0:T(8,128)(2,1)S(1)}, u32[]{:S(2)}, u32[]{:S(2)}) collective-permute-start(bf16[2,2112,128]{2,1,0:T(8,128)(2,1)} %maximum_select_fusion.1), channel_id=1, source_target_pairs={{0,16},{16,32},{32,48},{48,0},{1,17},{17,33},{33,49},{49,1},{2,18}... | collective-permute-start | bytes 3244040 | tf_op jit(solution)/shard_map/ppermute | solution.py:41
  739.9 27.5 %collective-permute-start.67 = (bf16[2,2112,128]{2,1,0:T(8,128)(2,1)}, bf16[2,2112,128]{2,1,0:T(8,128)(2,1)S(1)}, u32[]{:S(2)}, u32[]{:S(2)}) collective-permute-start(bf16[2,2112,128]{2,1,0:T(8,128)(2,1)} %maximum_select_fusion.1), channel_id=1, source_target_pairs={{0,48},{16,0},{32,16},{48,32},{1,49},{17,1},{33,17},{49,33},{2,50}... | collective-permute-start | bytes 3244040 | tf_op jit(solution)/shard_map/ppermute | solution.py:41
  (117 other events, 1134.4 us)
Sparse Core Ops, SparseCore 0:
  53.2 123.0 all-gather.2
  520.1 75.6 reduce-scatter.2
  598.1 109.2 reduce-scatter.4

commit v2 on v1

v2 whole, which is shorter than its diff:
```python
import jax
import jax.numpy as jnp
from jax import lax
from jax.experimental import pallas as pl
from jax.experimental.pallas import tpu as pltpu
from jax.sharding import Mesh
from jax.sharding import PartitionSpec as P

H = 32
KV = 4
HD = 64
D = 2048
FF = 5632
B = 128
HALF = 512
HEADS = 4
FFL = 704
PIECE = 88

eps = 1e-05
theta = 10000.0
F32 = jnp.float32
BF16 = jnp.bfloat16
AXES = ("zlo", "y", "zhi", "x", "core")
FSDP = ("zhi", "x", "core")
SEQ = ("zlo", "y")


def matmul(left, right):
    return jnp.dot(left, right, preferred_element_type=F32)


def times_transposed(left, right):
    return lax.dot_general(left, right, (((1,), (1,)), ((), ())), preferred_element_type=F32)


def outer_sum(left, right):
    return lax.dot_general(left, right, (((0,), (0,)), ((), ())), preferred_element_type=F32)


def shift(value, axis, by):
    if axis == "z":
        at = [2 * (z % 2) + z // 2 for z in range(4)]
        return lax.ppermute(value, ("zlo", "zhi"), [(at[z], at[(z + by) % 4]) for z in range(4)])
    size = lax.axis_size(axis)
    return lax.ppermute(value, axis, [(i, (i + by) % size) for i in range(size)])


def swap_core(value):
    return shift(value, "core", 1)


def ring_gather(block, axis):
    half = block.shape[0] // 2
    before = shift(block, axis, 1)
    after = shift(block, axis, -1)
    far_low = shift(before[:half], axis, 1)
    far_high = shift(after[half:], axis, -1)
    return block, after, jnp.concatenate([far_low, far_high], axis=0), before


def small_gather(block, axis):
    return block, shift(block, axis, -1), shift(block, axis, 2), shift(block, axis, 1)


def ring_scatter(parts, axis):
    half = parts[2].shape[0] // 2
    low = shift(parts[2][:half], axis, 1)
    high = shift(parts[2][half:], axis, -1)
    after = jnp.concatenate([add(parts[1][:half], low).astype(BF16), parts[1][half:]], axis=0)
    before = jnp.concatenate([parts[3][:half], add(parts[3][half:], high).astype(BF16)], axis=0)
    from_before = shift(after, axis, 1)
    from_after = shift(before, axis, -1)
    return add(parts[0], from_before) + from_after.astype(F32)


def tie(*values):
    return lax.optimization_barrier(values)


def ring_pieces(block, axis):
    half = block.shape[0] // 2
    before = shift(block, axis, 1)
    after = shift(block, axis, -1)
    return block, after, shift(before[:half], axis, 1), shift(after[half:], axis, -1), before


def add(left, right):
    return left.astype(F32) + right.astype(F32)


def along_y(value):
    pairs = []
    for i in range(4):
        pairs.append((2 * i, 2 * ((i + 1) % 4)))
        pairs.append((2 * i + 1, 2 * ((i + 3) % 4) + 1))
    return lax.ppermute(value, ("y", "core"), pairs)


def send_half(got):
    core = lax.axis_index("core")
    return lax.dynamic_slice_in_dim(got, core * (B // 2), B // 2, 1)


def gather_tokens(block):
    pair = jnp.stack([block, swap_core(block)])
    got = along_y(pair)
    far = along_y(send_half(got))
    return (pair, got, swap_core(got), far, swap_core(far))


FLIPPED = (0, 0, 1, 0, 1)
LENGTHS = (B, B, B, B // 2, B // 2)


def scatter_tokens(parts):
    core = lax.axis_index("core")
    first, behind, ahead, far, far_other = parts
    far = add(far, swap_core(far_other)[::-1]).astype(BF16)
    low = along_y(far)
    ahead = add(ahead, swap_core(behind)[::-1]).astype(BF16)
    own = add(first[0], swap_core(first[1]))
    mine = lax.dynamic_slice_in_dim(ahead, core * (B // 2), B // 2, 1)
    ahead = lax.dynamic_update_slice_in_dim(ahead, add(mine, low).astype(BF16), core * (B // 2), 1)
    got = along_y(ahead)
    return own + got[0].astype(F32) + swap_core(got[1]).astype(F32)


def put_tokens(refs, rows_ref, sems, start):
    copies = []
    row = 0
    for s in range(2):
        for ref, flip, length in zip(refs, FLIPPED, LENGTHS):
            copies.append(
                pltpu.make_async_copy(
                    ref.at[s ^ flip], rows_ref.at[pl.ds(row, length)], sems.at[start + len(copies)]
                )
            )
            row += length
    return copies


TILE = 256
VMEM_LIMIT = 56 * 2**20
ANYWHERE = pl.BlockSpec(memory_space=pl.ANY)


def params(*kinds):
    return pltpu.CompilerParams(dimension_semantics=kinds or None, vmem_limit_bytes=VMEM_LIMIT)


def cost(flops, megabytes):
    return pl.CostEstimate(flops=flops, bytes_accessed=int(megabytes * 2**20), transcendentals=0)


def shaped(*shape, kind=BF16):
    return jax.ShapeDtypeStruct(shape, kind)


PART_SPECS = [pl.BlockSpec((1, n, D), lambda i, *_: (i // 2, 0, 0)) for n in LENGTHS]
PART_SHAPES = [jax.ShapeDtypeStruct((2, n, D), BF16) for n in LENGTHS]


def put_parts(step, tile, refs):
    @pl.when(step % 2 == 0)
    def _():
        refs[0][0] = tile[:B]
        refs[1][0] = tile[B:]

    @pl.when(step % 2 == 1)
    def _():
        refs[2][0] = tile[:B]
        refs[3][0] = tile[B : B + B // 2]
        refs[4][0] = tile[B + B // 2 :]


def turned(values):
    lane = lax.broadcasted_iota(jnp.int32, values.shape, 1) % HD
    return jnp.where(lane < HD // 2, -pltpu.roll(values, 2 * HD - HD // 2, 1), pltpu.roll(values, HD // 2, 1))


def lane_block(zhi, x, core):
    return pl.ds(pl.multiple_of((zhi * 8 + x * 2 + core) * B, B), B)


def put_columns(place, refs, into, sems, start):
    copies = []
    for ref, by, first in zip(refs, (0, 1, 2, 2, 3), (0, 0, 0, 1, 0)):
        for i in range(ref.shape[0]):
            for core in range(2):
                lanes = lane_block(first + i, (place[3] + by) % 4, core)
                copies.append(
                    pltpu.make_async_copy(ref.at[i, core], into.at[:, lanes], sems.at[start + len(copies)])
                )
    return copies


def prepare_qkv_kernel(place, q_mine, q_other, w_key, w_value, gain, mine_ref, other_ref, k_rows, v_rows):
    scale = gain[...]
    k_rows[...] = (w_key[...].astype(F32) * scale).T
    v_rows[...] = (w_value[...].astype(F32) * scale).T
    rows = pl.ds(pl.multiple_of(place[1] * HD, HD), HD)
    for source, out in ((q_mine, mine_ref), (q_other, other_ref)):
        out[: HEADS * HD] = (source[...].astype(F32) * scale).T.astype(BF16)
        out[HEADS * HD : (HEADS + 1) * HD] = k_rows[rows].astype(BF16)
        out[(HEADS + 1) * HD :] = v_rows[rows].astype(BF16)


QKV = (HEADS + 2) * HD


def prepare_qkv(place, w_query, w_key, w_value, gain):
    whole = lambda *shape: pl.BlockSpec(shape, lambda i, p: (0,) * len(shape))
    return pl.pallas_call(
        prepare_qkv_kernel,
        grid_spec=pltpu.PrefetchScalarGridSpec(
            num_scalar_prefetch=1,
            grid=(1,),
            in_specs=[
                pl.BlockSpec((B, HEADS * HD), lambda i, p: (0, 2 * p[1] + p[2])),
                pl.BlockSpec((B, HEADS * HD), lambda i, p: (0, 2 * p[1] + 1 - p[2])),
                whole(B, KV * HD), whole(B, KV * HD), whole(B, 1),
            ],
            out_specs=[whole(QKV, B), whole(QKV, B)],
            scratch_shapes=[pltpu.VMEM((KV * HD, B), F32), pltpu.VMEM((KV * HD, B), F32)],
        ),
        out_shape=[shaped(QKV, B), shaped(QKV, B)],
        compiler_params=params("arbitrary"),
        cost_estimate=cost(0, 1),
        name="prepare_qkv",
    )(place, w_query, w_query, w_key, w_value, gain)


def prepare_ff_kernel(place, w_gate, w_up, w_down, gain, mine_ref, other_ref, down_ref, picked, rows, down_rows, sems):
    zlo, y, core = place[0], place[1], place[2]
    down = pltpu.make_async_copy(
        w_down.at[:, pl.ds(pl.multiple_of(zlo * (D // 2), D // 2), D // 2)], down_rows, sems.at[1]
    )
    down.start()

    @pl.when(zlo == 0)
    def _():
        copy = pltpu.make_async_copy(w_gate, picked, sems.at[0])
        copy.start()
        copy.wait()

    @pl.when(zlo == 1)
    def _():
        copy = pltpu.make_async_copy(w_up, picked, sems.at[0])
        copy.start()
        copy.wait()

    scale = gain[...]
    for i in range(FF // B):
        rows[i * B : (i + 1) * B] = (picked[:, i * B : (i + 1) * B].astype(F32) * scale).T
    for which, out in ((core, mine_ref), (1 - core, other_ref)):
        slabs = []
        for zx in range(8):
            at = pl.multiple_of(zx * 2 * 4 * PIECE + which * 4 * PIECE + y * PIECE, 8)
            slabs.append(rows[pl.ds(at, PIECE)])
        out[...] = jnp.concatenate(slabs, axis=0).astype(BF16)
    down.wait()
    for t in range(8):
        rows[t * 4 * PIECE : (t + 1) * 4 * PIECE] = down_rows[:, t * B : (t + 1) * B].astype(F32)
    slabs = [rows[pl.ds(pl.multiple_of(t * 4 * PIECE + y * PIECE, 8), PIECE)] for t in range(8)]
    down_ref[...] = jnp.concatenate(slabs, axis=0).astype(BF16)


def prepare_ff(place, w_gate, w_up, w_down, gain):
    return pl.pallas_call(
        prepare_ff_kernel,
        grid_spec=pltpu.PrefetchScalarGridSpec(
            num_scalar_prefetch=1,
            grid=(1,),
            in_specs=[ANYWHERE, ANYWHERE, ANYWHERE, pl.BlockSpec((B, 1), lambda i, p: (0, 0))],
            out_specs=[pl.BlockSpec((FFL, B), lambda i, p: (0, 0))] * 3,
            scratch_shapes=[
                pltpu.VMEM((B, FF), BF16),
                pltpu.VMEM((FF, B), F32),
                pltpu.VMEM((4 * PIECE, D // 2), BF16),
                pltpu.SemaphoreType.DMA((2,)),
            ],
        ),
        out_shape=[shaped(FFL, B)] * 3,
        compiler_params=params("arbitrary"),
        cost_estimate=cost(0, 6),
        name="prepare_ff",
    )(place, w_gate, w_up, w_down, gain)


def project_qkv_kernel(*refs):
    place, x_refs, w_refs = refs[0], refs[1:6], refs[6:11]
    scale_ref, cosine_ref, sine_ref, query_ref, kv_ref, w_out, rows, weights, sems = refs[11:]
    step = pl.program_id(0)
    tokens = put_tokens(x_refs, rows, sems, 0)
    columns = put_columns(place, w_refs, weights, sems, 10)
    back = pltpu.make_async_copy(weights, w_out, sems.at[26])

    @pl.when(step == 0)
    def _():
        for copy in columns + tokens:
            copy.start()
        for copy in columns:
            copy.wait()
        back.start()
        for copy in tokens:
            copy.wait()

    tile = rows[pl.ds(pl.multiple_of(step * TILE, TILE), TILE), :]
    pre = times_transposed(tile, weights[...]) * scale_ref[...]
    cosine, sine = cosine_ref[...], sine_ref[...]
    for i in range(2):
        part = pre[:, i * 2 * HD : (i + 1) * 2 * HD]
        part = (part * cosine + turned(part) * sine).astype(BF16) * HD ** (-0.5)
        query_ref[0, 2 * i] = part[:, :HD]
        query_ref[0, 2 * i + 1] = part[:, HD:]
    part = pre[:, HEADS * HD :]
    lane = lax.broadcasted_iota(jnp.int32, part.shape, 1)
    kv_ref[0] = jnp.where(lane < HD, part * cosine + turned(part) * sine, part).astype(BF16)

    @pl.when(step == 3)
    def _():
        back.wait()


def project_qkv(place, x_pieces, w_pieces, scale, cosine, sine):
    tile = lambda lanes: pl.BlockSpec((TILE, lanes), lambda i, p: (i, 0))
    return pl.pallas_call(
        project_qkv_kernel,
        grid_spec=pltpu.PrefetchScalarGridSpec(
            num_scalar_prefetch=1,
            grid=(4,),
            in_specs=[ANYWHERE] * 10 + [tile(1), tile(2 * HD), tile(2 * HD)],
            out_specs=[
                pl.BlockSpec((1, HEADS, TILE, HD), lambda i, p: (i // 2, 0, i % 2, 0)),
                pl.BlockSpec((1, TILE, 2 * HD), lambda i, p: (i // 2, i % 2, 0)),
                ANYWHERE,
            ],
            scratch_shapes=[
                pltpu.VMEM((2 * HALF, D), BF16),
                pltpu.VMEM((QKV, D), BF16),
                pltpu.SemaphoreType.DMA((27,)),
            ],
        ),
        out_shape=[shaped(2, HEADS, HALF, HD), shaped(2, HALF, 2 * HD), shaped(QKV, D)],
        compiler_params=params("arbitrary"),
        cost_estimate=cost(2 * 2 * HALF * QKV * D, 8),
        name="project_qkv",
    )(place, *x_pieces, *w_pieces, scale, cosine, sine)


def project_out_kernel(*refs):
    place, w_refs, left_ref = refs[0], refs[1:6], refs[6]
    parts, w_out, weights, sems = refs[7:12], refs[12], refs[13], refs[14]
    step = pl.program_id(0)
    columns = put_columns(place, w_refs, weights, sems, 0)
    back = pltpu.make_async_copy(weights, w_out, sems.at[16])

    @pl.when(step == 0)
    def _():
        for copy in columns:
            copy.start()
        for copy in columns:
            copy.wait()
        back.start()

    put_parts(step, matmul(left_ref[...], weights[...]).astype(BF16), parts)

    @pl.when(step == 3)
    def _():
        back.wait()


def project_out(place, w_pieces, mixed):
    return pl.pallas_call(
        project_out_kernel,
        grid_spec=pltpu.PrefetchScalarGridSpec(
            num_scalar_prefetch=1,
            grid=(4,),
            in_specs=[ANYWHERE] * 5 + [pl.BlockSpec((TILE, HEADS * HD), lambda i, p: (i, 0))],
            out_specs=PART_SPECS + [ANYWHERE],
            scratch_shapes=[pltpu.VMEM((HEADS * HD, D), BF16), pltpu.SemaphoreType.DMA((17,))],
        ),
        out_shape=PART_SHAPES + [shaped(HEADS * HD, D)],
        compiler_params=params("arbitrary"),
        cost_estimate=cost(2 * 2 * HALF * HEADS * HD * D, 7),
        name="project_out",
    )(place, *w_pieces, mixed)


def project_kernel(left_ref, weight_ref, *parts):
    put_parts(pl.program_id(0), matmul(left_ref[...], weight_ref[...]).astype(BF16), parts)


def project(left, weight):
    depth = left.shape[1]
    return pl.pallas_call(
        project_kernel,
        grid=(4,),
        in_specs=[pl.BlockSpec((TILE, depth), lambda i: (i, 0)), pl.BlockSpec((depth, D), lambda i: (0, 0))],
        out_specs=PART_SPECS,
        out_shape=PART_SHAPES,
        compiler_params=params("arbitrary"),
        cost_estimate=cost(2 * 2 * HALF * depth * D, 8),
        name="project",
    )(left, weight)


def grad_mixed_kernel(*refs):
    place, grad_refs, weight_ref, mixed_ref = refs[0], refs[1:6], refs[6], refs[7]
    grad_mixed_ref, term_ref, rows, sems = refs[8:]
    copies = put_tokens(grad_refs, rows, sems, 0)
    for copy in copies:
        copy.start()
    for copy in copies:
        copy.wait()
    for i in range(4):
        tile = rows[i * TILE : (i + 1) * TILE, :]
        grad_mixed_ref[i * TILE : (i + 1) * TILE, :] = times_transposed(tile, weight_ref[...]).astype(BF16)
    left = mixed_ref[...].astype(F32).T.astype(BF16)
    put_term(place, left, rows, term_ref)


def put_term(place, left, rows, term_ref):
    def one(zx, carry):
        lanes = pl.ds(pl.multiple_of(zx * 2 * B, 2 * B), 2 * B)
        term = matmul(left, rows[:, lanes]).astype(BF16)
        by = (zx % 4 + 4 - place[3]) % 4
        term_ref[by, zx // 4, 0] = term[:, :B]
        term_ref[by, zx // 4, 1] = term[:, B:]
        return carry

    lax.fori_loop(0, 8, one, 0)


def grad_of_mixed(place, grad_pieces, weight, mixed):
    whole = lambda *shape: pl.BlockSpec(shape, lambda i, p: (0,) * len(shape))
    rows = HEADS * HD
    return pl.pallas_call(
        grad_mixed_kernel,
        grid_spec=pltpu.PrefetchScalarGridSpec(
            num_scalar_prefetch=1,
            grid=(1,),
            in_specs=[ANYWHERE] * 5 + [whole(rows, D), whole(2 * HALF, rows)],
            out_specs=[whole(2 * HALF, rows), whole(4, 2, 2, rows, B)],
            scratch_shapes=[pltpu.VMEM((2 * HALF, D), BF16), pltpu.SemaphoreType.DMA((10,))],
        ),
        out_shape=[shaped(2 * HALF, rows), shaped(4, 2, 2, rows, B)],
        compiler_params=params("arbitrary"),
        cost_estimate=cost(4 * 2 * HALF * rows * D, 8),
        name="grad_of_mixed",
    )(place, *grad_pieces, weight, mixed)


def qkv_back_kernel(grad_q_ref, own_ref, later_ref, cosine_ref, sine_ref, scale_ref, weight_ref, *outs):
    parts, turned_ref = outs[:5], outs[5]
    cosine, sine = cosine_ref[...], sine_ref[...]
    lane = lax.broadcasted_iota(jnp.int32, cosine.shape, 1)
    pieces = []
    for i in range(2):
        part = grad_q_ref[0, :, i * 2 * HD : (i + 1) * 2 * HD]
        pieces.append(part * cosine - turned(part * sine))
    part = own_ref[0] + later_ref[0].astype(F32)
    pieces.append(jnp.where(lane < HD, part * cosine - turned(part * sine), part))
    grad_pre = jnp.concatenate(pieces, axis=1)
    put_parts(pl.program_id(0), matmul(grad_pre.astype(BF16), weight_ref[...]).astype(BF16), parts)
    turned_ref[...] = (grad_pre * scale_ref[...]).T.astype(BF16)


def qkv_back(grad_query, own, later, cosine, sine, scale, weight):
    tile = lambda lanes: pl.BlockSpec((TILE, lanes), lambda i: (i, 0))
    half = lambda lanes: pl.BlockSpec((1, TILE, lanes), lambda i: (i // 2, i % 2, 0))
    return pl.pallas_call(
        qkv_back_kernel,
        grid=(4,),
        in_specs=[
            half(HEADS * HD), half(2 * HD), half(2 * HD), tile(2 * HD), tile(2 * HD), tile(1),
            pl.BlockSpec((QKV, D), lambda i: (0, 0)),
        ],
        out_specs=PART_SPECS + [pl.BlockSpec((QKV, TILE), lambda i: (0, i))],
        out_shape=PART_SHAPES + [shaped(QKV, 2 * HALF)],
        compiler_params=params("arbitrary"),
        cost_estimate=cost(2 * 2 * HALF * QKV * D, 9),
        name="qkv_back",
    )(grad_query, own, later, cosine, sine, scale, weight)


def qkv_term_kernel(*refs):
    place, x_refs, left_ref, term_ref, rows, sems = refs[0], refs[1:6], refs[6], refs[7], refs[8], refs[9]
    copies = put_tokens(x_refs, rows, sems, 0)
    for copy in copies:
        copy.start()
    for copy in copies:
        copy.wait()
    put_term(place, left_ref[...], rows, term_ref)


def qkv_terms(place, x_pieces, left):
    whole = lambda *shape: pl.BlockSpec(shape, lambda i, p: (0,) * len(shape))
    return pl.pallas_call(
        qkv_term_kernel,
        grid_spec=pltpu.PrefetchScalarGridSpec(
            num_scalar_prefetch=1,
            grid=(1,),
            in_specs=[ANYWHERE] * 5 + [whole(QKV, 2 * HALF)],
            out_specs=whole(4, 2, 2, QKV, B),
            scratch_shapes=[pltpu.VMEM((2 * HALF, D), BF16), pltpu.SemaphoreType.DMA((10,))],
        ),
        out_shape=shaped(4, 2, 2, QKV, B),
        compiler_params=params("arbitrary"),
        cost_estimate=cost(2 * 2 * HALF * QKV * D, 7),
        name="qkv_terms",
    )(place, *x_pieces, left)


def token_places(at, y, core):
    step = 1 - 2 * core
    block = jnp.where(
        at < B, y, jnp.where(at < 2 * B, y + 4 - step, jnp.where(at < 3 * B, y + 4 + step, y + 2))
    )
    row = at % B
    row = jnp.where(at < 3 * B, row, (row + core * (B // 2)) % B)
    return (block % 4) * B + row


def set_bias(place_ref, bias_ref):
    zlo, y, core = place_ref[0], place_ref[1], place_ref[2]
    key_at = token_places(lax.broadcasted_iota(jnp.int32, (HALF, 1), 0), y, core)
    query_at = token_places(lax.broadcasted_iota(jnp.int32, (1, HALF), 1), y, core)
    bias_ref[:HALF, :] = jnp.broadcast_to(jnp.where(zlo == 1, 0.0, -1e30), (HALF, HALF))
    bias_ref[HALF:, :] = jnp.where(key_at <= query_at, 0.0, -1e30)


def attention_kernel(place_ref, query_ref, kv_ref, mixed_ref, log_ref, bias_ref):
    head = pl.program_id(1)

    @pl.when((pl.program_id(0) == 0) & (head == 0))
    def _():
        set_bias(place_ref, bias_ref)

    key, value = kv_ref[0, :, :HD], kv_ref[0, :, HD:]
    scores = times_transposed(key, query_ref[0, 0]) + bias_ref[...]
    top = jnp.max(scores, axis=0, keepdims=True)
    weights = jnp.exp(scores - top)
    total = jnp.sum(weights, axis=0, keepdims=True)
    low = (weights * (1.0 / total)).astype(BF16)
    mixed = outer_sum(value, low).T.astype(BF16)
    for i in range(HEADS):

        @pl.when(head == i)
        def _():
            mixed_ref[0, :, i * HD : (i + 1) * HD] = mixed

    log_ref[0, 0] = top + jnp.log(total)


def attention_back_kernel(
    place_ref, query_ref, kv_ref, grad_ref, log_ref, grad_query_ref, earlier_ref, own_ref, bias_ref, grad_one, total
):
    head = pl.program_id(1)

    @pl.when((pl.program_id(0) == 0) & (head == 0))
    def _():
        set_bias(place_ref, bias_ref)

    for i in range(HEADS):

        @pl.when(head == i)
        def _():
            grad_one[...] = grad_ref[0, :, i * HD : (i + 1) * HD]

    key, value = kv_ref[0, :, :HD], kv_ref[0, :, HD:]
    query, grad = query_ref[0, 0], grad_one[...]
    weights = jnp.exp(times_transposed(key, query) + bias_ref[...] - log_ref[0, 0])
    grad_weights = times_transposed(value, grad)
    delta = jnp.sum(weights * grad_weights, axis=0, keepdims=True)
    grad_scores = (weights * (grad_weights - delta)).astype(BF16)
    grad_query = outer_sum(key, grad_scores).T * HD ** (-0.5)
    for i in range(HEADS):

        @pl.when(head == i)
        def _():
            grad_query_ref[0, :, i * HD : (i + 1) * HD] = grad_query

    grads = jnp.concatenate([matmul(grad_scores, query), matmul(weights.astype(BF16), grad)], axis=1)

    @pl.when(head == 0)
    def _():
        total[...] = grads

    @pl.when(head > 0)
    def _():
        total[...] += grads

    @pl.when(head == HEADS - 1)
    def _():
        earlier_ref[0] = total[:HALF].astype(BF16)
        own_ref[0] = total[HALF:]


def head_block(*tail):
    return pl.BlockSpec((1, 1) + tail, lambda s, h, place: (s, h, 0, 0))


def sequence_block(*tail):
    return pl.BlockSpec((1,) + tail, lambda s, h, place: (s, 0, 0))


def attention_call(kernel, in_specs, out_specs, out_shape, scratch, flops, name):
    return pl.pallas_call(
        kernel,
        grid_spec=pltpu.PrefetchScalarGridSpec(
            num_scalar_prefetch=1,
            grid=(2, HEADS),
            in_specs=in_specs,
            out_specs=out_specs,
            scratch_shapes=[pltpu.VMEM((2 * HALF, HALF), F32)] + scratch,
        ),
        out_shape=out_shape,
        compiler_params=params("arbitrary", "arbitrary"),
        cost_estimate=cost(flops * 8 * 2 * HALF * HALF * HD * 2, 4),
        name=name,
    )


def attention(place, query, kv):
    return attention_call(
        attention_kernel,
        [head_block(HALF, HD), sequence_block(2 * HALF, 2 * HD)],
        [sequence_block(HALF, HEADS * HD), head_block(1, HALF)],
        [shaped(2, HALF, HEADS * HD), shaped(2, HEADS, 1, HALF, kind=F32)],
        [],
        2,
        "attention",
    )(place, query, kv)


def attention_back(place, query, kv, grad, log_total):
    return attention_call(
        attention_back_kernel,
        [
            head_block(HALF, HD), sequence_block(2 * HALF, 2 * HD),
            sequence_block(HALF, HEADS * HD), head_block(1, HALF),
        ],
        [sequence_block(HALF, HEADS * HD), sequence_block(HALF, 2 * HD), sequence_block(HALF, 2 * HD)],
        [
            shaped(2, HALF, HEADS * HD, kind=F32),
            shaped(2, HALF, 2 * HD),
            shaped(2, HALF, 2 * HD, kind=F32),
        ],
        [pltpu.VMEM((HALF, HD), BF16), pltpu.VMEM((2 * HALF, 2 * HD), F32)],
        5,
        "attention_back",
    )(place, query, kv, grad, log_total)


def own_rows(rows_all, y, core, per):
    return lax.dynamic_slice_in_dim(rows_all, (2 * y + core) * per, per, 0)


def feed_forward_kernel(*refs):
    place, token_refs, grad_refs, ff_ref = refs[0], refs[1:6], refs[6:11], refs[11]
    act_ref, act_t, gate_t, up_t = refs[12:16]
    parts, down_out = refs[16:21], refs[21]
    rows_h, rows_g, gate_up, down, slabs, sems = refs[22:]
    step = pl.program_id(0)
    tokens = put_tokens(token_refs, rows_h, sems, 0)
    grads = put_tokens(grad_refs, rows_g, sems, 10)
    weights, loads = [], []
    for x in range(4):
        for by in range(4):
            z = (2 * place[4] + place[0] + by) % 4
            zhi, zlo = z // 2, z % 2
            for core in range(2):
                weights.append(
                    pltpu.make_async_copy(
                        ff_ref.at[x, by, pl.ds(core * FFL, FFL)],
                        gate_up.at[zlo, :, lane_block(zhi, x, core)],
                        sems.at[20 + len(weights)],
                    )
                )
            loads.append(
                pltpu.make_async_copy(
                    ff_ref.at[x, by, pl.ds(2 * FFL, FFL)], slabs.at[zlo, zhi * 4 + x], sems.at[52 + len(loads)]
                )
            )
    back = pltpu.make_async_copy(down, down_out, sems.at[68])

    @pl.when(step == 0)
    def _():
        for copy in loads + tokens + weights + grads:
            copy.start()
        for copy in loads:
            copy.wait()

        def put(q, carry):
            for half in range(2):
                for p in range(4):
                    one = slabs[half, 2 * q, 2 * p * PIECE : 2 * (p + 1) * PIECE, :].astype(F32)
                    two = slabs[half, 2 * q + 1, 2 * p * PIECE : 2 * (p + 1) * PIECE, :].astype(F32)
                    lane = (half * 8 + 2 * p) * B
                    rows = pl.ds(pl.multiple_of(q * 2 * PIECE, 16), 2 * PIECE)
                    down[rows, lane : lane + B] = jnp.concatenate([one[:PIECE], two[:PIECE]], axis=0).astype(BF16)
                    down[rows, lane + B : lane + 2 * B] = jnp.concatenate(
                        [one[PIECE:], two[PIECE:]], axis=0
                    ).astype(BF16)
            return carry

        lax.fori_loop(0, 4, put, 0)
        back.start()
        for copy in tokens + weights + grads:
            copy.wait()

    rows = pl.ds(pl.multiple_of(step * TILE, TILE), TILE)
    normed = rows_h[rows, :]
    gate_pre = times_transposed(normed, gate_up[0])
    upward = times_transposed(normed, gate_up[1])
    grad_act = times_transposed(rows_g[rows, :], down[...])
    sigmoid = 1.0 / (1.0 + jnp.exp(-gate_pre))
    silu = gate_pre * sigmoid
    activation = silu * upward
    grad_up = grad_act * silu
    grad_gate = grad_act * upward * (sigmoid * (1.0 + gate_pre * (1.0 - sigmoid)))
    part = matmul(grad_gate.astype(BF16), gate_up[0]) + matmul(grad_up.astype(BF16), gate_up[1])
    put_parts(step, part.astype(BF16), parts)
    act_ref[...] = activation.astype(BF16)
    act_t[...] = activation.T.astype(BF16)
    gate_t[...] = grad_gate.T.astype(BF16)
    up_t[...] = grad_up.T.astype(BF16)

    @pl.when(step == 3)
    def _():
        back.wait()


def feed_forward(place, tokens, grads, ff_all):
    turned_spec = pl.BlockSpec((FFL, TILE), lambda i, p: (0, i))
    turned_shape = shaped(FFL, 2 * HALF)
    return pl.pallas_call(
        feed_forward_kernel,
        grid_spec=pltpu.PrefetchScalarGridSpec(
            num_scalar_prefetch=1,
            grid=(4,),
            in_specs=[ANYWHERE] * 11,
            out_specs=[pl.BlockSpec((TILE, FFL), lambda i, p: (i, 0))] + [turned_spec] * 3 + PART_SPECS + [ANYWHERE],
            scratch_shapes=[
                pltpu.VMEM((2 * HALF, D), BF16),
                pltpu.VMEM((2 * HALF, D), BF16),
                pltpu.VMEM((2, FFL, D), BF16),
                pltpu.VMEM((FFL, D), BF16),
                pltpu.VMEM((2, 8, FFL, B), BF16),
                pltpu.SemaphoreType.DMA((69,)),
            ],
        ),
        out_shape=[shaped(2 * HALF, FFL)] + [turned_shape] * 3 + PART_SHAPES + [shaped(FFL, D)],
        compiler_params=params("arbitrary"),
        cost_estimate=cost(2 * 5 * 2 * HALF * FFL * D, 32),
        name="feed_forward",
    )(place, *tokens, *grads, ff_all)


def along_z(place, zhi, zlo):
    return (2 * zhi + zlo + 4 - 2 * place[4] - place[0]) % 4


def gate_up_kernel(*refs):
    place, token_refs, gate_t, up_t, out_ref, rows, sems = refs[0], refs[1:6], *refs[6:]
    step = pl.program_id(0)
    copies = put_tokens(token_refs, rows, sems, 0)

    @pl.when(step == 0)
    def _():
        for copy in copies:
            copy.start()
        for copy in copies:
            copy.wait()

    normed = rows[:, pl.ds(pl.multiple_of(step * 2 * B, 2 * B), 2 * B)]
    for matrix, left in ((0, gate_t), (1, up_t)):
        term = matmul(left[...], normed).astype(BF16)
        by = along_z(place, step // 4, matrix)
        out_ref[step % 4, by, 0:FFL, :] = term[:, :B]
        out_ref[step % 4, by, FFL:, :] = term[:, B:]


def down_kernel(*refs):
    place, grad_refs, act_t, out_ref, rows, sems = refs[0], refs[1:6], *refs[6:]
    step = pl.program_id(0)
    copies = put_tokens(grad_refs, rows, sems, 0)

    @pl.when(step == 0)
    def _():
        for copy in copies:
            copy.start()
        for copy in copies:
            copy.wait()

    term = matmul(act_t[...], rows[:, pl.ds(pl.multiple_of(step * 2 * B, 2 * B), 2 * B)])
    half, p = step // 4, step % 4
    at = pl.ds(pl.multiple_of(p * 2 * PIECE, 16), 2 * PIECE)
    for zx in range(8):
        slab = term[zx * PIECE : (zx + 1) * PIECE]
        slab = jnp.concatenate([slab[:, :B], slab[:, B:]], axis=0).astype(BF16)
        out_ref[zx % 4, along_z(place, zx // 4, half), at, :] = slab


def ff_terms(kernel, place, pieces, lefts, rows, name):
    whole = pl.BlockSpec((FFL, 2 * HALF), lambda i, p: (0, 0))
    return pl.pallas_call(
        kernel,
        grid_spec=pltpu.PrefetchScalarGridSpec(
            num_scalar_prefetch=1,
            grid=(8,),
            in_specs=[ANYWHERE] * 5 + [whole] * len(lefts),
            out_specs=pl.BlockSpec((4, 4, rows, B), lambda i, p: (0, 0, 0, 0)),
            scratch_shapes=[pltpu.VMEM((2 * HALF, D), BF16), pltpu.SemaphoreType.DMA((10,))],
        ),
        out_shape=shaped(4, 4, rows, B),
        compiler_params=params("arbitrary"),
        cost_estimate=cost(2 * len(lefts) * 2 * HALF * FFL * D, 8 + 4 * len(lefts)),
        name=name,
    )(place, *pieces, *lefts)


def finish_hidden_kernel(*refs):
    place, piece_refs, weight_ref, gain_ref, out_ref, gain_out, rows = refs[0], refs[1:5], *refs[5:]
    y = place[1]
    for ref, by in zip(piece_refs, (0, 1, 2, 3)):
        at_y = (y + by) % 4
        for core in range(2):
            slab = ref[core].astype(F32)
            for zx in range(8):
                at = pl.multiple_of((2 * zx + core) * 4 * PIECE + at_y * PIECE, 8)
                rows[pl.ds(at, PIECE)] = slab[zx * PIECE : (zx + 1) * PIECE]
    gain = gain_ref[...]
    total = jnp.zeros((B, 1), F32)
    for i in range(FF // B):
        lanes = slice(i * B, (i + 1) * B)
        block = rows[lanes].T
        total = total + jnp.sum(block * weight_ref[:, lanes].astype(F32), axis=1, keepdims=True)
        out_ref[:, lanes] = block * gain
    gain_out[...] = total


def finish_hidden(place, pieces, weight, gain):
    whole = lambda *shape: pl.BlockSpec(shape, lambda i, p: (0,) * len(shape))
    return pl.pallas_call(
        finish_hidden_kernel,
        grid_spec=pltpu.PrefetchScalarGridSpec(
            num_scalar_prefetch=1,
            grid=(1,),
            in_specs=[whole(2, FFL, B)] * 4 + [whole(B, FF), whole(B, 1)],
            out_specs=[whole(B, FF), whole(B, 1)],
            scratch_shapes=[pltpu.VMEM((FF, B), F32)],
        ),
        out_shape=[shaped(B, FF, kind=F32), shaped(B, 1, kind=F32)],
        compiler_params=params("arbitrary"),
        cost_estimate=cost(0, 6),
        name="finish_hidden",
    )(place, *pieces, weight, gain)


def finish_down_kernel(place, *refs):
    piece_refs, out_ref = refs[:4], refs[4]
    for ref, by in zip(piece_refs, range(4)):
        rows = pl.ds(pl.multiple_of((place[1] + by) % 4 * PIECE, 8), PIECE)
        for half in range(2):
            slab = ref[half].astype(F32)
            for t in range(8):
                lane = (half * 8 + t) * B
                out_ref[rows, lane : lane + B] = slab[t * PIECE : (t + 1) * PIECE]


def finish_down(place, pieces):
    whole = lambda *shape: pl.BlockSpec(shape, lambda i, p: (0,) * len(shape))
    return pl.pallas_call(
        finish_down_kernel,
        grid_spec=pltpu.PrefetchScalarGridSpec(
            num_scalar_prefetch=1,
            grid=(1,),
            in_specs=[whole(2, FFL, B)] * 4,
            out_specs=whole(4 * PIECE, D),
            scratch_shapes=[],
        ),
        out_shape=shaped(4 * PIECE, D, kind=F32),
        compiler_params=params("arbitrary"),
        cost_estimate=cost(0, 5),
        name="finish_down",
    )(place, *pieces)


def on_device(
    layer_input,
    positions,
    attn_gain,
    w_query,
    w_key,
    w_value,
    w_output,
    mlp_gain,
    w_gate,
    w_up,
    w_down,
    out_grad,
):
    zlo, y, zhi, x, core = (lax.axis_index(axis) for axis in AXES)
    place = jnp.stack([zlo, y, core, x, zhi]).astype(jnp.int32)

    def by_core(mine, got):
        return jnp.where(core == 0, jnp.stack([mine, got]), jnp.stack([got, mine]))

    def by_zlo(mine, got):
        return jnp.where(zlo == 0, jnp.stack([mine, got]), jnp.stack([got, mine]))

    def by_zhi(mine, got):
        return jnp.where(zhi == 0, jnp.stack([mine, got]), jnp.stack([got, mine]))

    x_low = layer_input[0]
    x_pair = jnp.stack([x_low, swap_core(x_low)])
    qkv_mine, qkv_other = prepare_qkv(place, w_query, w_key, w_value, attn_gain[:, None])
    qkv_pair = by_core(qkv_mine, swap_core(qkv_other))
    x_pair, qkv_pair = tie(x_pair, qkv_pair)

    x_got = along_y(x_pair)
    qkv_column = by_zhi(qkv_pair, shift(qkv_pair, "zhi", 1))
    inputs = x_low.astype(F32)
    scale_one = lax.rsqrt(jnp.mean(inputs * inputs, axis=-1, keepdims=True) + eps)
    meta = jnp.concatenate([positions.astype(F32), scale_one.reshape(1, B)], axis=0)
    gain_two, meta, _ = tie(mlp_gain[:, None], meta, x_pair)
    ff_mine, ff_other, ff_down = prepare_ff(place, w_gate, w_up, w_down, gain_two)
    ff_piece = jnp.concatenate([by_core(ff_mine, swap_core(ff_other)).reshape(2 * FFL, B), ff_down], axis=0)
    x_got, qkv_column, ff_piece = tie(x_got, qkv_column, ff_piece)

    x_far = along_y(send_half(x_got))
    x_swapped = swap_core(x_got)
    qkv_before, qkv_after = shift(qkv_column, "x", 1), shift(qkv_column, "x", -1)
    ff_before, ff_after = shift(ff_piece, "z", 1), shift(ff_piece, "z", -1)
    meta = jnp.stack(small_gather(meta, "y"))
    x_far, x_swapped, qkv_before, qkv_after, ff_before, ff_after, meta = tie(
        x_far, x_swapped, qkv_before, qkv_after, ff_before, ff_after, meta
    )

    x_pieces = (x_pair, x_got, x_swapped, x_far, swap_core(x_far))
    qkv_pieces = (
        qkv_column, qkv_after, shift(qkv_before[:1], "x", 1), shift(qkv_after[1:], "x", -1), qkv_before,
    )
    half = 3 * FFL // 2
    ff_low, ff_high = shift(ff_before[:half], "z", 1), shift(ff_after[half:], "z", -1)
    ff_ring = jnp.concatenate([ff_piece, ff_after, ff_low, ff_high, ff_before], axis=0).reshape(4, 3 * FFL, B)
    meta = jnp.stack([meta, swap_core(meta)])
    near = jnp.where(core == 0, meta[:, 3], meta[:, 1])
    ahead = jnp.where(core == 0, meta[:, 1], meta[:, 3])
    far = jnp.where(core == 0, meta[:, 2], jnp.roll(meta[:, 2], B // 2, axis=-1))
    meta = jnp.concatenate([meta[:, 0], near, ahead, far], axis=-1)
    scale_all = meta[:, 1].reshape(2 * HALF, 1)
    frequency = theta ** (-jnp.arange(0, HD, 2).astype(F32) / HD)
    angles = meta[:, 0].reshape(2 * HALF, 1) * jnp.tile(frequency, 4)
    cosine, sine = jnp.cos(angles), jnp.sin(angles)
    x_pieces, qkv_pieces, ff_ring, out_low, w_out = tie(x_pieces, qkv_pieces, ff_ring, out_grad[0], w_output)

    ff_all = lax.all_gather(ff_ring, "x", axis=0, tiled=False)
    query, key_value, qkv_full = project_qkv(place, x_pieces, qkv_pieces, scale_all, cosine, sine)
    o_rows = lax.all_to_all(w_out.reshape(B, 16, B).transpose(1, 0, 2), FSDP, 0, 0, tiled=True).reshape(D, B)
    o_pair = by_core(
        own_rows(o_rows, y, core, HEADS * HD), swap_core(own_rows(o_rows, y, 1 - core, HEADS * HD))
    )
    o_column = by_zhi(o_pair, shift(o_pair, "zhi", 1))
    o_pieces = ring_pieces(o_column, "x")
    grad_pieces = gather_tokens(out_low)
    earlier = lax.ppermute(key_value, "zlo", [(0, 1)])
    key_value = jnp.concatenate([earlier, key_value], axis=1)
    mixed, log_total = attention(place, query, key_value)
    mixed = mixed.reshape(2 * HALF, HEADS * HD)
    *parts, o_full = project_out(place, o_pieces, mixed)
    hidden = inputs + scatter_tokens(parts)
    scale_two = lax.rsqrt(jnp.mean(hidden * hidden, axis=-1, keepdims=True) + eps)
    normed_pieces = gather_tokens((hidden * scale_two).astype(BF16))

    activation, act_t, gate_t, up_t, *parts, down_full = feed_forward(place, normed_pieces, grad_pieces, ff_all)
    grad_normed_two = scatter_tokens(parts)
    gate_up_terms = ff_terms(gate_up_kernel, place, normed_pieces, (gate_t, up_t), 2 * FFL, "gate_up_terms")
    down_terms = ff_terms(down_kernel, place, grad_pieces, (act_t,), FFL, "down_terms")
    down_parts = project(activation, down_full)

    mean_two = jnp.mean(grad_normed_two * hidden, axis=-1, keepdims=True)
    grad_hidden = (
        out_grad[0].astype(F32)
        + scale_two * grad_normed_two
        - hidden * (scale_two * scale_two * scale_two) * mean_two
    )
    hidden_low, gate_up_terms, down_terms = tie(grad_hidden.astype(BF16), gate_up_terms, down_terms)
    gate_up_sum = lax.psum_scatter(gate_up_terms, "x", scatter_dimension=0, tiled=True)[0]
    down_sum = lax.psum_scatter(down_terms, "x", scatter_dimension=0, tiled=True)[0]
    hidden_grad_pieces = gather_tokens(hidden_low)
    grad_mixed, output_terms = grad_of_mixed(place, hidden_grad_pieces, o_full, mixed)
    grad_mixed, down_parts = tie(grad_mixed, down_parts)
    result = hidden + scatter_tokens(down_parts)
    grad_query, grad_earlier, grad_own = attention_back(
        place, query, key_value, grad_mixed.reshape(2, HALF, HEADS * HD), log_total
    )
    later = lax.ppermute(grad_earlier, "zlo", [(1, 0)])
    *parts, grad_t = qkv_back(grad_query, grad_own, later, cosine, sine, scale_all, qkv_full)
    grad_normed = scatter_tokens(parts)
    qkv_term = qkv_terms(place, x_pieces, grad_t)
    mean_one = jnp.mean(grad_normed * inputs, axis=-1, keepdims=True)
    input_grad = (
        grad_hidden
        + scale_one * grad_normed
        - inputs * (scale_one * scale_one * scale_one) * mean_one
    )

    def own_block(pair):
        keep = lax.dynamic_index_in_dim(pair, core, 0, keepdims=False)
        return by_core(keep, swap_core(lax.dynamic_index_in_dim(pair, 1 - core, 0, keepdims=False)))

    def attention_sums(terms):
        rows = terms.shape[3]
        column = ring_scatter([terms[i] for i in range(4)], "x").astype(BF16)
        column = column.reshape(2, 2, 2, rows // 2, B).transpose(0, 2, 1, 3, 4).reshape(4, rows, B)
        z = 2 * zhi + zlo
        column = [lax.dynamic_index_in_dim(column, (z + i) % 4, 0, keepdims=False) for i in range(4)]
        own = own_block(ring_scatter(column, "z").astype(BF16).reshape(2, rows // 2, B))
        own = by_zlo(own, shift(own, "zlo", 1)).transpose(1, 0, 2, 3).reshape(2, rows, B)
        return jnp.roll(jnp.stack(ring_gather(own, "y")), y, axis=0)

    output_rows = attention_sums(output_terms).reshape(16, B, B)
    output_grad = lax.all_to_all(output_rows, FSDP, 0, 0, tiled=True)
    output_grad = output_grad.transpose(1, 0, 2).reshape(B, D).astype(F32)
    sums = attention_sums(qkv_term)
    query_grad = sums[:, :, : HEADS * HD].reshape(D, B).T.astype(F32)
    key_grad = jnp.sum(sums[:, :, HEADS * HD : (HEADS + 1) * HD].astype(F32), axis=1)
    key_grad = key_grad.reshape(KV * HD, B).T
    value_grad = jnp.sum(sums[:, :, (HEADS + 1) * HD :].astype(F32), axis=1)
    value_grad = value_grad.reshape(KV * HD, B).T
    attn_gain_grad = (
        jnp.sum(query_grad * w_query.astype(F32), axis=1)
        + jnp.sum(key_grad * w_key.astype(F32), axis=1)
        + jnp.sum(value_grad * w_value.astype(F32), axis=1)
    )

    gate_up = ring_scatter([gate_up_sum[i] for i in range(4)], "z").astype(BF16)
    gate_up = own_block(gate_up.reshape(2, FFL, B))
    gate_up = by_zlo(gate_up, shift(gate_up, "zlo", 1))
    gate_up = ring_gather(gate_up, "y")
    gain_two = mlp_gain[:, None]
    gate_grad, gate_gain = finish_hidden(place, [p[0] for p in gate_up], w_gate, gain_two)
    up_grad, up_gain = finish_hidden(place, [p[1] for p in gate_up], w_up, gain_two)
    down = ring_scatter([down_sum[i] for i in range(4)], "z").astype(BF16)
    down = by_zlo(down, shift(down, "zlo", 1))
    down_grad = finish_down(place, ring_gather(down, "y"))
    one = attn_gain[:, None]
    return (
        result.astype(BF16)[None],
        input_grad.astype(BF16)[None],
        attn_gain_grad,
        query_grad * one,
        key_grad * one,
        value_grad * one,
        output_grad,
        (gate_gain + up_gain)[:, 0],
        gate_grad,
        up_grad,
        down_grad,
    )


def solution(mesh):
    split = Mesh(mesh.devices.reshape(2, 4, 2, 4, 2), AXES)
    tokens = P(FSDP, SEQ, None)
    rows = P(FSDP, None)
    gain = P(FSDP)
    in_specs = (
        tokens, P(FSDP, SEQ), gain, rows, rows, rows, rows, gain, rows, rows, rows, tokens,
    )
    out_specs = (tokens, tokens, gain, rows, rows, rows, rows, gain, rows, rows, rows)
    return jax.shard_map(
        on_device, mesh=split, in_specs=in_specs, out_specs=out_specs, check_vma=False
    )
```

time: 824 us -> 663 us (0.80)
  Pallas kernels: 0 us -> 167 us
  matrix products: 132 us -> 0 us
  local copies, waits for them, and re-layouts: 165 us -> 45.9 us
  waiting for transfers between devices: 275 us -> 211 us
  other arithmetic: 56.6 us -> 45.5 us
    pallas_call x0 -> x16, Pallas kernels: none -> 167 us  [the longest x1 32.5 us: feed_forward(): pl.pallas_call(feed_forward_kernel, grid_spec=pltpu.PrefetchScalarGridSpe...]
    dot_general x27 -> x0, matrix products: 132 us -> none  [the longest x2 26.1 us: attend_back(): jnp.einsum('hqk,kd->qhd', grad_scores, key_part, preferred_element_type=F32)]
    ppermute x1 -> x37, waiting for transfers between devices: 0.01 us -> 101 us  [the longest x16 80.1 us: along_y(): return lax.ppermute(value, ('y', 'core'), pairs)]
    reduce_scatter x2, waiting for transfers between devices: 76.6 us -> 0.01 us  [the longest x1 0.01 us: on_device(): lax.psum_scatter(gate_up_terms, 'x', scatter_dimension=0, tiled=True)[0]]
    ppermute x69 -> x76, waiting for transfers between devices: 163 us -> 95.2 us  [shift(): lax.ppermute(value, axis, [(i, (i + by) % size) for i in range(size)])]
    reshape x12 -> x2, local copies, waits for them, and re-layouts: 54.8 us -> 0.05 us  [attention_sums(): column.reshape(2, 2, 2, rows // 2, B).transpose(0, 2, 1, 3, 4)]
    ppermute x1 -> x37, starting transfers between devices: 1.62 us -> 40.8 us  [the longest x20 25.1 us: shift(): lax.ppermute(value, ('zlo', 'zhi'), [(at[z], at[(z + by) % 4]) for z in r...]
    unnamed x193 -> x150, local copies, waits for them, and re-layouts: 49.7 us -> 17 us
  transfers between devices with their start and end apart: 76 -> 119, of which waited for: 33 -> 48; matrix products, arithmetic and copies ran while one was open for 21% -> 12% of each run, Pallas kernels for 0% -> 20%
where the time goes in v2:
time: 663 us; the launch traced here: 652 us
  waiting for transfers between devices  211 us (32%)
  Pallas kernels  167 us (25%)
  starting transfers between devices  166 us (25%)
  local copies, waits for them, and re-layouts  45.9 us (7%)
  other arithmetic  45.5 us (7%)
  between operations  15.8 us (2%)
    ppermute x76, starting transfers between devices, shift(): lax.ppermute(value, axis, [(i, (i + by) % size) for i in range(size)])  104 us
    ppermute x76, waiting for transfers between devices, shift(): lax.ppermute(value, axis, [(i, (i + by) % size) for i in range(size)])  95.2 us
    ppermute x16, waiting for transfers between devices, along_y(): return lax.ppermute(value, ('y', 'core'), pairs)  80.1 us
    pallas_call x1, Pallas kernels, feed_forward(): pl.pallas_call(feed_forward_kernel, grid_spec=pltpu.PrefetchScalarGridSpe...  32.5 us
    pallas_call x2, Pallas kernels, ff_terms(): pl.pallas_call(kernel, grid_spec=pltpu.PrefetchScalarGridSpec(num_scalar_...  25.7 us
    ppermute x20, starting transfers between devices, shift(): lax.ppermute(value, ('zlo', 'zhi'), [(at[z], at[(z + by) % 4]) for z in r...  25.1 us
    pallas_call x1, Pallas kernels, attention_back(): attention_call(attention_back_kernel, [head_block(HALF, HD), sequence_blo...  23.2 us
    unnamed x150, local copies, waits for them, and re-layouts  17 us
  transfers between devices with their start and end apart: 119, of which 48 were waited for; matrix products, arithmetic and copies ran while one was open for 12% of the time, Pallas kernels for 20%

profile of v2, /device:TPU:1, one launch (start us, length us, event | category | flops | bytes accessed | tf_op | source)
XLA Modules:
  0.0 652.0 jit_solution(5667163136133695543)
XLA Ops:
  48.3 7.7 %collective-permute-done.8.refs_7_ = bf16[2,2,384,128]{3,2,1,0:T(8,128)(2,1)S(1)} collective-permute-done((bf16[2,2,384,128]{3,2,1,0:T(8,128)(2,1)S(1)}, bf16[2,2,384,128]{3,2,1,0:T(8,128)(2,1)S(1)}, u32[]{:S(2)}, u32[]{:S(2)}) %collective-permute-start.8) | collective-permute-done | bytes 393248 | tf_op jit(solution)/shard_map/ppermute | solution.py:46
  72.8 6.0 all-to-all-start
  78.9 12.6 %all-to-all-done = bf16[16,128,128]{2,1,0:T(8,128)(2,1)S(1)} async-done(((bf16[16,128,128]{2,1,0:T(8,128)(2,1)}), bf16[16,128,128]{2,1,0:T(8,128)(2,1)S(1)}, u32[]{:S(2)}, u32[]{:S(2)}) %all-to-all-start) | async-done | bytes 524320 | tf_op jit(solution)/shard_map/all_to_all | solution.py:963
  98.0 10.2 %project_qkv.1 = (bf16[2,4,512,64]{3,2,1,0:T(8,128)(2,1)}, bf16[2,512,128]{2,1,0:T(8,128)(2,1)}, bf16[384,2048]{1,0:T(8,128)(2,1)}) custom-call(s32[5]{0:T(128)} %stack.286.place.refs_0_.place_ref, bf16[2,128,2048]{2,1,0:T(8,128)(2,1)} %copy-done.3, bf16[2,128,2048]{2,1,0:T(8,128)(2,1)} %collective-permute-done.2.refs_2_, bf16[2,128,2048]{2,1,0:T(8,128)(2,1)} %copy-done.7, ...), custom_call_target="tpu_custom_call" | custom-call | flops 1610612736 | bytes 8388608 | tf_op jit(solution)/shard_map/project_qkv/pallas_call | solution.py:328
  116.6 9.9 %collective-permute-done.22.refs_5_ = bf16[2,2,256,128]{3,2,1,0:T(8,128)(2,1)S(1)} collective-permute-done((bf16[2,2,256,128]{3,2,1,0:T(8,128)(2,1)S(1)}, bf16[2,2,256,128]{3,2,1,0:T(8,128)(2,1)S(1)}, u32[]{:S(2)}, u32[]{:S(2)}) %collective-permute-start.22) | collective-permute-done | bytes 262176 | tf_op jit(solution)/shard_map/ppermute | solution.py:46
  130.1 13.2 %attention.1 = (bf16[2,512,256]{2,1,0:T(8,128)(2,1)}, f32[2,4,1,512]{3,2,1,0:T(1,128)}) custom-call(s32[5]{0:T(128)} %stack.286.place.refs_0_.place_ref, bf16[2,4,512,64]{3,2,1,0:T(8,128)(2,1)} %get-tuple-element.123.query_ref, bf16[2,1024,128]{2,1,0:T(8,128)(2,1)} %copy-done.49), custom_call_target="tpu_custom_call" | custom-call | flops 1073741824 | bytes 4194304 | tf_op jit(solution)/shard_map/attention/pallas_call | solution.py:627
  144.0 7.4 %project_out.1 = (bf16[2,128,2048]{2,1,0:T(8,128)(2,1)}, bf16[2,128,2048]{2,1,0:T(8,128)(2,1)}, bf16[2,128,2048]{2,1,0:T(8,128)(2,1)}, bf16[2,64,2048]{2,1,0:T(8...) custom-call(s32[5]{0:T(128)} %stack.286.place.refs_0_.place_ref, ...), custom_call_target="tpu_custom_call" | custom-call | flops 1073741824 | bytes 7340032 | tf_op jit(solution)/shard_map/project_out/pallas_call | solution.py:375
  158.7 7.9 %collective-permute-done.30 = bf16[2,64,2048]{2,1,0:T(8,128)(2,1)S(1)} collective-permute-done((bf16[2,64,2048]{2,1,0:T(8,128)(2,1)S(1)}, bf16[2,64,2048]{2,1,0:T(8,128)(2,1)S(1)}, u32[]{:S(2)}, u32[]{:S(2)}) %collective-permute-start.30) | collective-permute-done | bytes 524320 | tf_op jit(solution)/shard_map/ppermute | solution.py:97
  169.5 11.4 %collective-permute-done.31 = bf16[2,128,2048]{2,1,0:T(8,128)(2,1)S(1)} collective-permute-done((bf16[2,128,2048]{2,1,0:T(8,128)(2,1)S(1)}, bf16[2,128,2048]{2,1,0:T(8,128)(2,1)S(1)}, u32[]{:S(2)}, u32[]{:S(2)}) %collective-permute-start.31) | collective-permute-done | bytes 1048608 | tf_op jit(solution)/shard_map/ppermute | solution.py:97
  189.9 12.4 %collective-permute-done.39.refs_7_.refs_2_ = bf16[2,128,2048]{2,1,0:T(8,128)(2,1)S(1)} collective-permute-done((bf16[2,128,2048]{2,1,0:T(8,128)(2,1)S(1)}, bf16[2,128,2048]{2,1,0:T(8,128)(2,1)S(1)}, u32[]{:S(2)}, u32[]{:S(2)}) %collective-permute-start.39) | collective-permute-done | bytes 1048608 | tf_op jit(solution)/shard_map/ppermute | solution.py:97
  204.7 8.8 %collective-permute-done.34.refs_2_ = bf16[2,128,2048]{2,1,0:T(8,128)(2,1)S(1)} collective-permute-done((bf16[2,128,2048]{2,1,0:T(8,128)(2,1)S(1)}, bf16[2,128,2048]{2,1,0:T(8,128)(2,1)S(1)}, u32[]{:S(2)}, u32[]{:S(2)}) %collective-permute-start.34) | collective-permute-done | bytes 1048608 | tf_op jit(solution)/shard_map/ppermute | solution.py:97
  229.3 32.5 %feed_forward.1 = (bf16[1024,704]{1,0:T(8,128)(2,1)}, bf16[704,1024]{1,0:T(8,128)(2,1)}, bf16[704,1024]{1,0:T(8,128)(2,1)}, bf16[704,1024]{1,0:T(8,128)(2,1)}, b...) custom-call(s32[5]{0:T(128)} %stack.286.place.refs_0_.place_ref, ...), custom_call_target="tpu_custom_call" | custom-call | flops 14763950080 | bytes 33554432 | tf_op jit(solution)/shard_map/feed_forward/pallas_call | solution.py:739
  267.3 7.8 %collective-permute-done.46 = bf16[2,64,2048]{2,1,0:T(8,128)(2,1)S(1)} collective-permute-done((bf16[2,64,2048]{2,1,0:T(8,128)(2,1)S(1)}, bf16[2,64,2048]{2,1,0:T(8,128)(2,1)S(1)}, u32[]{:S(2)}, u32[]{:S(2)}) %collective-permute-start.46) | collective-permute-done | bytes 524320 | tf_op jit(solution)/shard_map/ppermute | solution.py:97
  278.5 10.5 %down_terms.1 = bf16[4,4,704,128]{3,2,1,0:T(8,128)(2,1)} custom-call(s32[5]{0:T(128)} %stack.286.place.refs_0_.place_ref, bf16[2,128,2048]{2,1,0:T(8,128)(2,1)} %copy-done.26, bf16[2,128,2048]{2,1,0:T(8,128)(2,1)} %copy-done.46, bf16[2,128,2048]{2,1,0:T(8,128)(2,1)} %copy-done.56, bf16[2,64,2048]{2,1,0:T(8,128)(2,1)} %copy-done.60, ...), custom_call_target="tpu_custom_call" | custom-call | flops 2952790016 | bytes 12582912 | tf_op jit(solution)/shard_map/down_terms/pallas_call | solution.py:809
  295.6 15.2 %gate_up_terms.1 = bf16[4,4,1408,128]{3,2,1,0:T(8,128)(2,1)} custom-call(s32[5]{0:T(128)} %stack.286.place.refs_0_.place_ref, bf16[2,128,2048]{2,1,0:T(8,128)(2,1)} %copy-done.25, bf16[2,128,2048]{2,1,0:T(8,128)(2,1)} %copy-done.45, bf16[2,128,2048]{2,1,0:T(8,128)(2,1)} %copy-done.55, bf16[2,64,2048]{2,1,0:T(8,128)(2,1)} %copy-done.59, ...), custom_call_target="tpu_custom_call" | custom-call | flops 5905580032 | bytes 16777216 | tf_op jit(solution)/shard_map/gate_up_terms/pallas_call | solution.py:809
  318.7 14.0 %collective-permute-done.50.refs_2_ = bf16[2,128,2048]{2,1,0:T(8,128)(2,1)} collective-permute-done((bf16[2,128,2048]{2,1,0:T(8,128)(2,1)S(1)}, bf16[2,128,2048]{2,1,0:T(8,128)(2,1)}, u32[]{:S(2)}, u32[]{:S(2)}) %collective-permute-start.50) | collective-permute-done | bytes 1048608 | tf_op jit(solution)/shard_map/ppermute | solution.py:97
  336.2 6.1 collective-permute-done.52.refs_4_
  349.2 7.9 %project.1 = (bf16[2,128,2048]{2,1,0:T(8,128)(2,1)}, bf16[2,128,2048]{2,1,0:T(8,128)(2,1)}, bf16[2,128,2048]{2,1,0:T(8,128)(2,1)}, bf16[2,64,2048]{2,1,0:T(8,128)(2,1)}, bf16[2,64,2048]{2,1,0:T(8,128)(2,1)}) custom-call(bf16[1024,704]{1,0:T(8,128)(2,1)} %get-tuple-element.144.left_ref, bf16[704,2048]{1,0:T(8,128)(2,1)} %get-tuple-element.145.weight_ref), custom_call_target="tpu_custom_call" | custom-call | flops 2952790016 | bytes 8388608 | tf_op jit(solution)/shard_map/project/pallas_call | solution.py:397
  357.9 9.1 %grad_of_mixed.1 = (bf16[1024,256]{1,0:T(8,128)(2,1)}, bf16[4,2,2,256,128]{4,3,2,1,0:T(8,128)(2,1)}) custom-call(s32[5]{0:T(128)} %stack.286.place.refs_0_.place_ref, bf16[2,128,2048]{2,1,0:T(8,128)(2,1)} %copy-done.24, bf16[2,128,2048]{2,1,0:T(8,128)(2,1)} %collective-permute-done.50.refs_2_, bf16[2,128,2048]{2,1,0:T(8,128)(2,1)} %collective-permute-done.51.refs_3_, ...), custom_call_target="tpu_custom_call" | custom-call | flops 2147483648 | bytes 8388608 | tf_op jit(solution)/shard_map/grad_of_mixed/pallas_call | solution.py:439
  370.9 23.2 %attention_back.1 = (f32[2,512,256]{2,1,0:T(8,128)}, bf16[2,512,128]{2,1,0:T(8,128)(2,1)}, f32[2,512,128]{2,1,0:T(8,128)}) custom-call(s32[5]{0:T(128)} %stack.286.place.refs_0_.place_ref, bf16[2,4,512,64]{3,2,1,0:T(8,128)(2,1)} %get-tuple-element.123.query_ref, bf16[2,1024,128]{2,1,0:T(8,128)(2,1)} %copy-done.49, bf16[2,512,256]{2,1,0:T(8,128)(2,1)} %bitcast.462, ...), custom_call_target="tpu_custom_call" | custom-call | flops 2684354560 | bytes 4194304 | tf_op jit(solution)/shard_map/attention_back/pallas_call | solution.py:639
  397.7 5.8 collective-permute-done.60.later_ref
  404.2 8.3 %qkv_back.1 = (bf16[2,128,2048]{2,1,0:T(8,128)(2,1)}, bf16[2,128,2048]{2,1,0:T(8,128)(2,1)}, bf16[2,128,2048]{2,1,0:T(8,128)(2,1)}, bf16[2,64,2048]{2,1,0:T(8,12...) custom-call(f32[2,512,256]{2,1,0:T(8,128)} %get-tuple-element.158.grad_q_ref, ...), custom_call_target="tpu_custom_call" | custom-call | flops 1610612736 | bytes 9437184 | tf_op jit(solution)/shard_map/qkv_back/pallas_call | solution.py:473
  414.4 8.4 %qkv_terms.1 = bf16[4,2,2,384,128]{4,3,2,1,0:T(8,128)(2,1)} custom-call(s32[5]{0:T(128)} %stack.286.place.refs_0_.place_ref, bf16[2,128,2048]{2,1,0:T(8,128)(2,1)} %copy-done.3, bf16[2,128,2048]{2,1,0:T(8,128)(2,1)} %collective-permute-done.2.refs_2_, bf16[2,128,2048]{2,1,0:T(8,128)(2,1)} %copy-done.7, bf16[2,64,2048]{2,1,0:T(8,128)(2,1)} %copy-done.13, ...), custom_call_target="tpu_custom_call" | custom-call | flops 1610612736 | bytes 7340032 | tf_op jit(solution)/shard_map/qkv_terms/pallas_call | solution.py:500
  474.4 11.7 %all-to-all-start.1 = ((bf16[16,128,128]{2,1,0:T(8,128)(2,1)}), bf16[16,128,128]{2,1,0:T(8,128)(2,1)S(1)}, u32[]{:S(2)}, u32[]{:S(2)}) async-start(bf16[16,128,128]{2,1,0:T(8,128)(2,1)} %bitcast.136), calls=%async_computation.1 | async-start | bytes 1048576 | tf_op jit(solution)/shard_map/all_to_all | solution.py:1027
  532.8 7.1 %collective-permute-start.59 = (bf16[128,2048]{1,0:T(8,128)(2,1)}, bf16[128,2048]{1,0:T(8,128)(2,1)}, u32[]{:S(2)}, u32[]{:S(2)}) collective-permute-start(bf16[128,2048]{1,0:T(8,128)(2,1)} %slice_bitcast_fusion.2), channel_id=1, source_target_pairs={{0,1},{1,0},{2,3},{3,2},{4,5},{5,4},{6,7},{7,6},{8,9},{9,8},{10,11... | collective-permute-start | bytes 1572872 | tf_op jit(solution)/shard_map/ppermute | solution.py:46
  543.8 7.5 %collective-permute-start.66 = (bf16[128,2048]{1,0:T(8,128)(2,1)}, bf16[128,2048]{1,0:T(8,128)(2,1)S(1)}, u32[]{:S(2)}, u32[]{:S(2)}) collective-permute-start(bf16[128,2048]{1,0:T(8,128)(2,1)} %slice_bitcast_fusion), channel_id=1, source_target_pairs={{0,1},{1,0},{2,3},{3,2},{4,5},{5,4},{6,7},{7,6},{8,9},{9,8},{10,11... | collective-permute-start | bytes 1572872 | tf_op jit(solution)/shard_map/ppermute | solution.py:46
  568.4 6.8 %collective-permute-done.96 = bf16[1408,128]{1,0:T(8,128)(2,1)S(1)} collective-permute-done((bf16[1408,128]{1,0:T(8,128)(2,1)S(1)}, bf16[1408,128]{1,0:T(8,128)(2,1)S(1)}, u32[]{:S(2)}, u32[]{:S(2)}) %collective-permute-start.96) | collective-permute-done | bytes 360480 | tf_op jit(solution)/shard_map/ppermute | solution.py:44
  583.4 8.6 %collective-permute-done.100 = bf16[2,704,128]{2,1,0:T(8,128)(2,1)S(1)} collective-permute-done((bf16[2,704,128]{2,1,0:T(8,128)(2,1)S(1)}, bf16[2,704,128]{2,1,0:T(8,128)(2,1)S(1)}, u32[]{:S(2)}, u32[]{:S(2)}) %collective-permute-start.100) | collective-permute-done | bytes 360480 | tf_op jit(solution)/shard_map/ppermute | solution.py:46
  601.2 5.5 collective-permute-done.111.refs_3_
  606.8 10.2 %collective-permute-done.110.refs_1_ = bf16[2,704,128]{2,1,0:T(8,128)(2,1)S(1)} collective-permute-done((bf16[2,704,128]{2,1,0:T(8,128)(2,1)S(1)}, bf16[2,704,128]{2,1,0:T(8,128)(2,1)S(1)}, u32[]{:S(2)}, u32[]{:S(2)}) %collective-permute-start.110) | collective-permute-done | bytes 360480 | tf_op jit(solution)/shard_map/ppermute | solution.py:46
  632.2 5.4 finish_hidden.3
  638.3 5.2 finish_hidden.2
  (525 shorter events, 312.3 us)
Async XLA Ops:
  7.2 222.1 %all-gather.3.cloned.1.call-start = ((), (), s32[]{:S(2)}) async-start(), calls=%async_computation.6 | async-start | bytes 10813440 | tf_op jit(solution)/shard_map/all_gather | solution.py:961
  16.0 17.3 %collective-permute-start.2 = (bf16[2,128,2048]{2,1,0:T(8,128)(2,1)S(1)}, bf16[2,128,2048]{2,1,0:T(8,128)(2,1)}, u32[]{:S(2)}, u32[]{:S(2)}) collective-permute-start(bf16[2,128,2048]{2,1,0:T(8,128)(2,1)S(1)} %pad_maximum_fusion.refs_1_), channel_id=1, source_target_pairs={{0,16},{1,49},{16,32},{17,1},{32,48},{33,17},{48,0},{49,33},{2,18}... | collective-permute-start | bytes 3145736 | tf_op jit(solution)/shard_map/ppermute | solution.py:97
  33.3 22.7 %collective-permute-start.6 = (bf16[2,128,2048]{2,1,0:T(8,128)(2,1)}, bf16[2,128,2048]{2,1,0:T(8,128)(2,1)S(1)}, u32[]{:S(2)}, u32[]{:S(2)}) collective-permute-start(bf16[2,128,2048]{2,1,0:T(8,128)(2,1)} %collective-permute-done.2.refs_2_), channel_id=1, source_target_pairs={{0,1},{1,0},{2,3},{3,2},{4,5},{5,4},{6,7},{7,6},{8,9},{9,8},{10,11... | collective-permute-start | bytes 3145736 | tf_op jit(solution)/shard_map/ppermute | solution.py:46
  37.9 18.0 %collective-permute-start.10 = (bf16[2112,128]{1,0:T(8,128)(2,1)S(1)}, bf16[2112,128]{1,0:T(8,128)(2,1)S(1)}, u32[]{:S(2)}, u32[]{:S(2)}) collective-permute-start(bf16[2112,128]{1,0:T(8,128)(2,1)S(1)} %pad_maximum_fusion.4), channel_id=1, source_target_pairs={{0,72},{64,0},{8,64},{72,8},{1,73},{65,1},{9,65},{73,9},{2,74},{66... | collective-permute-start | bytes 1622024 | tf_op jit(solution)/shard_map/ppermute | solution.py:44
  72.8 18.7 %all-to-all-start = ((bf16[16,128,128]{2,1,0:T(8,128)(2,1)}), bf16[16,128,128]{2,1,0:T(8,128)(2,1)S(1)}, u32[]{:S(2)}, u32[]{:S(2)}) async-start(bf16[16,128,128]{2,1,0:T(8,128)(2,1)} %bitcast_bitcast_fusion), calls=%async_computation | async-start | bytes 1048576 | tf_op jit(solution)/shard_map/all_to_all | solution.py:963
  78.7 475.1 %reduce-scatter.3.cloned.1.call-start = ((), (), s32[]{:S(2)}) async-start(), calls=%async_computation.4 | async-start | bytes 7208960 | tf_op jit(solution)/shard_map/reduce_scatter | solution.py:992
  167.8 17.7 %collective-permute-start.27 = (bf16[128,2048]{1,0:T(8,128)(2,1)S(1)}, bf16[128,2048]{1,0:T(8,128)(2,1)S(1)}, u32[]{:S(2)}, u32[]{:S(2)}) collective-permute-start(bf16[128,2048]{1,0:T(8,128)(2,1)S(1)} %slice_bitcast_fusion.11), channel_id=1, source_target_pairs={{0,1},{1,0},{2,3},{3,2},{4,5},{5,4},{6,7},{7,6},{8,9},{9,8},{10,11... | collective-permute-start | bytes 1572872 | tf_op jit(solution)/shard_map/ppermute | solution.py:46
  189.8 23.7 %collective-permute-start.34 = (bf16[2,128,2048]{2,1,0:T(8,128)(2,1)S(1)}, bf16[2,128,2048]{2,1,0:T(8,128)(2,1)S(1)}, u32[]{:S(2)}, u32[]{:S(2)}) collective-permute-start(bf16[2,128,2048]{2,1,0:T(8,128)(2,1)S(1)} %pad_maximum_fusion.1.refs_1_), channel_id=1, source_target_pairs={{0,16},{1,49},{16,32},{17,1},{32,48},{33,17},{48,0},{49,33},{2,18}... | collective-permute-start | bytes 3145736 | tf_op jit(solution)/shard_map/ppermute | solution.py:97
  203.3 23.8 %collective-permute-start.40 = (bf16[2,128,2048]{2,1,0:T(8,128)(2,1)S(1)}, bf16[2,128,2048]{2,1,0:T(8,128)(2,1)S(1)}, u32[]{:S(2)}, u32[]{:S(2)}) collective-permute-start(bf16[2,128,2048]{2,1,0:T(8,128)(2,1)S(1)} %collective-permute-done.39.refs_7_.refs_2_), channel_id=1, source_target_pairs={{0,1},{1,0},{2,3},{3,2},{4,5},{5,4},{6,7},{7,6},{8,9},{9,8},{10,11... | collective-permute-start | bytes 3145736 | tf_op jit(solution)/shard_map/ppermute | solution.py:46
  277.2 33.6 %collective-permute-start.43 = (bf16[128,2048]{1,0:T(8,128)(2,1)}, bf16[128,2048]{1,0:T(8,128)(2,1)}, u32[]{:S(2)}, u32[]{:S(2)}) collective-permute-start(bf16[128,2048]{1,0:T(8,128)(2,1)} %slice_bitcast_fusion.10), channel_id=1, source_target_pairs={{0,1},{1,0},{2,3},{3,2},{4,5},{5,4},{6,7},{7,6},{8,9},{9,8},{10,11... | collective-permute-start | bytes 1572872 | tf_op jit(solution)/shard_map/ppermute | solution.py:46
  291.3 19.5 %collective-permute-start.48 = (bf16[128,2048]{1,0:T(8,128)(2,1)}, bf16[128,2048]{1,0:T(8,128)(2,1)}, u32[]{:S(2)}, u32[]{:S(2)}) collective-permute-start(bf16[128,2048]{1,0:T(8,128)(2,1)} %slice_bitcast_fusion.4), channel_id=1, source_target_pairs={{0,1},{1,0},{2,3},{3,2},{4,5},{5,4},{6,7},{7,6},{8,9},{9,8},{10,11... | collective-permute-start | bytes 1572872 | tf_op jit(solution)/shard_map/ppermute | solution.py:46
  315.6 242.5 %reduce-scatter.5.cloned.1.call-start = ((), (), s32[]{:S(2)}) async-start(), calls=%async_computation.5 | async-start | bytes 3604480 | tf_op jit(solution)/shard_map/reduce_scatter | solution.py:993
  335.2 22.0 %collective-permute-start.51 = (bf16[2,128,2048]{2,1,0:T(8,128)(2,1)}, bf16[2,128,2048]{2,1,0:T(8,128)(2,1)}, u32[]{:S(2)}, u32[]{:S(2)}) collective-permute-start(bf16[2,128,2048]{2,1,0:T(8,128)(2,1)} %collective-permute-done.50.refs_2_), channel_id=1, source_target_pairs={{0,1},{1,0},{2,3},{3,2},{4,5},{5,4},{6,7},{7,6},{8,9},{9,8},{10,11... | collective-permute-start | bytes 3145736 | tf_op jit(solution)/shard_map/ppermute | solution.py:46
  368.1 28.9 %collective-permute-start.81 = (bf16[1,2,256,128]{3,2,1,0:T(8,128)(2,1)S(1)}, bf16[1,2,256,128]{3,2,1,0:T(8,128)(2,1)S(1)}, u32[]{:S(2)}, u32[]{:S(2)}) collective-permute-start(bf16[1,2,256,128]{3,2,1,0:T(8,128)(2,1)S(1)} %get-tuple-element.233), channel_id=1, source_target_pairs={{0,2},{2,4},{4,6},{6,0},{1,3},{3,5},{5,7},{7,1},{8,10},{10,12},{12... | collective-permute-start | bytes 393224 | tf_op jit(solution)/shard_map/ppermute | solution.py:46
  368.2 29.2 %collective-permute-start.83 = (bf16[1,2,256,128]{3,2,1,0:T(8,128)(2,1)S(1)}, bf16[1,2,256,128]{3,2,1,0:T(8,128)(2,1)S(1)}, u32[]{:S(2)}, u32[]{:S(2)}) collective-permute-start(bf16[1,2,256,128]{3,2,1,0:T(8,128)(2,1)S(1)} %get-tuple-element.234), channel_id=1, source_target_pairs={{0,6},{2,0},{4,2},{6,4},{1,7},{3,1},{5,3},{7,5},{8,14},{10,8},{12,... | collective-permute-start | bytes 393224 | tf_op jit(solution)/shard_map/ppermute | solution.py:46
  395.3 51.6 %collective-permute-start.56 = (bf16[2,64,2048]{2,1,0:T(8,128)(2,1)S(1)}, bf16[2,64,2048]{2,1,0:T(8,128)(2,1)S(1)}, u32[]{:S(2)}, u32[]{:S(2)}) collective-permute-start(bf16[2,64,2048]{2,1,0:T(8,128)(2,1)S(1)} %copy-done.57), channel_id=1, source_target_pairs={{0,1},{1,0},{2,3},{3,2},{4,5},{5,4},{6,7},{7,6},{8,9},{9,8},{10,11... | collective-permute-start | bytes 1572872 | tf_op jit(solution)/shard_map/ppermute | solution.py:46
  396.1 95.1 %collective-permute-start.55 = (bf16[2,128,2048]{2,1,0:T(8,128)(2,1)}, bf16[2,128,2048]{2,1,0:T(8,128)(2,1)}, u32[]{:S(2)}, u32[]{:S(2)}) collective-permute-start(bf16[2,128,2048]{2,1,0:T(8,128)(2,1)} %get-tuple-element.153), channel_id=1, source_target_pairs={{0,1},{1,0},{2,3},{3,2},{4,5},{5,4},{6,7},{7,6},{8,9},{9,8},{10,11... | collective-permute-start | bytes 3145736 | tf_op jit(solution)/shard_map/ppermute | solution.py:46
  397.0 154.3 %collective-permute-start.54 = (bf16[128,2048]{1,0:T(8,128)(2,1)}, bf16[128,2048]{1,0:T(8,128)(2,1)}, u32[]{:S(2)}, u32[]{:S(2)}) collective-permute-start(bf16[128,2048]{1,0:T(8,128)(2,1)} %slice_bitcast_fusion.9), channel_id=1, source_target_pairs={{0,1},{1,0},{2,3},{3,2},{4,5},{5,4},{6,7},{7,6},{8,9},{9,8},{10,11... | collective-permute-start | bytes 1572872 | tf_op jit(solution)/shard_map/ppermute | solution.py:46
  397.6 25.2 %collective-permute-start.82 = (bf16[2,2,256,128]{3,2,1,0:T(8,128)(2,1)S(1)}, bf16[2,2,256,128]{3,2,1,0:T(8,128)(2,1)S(1)}, u32[]{:S(2)}, u32[]{:S(2)}) collective-permute-start(bf16[2,2,256,128]{3,2,1,0:T(8,128)(2,1)S(1)} %pad_maximum_fusion.10), channel_id=1, source_target_pairs={{0,2},{2,4},{4,6},{6,0},{1,3},{3,5},{5,7},{7,1},{8,10},{10,12},{12... | collective-permute-start | bytes 786440 | tf_op jit(solution)/shard_map/ppermute | solution.py:46
  403.5 19.3 %collective-permute-start.84 = (bf16[2,2,256,128]{3,2,1,0:T(8,128)(2,1)S(1)}, bf16[2,2,256,128]{3,2,1,0:T(8,128)(2,1)S(1)}, u32[]{:S(2)}, u32[]{:S(2)}) collective-permute-start(bf16[2,2,256,128]{3,2,1,0:T(8,128)(2,1)S(1)} %pad_maximum_fusion.11), channel_id=1, source_target_pairs={{0,6},{2,0},{4,2},{6,4},{1,7},{3,1},{5,3},{7,5},{8,14},{10,8},{12,... | collective-permute-start | bytes 786440 | tf_op jit(solution)/shard_map/ppermute | solution.py:46
  437.0 50.8 %collective-permute-start.63 = (bf16[2,64,2048]{2,1,0:T(8,128)(2,1)}, bf16[2,64,2048]{2,1,0:T(8,128)(2,1)}, u32[]{:S(2)}, u32[]{:S(2)}) collective-permute-start(bf16[2,64,2048]{2,1,0:T(8,128)(2,1)} %get-tuple-element.166), channel_id=1, source_target_pairs={{0,1},{1,0},{2,3},{3,2},{4,5},{5,4},{6,7},{7,6},{8,9},{9,8},{10,11... | collective-permute-start | bytes 1572872 | tf_op jit(solution)/shard_map/ppermute | solution.py:46
  474.4 30.8 %all-to-all-start.1 = ((bf16[16,128,128]{2,1,0:T(8,128)(2,1)}), bf16[16,128,128]{2,1,0:T(8,128)(2,1)S(1)}, u32[]{:S(2)}, u32[]{:S(2)}) async-start(bf16[16,128,128]{2,1,0:T(8,128)(2,1)} %bitcast.136), calls=%async_computation.1 | async-start | bytes 1048576 | tf_op jit(solution)/shard_map/all_to_all | solution.py:1027
  486.2 23.1 %collective-permute-start.62 = (bf16[2,128,2048]{2,1,0:T(8,128)(2,1)}, bf16[2,128,2048]{2,1,0:T(8,128)(2,1)}, u32[]{:S(2)}, u32[]{:S(2)}) collective-permute-start(bf16[2,128,2048]{2,1,0:T(8,128)(2,1)} %get-tuple-element.164), channel_id=1, source_target_pairs={{0,1},{1,0},{2,3},{3,2},{4,5},{5,4},{6,7},{7,6},{8,9},{9,8},{10,11... | collective-permute-start | bytes 3145736 | tf_op jit(solution)/shard_map/ppermute | solution.py:46
  486.4 93.3 %collective-permute-start.61 = (bf16[128,2048]{1,0:T(8,128)(2,1)}, bf16[128,2048]{1,0:T(8,128)(2,1)}, u32[]{:S(2)}, u32[]{:S(2)}) collective-permute-start(bf16[128,2048]{1,0:T(8,128)(2,1)} %slice_bitcast_fusion.8), channel_id=1, source_target_pairs={{0,1},{1,0},{2,3},{3,2},{4,5},{5,4},{6,7},{7,6},{8,9},{9,8},{10,11... | collective-permute-start | bytes 1572872 | tf_op jit(solution)/shard_map/ppermute | solution.py:46
  491.1 20.7 %collective-permute-start.64 = (bf16[2,64,2048]{2,1,0:T(8,128)(2,1)}, bf16[2,64,2048]{2,1,0:T(8,128)(2,1)}, u32[]{:S(2)}, u32[]{:S(2)}) collective-permute-start(bf16[2,64,2048]{2,1,0:T(8,128)(2,1)} %add_convert_fusion.5), channel_id=1, source_target_pairs={{0,16},{1,49},{16,32},{17,1},{32,48},{33,17},{48,0},{49,33},{2,18}... | collective-permute-start | bytes 1572872 | tf_op jit(solution)/shard_map/ppermute | solution.py:97
  502.3 28.5 %collective-permute-start.58 = (bf16[2,128,2048]{2,1,0:T(8,128)(2,1)}, bf16[2,128,2048]{2,1,0:T(8,128)(2,1)}, u32[]{:S(2)}, u32[]{:S(2)}) collective-permute-start(bf16[2,128,2048]{2,1,0:T(8,128)(2,1)} %fusion.18), channel_id=1, source_target_pairs={{0,16},{1,49},{16,32},{17,1},{32,48},{33,17},{48,0},{49,33},{2,18}... | collective-permute-start | bytes 3145736 | tf_op jit(solution)/shard_map/ppermute | solution.py:97
  532.8 18.5 %collective-permute-start.59 = (bf16[128,2048]{1,0:T(8,128)(2,1)}, bf16[128,2048]{1,0:T(8,128)(2,1)}, u32[]{:S(2)}, u32[]{:S(2)}) collective-permute-start(bf16[128,2048]{1,0:T(8,128)(2,1)} %slice_bitcast_fusion.2), channel_id=1, source_target_pairs={{0,1},{1,0},{2,3},{3,2},{4,5},{5,4},{6,7},{7,6},{8,9},{9,8},{10,11... | collective-permute-start | bytes 1572872 | tf_op jit(solution)/shard_map/ppermute | solution.py:46
  543.8 35.9 %collective-permute-start.66 = (bf16[128,2048]{1,0:T(8,128)(2,1)}, bf16[128,2048]{1,0:T(8,128)(2,1)S(1)}, u32[]{:S(2)}, u32[]{:S(2)}) collective-permute-start(bf16[128,2048]{1,0:T(8,128)(2,1)} %slice_bitcast_fusion), channel_id=1, source_target_pairs={{0,1},{1,0},{2,3},{3,2},{4,5},{5,4},{6,7},{7,6},{8,9},{9,8},{10,11... | collective-permute-start | bytes 1572872 | tf_op jit(solution)/shard_map/ppermute | solution.py:46
  592.2 26.4 %collective-permute-start.101 = (bf16[2,2,704,128]{3,2,1,0:T(8,128)(2,1)S(1)}, bf16[2,2,704,128]{3,2,1,0:T(8,128)(2,1)S(1)}, u32[]{:S(2)}, u32[]{:S(2)}) collective-permute-start(bf16[2,2,704,128]{3,2,1,0:T(8,128)(2,1)S(1)} %maximum_select_fusion), channel_id=1, source_target_pairs={{0,48},{16,0},{32,16},{48,32},{1,49},{17,1},{33,17},{49,33},{2,50}... | collective-permute-start | bytes 2162696 | tf_op jit(solution)/shard_map/ppermute | solution.py:46
  596.0 20.9 %collective-permute-start.110 = (bf16[2,704,128]{2,1,0:T(8,128)(2,1)S(1)}, bf16[2,704,128]{2,1,0:T(8,128)(2,1)S(1)}, u32[]{:S(2)}, u32[]{:S(2)}) collective-permute-start(bf16[2,704,128]{2,1,0:T(8,128)(2,1)S(1)} %maximum_select_fusion.5.refs_0_), channel_id=1, source_target_pairs={{0,48},{16,0},{32,16},{48,32},{1,49},{17,1},{33,17},{49,33},{2,50}... | collective-permute-start | bytes 1081352 | tf_op jit(solution)/shard_map/ppermute | solution.py:46
  598.7 23.4 %collective-permute-start.102 = (bf16[2,2,704,128]{3,2,1,0:T(8,128)(2,1)S(1)}, bf16[2,2,704,128]{3,2,1,0:T(8,128)(2,1)S(1)}, u32[]{:S(2)}, u32[]{:S(2)}) collective-permute-start(bf16[2,2,704,128]{3,2,1,0:T(8,128)(2,1)S(1)} %maximum_select_fusion), channel_id=1, source_target_pairs={{0,16},{16,32},{32,48},{48,0},{1,17},{17,33},{33,49},{49,1},{2,18}... | collective-permute-start | bytes 2162696 | tf_op jit(solution)/shard_map/ppermute | solution.py:46
  606.7 19.3 %collective-permute-start.112 = (bf16[1,704,128]{2,1,0:T(8,128)(2,1)S(1)}, bf16[1,704,128]{2,1,0:T(8,128)(2,1)S(1)}, u32[]{:S(2)}, u32[]{:S(2)}) collective-permute-start(bf16[1,704,128]{2,1,0:T(8,128)(2,1)S(1)} %slice.550), channel_id=1, source_target_pairs={{0,16},{16,32},{32,48},{48,0},{1,17},{17,33},{33,49},{49,1},{2,18}... | collective-permute-start | bytes 540680 | tf_op jit(solution)/shard_map/ppermute | solution.py:46
  (152 other events, 1497.0 us)
Sparse Core Ops, SparseCore 0:
  70.2 96.4 all-gather.2
  315.7 54.9 reduce-scatter.2
  373.7 44.2 reduce-scatter.4

commit v3 on v2

--- a/solution.py
+++ b/solution.py
@@ -50,39 +50,12 @@
     return shift(value, "core", 1)
 
 
-def ring_gather(block, axis):
-    half = block.shape[0] // 2
-    before = shift(block, axis, 1)
-    after = shift(block, axis, -1)
-    far_low = shift(before[:half], axis, 1)
-    far_high = shift(after[half:], axis, -1)
-    return block, after, jnp.concatenate([far_low, far_high], axis=0), before
-
-
 def small_gather(block, axis):
     return block, shift(block, axis, -1), shift(block, axis, 2), shift(block, axis, 1)
 
 
-def ring_scatter(parts, axis):
-    half = parts[2].shape[0] // 2
-    low = shift(parts[2][:half], axis, 1)
-    high = shift(parts[2][half:], axis, -1)
-    after = jnp.concatenate([add(parts[1][:half], low).astype(BF16), parts[1][half:]], axis=0)
-    before = jnp.concatenate([parts[3][:half], add(parts[3][half:], high).astype(BF16)], axis=0)
-    from_before = shift(after, axis, 1)
-    from_after = shift(before, axis, -1)
-    return add(parts[0], from_before) + from_after.astype(F32)
-
-
 def tie(*values):
     return lax.optimization_barrier(values)
-
-
-def ring_pieces(block, axis):
-    half = block.shape[0] // 2
-    before = shift(block, axis, 1)
-    after = shift(block, axis, -1)
-    return block, after, shift(before[:half], axis, 1), shift(after[half:], axis, -1), before
 
 
 def add(left, right):
@@ -102,28 +75,8 @@
     return lax.dynamic_slice_in_dim(got, core * (B // 2), B // 2, 1)
 
 
-def gather_tokens(block):
-    pair = jnp.stack([block, swap_core(block)])
-    got = along_y(pair)
-    far = along_y(send_half(got))
-    return (pair, got, swap_core(got), far, swap_core(far))
-
-
 FLIPPED = (0, 0, 1, 0, 1)
 LENGTHS = (B, B, B, B // 2, B // 2)
-
-
-def scatter_tokens(parts):
-    core = lax.axis_index("core")
-    first, behind, ahead, far, far_other = parts
-    far = add(far, swap_core(far_other)[::-1]).astype(BF16)
-    low = along_y(far)
-    ahead = add(ahead, swap_core(behind)[::-1]).astype(BF16)
-    own = add(first[0], swap_core(first[1]))
-    mine = lax.dynamic_slice_in_dim(ahead, core * (B // 2), B // 2, 1)
-    ahead = lax.dynamic_update_slice_in_dim(ahead, add(mine, low).astype(BF16), core * (B // 2), 1)
-    got = along_y(ahead)
-    return own + got[0].astype(F32) + swap_core(got[1]).astype(F32)
 
 
 def put_tokens(refs, rows_ref, sems, start):
@@ -290,7 +243,7 @@
 
 def project_qkv_kernel(*refs):
     place, x_refs, w_refs = refs[0], refs[1:6], refs[6:11]
-    scale_ref, cosine_ref, sine_ref, query_ref, kv_ref, w_out, rows, weights, sems = refs[11:]
+    cosine_ref, sine_ref, query_ref, kv_ref, scale_ref, w_out, rows, weights, sems = refs[11:]
     step = pl.program_id(0)
     tokens = put_tokens(x_refs, rows, sems, 0)
     columns = put_columns(place, w_refs, weights, sems, 10)
@@ -307,7 +260,10 @@
             copy.wait()
 
     tile = rows[pl.ds(pl.multiple_of(step * TILE, TILE), TILE), :]
-    pre = times_transposed(tile, weights[...]) * scale_ref[...]
+    wide = tile.astype(F32)
+    scale = lax.rsqrt(jnp.mean(wide * wide, axis=-1, keepdims=True) + eps)
+    scale_ref[...] = scale
+    pre = times_transposed(tile, weights[...]) * scale
     cosine, sine = cosine_ref[...], sine_ref[...]
     for i in range(2):
         part = pre[:, i * 2 * HD : (i + 1) * 2 * HD]
@@ -323,17 +279,18 @@
         back.wait()
 
 
-def project_qkv(place, x_pieces, w_pieces, scale, cosine, sine):
+def project_qkv(place, x_pieces, w_pieces, cosine, sine):
     tile = lambda lanes: pl.BlockSpec((TILE, lanes), lambda i, p: (i, 0))
     return pl.pallas_call(
         project_qkv_kernel,
         grid_spec=pltpu.PrefetchScalarGridSpec(
             num_scalar_prefetch=1,
             grid=(4,),
-            in_specs=[ANYWHERE] * 10 + [tile(1), tile(2 * HD), tile(2 * HD)],
+            in_specs=[ANYWHERE] * 10 + [tile(2 * HD), tile(2 * HD)],
             out_specs=[
                 pl.BlockSpec((1, HEADS, TILE, HD), lambda i, p: (i // 2, 0, i % 2, 0)),
                 pl.BlockSpec((1, TILE, 2 * HD), lambda i, p: (i // 2, i % 2, 0)),
+                tile(1),
                 ANYWHERE,
             ],
             scratch_shapes=[
@@ -342,11 +299,13 @@
                 pltpu.SemaphoreType.DMA((27,)),
             ],
         ),
-        out_shape=[shaped(2, HEADS, HALF, HD), shaped(2, HALF, 2 * HD), shaped(QKV, D)],
+        out_shape=[
+            shaped(2, HEADS, HALF, HD), shaped(2, HALF, 2 * HD), shaped(2 * HALF, 1, kind=F32), shaped(QKV, D),
+        ],
         compiler_params=params("arbitrary"),
         cost_estimate=cost(2 * 2 * HALF * QKV * D, 8),
         name="project_qkv",
-    )(place, *x_pieces, *w_pieces, scale, cosine, sine)
+    )(place, *x_pieces, *w_pieces, cosine, sine)
 
 
 def project_out_kernel(*refs):
@@ -532,92 +491,62 @@
 
 
 def attention_kernel(place_ref, query_ref, kv_ref, mixed_ref, log_ref, bias_ref):
-    head = pl.program_id(1)
-
-    @pl.when((pl.program_id(0) == 0) & (head == 0))
+    @pl.when(pl.program_id(0) == 0)
     def _():
         set_bias(place_ref, bias_ref)
 
     key, value = kv_ref[0, :, :HD], kv_ref[0, :, HD:]
-    scores = times_transposed(key, query_ref[0, 0]) + bias_ref[...]
-    top = jnp.max(scores, axis=0, keepdims=True)
-    weights = jnp.exp(scores - top)
-    total = jnp.sum(weights, axis=0, keepdims=True)
-    low = (weights * (1.0 / total)).astype(BF16)
-    mixed = outer_sum(value, low).T.astype(BF16)
-    for i in range(HEADS):
-
-        @pl.when(head == i)
-        def _():
-            mixed_ref[0, :, i * HD : (i + 1) * HD] = mixed
-
-    log_ref[0, 0] = top + jnp.log(total)
+    for head in range(HEADS):
+        scores = times_transposed(key, query_ref[0, head]) + bias_ref[...]
+        top = jnp.max(scores, axis=0, keepdims=True)
+        weights = jnp.exp(scores - top)
+        total = jnp.sum(weights, axis=0, keepdims=True)
+        low = (weights * (1.0 / total)).astype(BF16)
+        mixed_ref[0, :, head * HD : (head + 1) * HD] = outer_sum(value, low).T.astype(BF16)
+        log_ref[0, head] = top + jnp.log(total)
 
 
 def attention_back_kernel(
-    place_ref, query_ref, kv_ref, grad_ref, log_ref, grad_query_ref, earlier_ref, own_ref, bias_ref, grad_one, total
+    place_ref, query_ref, kv_ref, grad_ref, log_ref, grad_query_ref, earlier_ref, own_ref, bias_ref
 ):
-    head = pl.program_id(1)
-
-    @pl.when((pl.program_id(0) == 0) & (head == 0))
+    @pl.when(pl.program_id(0) == 0)
     def _():
         set_bias(place_ref, bias_ref)
 
-    for i in range(HEADS):
-
-        @pl.when(head == i)
-        def _():
-            grad_one[...] = grad_ref[0, :, i * HD : (i + 1) * HD]
-
     key, value = kv_ref[0, :, :HD], kv_ref[0, :, HD:]
-    query, grad = query_ref[0, 0], grad_one[...]
-    weights = jnp.exp(times_transposed(key, query) + bias_ref[...] - log_ref[0, 0])
-    grad_weights = times_transposed(value, grad)
-    delta = jnp.sum(weights * grad_weights, axis=0, keepdims=True)
-    grad_scores = (weights * (grad_weights - delta)).astype(BF16)
-    grad_query = outer_sum(key, grad_scores).T * HD ** (-0.5)
-    for i in range(HEADS):
-
-        @pl.when(head == i)
-        def _():
-            grad_query_ref[0, :, i * HD : (i + 1) * HD] = grad_query
-
-    grads = jnp.concatenate([matmul(grad_scores, query), matmul(weights.astype(BF16), grad)], axis=1)
-
-    @pl.when(head == 0)
-    def _():
-        total[...] = grads
-
-    @pl.when(head > 0)
-    def _():
-        total[...] += grads
-
-    @pl.when(head == HEADS - 1)
-    def _():
-        earlier_ref[0] = total[:HALF].astype(BF16)
-        own_ref[0] = total[HALF:]
-
-
-def head_block(*tail):
-    return pl.BlockSpec((1, 1) + tail, lambda s, h, place: (s, h, 0, 0))
+    grad_key = jnp.zeros((2 * HALF, HD), F32)
+    grad_value = jnp.zeros((2 * HALF, HD), F32)
+    for head in range(HEADS):
+        lanes = slice(head * HD, (head + 1) * HD)
+        query, grad = query_ref[0, head], grad_ref[0, :, lanes]
+        weights = jnp.exp(times_transposed(key, query) + bias_ref[...] - log_ref[0, head])
+        grad_weights = times_transposed(value, grad)
+        delta = jnp.sum(weights * grad_weights, axis=0, keepdims=True)
+        grad_scores = (weights * (grad_weights - delta)).astype(BF16)
+        grad_query_ref[0, :, lanes] = outer_sum(key, grad_scores).T * HD ** (-0.5)
+        grad_key += matmul(grad_scores, query)
+        grad_value += matmul(weights.astype(BF16), grad)
+    total = jnp.concatenate([grad_key, grad_value], axis=1)
+    earlier_ref[0] = total[:HALF].astype(BF16)
+    own_ref[0] = total[HALF:]
 
 
 def sequence_block(*tail):
-    return pl.BlockSpec((1,) + tail, lambda s, h, place: (s, 0, 0))
-
-
-def attention_call(kernel, in_specs, out_specs, out_shape, scratch, flops, name):
+    return pl.BlockSpec((1,) + tail, lambda s, place: (s,) + (0,) * len(tail))
+
+
+def attention_call(kernel, in_specs, out_specs, out_shape, flops, name):
     return pl.pallas_call(
         kernel,
         grid_spec=pltpu.PrefetchScalarGridSpec(
             num_scalar_prefetch=1,
-            grid=(2, HEADS),
+            grid=(2,),
             in_specs=in_specs,
             out_specs=out_specs,
-            scratch_shapes=[pltpu.VMEM((2 * HALF, HALF), F32)] + scratch,
+            scratch_shapes=[pltpu.VMEM((2 * HALF, HALF), F32)],
         ),
         out_shape=out_shape,
-        compiler_params=params("arbitrary", "arbitrary"),
+        compiler_params=params("arbitrary"),
         cost_estimate=cost(flops * 8 * 2 * HALF * HALF * HD * 2, 4),
         name=name,
     )
@@ -626,10 +555,9 @@
 def attention(place, query, kv):
     return attention_call(
         attention_kernel,
-        [head_block(HALF, HD), sequence_block(2 * HALF, 2 * HD)],
-        [sequence_block(HALF, HEADS * HD), head_block(1, HALF)],
+        [sequence_block(HEADS, HALF, HD), sequence_block(2 * HALF, 2 * HD)],
+        [sequence_block(HALF, HEADS * HD), sequence_block(HEADS, 1, HALF)],
         [shaped(2, HALF, HEADS * HD), shaped(2, HEADS, 1, HALF, kind=F32)],
-        [],
         2,
         "attention",
     )(place, query, kv)
@@ -639,8 +567,8 @@
     return attention_call(
         attention_back_kernel,
         [
-            head_block(HALF, HD), sequence_block(2 * HALF, 2 * HD),
-            sequence_block(HALF, HEADS * HD), head_block(1, HALF),
+            sequence_block(HEADS, HALF, HD), sequence_block(2 * HALF, 2 * HD),
+            sequence_block(HALF, HEADS * HD), sequence_block(HEADS, 1, HALF),
         ],
         [sequence_block(HALF, HEADS * HD), sequence_block(HALF, 2 * HD), sequence_block(HALF, 2 * HD)],
         [
@@ -648,7 +576,6 @@
             shaped(2, HALF, 2 * HD),
             shaped(2, HALF, 2 * HD, kind=F32),
         ],
-        [pltpu.VMEM((HALF, HD), BF16), pltpu.VMEM((2 * HALF, 2 * HD), F32)],
         5,
         "attention_back",
     )(place, query, kv, grad, log_total)
@@ -889,6 +816,68 @@
     )(place, *pieces)
 
 
+class Flow:
+    def __init__(self, steps):
+        self.steps, self.result, self.sent = steps, None, None
+        self.move(None)
+
+    def move(self, arrived):
+        try:
+            self.sent = self.steps.send(arrived)
+        except StopIteration as end:
+            self.sent, self.result = (), end.value
+
+
+def stage(flows, *values):
+    flows = [flow for flow in flows if flow.result is None]
+    sizes = [len(flow.sent) for flow in flows]
+    leaves, tree = jax.tree.flatten(values)
+    tied = tie(*[v for flow in flows for v in flow.sent], *leaves)
+    for flow, size in zip(flows, sizes):
+        flow.move(tied[:size])
+        tied = tied[size:]
+    return jax.tree.unflatten(tree, tied)
+
+
+def gather_steps(block):
+    (other,) = yield (swap_core(block),)
+    pair = jnp.stack([block, other])
+    (got,) = yield (along_y(pair),)
+    far, swapped = yield (along_y(send_half(got)), swap_core(got))
+    (far_swapped,) = yield (swap_core(far),)
+    return pair, got, swapped, far, far_swapped
+
+
+def scatter_steps(parts):
+    core = lax.axis_index("core")
+    first, behind, ahead, far, far_other = parts
+    far_got, behind_got, first_got = yield (swap_core(far_other), swap_core(behind), swap_core(first[1]))
+    far = add(far, far_got[::-1]).astype(BF16)
+    (low,) = yield (along_y(far),)
+    ahead = add(ahead, behind_got[::-1])
+    mine = lax.dynamic_slice_in_dim(ahead, core * (B // 2), B // 2, 1) + low.astype(F32)
+    ahead = lax.dynamic_update_slice_in_dim(ahead, mine, core * (B // 2), 1).astype(BF16)
+    (got,) = yield (along_y(ahead),)
+    (last,) = yield (swap_core(got[1]),)
+    return add(first[0], first_got) + got[0].astype(F32) + last.astype(F32)
+
+
+def ring_gather_steps(block, axis):
+    half = block.shape[0] // 2
+    before, after = yield (shift(block, axis, 1), shift(block, axis, -1))
+    low, high = yield (shift(before[:half], axis, 1), shift(after[half:], axis, -1))
+    return block, after, low, high, before
+
+
+def ring_scatter_steps(parts, axis):
+    half = parts[2].shape[0] // 2
+    low, high = yield (shift(parts[2][:half], axis, 1), shift(parts[2][half:], axis, -1))
+    after = jnp.concatenate([add(parts[1][:half], low).astype(BF16), parts[1][half:]], axis=0)
+    before = jnp.concatenate([parts[3][:half], add(parts[3][half:], high).astype(BF16)], axis=0)
+    from_before, from_after = yield (shift(after, axis, 1), shift(before, axis, -1))
+    return add(parts[0], from_before) + from_after.astype(F32)
+
+
 def on_device(
     layer_input,
     positions,
@@ -915,118 +904,172 @@
     def by_zhi(mine, got):
         return jnp.where(zhi == 0, jnp.stack([mine, got]), jnp.stack([got, mine]))
 
+    def column_steps(mine, other):
+        (got,) = yield (swap_core(other),)
+        pair = by_core(mine, got)
+        (got,) = yield (shift(pair, "zhi", 1),)
+        return (yield from ring_gather_steps(by_zhi(pair, got), "x"))
+
+    def hidden_steps(mine, other, down):
+        (got,) = yield (swap_core(other),)
+        piece = jnp.concatenate([by_core(mine, got).reshape(2 * FFL, B), down], axis=0)
+        pieces = yield from ring_gather_steps(piece, "z")
+        return jnp.concatenate(pieces, axis=0).reshape(4, 3 * FFL, B)
+
+    def block_steps(pair):
+        keep = lax.dynamic_index_in_dim(pair, core, 0, keepdims=False)
+        (got,) = yield (swap_core(lax.dynamic_index_in_dim(pair, 1 - core, 0, keepdims=False)),)
+        own = by_core(keep, got)
+        (got,) = yield (shift(own, "zlo", 1),)
+        return (yield from ring_gather_steps(by_zlo(own, got), "y"))
+
+    def whole_ring(pieces):
+        own, after, low, high, before = pieces
+        return own, after, jnp.concatenate([low, high], axis=0), before
+
+    def attention_steps(terms):
+        rows = terms.shape[3]
+        column = yield from ring_scatter_steps([terms[i] for i in range(4)], "x")
+        column = column.astype(BF16).reshape(2, 2, 2, rows // 2, B).transpose(0, 2, 1, 3, 4).reshape(4, rows, B)
+        z = 2 * zhi + zlo
+        column = [lax.dynamic_index_in_dim(column, (z + i) % 4, 0, keepdims=False) for i in range(4)]
+        own = yield from ring_scatter_steps(column, "z")
+        pieces = yield from block_steps(own.astype(BF16).reshape(2, rows // 2, B))
+        ring = jnp.roll(jnp.stack(whole_ring(pieces)), y, axis=0)
+        return ring.transpose(0, 2, 1, 3, 4).reshape(4, 2, rows, B)
+
+    def gate_up_steps(sums):
+        own = yield from ring_scatter_steps([sums[i] for i in range(4)], "z")
+        pieces = yield from block_steps(own.astype(BF16).reshape(2, FFL, B))
+        return whole_ring(pieces)
+
+    def down_steps(sums):
+        own = yield from ring_scatter_steps([sums[i] for i in range(4)], "z")
+        own = own.astype(BF16)
+        (got,) = yield (shift(own, "zlo", 1),)
+        pieces = yield from ring_gather_steps(by_zlo(own, got), "y")
+        return whole_ring(pieces)
+
+    def all_to_all_steps(value):
+        (got,) = yield (lax.all_to_all(value, FSDP, 0, 0, tiled=True),)
+        return got
+
     x_low = layer_input[0]
-    x_pair = jnp.stack([x_low, swap_core(x_low)])
-    qkv_mine, qkv_other = prepare_qkv(place, w_query, w_key, w_value, attn_gain[:, None])
-    qkv_pair = by_core(qkv_mine, swap_core(qkv_other))
-    x_pair, qkv_pair = tie(x_pair, qkv_pair)
-
-    x_got = along_y(x_pair)
-    qkv_column = by_zhi(qkv_pair, shift(qkv_pair, "zhi", 1))
+    place_rows = positions.astype(F32)
+    tokens = Flow(gather_steps(x_low))
+    places = small_gather(place_rows, "y")
+    qkv = Flow(column_steps(*prepare_qkv(place, w_query, w_key, w_value, attn_gain[:, None])))
+    hidden_rows = Flow(hidden_steps(*prepare_ff(place, w_gate, w_up, w_down, mlp_gain[:, None])))
+    places, w_out = stage([tokens, qkv, hidden_rows], places, w_output)
+
+    places = jnp.stack(places)
+    places_other = swap_core(places)
+    output_rows = Flow(all_to_all_steps(w_out.reshape(B, 16, B).transpose(1, 0, 2)))
+    places, places_other, x_low = stage([tokens, qkv, hidden_rows], places, places_other, x_low)
+
+    places = jnp.stack([places, places_other])
+    near = jnp.where(core == 0, places[:, 3], places[:, 1])
+    ahead = jnp.where(core == 0, places[:, 1], places[:, 3])
+    far = jnp.where(core == 0, places[:, 2], jnp.roll(places[:, 2], B // 2, axis=-1))
+    places = jnp.concatenate([places[:, 0], near, ahead, far], axis=-1).reshape(2 * HALF, 1)
+    frequency = theta ** (-jnp.arange(0, HD, 2).astype(F32) / HD)
+    angles = places * jnp.tile(frequency, 4)
+    cosine, sine = jnp.cos(angles), jnp.sin(angles)
     inputs = x_low.astype(F32)
     scale_one = lax.rsqrt(jnp.mean(inputs * inputs, axis=-1, keepdims=True) + eps)
-    meta = jnp.concatenate([positions.astype(F32), scale_one.reshape(1, B)], axis=0)
-    gain_two, meta, _ = tie(mlp_gain[:, None], meta, x_pair)
-    ff_mine, ff_other, ff_down = prepare_ff(place, w_gate, w_up, w_down, gain_two)
-    ff_piece = jnp.concatenate([by_core(ff_mine, swap_core(ff_other)).reshape(2 * FFL, B), ff_down], axis=0)
-    x_got, qkv_column, ff_piece = tie(x_got, qkv_column, ff_piece)
-
-    x_far = along_y(send_half(x_got))
-    x_swapped = swap_core(x_got)
-    qkv_before, qkv_after = shift(qkv_column, "x", 1), shift(qkv_column, "x", -1)
-    ff_before, ff_after = shift(ff_piece, "z", 1), shift(ff_piece, "z", -1)
-    meta = jnp.stack(small_gather(meta, "y"))
-    x_far, x_swapped, qkv_before, qkv_after, ff_before, ff_after, meta = tie(
-        x_far, x_swapped, qkv_before, qkv_after, ff_before, ff_after, meta
+    cosine, sine, scale_one, grad_low = stage(
+        [tokens, qkv, hidden_rows, output_rows], cosine, sine, scale_one, out_grad[0]
     )
 
-    x_pieces = (x_pair, x_got, x_swapped, x_far, swap_core(x_far))
-    qkv_pieces = (
-        qkv_column, qkv_after, shift(qkv_before[:1], "x", 1), shift(qkv_after[1:], "x", -1), qkv_before,
+    o_rows = output_rows.result.reshape(D, B)
+    o_block = Flow(
+        column_steps(own_rows(o_rows, y, core, HEADS * HD), own_rows(o_rows, y, 1 - core, HEADS * HD))
     )
-    half = 3 * FFL // 2
-    ff_low, ff_high = shift(ff_before[:half], "z", 1), shift(ff_after[half:], "z", -1)
-    ff_ring = jnp.concatenate([ff_piece, ff_after, ff_low, ff_high, ff_before], axis=0).reshape(4, 3 * FFL, B)
-    meta = jnp.stack([meta, swap_core(meta)])
-    near = jnp.where(core == 0, meta[:, 3], meta[:, 1])
-    ahead = jnp.where(core == 0, meta[:, 1], meta[:, 3])
-    far = jnp.where(core == 0, meta[:, 2], jnp.roll(meta[:, 2], B // 2, axis=-1))
-    meta = jnp.concatenate([meta[:, 0], near, ahead, far], axis=-1)
-    scale_all = meta[:, 1].reshape(2 * HALF, 1)
-    frequency = theta ** (-jnp.arange(0, HD, 2).astype(F32) / HD)
-    angles = meta[:, 0].reshape(2 * HALF, 1) * jnp.tile(frequency, 4)
-    cosine, sine = jnp.cos(angles), jnp.sin(angles)
-    x_pieces, qkv_pieces, ff_ring, out_low, w_out = tie(x_pieces, qkv_pieces, ff_ring, out_grad[0], w_output)
-
-    ff_all = lax.all_gather(ff_ring, "x", axis=0, tiled=False)
-    query, key_value, qkv_full = project_qkv(place, x_pieces, qkv_pieces, scale_all, cosine, sine)
-    o_rows = lax.all_to_all(w_out.reshape(B, 16, B).transpose(1, 0, 2), FSDP, 0, 0, tiled=True).reshape(D, B)
-    o_pair = by_core(
-        own_rows(o_rows, y, core, HEADS * HD), swap_core(own_rows(o_rows, y, 1 - core, HEADS * HD))
-    )
-    o_column = by_zhi(o_pair, shift(o_pair, "zhi", 1))
-    o_pieces = ring_pieces(o_column, "x")
-    grad_pieces = gather_tokens(out_low)
+    grads = Flow(gather_steps(grad_low))
+    stage([tokens, qkv, hidden_rows, o_block, grads])
+
+    x_pieces = tokens.result
+    ff_all = lax.all_gather(hidden_rows.result, "x", axis=0, tiled=False)
+    query, key_value, scale_all, qkv_full = project_qkv(place, x_pieces, qkv.result, cosine, sine)
+    query, key_value = stage([o_block, grads], query, key_value)
     earlier = lax.ppermute(key_value, "zlo", [(0, 1)])
+    query, key_value, earlier = stage([o_block, grads], query, key_value, earlier)
     key_value = jnp.concatenate([earlier, key_value], axis=1)
     mixed, log_total = attention(place, query, key_value)
+    (mixed,) = stage([o_block, grads], mixed)
     mixed = mixed.reshape(2 * HALF, HEADS * HD)
-    *parts, o_full = project_out(place, o_pieces, mixed)
-    hidden = inputs + scatter_tokens(parts)
+    *parts, o_full = project_out(place, o_block.result, mixed)
+    grad_pieces = grads.result
+    sums = Flow(scatter_steps(parts))
+    for _ in range(4):
+        stage([sums])
+    hidden = inputs + sums.result
     scale_two = lax.rsqrt(jnp.mean(hidden * hidden, axis=-1, keepdims=True) + eps)
-    normed_pieces = gather_tokens((hidden * scale_two).astype(BF16))
+    normed = Flow(gather_steps((hidden * scale_two).astype(BF16)))
+    for _ in range(4):
+        stage([normed])
+    normed_pieces = normed.result
 
     activation, act_t, gate_t, up_t, *parts, down_full = feed_forward(place, normed_pieces, grad_pieces, ff_all)
-    grad_normed_two = scatter_tokens(parts)
+    sums = Flow(scatter_steps(parts))
+    (act_t,) = stage([sums], act_t)
+    down_terms = ff_terms(down_kernel, place, grad_pieces, (act_t,), FFL, "down_terms")
+    down_terms, gate_t = stage([sums], down_terms, gate_t)
+    down_sum = lax.psum_scatter(down_terms, "x", scatter_dimension=0, tiled=True)[0]
     gate_up_terms = ff_terms(gate_up_kernel, place, normed_pieces, (gate_t, up_t), 2 * FFL, "gate_up_terms")
-    down_terms = ff_terms(down_kernel, place, grad_pieces, (act_t,), FFL, "down_terms")
-    down_parts = project(activation, down_full)
-
+    (gate_up_terms,) = stage([sums], gate_up_terms)
+    gate_up_sum = lax.psum_scatter(gate_up_terms, "x", scatter_dimension=0, tiled=True)[0]
+    stage([sums])
+
+    grad_normed_two = sums.result
     mean_two = jnp.mean(grad_normed_two * hidden, axis=-1, keepdims=True)
     grad_hidden = (
         out_grad[0].astype(F32)
         + scale_two * grad_normed_two
         - hidden * (scale_two * scale_two * scale_two) * mean_two
     )
-    hidden_low, gate_up_terms, down_terms = tie(grad_hidden.astype(BF16), gate_up_terms, down_terms)
-    gate_up_sum = lax.psum_scatter(gate_up_terms, "x", scatter_dimension=0, tiled=True)[0]
-    down_sum = lax.psum_scatter(down_terms, "x", scatter_dimension=0, tiled=True)[0]
-    hidden_grad_pieces = gather_tokens(hidden_low)
-    grad_mixed, output_terms = grad_of_mixed(place, hidden_grad_pieces, o_full, mixed)
-    grad_mixed, down_parts = tie(grad_mixed, down_parts)
-    result = hidden + scatter_tokens(down_parts)
+    hidden_grads = Flow(gather_steps(grad_hidden.astype(BF16)))
+    (activation,) = stage([hidden_grads], activation)
+    down_parts = project(activation, down_full)
+    down_parts = stage([hidden_grads], *down_parts)
+    result = Flow(scatter_steps(down_parts))
+    stage([hidden_grads, result])
+    stage([hidden_grads])
+
+    grad_mixed, output_terms = grad_of_mixed(place, hidden_grads.result, o_full, mixed)
+    grad_mixed, output_terms = stage([result], grad_mixed, output_terms)
+    output_sums = Flow(attention_steps(output_terms))
     grad_query, grad_earlier, grad_own = attention_back(
         place, query, key_value, grad_mixed.reshape(2, HALF, HEADS * HD), log_total
     )
+    grad_query, grad_earlier, grad_own = stage([result, output_sums], grad_query, grad_earlier, grad_own)
     later = lax.ppermute(grad_earlier, "zlo", [(1, 0)])
+    later, grad_query = stage([result, output_sums], later, grad_query)
     *parts, grad_t = qkv_back(grad_query, grad_own, later, cosine, sine, scale_all, qkv_full)
-    grad_normed = scatter_tokens(parts)
+    sums = Flow(scatter_steps(parts))
+    (grad_t,) = stage([sums, output_sums], grad_t)
     qkv_term = qkv_terms(place, x_pieces, grad_t)
+    qkv_term, down_sum = stage([sums, output_sums], qkv_term, down_sum)
+    down = Flow(down_steps(down_sum))
+    qkv_sums = Flow(attention_steps(qkv_term))
+    (gate_up_sum,) = stage([sums, qkv_sums, down, output_sums], gate_up_sum)
+    gate_up = Flow(gate_up_steps(gate_up_sum))
+    stage([sums, output_sums, qkv_sums, down, gate_up])
+    grad_normed = sums.result
     mean_one = jnp.mean(grad_normed * inputs, axis=-1, keepdims=True)
     input_grad = (
         grad_hidden
         + scale_one * grad_normed
         - inputs * (scale_one * scale_one * scale_one) * mean_one
     )
-
-    def own_block(pair):
-        keep = lax.dynamic_index_in_dim(pair, core, 0, keepdims=False)
-        return by_core(keep, swap_core(lax.dynamic_index_in_dim(pair, 1 - core, 0, keepdims=False)))
-
-    def attention_sums(terms):
-        rows = terms.shape[3]
-        column = ring_scatter([terms[i] for i in range(4)], "x").astype(BF16)
-        column = column.reshape(2, 2, 2, rows // 2, B).transpose(0, 2, 1, 3, 4).reshape(4, rows, B)
-        z = 2 * zhi + zlo
-        column = [lax.dynamic_index_in_dim(column, (z + i) % 4, 0, keepdims=False) for i in range(4)]
-        own = own_block(ring_scatter(column, "z").astype(BF16).reshape(2, rows // 2, B))
-        own = by_zlo(own, shift(own, "zlo", 1)).transpose(1, 0, 2, 3).reshape(2, rows, B)
-        return jnp.roll(jnp.stack(ring_gather(own, "y")), y, axis=0)
-
-    output_rows = attention_sums(output_terms).reshape(16, B, B)
-    output_grad = lax.all_to_all(output_rows, FSDP, 0, 0, tiled=True)
+    input_grad = input_grad.astype(BF16)
+    rest = [gate_up, qkv_sums, down, output_sums]
+    while any(flow.result is None for flow in rest):
+        stage(rest)
+
+    output_grad = lax.all_to_all(output_sums.result.reshape(16, B, B), FSDP, 0, 0, tiled=True)
     output_grad = output_grad.transpose(1, 0, 2).reshape(B, D).astype(F32)
-    sums = attention_sums(qkv_term)
+    sums = qkv_sums.result
     query_grad = sums[:, :, : HEADS * HD].reshape(D, B).T.astype(F32)
     key_grad = jnp.sum(sums[:, :, HEADS * HD : (HEADS + 1) * HD].astype(F32), axis=1)
     key_grad = key_grad.reshape(KV * HD, B).T
@@ -1037,21 +1080,14 @@
         + jnp.sum(key_grad * w_key.astype(F32), axis=1)
         + jnp.sum(value_grad * w_value.astype(F32), axis=1)
     )
-
-    gate_up = ring_scatter([gate_up_sum[i] for i in range(4)], "z").astype(BF16)
-    gate_up = own_block(gate_up.reshape(2, FFL, B))
-    gate_up = by_zlo(gate_up, shift(gate_up, "zlo", 1))
-    gate_up = ring_gather(gate_up, "y")
     gain_two = mlp_gain[:, None]
-    gate_grad, gate_gain = finish_hidden(place, [p[0] for p in gate_up], w_gate, gain_two)
-    up_grad, up_gain = finish_hidden(place, [p[1] for p in gate_up], w_up, gain_two)
-    down = ring_scatter([down_sum[i] for i in range(4)], "z").astype(BF16)
-    down = by_zlo(down, shift(down, "zlo", 1))
-    down_grad = finish_down(place, ring_gather(down, "y"))
+    gate_grad, gate_gain = finish_hidden(place, [p[0] for p in gate_up.result], w_gate, gain_two)
+    up_grad, up_gain = finish_hidden(place, [p[1] for p in gate_up.result], w_up, gain_two)
+    down_grad = finish_down(place, down.result)
     one = attn_gain[:, None]
     return (
-        result.astype(BF16)[None],
-        input_grad.astype(BF16)[None],
+        (hidden + result.result).astype(BF16)[None],
+        input_grad[None],
         attn_gain_grad,
         query_grad * one,
         key_grad * one,

time: 663 us -> 570 us (0.86)
  the two profiles are of different devices: /device:TPU:1 before, /device:TPU:0 now
where the time goes in v3:
time: 570 us; the launch traced here: 559 us
  waiting for transfers between devices  175 us (31%)
  Pallas kernels  159 us (28%)
  starting transfers between devices  122 us (21%)
  local copies, waits for them, and re-layouts  43.5 us (8%)
  other arithmetic  43.1 us (8%)
  between operations  16.4 us (3%)
    ppermute x16, waiting for transfers between devices, along_y(): return lax.ppermute(value, ('y', 'core'), pairs)  76.5 us
    ppermute x76, waiting for transfers between devices, shift(): lax.ppermute(value, axis, [(i, (i + by) % size) for i in range(size)])  73.3 us
    ppermute x76, starting transfers between devices, shift(): lax.ppermute(value, axis, [(i, (i + by) % size) for i in range(size)])  69.9 us
    pallas_call x1, Pallas kernels, feed_forward(): pl.pallas_call(feed_forward_kernel, grid_spec=pltpu.PrefetchScalarGridSpe...  32.5 us
    ppermute x20, starting transfers between devices, shift(): lax.ppermute(value, ('zlo', 'zhi'), [(at[z], at[(z + by) % 4]) for z in r...  30.9 us
    pallas_call x2, Pallas kernels, ff_terms(): pl.pallas_call(kernel, grid_spec=pltpu.PrefetchScalarGridSpec(num_scalar_...  25.7 us
    ppermute x20, waiting for transfers between devices, shift(): lax.ppermute(value, ('zlo', 'zhi'), [(at[z], at[(z + by) % 4]) for z in r...  24.7 us
    unnamed x192, local copies, waits for them, and re-layouts  19.9 us
  transfers between devices with their start and end apart: 119, of which 48 were waited for; matrix products, arithmetic and copies ran while one was open for 12% of the time, Pallas kernels for 23%

profile of v3, /device:TPU:0, one launch (start us, length us, event | category | flops | bytes accessed | tf_op | source)
XLA Modules:
  0.0 559.2 jit_solution(2081957889884031083)
XLA Ops:
  9.4 4.9 prepare_ff.1
  36.2 5.6 all-to-all-start
  43.3 11.7 %collective-permute-done.7 = bf16[2,384,128]{2,1,0:T(8,128)(2,1)} collective-permute-done((bf16[2,384,128]{2,1,0:T(8,128)(2,1)}, bf16[2,384,128]{2,1,0:T(8,128)(2,1)}, u32[]{:S(2)}, u32[]{:S(2)}) %collective-permute-start.7) | collective-permute-done | bytes 196640 | tf_op jit(solution)/shard_map/ppermute | solution.py:46
  68.6 4.2 collective-permute-done.15
  99.0 10.4 %project_qkv.1 = (bf16[2,4,512,64]{3,2,1,0:T(8,128)(2,1)}, bf16[2,512,128]{2,1,0:T(8,128)(2,1)}, f32[1024,1]{1,0:T(8,128)}, bf16[384,2048]{1,0:T(8,128)(2,1)}) custom-call(s32[5]{0:T(128)} %stack.310.place.refs_0_.place_ref, bf16[2,128,2048]{2,1,0:T(8,128)(2,1)} %copy-done.4, bf16[2,128,2048]{2,1,0:T(8,128)(2,1)} %collective-permute-done.6.refs_2_, ...), custom_call_target="tpu_custom_call" | custom-call | flops 1610612736 | bytes 8388608 | tf_op jit(solution)/shard_map/project_qkv/pallas_call | solution.py:284
  119.1 9.7 %collective-permute-done.24.refs_5_ = bf16[2,2,256,128]{3,2,1,0:T(8,128)(2,1)S(1)} collective-permute-done((bf16[2,2,256,128]{3,2,1,0:T(8,128)(2,1)S(1)}, bf16[2,2,256,128]{3,2,1,0:T(8,128)(2,1)S(1)}, u32[]{:S(2)}, u32[]{:S(2)}) %collective-permute-start.24) | collective-permute-done | bytes 262176 | tf_op jit(solution)/shard_map/ppermute | solution.py:46
  133.5 11.0 %attention.1 = (bf16[2,512,256]{2,1,0:T(8,128)(2,1)}, f32[2,4,1,512]{3,2,1,0:T(1,128)}) custom-call(s32[5]{0:T(128)} %stack.310.place.refs_0_.place_ref, bf16[2,4,512,64]{3,2,1,0:T(8,128)(2,1)} %get-tuple-element.240.query_ref, bf16[2,1024,128]{2,1,0:T(8,128)(2,1)} %copy-done.59), custom_call_target="tpu_custom_call" | custom-call | flops 1073741824 | bytes 4194304 | tf_op jit(solution)/shard_map/attention/pallas_call | solution.py:556
  145.3 7.4 %project_out.1 = (bf16[2,128,2048]{2,1,0:T(8,128)(2,1)}, bf16[2,128,2048]{2,1,0:T(8,128)(2,1)}, bf16[2,128,2048]{2,1,0:T(8,128)(2,1)}, bf16[2,64,2048]{2,1,0:T(8...) custom-call(s32[5]{0:T(128)} %stack.310.place.refs_0_.place_ref, ...), custom_call_target="tpu_custom_call" | custom-call | flops 1073741824 | bytes 7340032 | tf_op jit(solution)/shard_map/project_out/pallas_call | solution.py:334
  160.3 8.4 %collective-permute-done.35 = bf16[2,64,2048]{2,1,0:T(8,128)(2,1)S(1)} collective-permute-done((bf16[2,64,2048]{2,1,0:T(8,128)(2,1)S(1)}, bf16[2,64,2048]{2,1,0:T(8,128)(2,1)S(1)}, u32[]{:S(2)}, u32[]{:S(2)}) %collective-permute-start.35) | collective-permute-done | bytes 524320 | tf_op jit(solution)/shard_map/ppermute | solution.py:70
  169.5 15.6 %collective-permute-done.36 = bf16[2,128,2048]{2,1,0:T(8,128)(2,1)S(1)} collective-permute-done((bf16[2,128,2048]{2,1,0:T(8,128)(2,1)S(1)}, bf16[2,128,2048]{2,1,0:T(8,128)(2,1)S(1)}, u32[]{:S(2)}, u32[]{:S(2)}) %collective-permute-start.36) | collective-permute-done | bytes 1048608 | tf_op jit(solution)/shard_map/ppermute | solution.py:70
  190.3 16.0 %collective-permute-done.39.refs_2_ = bf16[2,128,2048]{2,1,0:T(8,128)(2,1)S(1)} collective-permute-done((bf16[2,128,2048]{2,1,0:T(8,128)(2,1)S(1)}, bf16[2,128,2048]{2,1,0:T(8,128)(2,1)S(1)}, u32[]{:S(2)}, u32[]{:S(2)}) %collective-permute-start.39) | collective-permute-done | bytes 1048608 | tf_op jit(solution)/shard_map/ppermute | solution.py:70
  206.4 10.4 %collective-permute-done.40.refs_4_ = bf16[2,64,2048]{2,1,0:T(8,128)(2,1)S(1)} collective-permute-done((bf16[2,64,2048]{2,1,0:T(8,128)(2,1)S(1)}, bf16[2,64,2048]{2,1,0:T(8,128)(2,1)S(1)}, u32[]{:S(2)}, u32[]{:S(2)}) %collective-permute-start.40) | collective-permute-done | bytes 524320 | tf_op jit(solution)/shard_map/ppermute | solution.py:70
  219.8 32.5 %feed_forward.1 = (bf16[1024,704]{1,0:T(8,128)(2,1)}, bf16[704,1024]{1,0:T(8,128)(2,1)}, bf16[704,1024]{1,0:T(8,128)(2,1)}, bf16[704,1024]{1,0:T(8,128)(2,1)}, b...) custom-call(s32[5]{0:T(128)} %stack.310.place.refs_0_.place_ref, ...), custom_call_target="tpu_custom_call" | custom-call | flops 14763950080 | bytes 33554432 | tf_op jit(solution)/shard_map/feed_forward/pallas_call | solution.py:666
  258.8 10.5 %down_terms.1 = bf16[4,4,704,128]{3,2,1,0:T(8,128)(2,1)} custom-call(s32[5]{0:T(128)} %stack.310.place.refs_0_.place_ref, bf16[2,128,2048]{2,1,0:T(8,128)(2,1)} %copy-done.23, bf16[2,128,2048]{2,1,0:T(8,128)(2,1)} %copy-done.49, bf16[2,128,2048]{2,1,0:T(8,128)(2,1)} %copy-done.75, bf16[2,64,2048]{2,1,0:T(8,128)(2,1)} %copy-done.78, ...), custom_call_target="tpu_custom_call" | custom-call | flops 2952790016 | bytes 12582912 | tf_op jit(solution)/shard_map/down_terms/pallas_call | solution.py:736
  273.3 15.2 %gate_up_terms.1 = bf16[4,4,1408,128]{3,2,1,0:T(8,128)(2,1)} custom-call(s32[5]{0:T(128)} %stack.310.place.refs_0_.place_ref, bf16[2,128,2048]{2,1,0:T(8,128)(2,1)} %copy-done.24, bf16[2,128,2048]{2,1,0:T(8,128)(2,1)} %copy-done.50, bf16[2,128,2048]{2,1,0:T(8,128)(2,1)} %copy-done.76, bf16[2,64,2048]{2,1,0:T(8,128)(2,1)} %copy-done.80, ...), custom_call_target="tpu_custom_call" | custom-call | flops 5905580032 | bytes 16777216 | tf_op jit(solution)/shard_map/gate_up_terms/pallas_call | solution.py:736
  299.8 8.0 %project.1 = (bf16[2,128,2048]{2,1,0:T(8,128)(2,1)}, bf16[2,128,2048]{2,1,0:T(8,128)(2,1)}, bf16[2,128,2048]{2,1,0:T(8,128)(2,1)}, bf16[2,64,2048]{2,1,0:T(8,128)(2,1)}, bf16[2,64,2048]{2,1,0:T(8,128)(2,1)}) custom-call(bf16[1024,704]{1,0:T(8,128)(2,1)} %get-tuple-element.278.left_ref, bf16[704,2048]{1,0:T(8,128)(2,1)} %get-tuple-element.279.weight_ref), custom_call_target="tpu_custom_call" | custom-call | flops 2952790016 | bytes 8388608 | tf_op jit(solution)/shard_map/project/pallas_call | solution.py:356
  307.8 7.5 %collective-permute-done.50.refs_2_ = bf16[2,128,2048]{2,1,0:T(8,128)(2,1)S(1)} collective-permute-done((bf16[2,128,2048]{2,1,0:T(8,128)(2,1)S(1)}, bf16[2,128,2048]{2,1,0:T(8,128)(2,1)S(1)}, u32[]{:S(2)}, u32[]{:S(2)}) %collective-permute-start.50) | collective-permute-done | bytes 1048608 | tf_op jit(solution)/shard_map/ppermute | solution.py:70
  318.6 7.7 %collective-permute-done.51.refs_4_ = bf16[2,64,2048]{2,1,0:T(8,128)(2,1)S(1)} collective-permute-done((bf16[2,64,2048]{2,1,0:T(8,128)(2,1)S(1)}, bf16[2,64,2048]{2,1,0:T(8,128)(2,1)S(1)}, u32[]{:S(2)}, u32[]{:S(2)}) %collective-permute-start.51) | collective-permute-done | bytes 524320 | tf_op jit(solution)/shard_map/ppermute | solution.py:70
  330.1 9.1 %grad_of_mixed.1 = (bf16[1024,256]{1,0:T(8,128)(2,1)}, bf16[4,2,2,256,128]{4,3,2,1,0:T(8,128)(2,1)}) custom-call(s32[5]{0:T(128)} %stack.310.place.refs_0_.place_ref, bf16[2,128,2048]{2,1,0:T(8,128)(2,1)} %copy-done.25, bf16[2,128,2048]{2,1,0:T(8,128)(2,1)} %copy-done.51, bf16[2,128,2048]{2,1,0:T(8,128)(2,1)} %copy-done.77, bf16[2,64,2048]{2,1,0:T(8,128)(2,1)} %copy-done.81, ...), custom_call_target="tpu_custom_call" | custom-call | flops 2147483648 | bytes 8388608 | tf_op jit(solution)/shard_map/grad_of_mixed/pallas_call | solution.py:398
  344.4 16.2 %attention_back.1 = (f32[2,512,256]{2,1,0:T(8,128)}, bf16[2,512,128]{2,1,0:T(8,128)(2,1)}, f32[2,512,128]{2,1,0:T(8,128)}) custom-call(s32[5]{0:T(128)} %stack.310.place.refs_0_.place_ref, bf16[2,4,512,64]{3,2,1,0:T(8,128)(2,1)} %get-tuple-element.240.query_ref, bf16[2,1024,128]{2,1,0:T(8,128)(2,1)} %copy-done.59, bf16[2,512,256]{2,1,0:T(8,128)(2,1)} %bitcast.437, ...), custom_call_target="tpu_custom_call" | custom-call | flops 2684354560 | bytes 4194304 | tf_op jit(solution)/shard_map/attention_back/pallas_call | solution.py:567
  366.9 6.7 %collective-permute-done.63 = bf16[2,2,256,128]{3,2,1,0:T(8,128)(2,1)} collective-permute-done((bf16[2,2,256,128]{3,2,1,0:T(8,128)(2,1)}, bf16[2,2,256,128]{3,2,1,0:T(8,128)(2,1)}, u32[]{:S(2)}, u32[]{:S(2)}) %collective-permute-start.63) | collective-permute-done | bytes 262176 | tf_op jit(solution)/shard_map/ppermute | solution.py:46
  375.6 8.4 %qkv_back.1 = (bf16[2,128,2048]{2,1,0:T(8,128)(2,1)}, bf16[2,128,2048]{2,1,0:T(8,128)(2,1)}, bf16[2,128,2048]{2,1,0:T(8,128)(2,1)}, bf16[2,64,2048]{2,1,0:T(8,12...) custom-call(f32[2,512,256]{2,1,0:T(8,128)} %get-tuple-element.313.grad_q_ref, ...), custom_call_target="tpu_custom_call" | custom-call | flops 1610612736 | bytes 9437184 | tf_op jit(solution)/shard_map/qkv_back/pallas_call | solution.py:432
  399.1 8.3 %qkv_terms.1 = bf16[4,2,2,384,128]{4,3,2,1,0:T(8,128)(2,1)} custom-call(s32[5]{0:T(128)} %stack.310.place.refs_0_.place_ref, bf16[2,128,2048]{2,1,0:T(8,128)(2,1)} %copy-done.4, bf16[2,128,2048]{2,1,0:T(8,128)(2,1)} %collective-permute-done.6.refs_2_, bf16[2,128,2048]{2,1,0:T(8,128)(2,1)} %copy-done.9, bf16[2,64,2048]{2,1,0:T(8,128)(2,1)} %copy-done.14, ...), custom_call_target="tpu_custom_call" | custom-call | flops 1610612736 | bytes 7340032 | tf_op jit(solution)/shard_map/qkv_terms/pallas_call | solution.py:459
  421.2 5.1 collective-permute-done.73
  480.9 4.5 collective-permute-done.95
  485.8 3.7 collective-permute-start.104
  502.3 3.8 finish_down.1
  509.0 4.6 collective-permute-done.107
  525.9 5.1 collective-permute-done.108
  531.7 3.7 collective-permute-start.113
  535.4 5.2 finish_hidden.3
  540.7 5.4 finish_hidden.2
  (576 shorter events, 256.1 us)
Async XLA Ops:
  7.2 19.6 %collective-permute-start = (bf16[128,2048]{1,0:T(8,128)(2,1)}, bf16[128,2048]{1,0:T(8,128)(2,1)S(1)}, u32[]{:S(2)}, u32[]{:S(2)}) collective-permute-start(bf16[128,2048]{1,0:T(8,128)(2,1)} %bitcast.355), channel_id=1, source_target_pairs={{0,1},{1,0},{2,3},{3,2},{4,5},{5,4},{6,7},{7,6},{8,9},{9,8},{10,11... | collective-permute-start | bytes 1572872 | tf_op jit(solution)/shard_map/ppermute | solution.py:46
  27.4 27.6 %collective-permute-start.6 = (bf16[2,128,2048]{2,1,0:T(8,128)(2,1)S(1)}, bf16[2,128,2048]{2,1,0:T(8,128)(2,1)}, u32[]{:S(2)}, u32[]{:S(2)}) collective-permute-start(bf16[2,128,2048]{2,1,0:T(8,128)(2,1)S(1)} %pad_maximum_fusion.refs_1_), channel_id=1, source_target_pairs={{0,16},{1,49},{16,32},{17,1},{32,48},{33,17},{48,0},{49,33},{2,18}... | collective-permute-start | bytes 3145736 | tf_op jit(solution)/shard_map/ppermute | solution.py:70
  28.5 26.5 %collective-permute-start.8 = (bf16[2112,128]{1,0:T(8,128)(2,1)}, bf16[2112,128]{1,0:T(8,128)(2,1)S(1)}, u32[]{:S(2)}, u32[]{:S(2)}) collective-permute-start(bf16[2112,128]{1,0:T(8,128)(2,1)} %pad_maximum_fusion.4), channel_id=1, source_target_pairs={{0,64},{64,8},{8,72},{72,0},{1,65},{65,9},{9,73},{73,1},{2,66},{66... | collective-permute-start | bytes 1622024 | tf_op jit(solution)/shard_map/ppermute | solution.py:44
  30.5 24.6 %collective-permute-start.9 = (bf16[2112,128]{1,0:T(8,128)(2,1)}, bf16[2112,128]{1,0:T(8,128)(2,1)}, u32[]{:S(2)}, u32[]{:S(2)}) collective-permute-start(bf16[2112,128]{1,0:T(8,128)(2,1)} %pad_maximum_fusion.4), channel_id=1, source_target_pairs={{0,72},{64,0},{8,64},{72,8},{1,73},{65,1},{9,65},{73,9},{2,74},{66... | collective-permute-start | bytes 1622024 | tf_op jit(solution)/shard_map/ppermute | solution.py:44
  33.4 21.6 %collective-permute-start.7 = (bf16[2,384,128]{2,1,0:T(8,128)(2,1)}, bf16[2,384,128]{2,1,0:T(8,128)(2,1)}, u32[]{:S(2)}, u32[]{:S(2)}) collective-permute-start(bf16[2,384,128]{2,1,0:T(8,128)(2,1)} %maximum_select_fusion.7), channel_id=1, source_target_pairs={{0,8},{8,0},{1,9},{9,1},{2,10},{10,2},{3,11},{11,3},{4,12},{12,4},... | collective-permute-start | bytes 589832 | tf_op jit(solution)/shard_map/ppermute | solution.py:46
  36.2 41.4 %all-to-all-start = ((bf16[16,128,128]{2,1,0:T(8,128)(2,1)}), bf16[16,128,128]{2,1,0:T(8,128)(2,1)}, u32[]{:S(2)}, u32[]{:S(2)}) async-start(bf16[16,128,128]{2,1,0:T(8,128)(2,1)} %bitcast_bitcast_fusion), calls=%async_computation | async-start | bytes 1048576 | tf_op jit(solution)/shard_map/all_to_all | solution.py:954
  41.8 178.0 %all-gather.2.cloned.1.call-start = ((), (), s32[]{:S(2)}) async-start(), calls=%async_computation.4 | async-start | bytes 10813440 | tf_op jit(solution)/shard_map/all_gather | solution.py:992
  56.2 24.5 %collective-permute-start.13 = (bf16[2,2,384,128]{3,2,1,0:T(8,128)(2,1)S(1)}, bf16[2,2,384,128]{3,2,1,0:T(8,128)(2,1)S(1)}, u32[]{:S(2)}, u32[]{:S(2)}) collective-permute-start(bf16[2,2,384,128]{3,2,1,0:T(8,128)(2,1)S(1)} %maximum_select_fusion.1.refs_6_), channel_id=1, source_target_pairs={{0,2},{2,4},{4,6},{6,0},{1,3},{3,5},{5,7},{7,1},{8,10},{10,12},{12... | collective-permute-start | bytes 1179656 | tf_op jit(solution)/shard_map/ppermute | solution.py:46
  57.7 23.0 %collective-permute-start.14 = (bf16[2,2,384,128]{3,2,1,0:T(8,128)(2,1)S(1)}, bf16[2,2,384,128]{3,2,1,0:T(8,128)(2,1)}, u32[]{:S(2)}, u32[]{:S(2)}) collective-permute-start(bf16[2,2,384,128]{3,2,1,0:T(8,128)(2,1)S(1)} %maximum_select_fusion.1.refs_6_), channel_id=1, source_target_pairs={{0,6},{2,0},{4,2},{6,4},{1,7},{3,1},{5,3},{7,5},{8,14},{10,8},{12,... | collective-permute-start | bytes 1179656 | tf_op jit(solution)/shard_map/ppermute | solution.py:46
  59.6 21.2 %collective-permute-start.12 = (bf16[2,128,2048]{2,1,0:T(8,128)(2,1)}, bf16[2,128,2048]{2,1,0:T(8,128)(2,1)S(1)}, u32[]{:S(2)}, u32[]{:S(2)}) collective-permute-start(bf16[2,128,2048]{2,1,0:T(8,128)(2,1)} %collective-permute-done.6.refs_2_), channel_id=1, source_target_pairs={{0,1},{1,0},{2,3},{3,2},{4,5},{5,4},{6,7},{7,6},{8,9},{9,8},{10,11... | collective-permute-start | bytes 3145736 | tf_op jit(solution)/shard_map/ppermute | solution.py:46
  61.5 19.2 %collective-permute-start.11 = (bf16[2,64,2048]{2,1,0:T(8,128)(2,1)}, bf16[2,64,2048]{2,1,0:T(8,128)(2,1)S(1)}, u32[]{:S(2)}, u32[]{:S(2)}) collective-permute-start(bf16[2,64,2048]{2,1,0:T(8,128)(2,1)} %constant_dynamic-slice_fusion.7), channel_id=1, source_target_pairs={{0,16},{1,49},{16,32},{17,1},{32,48},{33,17},{48,0},{49,33},{2,18}... | collective-permute-start | bytes 1572872 | tf_op jit(solution)/shard_map/ppermute | solution.py:70
  86.2 321.2 %reduce-scatter.3.cloned.1.call-start = ((), (), s32[]{:S(2)}) async-start(), calls=%async_computation.5 | async-start | bytes 3604480 | tf_op jit(solution)/shard_map/reduce_scatter | solution.py:1018
  96.5 16.1 %collective-permute-start.23 = (bf16[2,128,2048]{2,1,0:T(8,128)(2,1)S(1)}, bf16[2,128,2048]{2,1,0:T(8,128)(2,1)S(1)}, u32[]{:S(2)}, u32[]{:S(2)}) collective-permute-start(bf16[2,128,2048]{2,1,0:T(8,128)(2,1)S(1)} %pad_maximum_fusion.1.refs_6_.refs_1_), channel_id=1, source_target_pairs={{0,16},{1,49},{16,32},{17,1},{32,48},{33,17},{48,0},{49,33},{2,18}... | collective-permute-start | bytes 3145736 | tf_op jit(solution)/shard_map/ppermute | solution.py:70
  112.6 16.4 %collective-permute-start.27 = (bf16[2,128,2048]{2,1,0:T(8,128)(2,1)S(1)}, bf16[2,128,2048]{2,1,0:T(8,128)(2,1)S(1)}, u32[]{:S(2)}, u32[]{:S(2)}) collective-permute-start(bf16[2,128,2048]{2,1,0:T(8,128)(2,1)S(1)} %collective-permute-done.23.refs_7_.refs_2_), channel_id=1, source_target_pairs={{0,1},{1,0},{2,3},{3,2},{4,5},{5,4},{6,7},{7,6},{8,9},{9,8},{10,11... | collective-permute-start | bytes 3145736 | tf_op jit(solution)/shard_map/ppermute | solution.py:46
  112.6 16.3 %collective-permute-start.26 = (bf16[2,64,2048]{2,1,0:T(8,128)(2,1)S(1)}, bf16[2,64,2048]{2,1,0:T(8,128)(2,1)S(1)}, u32[]{:S(2)}, u32[]{:S(2)}) collective-permute-start(bf16[2,64,2048]{2,1,0:T(8,128)(2,1)S(1)} %constant_dynamic-slice_fusion.5), channel_id=1, source_target_pairs={{0,16},{1,49},{16,32},{17,1},{32,48},{33,17},{48,0},{49,33},{2,18}... | collective-permute-start | bytes 1572872 | tf_op jit(solution)/shard_map/ppermute | solution.py:70
  112.8 16.1 %collective-permute-start.24 = (bf16[2,2,256,128]{3,2,1,0:T(8,128)(2,1)S(1)}, bf16[2,2,256,128]{3,2,1,0:T(8,128)(2,1)S(1)}, u32[]{:S(2)}, u32[]{:S(2)}) collective-permute-start(bf16[2,2,256,128]{3,2,1,0:T(8,128)(2,1)S(1)} %maximum_select_fusion.6.refs_1_), channel_id=1, source_target_pairs={{0,2},{2,4},{4,6},{6,0},{1,3},{3,5},{5,7},{7,1},{8,10},{10,12},{12... | collective-permute-start | bytes 786440 | tf_op jit(solution)/shard_map/ppermute | solution.py:46
  169.1 16.1 %collective-permute-start.36 = (bf16[2,128,2048]{2,1,0:T(8,128)(2,1)S(1)}, bf16[2,128,2048]{2,1,0:T(8,128)(2,1)S(1)}, u32[]{:S(2)}, u32[]{:S(2)}) collective-permute-start(bf16[2,128,2048]{2,1,0:T(8,128)(2,1)S(1)} %convert_element_type.495), channel_id=1, source_target_pairs={{0,16},{1,49},{16,32},{17,1},{32,48},{33,17},{48,0},{49,33},{2,18}... | collective-permute-start | bytes 3145736 | tf_op jit(solution)/shard_map/ppermute | solution.py:70
  190.2 16.1 %collective-permute-start.39 = (bf16[2,128,2048]{2,1,0:T(8,128)(2,1)S(1)}, bf16[2,128,2048]{2,1,0:T(8,128)(2,1)S(1)}, u32[]{:S(2)}, u32[]{:S(2)}) collective-permute-start(bf16[2,128,2048]{2,1,0:T(8,128)(2,1)S(1)} %pad_maximum_fusion.2.refs_1_), channel_id=1, source_target_pairs={{0,16},{1,49},{16,32},{17,1},{32,48},{33,17},{48,0},{49,33},{2,18}... | collective-permute-start | bytes 3145736 | tf_op jit(solution)/shard_map/ppermute | solution.py:70
  269.5 156.8 %reduce-scatter.5.cloned.1.call-start = ((), (), s32[]{:S(2)}) async-start(), calls=%async_computation.6 | async-start | bytes 7208960 | tf_op jit(solution)/shard_map/reduce_scatter | solution.py:1021
  273.3 16.2 %collective-permute-start.47 = (bf16[2,128,2048]{2,1,0:T(8,128)(2,1)}, bf16[2,128,2048]{2,1,0:T(8,128)(2,1)S(1)}, u32[]{:S(2)}, u32[]{:S(2)}) collective-permute-start(bf16[2,128,2048]{2,1,0:T(8,128)(2,1)} %convert_element_type.510), channel_id=1, source_target_pairs={{0,16},{1,49},{16,32},{17,1},{32,48},{33,17},{48,0},{49,33},{2,18}... | collective-permute-start | bytes 3145736 | tf_op jit(solution)/shard_map/ppermute | solution.py:70
  299.2 16.1 %collective-permute-start.50 = (bf16[2,128,2048]{2,1,0:T(8,128)(2,1)S(1)}, bf16[2,128,2048]{2,1,0:T(8,128)(2,1)S(1)}, u32[]{:S(2)}, u32[]{:S(2)}) collective-permute-start(bf16[2,128,2048]{2,1,0:T(8,128)(2,1)S(1)} %pad_maximum_fusion.3.refs_1_), channel_id=1, source_target_pairs={{0,16},{1,49},{16,32},{17,1},{32,48},{33,17},{48,0},{49,33},{2,18}... | collective-permute-start | bytes 3145736 | tf_op jit(solution)/shard_map/ppermute | solution.py:70
  339.6 21.0 %collective-permute-start.58 = (bf16[2,128,2048]{2,1,0:T(8,128)(2,1)S(1)}, bf16[2,128,2048]{2,1,0:T(8,128)(2,1)S(1)}, u32[]{:S(2)}, u32[]{:S(2)}) collective-permute-start(bf16[2,128,2048]{2,1,0:T(8,128)(2,1)S(1)} %convert_element_type.524), channel_id=1, source_target_pairs={{0,16},{1,49},{16,32},{17,1},{32,48},{33,17},{48,0},{49,33},{2,18}... | collective-permute-start | bytes 3145736 | tf_op jit(solution)/shard_map/ppermute | solution.py:70
  340.7 19.9 %collective-permute-start.59 = (bf16[1,2,256,128]{3,2,1,0:T(8,128)(2,1)S(1)}, bf16[1,2,256,128]{3,2,1,0:T(8,128)(2,1)S(1)}, u32[]{:S(2)}, u32[]{:S(2)}) collective-permute-start(bf16[1,2,256,128]{3,2,1,0:T(8,128)(2,1)S(1)} %get-tuple-element.452), channel_id=1, source_target_pairs={{0,2},{2,4},{4,6},{6,0},{1,3},{3,5},{5,7},{7,1},{8,10},{10,12},{12... | collective-permute-start | bytes 393224 | tf_op jit(solution)/shard_map/ppermute | solution.py:46
  340.8 19.8 %collective-permute-start.60 = (bf16[1,2,256,128]{3,2,1,0:T(8,128)(2,1)S(1)}, bf16[1,2,256,128]{3,2,1,0:T(8,128)(2,1)S(1)}, u32[]{:S(2)}, u32[]{:S(2)}) collective-permute-start(bf16[1,2,256,128]{3,2,1,0:T(8,128)(2,1)S(1)} %get-tuple-element.451), channel_id=1, source_target_pairs={{0,6},{2,0},{4,2},{6,4},{1,7},{3,1},{5,3},{7,5},{8,14},{10,8},{12,... | collective-permute-start | bytes 393224 | tf_op jit(solution)/shard_map/ppermute | solution.py:46
  410.1 16.2 %collective-permute-start.73 = (bf16[2,128,2048]{2,1,0:T(8,128)(2,1)S(1)}, bf16[2,128,2048]{2,1,0:T(8,128)(2,1)}, u32[]{:S(2)}, u32[]{:S(2)}) collective-permute-start(bf16[2,128,2048]{2,1,0:T(8,128)(2,1)S(1)} %convert_element_type.559), channel_id=1, source_target_pairs={{0,16},{1,49},{16,32},{17,1},{32,48},{33,17},{48,0},{49,33},{2,18}... | collective-permute-start | bytes 3145736 | tf_op jit(solution)/shard_map/ppermute | solution.py:70
  448.1 16.6 %collective-permute-start.92 = (bf16[2,2,128,128]{3,2,1,0:T(8,128)(2,1)S(1)}, bf16[2,2,128,128]{3,2,1,0:T(8,128)(2,1)S(1)}, u32[]{:S(2)}, u32[]{:S(2)}) collective-permute-start(bf16[2,2,128,128]{3,2,1,0:T(8,128)(2,1)S(1)} %maximum_select_fusion.13), channel_id=1, source_target_pairs={{0,16},{16,32},{32,48},{48,0},{1,17},{17,33},{33,49},{49,1},{2,18}... | collective-permute-start | bytes 393224 | tf_op jit(solution)/shard_map/ppermute | solution.py:46
  448.2 16.5 %collective-permute-start.93 = (bf16[2,2,128,128]{3,2,1,0:T(8,128)(2,1)S(1)}, bf16[2,2,128,128]{3,2,1,0:T(8,128)(2,1)S(1)}, u32[]{:S(2)}, u32[]{:S(2)}) collective-permute-start(bf16[2,2,128,128]{3,2,1,0:T(8,128)(2,1)S(1)} %maximum_select_fusion.13), channel_id=1, source_target_pairs={{0,48},{16,0},{32,16},{48,32},{1,49},{17,1},{33,17},{49,33},{2,50}... | collective-permute-start | bytes 393224 | tf_op jit(solution)/shard_map/ppermute | solution.py:46
  493.7 20.0 %collective-permute-start.105 = (bf16[2,2,704,128]{3,2,1,0:T(8,128)(2,1)S(1)}, bf16[2,2,704,128]{3,2,1,0:T(8,128)(2,1)}, u32[]{:S(2)}, u32[]{:S(2)}) collective-permute-start(bf16[2,2,704,128]{3,2,1,0:T(8,128)(2,1)S(1)} %maximum_select_fusion), channel_id=1, source_target_pairs={{0,16},{16,32},{32,48},{48,0},{1,17},{17,33},{33,49},{49,1},{2,18}... | collective-permute-start | bytes 2162696 | tf_op jit(solution)/shard_map/ppermute | solution.py:46
  495.1 18.5 %collective-permute-start.106 = (bf16[2,2,704,128]{3,2,1,0:T(8,128)(2,1)S(1)}, bf16[2,2,704,128]{3,2,1,0:T(8,128)(2,1)S(1)}, u32[]{:S(2)}, u32[]{:S(2)}) collective-permute-start(bf16[2,2,704,128]{3,2,1,0:T(8,128)(2,1)S(1)} %maximum_select_fusion), channel_id=1, source_target_pairs={{0,48},{16,0},{32,16},{48,32},{1,49},{17,1},{33,17},{49,33},{2,50}... | collective-permute-start | bytes 2162696 | tf_op jit(solution)/shard_map/ppermute | solution.py:46
  498.0 26.1 %all-to-all-start.1 = ((bf16[16,128,128]{2,1,0:T(8,128)(2,1)}), bf16[16,128,128]{2,1,0:T(8,128)(2,1)S(1)}, u32[]{:S(2)}, u32[]{:S(2)}) async-start(bf16[16,128,128]{2,1,0:T(8,128)(2,1)} %bitcast.159), calls=%async_computation.3 | async-start | bytes 1048576 | tf_op jit(solution)/shard_map/all_to_all | solution.py:1070
  531.4 16.1 %collective-permute-start.112 = (bf16[1,2,192,128]{3,2,1,0:T(8,128)(2,1)S(1)}, bf16[1,2,192,128]{3,2,1,0:T(8,128)(2,1)S(1)}, u32[]{:S(2)}, u32[]{:S(2)}) collective-permute-start(bf16[1,2,192,128]{3,2,1,0:T(8,128)(2,1)S(1)} %slice.474), channel_id=1, source_target_pairs={{0,16},{16,32},{32,48},{48,0},{1,17},{17,33},{33,49},{49,1},{2,18}... | collective-permute-start | bytes 294920 | tf_op jit(solution)/shard_map/ppermute | solution.py:46
  531.7 15.8 %collective-permute-start.113 = (bf16[1,2,192,128]{3,2,1,0:T(8,128)(2,1)S(1)}, bf16[1,2,192,128]{3,2,1,0:T(8,128)(2,1)S(1)}, u32[]{:S(2)}, u32[]{:S(2)}) collective-permute-start(bf16[1,2,192,128]{3,2,1,0:T(8,128)(2,1)S(1)} %slice.475), channel_id=1, source_target_pairs={{0,48},{16,0},{32,16},{48,32},{1,49},{17,1},{33,17},{49,33},{2,50}... | collective-permute-start | bytes 294920 | tf_op jit(solution)/shard_map/ppermute | solution.py:46
  (174 other events, 1477.7 us)
Sparse Core Ops, SparseCore 0:
  86.3 93.0 all-gather.1
  269.6 36.3 reduce-scatter.2
  308.5 63.3 reduce-scatter.4

commit v4 on v3

--- a/solution.py
+++ b/solution.py
@@ -51,7 +51,7 @@
 
 
 def small_gather(block, axis):
-    return block, shift(block, axis, -1), shift(block, axis, 2), shift(block, axis, 1)
+    return shift(block, axis, -1), shift(block, axis, 2), shift(block, axis, 1)
 
 
 def tie(*values):
@@ -80,13 +80,14 @@
 
 
 def put_tokens(refs, rows_ref, sems, start):
+    lanes = pl.ds(0, rows_ref.shape[1])
     copies = []
     row = 0
     for s in range(2):
         for ref, flip, length in zip(refs, FLIPPED, LENGTHS):
             copies.append(
                 pltpu.make_async_copy(
-                    ref.at[s ^ flip], rows_ref.at[pl.ds(row, length)], sems.at[start + len(copies)]
+                    ref.at[s ^ flip, :, lanes], rows_ref.at[pl.ds(row, length)], sems.at[start + len(copies)]
                 )
             )
             row += length
@@ -94,6 +95,7 @@
 
 
 TILE = 256
+WIDE = D + B
 VMEM_LIMIT = 56 * 2**20
 ANYWHERE = pl.BlockSpec(memory_space=pl.ANY)
 
@@ -243,7 +245,7 @@
 
 def project_qkv_kernel(*refs):
     place, x_refs, w_refs = refs[0], refs[1:6], refs[6:11]
-    cosine_ref, sine_ref, query_ref, kv_ref, scale_ref, w_out, rows, weights, sems = refs[11:]
+    query_ref, kv_ref, scale_ref, cosine_ref, sine_ref, w_out, rows, weights, sems = refs[11:]
     step = pl.program_id(0)
     tokens = put_tokens(x_refs, rows, sems, 0)
     columns = put_columns(place, w_refs, weights, sems, 10)
@@ -259,12 +261,18 @@
         for copy in tokens:
             copy.wait()
 
-    tile = rows[pl.ds(pl.multiple_of(step * TILE, TILE), TILE), :]
+    at = pl.ds(pl.multiple_of(step * TILE, TILE), TILE)
+    tile = rows[at, :D]
     wide = tile.astype(F32)
     scale = lax.rsqrt(jnp.mean(wide * wide, axis=-1, keepdims=True) + eps)
     scale_ref[...] = scale
     pre = times_transposed(tile, weights[...]) * scale
-    cosine, sine = cosine_ref[...], sine_ref[...]
+    tables = rows[at, D:].astype(F32)
+    tables = tables + pltpu.roll(tables, B - HD // 2, 1)
+    cosine = jnp.concatenate([tables[:, : HD // 2]] * 4, axis=1)
+    sine = jnp.concatenate([tables[:, HD : HD + HD // 2]] * 4, axis=1)
+    cosine_ref[...] = cosine
+    sine_ref[...] = sine
     for i in range(2):
         part = pre[:, i * 2 * HD : (i + 1) * 2 * HD]
         part = (part * cosine + turned(part) * sine).astype(BF16) * HD ** (-0.5)
@@ -279,33 +287,34 @@
         back.wait()
 
 
-def project_qkv(place, x_pieces, w_pieces, cosine, sine):
+def project_qkv(place, x_pieces, w_pieces):
     tile = lambda lanes: pl.BlockSpec((TILE, lanes), lambda i, p: (i, 0))
     return pl.pallas_call(
         project_qkv_kernel,
         grid_spec=pltpu.PrefetchScalarGridSpec(
             num_scalar_prefetch=1,
             grid=(4,),
-            in_specs=[ANYWHERE] * 10 + [tile(2 * HD), tile(2 * HD)],
+            in_specs=[ANYWHERE] * 10,
             out_specs=[
                 pl.BlockSpec((1, HEADS, TILE, HD), lambda i, p: (i // 2, 0, i % 2, 0)),
                 pl.BlockSpec((1, TILE, 2 * HD), lambda i, p: (i // 2, i % 2, 0)),
-                tile(1),
+                tile(1), tile(2 * HD), tile(2 * HD),
                 ANYWHERE,
             ],
             scratch_shapes=[
-                pltpu.VMEM((2 * HALF, D), BF16),
+                pltpu.VMEM((2 * HALF, WIDE), BF16),
                 pltpu.VMEM((QKV, D), BF16),
                 pltpu.SemaphoreType.DMA((27,)),
             ],
         ),
         out_shape=[
-            shaped(2, HEADS, HALF, HD), shaped(2, HALF, 2 * HD), shaped(2 * HALF, 1, kind=F32), shaped(QKV, D),
+            shaped(2, HEADS, HALF, HD), shaped(2, HALF, 2 * HD), shaped(2 * HALF, 1, kind=F32),
+            shaped(2 * HALF, 2 * HD, kind=F32), shaped(2 * HALF, 2 * HD, kind=F32), shaped(QKV, D),
         ],
         compiler_params=params("arbitrary"),
         cost_estimate=cost(2 * 2 * HALF * QKV * D, 8),
         name="project_qkv",
-    )(place, *x_pieces, *w_pieces, cosine, sine)
+    )(place, *x_pieces, *w_pieces)
 
 
 def project_out_kernel(*refs):
@@ -366,8 +375,8 @@
 
 
 def grad_mixed_kernel(*refs):
-    place, grad_refs, weight_ref, mixed_ref = refs[0], refs[1:6], refs[6], refs[7]
-    grad_mixed_ref, term_ref, rows, sems = refs[8:]
+    grad_refs, weight_ref = refs[1:6], refs[6]
+    grad_mixed_ref, rows, sems = refs[7:]
     copies = put_tokens(grad_refs, rows, sems, 0)
     for copy in copies:
         copy.start()
@@ -376,23 +385,22 @@
     for i in range(4):
         tile = rows[i * TILE : (i + 1) * TILE, :]
         grad_mixed_ref[i * TILE : (i + 1) * TILE, :] = times_transposed(tile, weight_ref[...]).astype(BF16)
-    left = mixed_ref[...].astype(F32).T.astype(BF16)
-    put_term(place, left, rows, term_ref)
 
 
 def put_term(place, left, rows, term_ref):
-    def one(zx, carry):
-        lanes = pl.ds(pl.multiple_of(zx * 2 * B, 2 * B), 2 * B)
-        term = matmul(left, rows[:, lanes]).astype(BF16)
-        by = (zx % 4 + 4 - place[3]) % 4
-        term_ref[by, zx // 4, 0] = term[:, :B]
-        term_ref[by, zx // 4, 1] = term[:, B:]
+    def one(i, carry):
+        term = matmul(left, rows[:, pl.ds(pl.multiple_of(i * 4 * B, 4 * B), 4 * B)]).astype(BF16)
+        for j in range(2):
+            zx = 2 * i + j
+            by = (zx % 4 + 4 - place[3]) % 4
+            term_ref[by, zx // 4, 0] = term[:, 2 * j * B : (2 * j + 1) * B]
+            term_ref[by, zx // 4, 1] = term[:, (2 * j + 1) * B : (2 * j + 2) * B]
         return carry
 
-    lax.fori_loop(0, 8, one, 0)
-
-
-def grad_of_mixed(place, grad_pieces, weight, mixed):
+    lax.fori_loop(0, 4, one, 0)
+
+
+def grad_of_mixed(place, grad_pieces, weight):
     whole = lambda *shape: pl.BlockSpec(shape, lambda i, p: (0,) * len(shape))
     rows = HEADS * HD
     return pl.pallas_call(
@@ -400,15 +408,15 @@
         grid_spec=pltpu.PrefetchScalarGridSpec(
             num_scalar_prefetch=1,
             grid=(1,),
-            in_specs=[ANYWHERE] * 5 + [whole(rows, D), whole(2 * HALF, rows)],
-            out_specs=[whole(2 * HALF, rows), whole(4, 2, 2, rows, B)],
+            in_specs=[ANYWHERE] * 5 + [whole(rows, D)],
+            out_specs=whole(2 * HALF, rows),
             scratch_shapes=[pltpu.VMEM((2 * HALF, D), BF16), pltpu.SemaphoreType.DMA((10,))],
         ),
-        out_shape=[shaped(2 * HALF, rows), shaped(4, 2, 2, rows, B)],
-        compiler_params=params("arbitrary"),
-        cost_estimate=cost(4 * 2 * HALF * rows * D, 8),
+        out_shape=shaped(2 * HALF, rows),
+        compiler_params=params("arbitrary"),
+        cost_estimate=cost(2 * 2 * HALF * rows * D, 6),
         name="grad_of_mixed",
-    )(place, *grad_pieces, weight, mixed)
+    )(place, *grad_pieces, weight)
 
 
 def qkv_back_kernel(grad_q_ref, own_ref, later_ref, cosine_ref, sine_ref, scale_ref, weight_ref, *outs):
@@ -444,32 +452,36 @@
     )(grad_query, own, later, cosine, sine, scale, weight)
 
 
-def qkv_term_kernel(*refs):
-    place, x_refs, left_ref, term_ref, rows, sems = refs[0], refs[1:6], refs[6], refs[7], refs[8], refs[9]
-    copies = put_tokens(x_refs, rows, sems, 0)
+def attention_term_kernel(*refs):
+    place, token_refs, left_ref, term_ref, rows, sems = refs[0], refs[1:6], *refs[6:]
+    copies = put_tokens(token_refs, rows, sems, 0)
     for copy in copies:
         copy.start()
+    left = left_ref[...]
+    if left.shape[0] == 2 * HALF:
+        left = left.T
     for copy in copies:
         copy.wait()
-    put_term(place, left_ref[...], rows, term_ref)
-
-
-def qkv_terms(place, x_pieces, left):
+    put_term(place, left, rows, term_ref)
+
+
+def attention_terms(place, pieces, left, name):
     whole = lambda *shape: pl.BlockSpec(shape, lambda i, p: (0,) * len(shape))
-    return pl.pallas_call(
-        qkv_term_kernel,
+    rows = min(left.shape)
+    return pl.pallas_call(
+        attention_term_kernel,
         grid_spec=pltpu.PrefetchScalarGridSpec(
             num_scalar_prefetch=1,
             grid=(1,),
-            in_specs=[ANYWHERE] * 5 + [whole(QKV, 2 * HALF)],
-            out_specs=whole(4, 2, 2, QKV, B),
+            in_specs=[ANYWHERE] * 5 + [whole(*left.shape)],
+            out_specs=whole(4, 2, 2, rows, B),
             scratch_shapes=[pltpu.VMEM((2 * HALF, D), BF16), pltpu.SemaphoreType.DMA((10,))],
         ),
-        out_shape=shaped(4, 2, 2, QKV, B),
-        compiler_params=params("arbitrary"),
-        cost_estimate=cost(2 * 2 * HALF * QKV * D, 7),
-        name="qkv_terms",
-    )(place, *x_pieces, left)
+        out_shape=shaped(4, 2, 2, rows, B),
+        compiler_params=params("arbitrary"),
+        cost_estimate=cost(2 * 2 * HALF * rows * D, 7),
+        name=name,
+    )(place, *pieces, left)
 
 
 def token_places(at, y, core):
@@ -615,8 +627,18 @@
 
     @pl.when(step == 0)
     def _():
-        for copy in loads + tokens + weights + grads:
+        for copy in tokens + weights + loads + grads:
             copy.start()
+        for copy in tokens + weights:
+            copy.wait()
+
+    rows = pl.ds(pl.multiple_of(step * TILE, TILE), TILE)
+    normed = rows_h[rows, :]
+    gate_pre = times_transposed(normed, gate_up[0])
+    upward = times_transposed(normed, gate_up[1])
+
+    @pl.when(step == 0)
+    def _():
         for copy in loads:
             copy.wait()
 
@@ -635,13 +657,9 @@
 
         lax.fori_loop(0, 4, put, 0)
         back.start()
-        for copy in tokens + weights + grads:
+        for copy in grads:
             copy.wait()
 
-    rows = pl.ds(pl.multiple_of(step * TILE, TILE), TILE)
-    normed = rows_h[rows, :]
-    gate_pre = times_transposed(normed, gate_up[0])
-    upward = times_transposed(normed, gate_up[1])
     grad_act = times_transposed(rows_g[rows, :], down[...])
     sigmoid = 1.0 / (1.0 + jnp.exp(-gate_pre))
     silu = gate_pre * sigmoid
@@ -702,12 +720,14 @@
         for copy in copies:
             copy.wait()
 
-    normed = rows[:, pl.ds(pl.multiple_of(step * 2 * B, 2 * B), 2 * B)]
+    normed = rows[:, pl.ds(pl.multiple_of(step * 4 * B, 4 * B), 4 * B)]
     for matrix, left in ((0, gate_t), (1, up_t)):
         term = matmul(left[...], normed).astype(BF16)
-        by = along_z(place, step // 4, matrix)
-        out_ref[step % 4, by, 0:FFL, :] = term[:, :B]
-        out_ref[step % 4, by, FFL:, :] = term[:, B:]
+        for j in range(2):
+            zx = 2 * step + j
+            by = along_z(place, zx // 4, matrix)
+            out_ref[zx % 4, by, 0:FFL, :] = term[:, 2 * j * B : (2 * j + 1) * B]
+            out_ref[zx % 4, by, FFL:, :] = term[:, (2 * j + 1) * B : (2 * j + 2) * B]
 
 
 def down_kernel(*refs):
@@ -722,13 +742,15 @@
         for copy in copies:
             copy.wait()
 
-    term = matmul(act_t[...], rows[:, pl.ds(pl.multiple_of(step * 2 * B, 2 * B), 2 * B)])
-    half, p = step // 4, step % 4
-    at = pl.ds(pl.multiple_of(p * 2 * PIECE, 16), 2 * PIECE)
-    for zx in range(8):
-        slab = term[zx * PIECE : (zx + 1) * PIECE]
-        slab = jnp.concatenate([slab[:, :B], slab[:, B:]], axis=0).astype(BF16)
-        out_ref[zx % 4, along_z(place, zx // 4, half), at, :] = slab
+    term = matmul(act_t[...], rows[:, pl.ds(pl.multiple_of(step * 4 * B, 4 * B), 4 * B)])
+    for j in range(2):
+        half, p = step // 2, (2 * step + j) % 4
+        at = pl.ds(pl.multiple_of(p * 2 * PIECE, 16), 2 * PIECE)
+        for zx in range(8):
+            slab = term[zx * PIECE : (zx + 1) * PIECE]
+            low, high = slab[:, 2 * j * B : (2 * j + 1) * B], slab[:, (2 * j + 1) * B : (2 * j + 2) * B]
+            slab = jnp.concatenate([low, high], axis=0).astype(BF16)
+            out_ref[zx % 4, along_z(place, zx // 4, half), at, :] = slab
 
 
 def ff_terms(kernel, place, pieces, lefts, rows, name):
@@ -737,7 +759,7 @@
         kernel,
         grid_spec=pltpu.PrefetchScalarGridSpec(
             num_scalar_prefetch=1,
-            grid=(8,),
+            grid=(4,),
             in_specs=[ANYWHERE] * 5 + [whole] * len(lefts),
             out_specs=pl.BlockSpec((4, 4, rows, B), lambda i, p: (0, 0, 0, 0)),
             scratch_shapes=[pltpu.VMEM((2 * HALF, D), BF16), pltpu.SemaphoreType.DMA((10,))],
@@ -904,43 +926,45 @@
     def by_zhi(mine, got):
         return jnp.where(zhi == 0, jnp.stack([mine, got]), jnp.stack([got, mine]))
 
+    def trio(mine, other, axis):
+        across = lax.ppermute(other, (axis, "core"), [(i, 3 - i) for i in range(4)])
+        return shift(mine, axis, 1), swap_core(other), across
+
     def column_steps(mine, other):
-        (got,) = yield (swap_core(other),)
-        pair = by_core(mine, got)
-        (got,) = yield (shift(pair, "zhi", 1),)
-        return (yield from ring_gather_steps(by_zhi(pair, got), "x"))
-
-    def hidden_steps(mine, other, down):
-        (got,) = yield (swap_core(other),)
+        there, here, across = yield trio(mine, other, "zhi")
+        column = by_zhi(by_core(mine, here), by_core(there, across))
+        return (yield from ring_gather_steps(column, "x"))
+
+    def hidden_steps(mine, got, down):
         piece = jnp.concatenate([by_core(mine, got).reshape(2 * FFL, B), down], axis=0)
         pieces = yield from ring_gather_steps(piece, "z")
         return jnp.concatenate(pieces, axis=0).reshape(4, 3 * FFL, B)
 
-    def block_steps(pair):
-        keep = lax.dynamic_index_in_dim(pair, core, 0, keepdims=False)
-        (got,) = yield (swap_core(lax.dynamic_index_in_dim(pair, 1 - core, 0, keepdims=False)),)
-        own = by_core(keep, got)
-        (got,) = yield (shift(own, "zlo", 1),)
-        return (yield from ring_gather_steps(by_zlo(own, got), "y"))
+    def of_core(pair, other=False):
+        return lax.dynamic_index_in_dim(pair, 1 - core if other else core, 0, keepdims=False)
 
     def whole_ring(pieces):
         own, after, low, high, before = pieces
         return own, after, jnp.concatenate([low, high], axis=0), before
 
     def attention_steps(terms):
-        rows = terms.shape[3]
         column = yield from ring_scatter_steps([terms[i] for i in range(4)], "x")
-        column = column.astype(BF16).reshape(2, 2, 2, rows // 2, B).transpose(0, 2, 1, 3, 4).reshape(4, rows, B)
-        z = 2 * zhi + zlo
-        column = [lax.dynamic_index_in_dim(column, (z + i) % 4, 0, keepdims=False) for i in range(4)]
-        own = yield from ring_scatter_steps(column, "z")
-        pieces = yield from block_steps(own.astype(BF16).reshape(2, rows // 2, B))
-        ring = jnp.roll(jnp.stack(whole_ring(pieces)), y, axis=0)
-        return ring.transpose(0, 2, 1, 3, 4).reshape(4, 2, rows, B)
+        keep = lax.dynamic_index_in_dim(column, zhi, 0, keepdims=False)
+        send = lax.dynamic_index_in_dim(column, 1 - zhi, 0, keepdims=False).astype(BF16)
+        (got,) = yield (shift(send, "zhi", 1),)
+        pair = (keep + got.astype(F32)).astype(BF16)
+        mine, other = of_core(pair), of_core(pair, True)
+        there, here, across = yield trio(mine, other, "zlo")
+        own = by_core(add(mine, there), add(here, across)).astype(BF16)
+        ring = yield small_gather(own, "y")
+        return jnp.roll(jnp.stack([own, *ring]), y, axis=0)
 
     def gate_up_steps(sums):
         own = yield from ring_scatter_steps([sums[i] for i in range(4)], "z")
-        pieces = yield from block_steps(own.astype(BF16).reshape(2, FFL, B))
+        pair = own.astype(BF16).reshape(2, FFL, B)
+        mine, other = of_core(pair), of_core(pair, True)
+        there, here, across = yield trio(mine, other, "zlo")
+        pieces = yield from ring_gather_steps(by_zlo(by_core(mine, here), by_core(there, across)), "y")
         return whole_ring(pieces)
 
     def down_steps(sums):
@@ -955,53 +979,51 @@
         return got
 
     x_low = layer_input[0]
-    place_rows = positions.astype(F32)
-    tokens = Flow(gather_steps(x_low))
-    places = small_gather(place_rows, "y")
-    qkv = Flow(column_steps(*prepare_qkv(place, w_query, w_key, w_value, attn_gain[:, None])))
-    hidden_rows = Flow(hidden_steps(*prepare_ff(place, w_gate, w_up, w_down, mlp_gain[:, None])))
-    places, w_out = stage([tokens, qkv, hidden_rows], places, w_output)
-
-    places = jnp.stack(places)
-    places_other = swap_core(places)
+    frequency = theta ** (-jnp.arange(0, HD, 2).astype(F32) / HD)
+    angles = positions[0].astype(F32)[:, None] * frequency
+    tables = []
+    for table in (jnp.cos(angles), jnp.sin(angles)):
+        high = lax.reduce_precision(table, 8, 7)
+        tables += [high.astype(BF16), (table - high).astype(BF16)]
+    tokens = Flow(gather_steps(jnp.concatenate([x_low, *tables], axis=1)))
+    grads = Flow(gather_steps(out_grad[0]))
+    mine, other = prepare_qkv(place, w_query, w_key, w_value, attn_gain[:, None])
+    mine, other, gain_two, w_out = stage([tokens], mine, other, mlp_gain[:, None], w_output)
+
+    qkv = Flow(column_steps(mine, other))
     output_rows = Flow(all_to_all_steps(w_out.reshape(B, 16, B).transpose(1, 0, 2)))
-    places, places_other, x_low = stage([tokens, qkv, hidden_rows], places, places_other, x_low)
-
-    places = jnp.stack([places, places_other])
-    near = jnp.where(core == 0, places[:, 3], places[:, 1])
-    ahead = jnp.where(core == 0, places[:, 1], places[:, 3])
-    far = jnp.where(core == 0, places[:, 2], jnp.roll(places[:, 2], B // 2, axis=-1))
-    places = jnp.concatenate([places[:, 0], near, ahead, far], axis=-1).reshape(2 * HALF, 1)
-    frequency = theta ** (-jnp.arange(0, HD, 2).astype(F32) / HD)
-    angles = places * jnp.tile(frequency, 4)
-    cosine, sine = jnp.cos(angles), jnp.sin(angles)
+    ff_mine, ff_other, ff_down = prepare_ff(place, w_gate, w_up, w_down, gain_two)
+    ff_got = swap_core(ff_other)
+    ff_mine, ff_got, ff_down = stage([tokens, qkv], ff_mine, ff_got, ff_down)
+
+    hidden_rows = Flow(hidden_steps(ff_mine, ff_got, ff_down))
     inputs = x_low.astype(F32)
     scale_one = lax.rsqrt(jnp.mean(inputs * inputs, axis=-1, keepdims=True) + eps)
-    cosine, sine, scale_one, grad_low = stage(
-        [tokens, qkv, hidden_rows, output_rows], cosine, sine, scale_one, out_grad[0]
-    )
+    (scale_one,) = stage([tokens, qkv, hidden_rows, output_rows], scale_one)
 
     o_rows = output_rows.result.reshape(D, B)
+    stage([tokens, qkv, hidden_rows, grads])
+
     o_block = Flow(
         column_steps(own_rows(o_rows, y, core, HEADS * HD), own_rows(o_rows, y, 1 - core, HEADS * HD))
     )
-    grads = Flow(gather_steps(grad_low))
-    stage([tokens, qkv, hidden_rows, o_block, grads])
-
     x_pieces = tokens.result
     ff_all = lax.all_gather(hidden_rows.result, "x", axis=0, tiled=False)
-    query, key_value, scale_all, qkv_full = project_qkv(place, x_pieces, qkv.result, cosine, sine)
-    query, key_value = stage([o_block, grads], query, key_value)
+    query, key_value, scale_all, cosine, sine, qkv_full = project_qkv(place, x_pieces, qkv.result)
+    query, key_value = stage([o_block], query, key_value)
+
     earlier = lax.ppermute(key_value, "zlo", [(0, 1)])
-    query, key_value, earlier = stage([o_block, grads], query, key_value, earlier)
+    query, key_value, earlier = stage([grads, o_block], query, key_value, earlier)
+
     key_value = jnp.concatenate([earlier, key_value], axis=1)
     mixed, log_total = attention(place, query, key_value)
     (mixed,) = stage([o_block, grads], mixed)
     mixed = mixed.reshape(2 * HALF, HEADS * HD)
     *parts, o_full = project_out(place, o_block.result, mixed)
+    sums = Flow(scatter_steps(parts))
+    stage([sums, grads])
     grad_pieces = grads.result
-    sums = Flow(scatter_steps(parts))
-    for _ in range(4):
+    for _ in range(3):
         stage([sums])
     hidden = inputs + sums.result
     scale_two = lax.rsqrt(jnp.mean(hidden * hidden, axis=-1, keepdims=True) + eps)
@@ -1034,27 +1056,30 @@
     down_parts = stage([hidden_grads], *down_parts)
     result = Flow(scatter_steps(down_parts))
     stage([hidden_grads, result])
-    stage([hidden_grads])
-
-    grad_mixed, output_terms = grad_of_mixed(place, hidden_grads.result, o_full, mixed)
-    grad_mixed, output_terms = stage([result], grad_mixed, output_terms)
-    output_sums = Flow(attention_steps(output_terms))
+    (down_sum,) = stage([hidden_grads], down_sum)
+
+    hidden_grad_pieces = hidden_grads.result
+    down = Flow(down_steps(down_sum))
+    grad_mixed = grad_of_mixed(place, hidden_grad_pieces, o_full)
+    (grad_mixed,) = stage([result, down], grad_mixed)
     grad_query, grad_earlier, grad_own = attention_back(
         place, query, key_value, grad_mixed.reshape(2, HALF, HEADS * HD), log_total
     )
-    grad_query, grad_earlier, grad_own = stage([result, output_sums], grad_query, grad_earlier, grad_own)
+    grad_query, grad_earlier, grad_own, mixed = stage([result, down], grad_query, grad_earlier, grad_own, mixed)
     later = lax.ppermute(grad_earlier, "zlo", [(1, 0)])
-    later, grad_query = stage([result, output_sums], later, grad_query)
+    output_terms = attention_terms(place, hidden_grad_pieces, mixed, "output_terms")
+    later, grad_query, output_terms = stage([result, down], later, grad_query, output_terms)
+    output_sums = Flow(attention_steps(output_terms))
     *parts, grad_t = qkv_back(grad_query, grad_own, later, cosine, sine, scale_all, qkv_full)
+    *parts, grad_t = stage([output_sums, down], *parts, grad_t)
     sums = Flow(scatter_steps(parts))
-    (grad_t,) = stage([sums, output_sums], grad_t)
-    qkv_term = qkv_terms(place, x_pieces, grad_t)
-    qkv_term, down_sum = stage([sums, output_sums], qkv_term, down_sum)
-    down = Flow(down_steps(down_sum))
+    qkv_term = attention_terms(place, x_pieces, grad_t, "qkv_terms")
+    (qkv_term,) = stage([sums, output_sums, down], qkv_term)
     qkv_sums = Flow(attention_steps(qkv_term))
-    (gate_up_sum,) = stage([sums, qkv_sums, down, output_sums], gate_up_sum)
+    (gate_up_sum,) = stage([sums, output_sums, qkv_sums], gate_up_sum)
     gate_up = Flow(gate_up_steps(gate_up_sum))
-    stage([sums, output_sums, qkv_sums, down, gate_up])
+    stage([sums, output_sums, qkv_sums, gate_up])
+    stage([sums, output_sums, qkv_sums, gate_up])
     grad_normed = sums.result
     mean_one = jnp.mean(grad_normed * inputs, axis=-1, keepdims=True)
     input_grad = (
@@ -1063,11 +1088,11 @@
         - inputs * (scale_one * scale_one * scale_one) * mean_one
     )
     input_grad = input_grad.astype(BF16)
-    rest = [gate_up, qkv_sums, down, output_sums]
+    output_grad = lax.all_to_all(output_sums.result.reshape(16, B, B), FSDP, 0, 0, tiled=True)
+    rest = [gate_up, qkv_sums]
     while any(flow.result is None for flow in rest):
         stage(rest)
 
-    output_grad = lax.all_to_all(output_sums.result.reshape(16, B, B), FSDP, 0, 0, tiled=True)
     output_grad = output_grad.transpose(1, 0, 2).reshape(B, D).astype(F32)
     sums = qkv_sums.result
     query_grad = sums[:, :, : HEADS * HD].reshape(D, B).T.astype(F32)

time: 570 us -> 562 us (0.986)
  the two profiles are of different devices: /device:TPU:0 before, /device:TPU:2 now
where the time goes in v4:
time: 562 us; the launch traced here: 551 us
  waiting for transfers between devices  170 us (30%)
  Pallas kernels  159 us (28%)
  starting transfers between devices  109 us (19%)
  local copies, waits for them, and re-layouts  56.6 us (10%)
  other arithmetic  39 us (7%)
  between operations  16.1 us (3%)
    ppermute x72, waiting for transfers between devices, shift(): lax.ppermute(value, axis, [(i, (i + by) % size) for i in range(size)])  83.1 us
    ppermute x16, waiting for transfers between devices, along_y(): return lax.ppermute(value, ('y', 'core'), pairs)  72.2 us
    ppermute x72, starting transfers between devices, shift(): lax.ppermute(value, axis, [(i, (i + by) % size) for i in range(size)])  65.8 us
    pallas_call x1, Pallas kernels, feed_forward(): pl.pallas_call(feed_forward_kernel, grid_spec=pltpu.PrefetchScalarGridSpe...  31.7 us
    unnamed x195, local copies, waits for them, and re-layouts  25.1 us
    pallas_call x2, Pallas kernels, ff_terms(): pl.pallas_call(kernel, grid_spec=pltpu.PrefetchScalarGridSpec(num_scalar_...  23.9 us
    ppermute x12, starting transfers between devices, shift(): lax.ppermute(value, ('zlo', 'zhi'), [(at[z], at[(z + by) % 4]) for z in r...  19.4 us
    pallas_call x1, Pallas kernels, attention_back(): attention_call(attention_back_kernel, [sequence_block(HEADS, HALF, HD), s...  16.3 us
  transfers between devices with their start and end apart: 112, of which 42 were waited for; matrix products, arithmetic and copies ran while one was open for 13% of the time, Pallas kernels for 21%

profile of v4, /device:TPU:2, one launch (start us, length us, event | category | flops | bytes accessed | tf_op | source)
XLA Modules:
  0.0 550.5 jit_solution(17277382538059156395)
XLA Ops:
  16.6 4.9 prepare_ff.1
  23.3 3.9 collective-permute-start.2
  46.9 6.9 %all-to-all-start = ((bf16[16,128,128]{2,1,0:T(8,128)(2,1)}), bf16[16,128,128]{2,1,0:T(8,128)(2,1)S(1)}, u32[]{:S(2)}, u32[]{:S(2)}) async-start(bf16[16,128,128]{2,1,0:T(8,128)(2,1)} %bitcast_bitcast_fusion), calls=%async_computation | async-start | bytes 1048576 | tf_op jit(solution)/shard_map/all_to_all | solution.py:978
  54.3 8.3 %all-to-all-done = bf16[16,128,128]{2,1,0:T(8,128)(2,1)S(1)} async-done(((bf16[16,128,128]{2,1,0:T(8,128)(2,1)}), bf16[16,128,128]{2,1,0:T(8,128)(2,1)S(1)}, u32[]{:S(2)}, u32[]{:S(2)}) %all-to-all-start) | async-done | bytes 524320 | tf_op jit(solution)/shard_map/all_to_all | solution.py:978
  90.0 9.6 %project_qkv.1 = (bf16[2,4,512,64]{3,2,1,0:T(8,128)(2,1)}, bf16[2,512,128]{2,1,0:T(8,128)(2,1)}, f32[1024,1]{1,0:T(8,128)}, f32[1024,128]{1,0:T(8,128)}, f32[1024,128]{1,0:T(8,128)}, /*index=5*/bf16[384,2048]{1,0:T(8,128)(2,1)}) custom-call(s32[5]{0:T(128)} %stack.264.place.refs_0_.place_ref, bf16[2,128,2176]{2,1,0:T(8,128)(2,1)} %copy-done.4, ...), custom_call_target="tpu_custom_call" | custom-call | flops 1610612736 | bytes 8388608 | tf_op jit(solution)/shard_map/project_qkv/pallas_call | solution.py:292
  99.7 3.4 collective-permute-start.22
  104.4 11.1 %collective-permute-done.22.refs_5_ = bf16[2,2,256,128]{3,2,1,0:T(8,128)(2,1)S(1)} collective-permute-done((bf16[2,2,256,128]{3,2,1,0:T(8,128)(2,1)S(1)}, bf16[2,2,256,128]{3,2,1,0:T(8,128)(2,1)S(1)}, u32[]{:S(2)}, u32[]{:S(2)}) %collective-permute-start.22) | collective-permute-done | bytes 262176 | tf_op jit(solution)/shard_map/ppermute | solution.py:46
  123.4 11.1 %attention.1 = (bf16[2,512,256]{2,1,0:T(8,128)(2,1)}, f32[2,4,1,512]{3,2,1,0:T(1,128)}) custom-call(s32[5]{0:T(128)} %stack.264.place.refs_0_.place_ref, bf16[2,4,512,64]{3,2,1,0:T(8,128)(2,1)} %get-tuple-element.235.query_ref, bf16[2,1024,128]{2,1,0:T(8,128)(2,1)} %copy-done.69), custom_call_target="tpu_custom_call" | custom-call | flops 1073741824 | bytes 4194304 | tf_op jit(solution)/shard_map/attention/pallas_call | solution.py:568
  135.5 7.3 %project_out.1 = (bf16[2,128,2048]{2,1,0:T(8,128)(2,1)}, bf16[2,128,2048]{2,1,0:T(8,128)(2,1)}, bf16[2,128,2048]{2,1,0:T(8,128)(2,1)}, bf16[2,64,2048]{2,1,0:T(8...) custom-call(s32[5]{0:T(128)} %stack.264.place.refs_0_.place_ref, ...), custom_call_target="tpu_custom_call" | custom-call | flops 1073741824 | bytes 7340032 | tf_op jit(solution)/shard_map/project_out/pallas_call | solution.py:343
  151.9 9.1 %collective-permute-done.33 = bf16[2,64,2048]{2,1,0:T(8,128)(2,1)S(1)} collective-permute-done((bf16[2,64,2048]{2,1,0:T(8,128)(2,1)S(1)}, bf16[2,64,2048]{2,1,0:T(8,128)(2,1)S(1)}, u32[]{:S(2)}, u32[]{:S(2)}) %collective-permute-start.33) | collective-permute-done | bytes 524320 | tf_op jit(solution)/shard_map/ppermute | solution.py:70
  161.4 16.0 %collective-permute-done.34 = bf16[2,128,2048]{2,1,0:T(8,128)(2,1)S(1)} collective-permute-done((bf16[2,128,2048]{2,1,0:T(8,128)(2,1)S(1)}, bf16[2,128,2048]{2,1,0:T(8,128)(2,1)S(1)}, u32[]{:S(2)}, u32[]{:S(2)}) %collective-permute-start.34) | collective-permute-done | bytes 1048608 | tf_op jit(solution)/shard_map/ppermute | solution.py:70
  182.3 16.0 %collective-permute-done.37.refs_2_ = bf16[2,128,2048]{2,1,0:T(8,128)(2,1)S(1)} collective-permute-done((bf16[2,128,2048]{2,1,0:T(8,128)(2,1)S(1)}, bf16[2,128,2048]{2,1,0:T(8,128)(2,1)S(1)}, u32[]{:S(2)}, u32[]{:S(2)}) %collective-permute-start.37) | collective-permute-done | bytes 1048608 | tf_op jit(solution)/shard_map/ppermute | solution.py:70
  198.5 10.4 %collective-permute-done.38.refs_4_ = bf16[2,64,2048]{2,1,0:T(8,128)(2,1)S(1)} collective-permute-done((bf16[2,64,2048]{2,1,0:T(8,128)(2,1)S(1)}, bf16[2,64,2048]{2,1,0:T(8,128)(2,1)S(1)}, u32[]{:S(2)}, u32[]{:S(2)}) %collective-permute-start.38) | collective-permute-done | bytes 524320 | tf_op jit(solution)/shard_map/ppermute | solution.py:70
  212.1 31.7 %feed_forward.1 = (bf16[1024,704]{1,0:T(8,128)(2,1)}, bf16[704,1024]{1,0:T(8,128)(2,1)}, bf16[704,1024]{1,0:T(8,128)(2,1)}, bf16[704,1024]{1,0:T(8,128)(2,1)}, b...) custom-call(s32[5]{0:T(128)} %stack.264.place.refs_0_.place_ref, ...), custom_call_target="tpu_custom_call" | custom-call | flops 14763950080 | bytes 33554432 | tf_op jit(solution)/shard_map/feed_forward/pallas_call | solution.py:684
  250.2 9.7 %down_terms.1 = bf16[4,4,704,128]{3,2,1,0:T(8,128)(2,1)} custom-call(s32[5]{0:T(128)} %stack.264.place.refs_0_.place_ref, bf16[2,128,2048]{2,1,0:T(8,128)(2,1)} %copy-done.33, bf16[2,128,2048]{2,1,0:T(8,128)(2,1)} %copy-done.63, bf16[2,128,2048]{2,1,0:T(8,128)(2,1)} %copy-done.77, bf16[2,64,2048]{2,1,0:T(8,128)(2,1)} %copy-done.79, ...), custom_call_target="tpu_custom_call" | custom-call | flops 2952790016 | bytes 12582912 | tf_op jit(solution)/shard_map/down_terms/pallas_call | solution.py:758
  263.0 14.2 %gate_up_terms.1 = bf16[4,4,1408,128]{3,2,1,0:T(8,128)(2,1)} custom-call(s32[5]{0:T(128)} %stack.264.place.refs_0_.place_ref, bf16[2,128,2048]{2,1,0:T(8,128)(2,1)} %copy-done.34, bf16[2,128,2048]{2,1,0:T(8,128)(2,1)} %copy-done.64, bf16[2,128,2048]{2,1,0:T(8,128)(2,1)} %copy-done.78, bf16[2,64,2048]{2,1,0:T(8,128)(2,1)} %copy-done.81, ...), custom_call_target="tpu_custom_call" | custom-call | flops 5905580032 | bytes 16777216 | tf_op jit(solution)/shard_map/gate_up_terms/pallas_call | solution.py:758
  288.9 8.0 %project.1 = (bf16[2,128,2048]{2,1,0:T(8,128)(2,1)}, bf16[2,128,2048]{2,1,0:T(8,128)(2,1)}, bf16[2,128,2048]{2,1,0:T(8,128)(2,1)}, bf16[2,64,2048]{2,1,0:T(8,128)(2,1)}, bf16[2,64,2048]{2,1,0:T(8,128)(2,1)}) custom-call(bf16[1024,704]{1,0:T(8,128)(2,1)} %get-tuple-element.274.left_ref, bf16[704,2048]{1,0:T(8,128)(2,1)} %get-tuple-element.275.weight_ref), custom_call_target="tpu_custom_call" | custom-call | flops 2952790016 | bytes 8388608 | tf_op jit(solution)/shard_map/project/pallas_call | solution.py:365
  297.0 8.0 %collective-permute-done.48.refs_2_ = bf16[2,128,2048]{2,1,0:T(8,128)(2,1)S(1)} collective-permute-done((bf16[2,128,2048]{2,1,0:T(8,128)(2,1)S(1)}, bf16[2,128,2048]{2,1,0:T(8,128)(2,1)S(1)}, u32[]{:S(2)}, u32[]{:S(2)}) %collective-permute-start.48) | collective-permute-done | bytes 1048608 | tf_op jit(solution)/shard_map/ppermute | solution.py:70
  307.7 8.3 %collective-permute-done.49.refs_4_ = bf16[2,64,2048]{2,1,0:T(8,128)(2,1)S(1)} collective-permute-done((bf16[2,64,2048]{2,1,0:T(8,128)(2,1)S(1)}, bf16[2,64,2048]{2,1,0:T(8,128)(2,1)S(1)}, u32[]{:S(2)}, u32[]{:S(2)}) %collective-permute-start.49) | collective-permute-done | bytes 524320 | tf_op jit(solution)/shard_map/ppermute | solution.py:70
  323.2 6.3 %grad_of_mixed.1 = bf16[1024,256]{1,0:T(8,128)(2,1)} custom-call(s32[5]{0:T(128)} %stack.264.place.refs_0_.place_ref, bf16[2,128,2048]{2,1,0:T(8,128)(2,1)} %copy-done.5, bf16[2,128,2048]{2,1,0:T(8,128)(2,1)} %copy-done.6, bf16[2,128,2048]{2,1,0:T(8,128)(2,1)} %copy-done.13, bf16[2,64,2048]{2,1,0:T(8,128)(2,1)} %copy-done.20, ...), custom_call_target="tpu_custom_call" | custom-call | flops 1073741824 | bytes 6291456 | tf_op jit(solution)/shard_map/grad_of_mixed/pallas_call | solution.py:406
  334.3 16.3 %attention_back.1 = (f32[2,512,256]{2,1,0:T(8,128)}, bf16[2,512,128]{2,1,0:T(8,128)(2,1)}, f32[2,512,128]{2,1,0:T(8,128)}) custom-call(s32[5]{0:T(128)} %stack.264.place.refs_0_.place_ref, bf16[2,4,512,64]{3,2,1,0:T(8,128)(2,1)} %get-tuple-element.235.query_ref, bf16[2,1024,128]{2,1,0:T(8,128)(2,1)} %copy-done.69, bf16[2,512,256]{2,1,0:T(8,128)(2,1)} %bitcast.315, ...), custom_call_target="tpu_custom_call" | custom-call | flops 2684354560 | bytes 4194304 | tf_op jit(solution)/shard_map/attention_back/pallas_call | solution.py:579
  358.1 6.8 %output_terms.1 = bf16[4,2,2,256,128]{4,3,2,1,0:T(8,128)(2,1)} custom-call(s32[5]{0:T(128)} %stack.264.place.refs_0_.place_ref, bf16[2,128,2048]{2,1,0:T(8,128)(2,1)} %copy-done.5, bf16[2,128,2048]{2,1,0:T(8,128)(2,1)} %copy-done.6, bf16[2,128,2048]{2,1,0:T(8,128)(2,1)} %copy-done.13, bf16[2,64,2048]{2,1,0:T(8,128)(2,1)} %copy-done.20, ...), custom_call_target="tpu_custom_call" | custom-call | flops 1073741824 | bytes 7340032 | tf_op jit(solution)/shard_map/output_terms/pallas_call | solution.py:471
  373.1 8.4 %qkv_back.1 = (bf16[2,128,2048]{2,1,0:T(8,128)(2,1)}, bf16[2,128,2048]{2,1,0:T(8,128)(2,1)}, bf16[2,128,2048]{2,1,0:T(8,128)(2,1)}, bf16[2,64,2048]{2,1,0:T(8,12...) custom-call(f32[2,512,256]{2,1,0:T(8,128)} %get-tuple-element.314.grad_q_ref, ...), custom_call_target="tpu_custom_call" | custom-call | flops 1610612736 | bytes 9437184 | tf_op jit(solution)/shard_map/qkv_back/pallas_call | solution.py:440
  387.1 4.7 collective-permute-done.73
  395.0 7.7 %qkv_terms.1 = bf16[4,2,2,384,128]{4,3,2,1,0:T(8,128)(2,1)} custom-call(s32[5]{0:T(128)} %stack.264.place.refs_0_.place_ref, bf16[2,128,2176]{2,1,0:T(8,128)(2,1)} %copy-done.4, bf16[2,128,2176]{2,1,0:T(8,128)(2,1)} %collective-permute-done.1.refs_2_, bf16[2,128,2176]{2,1,0:T(8,128)(2,1)} %copy-done.10, bf16[2,64,2176]{2,1,0:T(8,128)(2,1)} %copy-done.18, ...), custom_call_target="tpu_custom_call" | custom-call | flops 1610612736 | bytes 7340032 | tf_op jit(solution)/shard_map/qkv_terms/pallas_call | solution.py:471
  440.3 3.3 collective-permute-start.93
  450.0 3.8 finish_down.1
  463.3 5.6 %all-to-all-start.1 = ((bf16[16,128,128]{2,1,0:T(8,128)(2,1)}), bf16[16,128,128]{2,1,0:T(8,128)(2,1)S(1)}, u32[]{:S(2)}, u32[]{:S(2)}) async-start(bf16[16,128,128]{2,1,0:T(8,128)(2,1)} %bitcast.301), calls=%async_computation.3 | async-start | bytes 1048576 | tf_op jit(solution)/shard_map/all_to_all | solution.py:1091
  474.2 7.3 %collective-permute-done.94 = bf16[704,128]{1,0:T(8,128)(2,1)S(1)} collective-permute-done((bf16[704,128]{1,0:T(8,128)(2,1)S(1)}, bf16[704,128]{1,0:T(8,128)(2,1)S(1)}, u32[]{:S(2)}, u32[]{:S(2)}) %collective-permute-start.94) | collective-permute-done | bytes 180256 | tf_op jit(solution)/shard_map/ppermute | solution.py:46
  493.4 16.4 %collective-permute-done.102 = bf16[2,384,128]{2,1,0:T(8,128)(2,1)} collective-permute-done((bf16[2,384,128]{2,1,0:T(8,128)(2,1)}, bf16[2,384,128]{2,1,0:T(8,128)(2,1)}, u32[]{:S(2)}, u32[]{:S(2)}) %collective-permute-start.102) | collective-permute-done | bytes 196640 | tf_op jit(solution)/shard_map/ppermute | solution.py:46
  531.3 5.4 finish_hidden.3
  536.7 5.4 finish_hidden.2
  (537 shorter events, 239.4 us)
Async XLA Ops:
  14.2 18.9 %collective-permute-start.1 = (bf16[2,128,2176]{2,1,0:T(8,128)(2,1)S(1)}, bf16[2,128,2176]{2,1,0:T(8,128)(2,1)}, u32[]{:S(2)}, u32[]{:S(2)}) collective-permute-start(bf16[2,128,2176]{2,1,0:T(8,128)(2,1)S(1)} %pad_maximum_fusion.refs_1_), channel_id=1, source_target_pairs={{0,16},{1,49},{16,32},{17,1},{32,48},{33,17},{48,0},{49,33},{2,18}... | collective-permute-start | bytes 3342344 | tf_op jit(solution)/shard_map/ppermute | solution.py:70
  35.5 27.1 %collective-permute-start.7 = (bf16[2,128,2176]{2,1,0:T(8,128)(2,1)}, bf16[2,128,2176]{2,1,0:T(8,128)(2,1)S(1)}, u32[]{:S(2)}, u32[]{:S(2)}) collective-permute-start(bf16[2,128,2176]{2,1,0:T(8,128)(2,1)} %collective-permute-done.1.refs_2_), channel_id=1, source_target_pairs={{0,1},{1,0},{2,3},{3,2},{4,5},{5,4},{6,7},{7,6},{8,9},{9,8},{10,11... | collective-permute-start | bytes 3342344 | tf_op jit(solution)/shard_map/ppermute | solution.py:46
  37.6 25.0 %collective-permute-start.10 = (bf16[2112,128]{1,0:T(8,128)(2,1)}, bf16[2112,128]{1,0:T(8,128)(2,1)}, u32[]{:S(2)}, u32[]{:S(2)}) collective-permute-start(bf16[2112,128]{1,0:T(8,128)(2,1)} %pad_maximum_fusion.4), channel_id=1, source_target_pairs={{0,64},{64,8},{8,72},{72,0},{1,65},{65,9},{9,73},{73,1},{2,66},{66... | collective-permute-start | bytes 1622024 | tf_op jit(solution)/shard_map/ppermute | solution.py:44
  38.6 24.0 %collective-permute-start.11 = (bf16[2112,128]{1,0:T(8,128)(2,1)}, bf16[2112,128]{1,0:T(8,128)(2,1)}, u32[]{:S(2)}, u32[]{:S(2)}) collective-permute-start(bf16[2112,128]{1,0:T(8,128)(2,1)} %pad_maximum_fusion.4), channel_id=1, source_target_pairs={{0,72},{64,0},{8,64},{72,8},{1,73},{65,1},{9,65},{73,9},{2,74},{66... | collective-permute-start | bytes 1622024 | tf_op jit(solution)/shard_map/ppermute | solution.py:44
  45.8 16.8 %collective-permute-start.6 = (bf16[2,64,2176]{2,1,0:T(8,128)(2,1)}, bf16[2,64,2176]{2,1,0:T(8,128)(2,1)S(1)}, u32[]{:S(2)}, u32[]{:S(2)}) collective-permute-start(bf16[2,64,2176]{2,1,0:T(8,128)(2,1)} %constant_dynamic-slice_fusion.7), channel_id=1, source_target_pairs={{0,16},{1,49},{16,32},{17,1},{32,48},{33,17},{48,0},{49,33},{2,18}... | collective-permute-start | bytes 1671176 | tf_op jit(solution)/shard_map/ppermute | solution.py:70
  53.8 158.3 %all-gather.2.cloned.1.call-start = ((), (), s32[]{:S(2)}) async-start(), calls=%async_computation.4 | async-start | bytes 10813440 | tf_op jit(solution)/shard_map/all_gather | solution.py:1011
  54.1 19.7 %collective-permute-start.20 = (bf16[128,2048]{1,0:T(8,128)(2,1)}, bf16[128,2048]{1,0:T(8,128)(2,1)}, u32[]{:S(2)}, u32[]{:S(2)}) collective-permute-start(bf16[128,2048]{1,0:T(8,128)(2,1)} %bitcast.300), channel_id=1, source_target_pairs={{0,1},{1,0},{2,3},{3,2},{4,5},{5,4},{6,7},{7,6},{8,9},{9,8},{10,11... | collective-permute-start | bytes 1572872 | tf_op jit(solution)/shard_map/ppermute | solution.py:46
  62.6 17.4 %collective-permute-start.15 = (bf16[2,64,2176]{2,1,0:T(8,128)(2,1)S(1)}, bf16[2,64,2176]{2,1,0:T(8,128)(2,1)S(1)}, u32[]{:S(2)}, u32[]{:S(2)}) collective-permute-start(bf16[2,64,2176]{2,1,0:T(8,128)(2,1)S(1)} %collective-permute-done.6.refs_4_), channel_id=1, source_target_pairs={{0,1},{1,0},{2,3},{3,2},{4,5},{5,4},{6,7},{7,6},{8,9},{9,8},{10,11... | collective-permute-start | bytes 1671176 | tf_op jit(solution)/shard_map/ppermute | solution.py:46
  83.5 235.4 %reduce-scatter.3.cloned.1.call-start = ((), (), s32[]{:S(2)}) async-start(), calls=%async_computation.5 | async-start | bytes 3604480 | tf_op jit(solution)/shard_map/reduce_scatter | solution.py:1040
  84.7 33.8 %collective-permute-start.21 = (bf16[2,128,2048]{2,1,0:T(8,128)(2,1)S(1)}, bf16[2,128,2048]{2,1,0:T(8,128)(2,1)S(1)}, u32[]{:S(2)}, u32[]{:S(2)}) collective-permute-start(bf16[2,128,2048]{2,1,0:T(8,128)(2,1)S(1)} %pad_maximum_fusion.1.refs_6_.refs_1_), channel_id=1, source_target_pairs={{0,16},{1,49},{16,32},{17,1},{32,48},{33,17},{48,0},{49,33},{2,18}... | collective-permute-start | bytes 3145736 | tf_op jit(solution)/shard_map/ppermute | solution.py:70
  118.4 16.1 %collective-permute-start.28 = (bf16[2,128,2048]{2,1,0:T(8,128)(2,1)S(1)}, bf16[2,128,2048]{2,1,0:T(8,128)(2,1)S(1)}, u32[]{:S(2)}, u32[]{:S(2)}) collective-permute-start(bf16[2,128,2048]{2,1,0:T(8,128)(2,1)S(1)} %collective-permute-done.21.refs_7_.refs_2_), channel_id=1, source_target_pairs={{0,1},{1,0},{2,3},{3,2},{4,5},{5,4},{6,7},{7,6},{8,9},{9,8},{10,11... | collective-permute-start | bytes 3145736 | tf_op jit(solution)/shard_map/ppermute | solution.py:46
  161.3 16.1 %collective-permute-start.34 = (bf16[2,128,2048]{2,1,0:T(8,128)(2,1)S(1)}, bf16[2,128,2048]{2,1,0:T(8,128)(2,1)S(1)}, u32[]{:S(2)}, u32[]{:S(2)}) collective-permute-start(bf16[2,128,2048]{2,1,0:T(8,128)(2,1)S(1)} %convert_element_type.507), channel_id=1, source_target_pairs={{0,16},{1,49},{16,32},{17,1},{32,48},{33,17},{48,0},{49,33},{2,18}... | collective-permute-start | bytes 3145736 | tf_op jit(solution)/shard_map/ppermute | solution.py:70
  260.9 154.0 %reduce-scatter.5.cloned.1.call-start = ((), (), s32[]{:S(2)}) async-start(), calls=%async_computation.6 | async-start | bytes 7208960 | tf_op jit(solution)/shard_map/reduce_scatter | solution.py:1043
  262.9 16.1 %collective-permute-start.45 = (bf16[2,128,2048]{2,1,0:T(8,128)(2,1)S(1)}, bf16[2,128,2048]{2,1,0:T(8,128)(2,1)S(1)}, u32[]{:S(2)}, u32[]{:S(2)}) collective-permute-start(bf16[2,128,2048]{2,1,0:T(8,128)(2,1)S(1)} %convert_element_type.522), channel_id=1, source_target_pairs={{0,16},{1,49},{16,32},{17,1},{32,48},{33,17},{48,0},{49,33},{2,18}... | collective-permute-start | bytes 3145736 | tf_op jit(solution)/shard_map/ppermute | solution.py:70
  288.5 16.5 %collective-permute-start.48 = (bf16[2,128,2048]{2,1,0:T(8,128)(2,1)S(1)}, bf16[2,128,2048]{2,1,0:T(8,128)(2,1)S(1)}, u32[]{:S(2)}, u32[]{:S(2)}) collective-permute-start(bf16[2,128,2048]{2,1,0:T(8,128)(2,1)S(1)} %pad_maximum_fusion.3.refs_1_), channel_id=1, source_target_pairs={{0,16},{1,49},{16,32},{17,1},{32,48},{33,17},{48,0},{49,33},{2,18}... | collective-permute-start | bytes 3145736 | tf_op jit(solution)/shard_map/ppermute | solution.py:70
  331.0 19.7 %collective-permute-start.58 = (bf16[2,128,2048]{2,1,0:T(8,128)(2,1)S(1)}, bf16[2,128,2048]{2,1,0:T(8,128)(2,1)S(1)}, u32[]{:S(2)}, u32[]{:S(2)}) collective-permute-start(bf16[2,128,2048]{2,1,0:T(8,128)(2,1)S(1)} %convert_element_type.536), channel_id=1, source_target_pairs={{0,16},{1,49},{16,32},{17,1},{32,48},{33,17},{48,0},{49,33},{2,18}... | collective-permute-start | bytes 3145736 | tf_op jit(solution)/shard_map/ppermute | solution.py:70
  332.0 18.7 %collective-permute-start.60 = (bf16[704,128]{1,0:T(8,128)(2,1)S(1)}, bf16[704,128]{1,0:T(8,128)(2,1)S(1)}, u32[]{:S(2)}, u32[]{:S(2)}) collective-permute-start(bf16[704,128]{1,0:T(8,128)(2,1)S(1)} %pad_maximum_fusion.13), channel_id=1, source_target_pairs={{0,72},{64,0},{8,64},{72,8},{1,73},{65,1},{9,65},{73,9},{2,74},{66... | collective-permute-start | bytes 540680 | tf_op jit(solution)/shard_map/ppermute | solution.py:44
  332.1 18.5 %collective-permute-start.59 = (bf16[704,128]{1,0:T(8,128)(2,1)S(1)}, bf16[704,128]{1,0:T(8,128)(2,1)S(1)}, u32[]{:S(2)}, u32[]{:S(2)}) collective-permute-start(bf16[704,128]{1,0:T(8,128)(2,1)S(1)} %pad_maximum_fusion.12), channel_id=1, source_target_pairs={{0,64},{64,8},{8,72},{72,0},{1,65},{65,9},{9,73},{73,1},{2,66},{66... | collective-permute-start | bytes 540680 | tf_op jit(solution)/shard_map/ppermute | solution.py:44
  381.6 21.3 %collective-permute-start.69 = (bf16[2,128,2048]{2,1,0:T(8,128)(2,1)}, bf16[2,128,2048]{2,1,0:T(8,128)(2,1)S(1)}, u32[]{:S(2)}, u32[]{:S(2)}) collective-permute-start(bf16[2,128,2048]{2,1,0:T(8,128)(2,1)} %get-tuple-element.329), channel_id=1, source_target_pairs={{0,1},{1,0},{2,3},{3,2},{4,5},{5,4},{6,7},{7,6},{8,9},{9,8},{10,11... | collective-permute-start | bytes 3145736 | tf_op jit(solution)/shard_map/ppermute | solution.py:46
  382.9 19.9 %collective-permute-start.70 = (bf16[128,2048]{1,0:T(8,128)(2,1)S(1)}, bf16[128,2048]{1,0:T(8,128)(2,1)S(1)}, u32[]{:S(2)}, u32[]{:S(2)}) collective-permute-start(bf16[128,2048]{1,0:T(8,128)(2,1)S(1)} %slice_bitcast_fusion.3), channel_id=1, source_target_pairs={{0,1},{1,0},{2,3},{3,2},{4,5},{5,4},{6,7},{7,6},{8,9},{9,8},{10,11... | collective-permute-start | bytes 1572872 | tf_op jit(solution)/shard_map/ppermute | solution.py:46
  383.3 19.5 %collective-permute-start.68 = (bf16[2,64,2048]{2,1,0:T(8,128)(2,1)}, bf16[2,64,2048]{2,1,0:T(8,128)(2,1)S(1)}, u32[]{:S(2)}, u32[]{:S(2)}) collective-permute-start(bf16[2,64,2048]{2,1,0:T(8,128)(2,1)} %get-tuple-element.328), channel_id=1, source_target_pairs={{0,1},{1,0},{2,3},{3,2},{4,5},{5,4},{6,7},{7,6},{8,9},{9,8},{10,11... | collective-permute-start | bytes 1572872 | tf_op jit(solution)/shard_map/ppermute | solution.py:46
  417.7 19.6 %collective-permute-start.79 = (bf16[2,128,2048]{2,1,0:T(8,128)(2,1)S(1)}, bf16[2,128,2048]{2,1,0:T(8,128)(2,1)S(1)}, u32[]{:S(2)}, u32[]{:S(2)}) collective-permute-start(bf16[2,128,2048]{2,1,0:T(8,128)(2,1)S(1)} %convert_element_type.577), channel_id=1, source_target_pairs={{0,16},{1,49},{16,32},{17,1},{32,48},{33,17},{48,0},{49,33},{2,18}... | collective-permute-start | bytes 3145736 | tf_op jit(solution)/shard_map/ppermute | solution.py:70
  440.3 16.3 %collective-permute-start.93 = (bf16[1408,128]{1,0:T(8,128)(2,1)S(1)}, bf16[1408,128]{1,0:T(8,128)(2,1)S(1)}, u32[]{:S(2)}, u32[]{:S(2)}) collective-permute-start(bf16[1408,128]{1,0:T(8,128)(2,1)S(1)} %pad_maximum_fusion.8), channel_id=1, source_target_pairs={{0,72},{64,0},{8,64},{72,8},{1,73},{65,1},{9,65},{73,9},{2,74},{66... | collective-permute-start | bytes 1081352 | tf_op jit(solution)/shard_map/ppermute | solution.py:44
  459.7 21.8 %collective-permute-start.95 = (bf16[704,128]{1,0:T(8,128)(2,1)}, bf16[704,128]{1,0:T(8,128)(2,1)}, u32[]{:S(2)}, u32[]{:S(2)}) collective-permute-start(bf16[704,128]{1,0:T(8,128)(2,1)} %get-tuple-element.470), channel_id=1, source_target_pairs={{0,1},{1,0},{2,3},{3,2},{4,5},{5,4},{6,7},{7,6},{8,9},{9,8},{10,11... | collective-permute-start | bytes 540680 | tf_op jit(solution)/shard_map/ppermute | solution.py:46
  460.2 21.3 %collective-permute-start.96 = (bf16[704,128]{1,0:T(8,128)(2,1)}, bf16[704,128]{1,0:T(8,128)(2,1)}, u32[]{:S(2)}, u32[]{:S(2)}) collective-permute-start(bf16[704,128]{1,0:T(8,128)(2,1)} %get-tuple-element.470), channel_id=1, source_target_pairs={{0,65},{1,64},{64,1},{65,0},{2,67},{3,66},{66,3},{67,2},{4,69},{5,... | collective-permute-start | bytes 540680 | tf_op jit(solution)/shard_map/ppermute | solution.py:930
  463.3 28.4 %all-to-all-start.1 = ((bf16[16,128,128]{2,1,0:T(8,128)(2,1)}), bf16[16,128,128]{2,1,0:T(8,128)(2,1)S(1)}, u32[]{:S(2)}, u32[]{:S(2)}) async-start(bf16[16,128,128]{2,1,0:T(8,128)(2,1)} %bitcast.301), calls=%async_computation.3 | async-start | bytes 1048576 | tf_op jit(solution)/shard_map/all_to_all | solution.py:1091
  482.9 27.7 %collective-permute-start.100 = (bf16[2,2,704,128]{3,2,1,0:T(8,128)(2,1)S(1)}, bf16[2,2,704,128]{3,2,1,0:T(8,128)(2,1)}, u32[]{:S(2)}, u32[]{:S(2)}) collective-permute-start(bf16[2,2,704,128]{3,2,1,0:T(8,128)(2,1)S(1)} %maximum_select_fusion), channel_id=1, source_target_pairs={{0,16},{16,32},{32,48},{48,0},{1,17},{17,33},{33,49},{49,1},{2,18}... | collective-permute-start | bytes 2162696 | tf_op jit(solution)/shard_map/ppermute | solution.py:46
  483.0 27.6 %collective-permute-start.101 = (bf16[2,2,704,128]{3,2,1,0:T(8,128)(2,1)S(1)}, bf16[2,2,704,128]{3,2,1,0:T(8,128)(2,1)}, u32[]{:S(2)}, u32[]{:S(2)}) collective-permute-start(bf16[2,2,704,128]{3,2,1,0:T(8,128)(2,1)S(1)} %maximum_select_fusion), channel_id=1, source_target_pairs={{0,48},{16,0},{32,16},{48,32},{1,49},{17,1},{33,17},{49,33},{2,50}... | collective-permute-start | bytes 2162696 | tf_op jit(solution)/shard_map/ppermute | solution.py:46
  488.0 21.9 %collective-permute-start.102 = (bf16[2,384,128]{2,1,0:T(8,128)(2,1)}, bf16[2,384,128]{2,1,0:T(8,128)(2,1)}, u32[]{:S(2)}, u32[]{:S(2)}) collective-permute-start(bf16[2,384,128]{2,1,0:T(8,128)(2,1)} %fusion.19), channel_id=1, source_target_pairs={{0,48},{16,0},{32,16},{48,32},{1,49},{17,1},{33,17},{49,33},{2,50}... | collective-permute-start | bytes 589832 | tf_op jit(solution)/shard_map/ppermute | solution.py:46
  488.4 21.4 %collective-permute-start.103 = (bf16[2,384,128]{2,1,0:T(8,128)(2,1)}, bf16[2,384,128]{2,1,0:T(8,128)(2,1)}, u32[]{:S(2)}, u32[]{:S(2)}) collective-permute-start(bf16[2,384,128]{2,1,0:T(8,128)(2,1)} %fusion.19), channel_id=1, source_target_pairs={{0,32},{16,48},{32,0},{48,16},{1,33},{17,49},{33,1},{49,17},{2,34}... | collective-permute-start | bytes 589832 | tf_op jit(solution)/shard_map/ppermute | solution.py:46
  488.9 21.6 %collective-permute-start.104 = (bf16[2,384,128]{2,1,0:T(8,128)(2,1)}, bf16[2,384,128]{2,1,0:T(8,128)(2,1)}, u32[]{:S(2)}, u32[]{:S(2)}) collective-permute-start(bf16[2,384,128]{2,1,0:T(8,128)(2,1)} %fusion.19), channel_id=1, source_target_pairs={{0,16},{16,32},{32,48},{48,0},{1,17},{17,33},{33,49},{49,1},{2,18}... | collective-permute-start | bytes 589832 | tf_op jit(solution)/shard_map/ppermute | solution.py:46
  512.8 17.7 %collective-permute-start.105 = (bf16[1,2,704,128]{3,2,1,0:T(8,128)(2,1)}, bf16[1,2,704,128]{3,2,1,0:T(8,128)(2,1)S(1)}, u32[]{:S(2)}, u32[]{:S(2)}) collective-permute-start(bf16[1,2,704,128]{3,2,1,0:T(8,128)(2,1)} %get-tuple-element.455), channel_id=1, source_target_pairs={{0,16},{16,32},{32,48},{48,0},{1,17},{17,33},{33,49},{49,1},{2,18}... | collective-permute-start | bytes 1081352 | tf_op jit(solution)/shard_map/ppermute | solution.py:46
  (167 other events, 1587.2 us)
Sparse Core Ops, SparseCore 0:
  83.6 94.3 all-gather.1
  261.1 33.0 reduce-scatter.2
  296.5 59.3 reduce-scatter.4

commit v5 on v4

--- a/solution.py
+++ b/solution.py
@@ -138,14 +138,15 @@
     return pl.ds(pl.multiple_of((zhi * 8 + x * 2 + core) * B, B), B)
 
 
-def put_columns(place, refs, into, sems, start):
+def put_columns(place, refs, at, into, sems, start):
+    rows = pl.ds(at, into.shape[0])
     copies = []
     for ref, by, first in zip(refs, (0, 1, 2, 2, 3), (0, 0, 0, 1, 0)):
         for i in range(ref.shape[0]):
             for core in range(2):
                 lanes = lane_block(first + i, (place[3] + by) % 4, core)
                 copies.append(
-                    pltpu.make_async_copy(ref.at[i, core], into.at[:, lanes], sems.at[start + len(copies)])
+                    pltpu.make_async_copy(ref.at[i, core, rows], into.at[:, lanes], sems.at[start + len(copies)])
                 )
     return copies
 
@@ -248,7 +249,7 @@
     query_ref, kv_ref, scale_ref, cosine_ref, sine_ref, w_out, rows, weights, sems = refs[11:]
     step = pl.program_id(0)
     tokens = put_tokens(x_refs, rows, sems, 0)
-    columns = put_columns(place, w_refs, weights, sems, 10)
+    columns = put_columns(place, w_refs, 0, weights, sems, 10)
     back = pltpu.make_async_copy(weights, w_out, sems.at[26])
 
     @pl.when(step == 0)
@@ -321,7 +322,7 @@
     place, w_refs, left_ref = refs[0], refs[1:6], refs[6]
     parts, w_out, weights, sems = refs[7:12], refs[12], refs[13], refs[14]
     step = pl.program_id(0)
-    columns = put_columns(place, w_refs, weights, sems, 0)
+    columns = put_columns(place, w_refs, QKV, weights, sems, 0)
     back = pltpu.make_async_copy(weights, w_out, sems.at[16])
 
     @pl.when(step == 0)
@@ -393,8 +394,8 @@
         for j in range(2):
             zx = 2 * i + j
             by = (zx % 4 + 4 - place[3]) % 4
-            term_ref[by, zx // 4, 0] = term[:, 2 * j * B : (2 * j + 1) * B]
-            term_ref[by, zx // 4, 1] = term[:, (2 * j + 1) * B : (2 * j + 2) * B]
+            term_ref[by, zx // 4, 0, : left.shape[0]] = term[:, 2 * j * B : (2 * j + 1) * B]
+            term_ref[by, zx // 4, 1, : left.shape[0]] = term[:, (2 * j + 1) * B : (2 * j + 2) * B]
         return carry
 
     lax.fori_loop(0, 4, one, 0)
@@ -453,35 +454,39 @@
 
 
 def attention_term_kernel(*refs):
-    place, token_refs, left_ref, term_ref, rows, sems = refs[0], refs[1:6], *refs[6:]
+    place, token_refs, left_ref = refs[0], refs[1:6], refs[6]
+    term_ref, rows, sems = refs[-3:]
     copies = put_tokens(token_refs, rows, sems, 0)
     for copy in copies:
         copy.start()
     left = left_ref[...]
     if left.shape[0] == 2 * HALF:
         left = left.T
+    if len(refs) == 11:
+        term_ref[:, :, :, left.shape[0] :] = refs[7][...]
     for copy in copies:
         copy.wait()
     put_term(place, left, rows, term_ref)
 
 
-def attention_terms(place, pieces, left, name):
+def attention_terms(place, pieces, left, name, *more):
     whole = lambda *shape: pl.BlockSpec(shape, lambda i, p: (0,) * len(shape))
     rows = min(left.shape)
+    total = rows + sum(terms.shape[3] for terms in more)
     return pl.pallas_call(
         attention_term_kernel,
         grid_spec=pltpu.PrefetchScalarGridSpec(
             num_scalar_prefetch=1,
             grid=(1,),
-            in_specs=[ANYWHERE] * 5 + [whole(*left.shape)],
-            out_specs=whole(4, 2, 2, rows, B),
+            in_specs=[ANYWHERE] * 5 + [whole(*left.shape)] + [whole(*terms.shape) for terms in more],
+            out_specs=whole(4, 2, 2, total, B),
             scratch_shapes=[pltpu.VMEM((2 * HALF, D), BF16), pltpu.SemaphoreType.DMA((10,))],
         ),
-        out_shape=shaped(4, 2, 2, rows, B),
+        out_shape=shaped(4, 2, 2, total, B),
         compiler_params=params("arbitrary"),
         cost_estimate=cost(2 * 2 * HALF * rows * D, 7),
         name=name,
-    )(place, *pieces, left)
+    )(place, *pieces, left, *more)
 
 
 def token_places(at, y, core):
@@ -632,7 +637,7 @@
         for copy in tokens + weights:
             copy.wait()
 
-    rows = pl.ds(pl.multiple_of(step * TILE, TILE), TILE)
+    rows = pl.ds(pl.multiple_of(step * HALF, HALF), HALF)
     normed = rows_h[rows, :]
     gate_pre = times_transposed(normed, gate_up[0])
     upward = times_transposed(normed, gate_up[1])
@@ -667,27 +672,34 @@
     grad_up = grad_act * silu
     grad_gate = grad_act * upward * (sigmoid * (1.0 + gate_pre * (1.0 - sigmoid)))
     part = matmul(grad_gate.astype(BF16), gate_up[0]) + matmul(grad_up.astype(BF16), gate_up[1])
-    put_parts(step, part.astype(BF16), parts)
+    part = part.astype(BF16)
+    row = 0
+    for ref, length in zip(parts, LENGTHS):
+        ref[0] = part[row : row + length]
+        row += length
     act_ref[...] = activation.astype(BF16)
     act_t[...] = activation.T.astype(BF16)
     gate_t[...] = grad_gate.T.astype(BF16)
     up_t[...] = grad_up.T.astype(BF16)
 
-    @pl.when(step == 3)
+    @pl.when(step == 1)
     def _():
         back.wait()
 
 
 def feed_forward(place, tokens, grads, ff_all):
-    turned_spec = pl.BlockSpec((FFL, TILE), lambda i, p: (0, i))
+    turned_spec = pl.BlockSpec((FFL, HALF), lambda i, p: (0, i))
     turned_shape = shaped(FFL, 2 * HALF)
     return pl.pallas_call(
         feed_forward_kernel,
         grid_spec=pltpu.PrefetchScalarGridSpec(
             num_scalar_prefetch=1,
-            grid=(4,),
+            grid=(2,),
             in_specs=[ANYWHERE] * 11,
-            out_specs=[pl.BlockSpec((TILE, FFL), lambda i, p: (i, 0))] + [turned_spec] * 3 + PART_SPECS + [ANYWHERE],
+            out_specs=[pl.BlockSpec((HALF, FFL), lambda i, p: (i, 0))]
+            + [turned_spec] * 3
+            + [pl.BlockSpec((1, n, D), lambda i, p: (i, 0, 0)) for n in LENGTHS]
+            + [ANYWHERE],
             scratch_shapes=[
                 pltpu.VMEM((2 * HALF, D), BF16),
                 pltpu.VMEM((2 * HALF, D), BF16),
@@ -873,9 +885,9 @@
 def scatter_steps(parts):
     core = lax.axis_index("core")
     first, behind, ahead, far, far_other = parts
-    far_got, behind_got, first_got = yield (swap_core(far_other), swap_core(behind), swap_core(first[1]))
+    (far_got,) = yield (swap_core(far_other),)
     far = add(far, far_got[::-1]).astype(BF16)
-    (low,) = yield (along_y(far),)
+    low, behind_got, first_got = yield (along_y(far), swap_core(behind), swap_core(first[1]))
     ahead = add(ahead, behind_got[::-1])
     mine = lax.dynamic_slice_in_dim(ahead, core * (B // 2), B // 2, 1) + low.astype(F32)
     ahead = lax.dynamic_update_slice_in_dim(ahead, mine, core * (B // 2), 1).astype(BF16)
@@ -930,10 +942,10 @@
         across = lax.ppermute(other, (axis, "core"), [(i, 3 - i) for i in range(4)])
         return shift(mine, axis, 1), swap_core(other), across
 
-    def column_steps(mine, other):
-        there, here, across = yield trio(mine, other, "zhi")
-        column = by_zhi(by_core(mine, here), by_core(there, across))
-        return (yield from ring_gather_steps(column, "x"))
+    def column_steps(mine, got):
+        pair = by_core(mine, got)
+        (got,) = yield (shift(pair, "zhi", 1),)
+        return (yield from ring_gather_steps(by_zhi(pair, got), "x"))
 
     def hidden_steps(mine, got, down):
         piece = jnp.concatenate([by_core(mine, got).reshape(2 * FFL, B), down], axis=0)
@@ -959,20 +971,16 @@
         ring = yield small_gather(own, "y")
         return jnp.roll(jnp.stack([own, *ring]), y, axis=0)
 
-    def gate_up_steps(sums):
-        own = yield from ring_scatter_steps([sums[i] for i in range(4)], "z")
-        pair = own.astype(BF16).reshape(2, FFL, B)
-        mine, other = of_core(pair), of_core(pair, True)
-        there, here, across = yield trio(mine, other, "zlo")
-        pieces = yield from ring_gather_steps(by_zlo(by_core(mine, here), by_core(there, across)), "y")
-        return whole_ring(pieces)
-
-    def down_steps(sums):
+    def ff_steps(sums):
         own = yield from ring_scatter_steps([sums[i] for i in range(4)], "z")
         own = own.astype(BF16)
-        (got,) = yield (shift(own, "zlo", 1),)
-        pieces = yield from ring_gather_steps(by_zlo(own, got), "y")
-        return whole_ring(pieces)
+        pair, down = own[: 2 * FFL].reshape(2, FFL, B), own[2 * FFL :]
+        mine, other = of_core(pair), of_core(pair, True)
+        there, here, across = yield trio(jnp.concatenate([mine, down], axis=0), other, "zlo")
+        both = by_zlo(by_core(mine, here), by_core(there[:FFL], across))
+        both = jnp.concatenate([both, by_zlo(down, there[FFL:])[:, None]], axis=1)
+        ring = whole_ring((yield from ring_gather_steps(both, "y")))
+        return [piece[:, :2] for piece in ring], [piece[:, 2] for piece in ring]
 
     def all_to_all_steps(value):
         (got,) = yield (lax.all_to_all(value, FSDP, 0, 0, tiled=True),)
@@ -987,39 +995,41 @@
         tables += [high.astype(BF16), (table - high).astype(BF16)]
     tokens = Flow(gather_steps(jnp.concatenate([x_low, *tables], axis=1)))
     grads = Flow(gather_steps(out_grad[0]))
-    mine, other = prepare_qkv(place, w_query, w_key, w_value, attn_gain[:, None])
-    mine, other, gain_two, w_out = stage([tokens], mine, other, mlp_gain[:, None], w_output)
-
-    qkv = Flow(column_steps(mine, other))
-    output_rows = Flow(all_to_all_steps(w_out.reshape(B, 16, B).transpose(1, 0, 2)))
-    ff_mine, ff_other, ff_down = prepare_ff(place, w_gate, w_up, w_down, gain_two)
+    output_rows = Flow(all_to_all_steps(w_output.reshape(B, 16, B).transpose(1, 0, 2)))
+    (gain_one,) = stage([tokens], attn_gain[:, None])
+
+    qkv_mine, qkv_other = prepare_qkv(place, w_query, w_key, w_value, gain_one)
+    ff_mine, ff_other, ff_down = prepare_ff(place, w_gate, w_up, w_down, mlp_gain[:, None])
     ff_got = swap_core(ff_other)
-    ff_mine, ff_got, ff_down = stage([tokens, qkv], ff_mine, ff_got, ff_down)
-
-    hidden_rows = Flow(hidden_steps(ff_mine, ff_got, ff_down))
+    qkv_mine, qkv_other, ff_mine, ff_got, ff_down = stage(
+        [tokens, output_rows], qkv_mine, qkv_other, ff_mine, ff_got, ff_down
+    )
+
+    o_rows = output_rows.result.reshape(D, B)
+    mine = jnp.concatenate([qkv_mine, own_rows(o_rows, y, core, HEADS * HD)], axis=0)
+    other = jnp.concatenate([qkv_other, own_rows(o_rows, y, 1 - core, HEADS * HD)], axis=0)
+    columns = Flow(column_steps(mine, swap_core(other)))
     inputs = x_low.astype(F32)
     scale_one = lax.rsqrt(jnp.mean(inputs * inputs, axis=-1, keepdims=True) + eps)
-    (scale_one,) = stage([tokens, qkv, hidden_rows, output_rows], scale_one)
-
-    o_rows = output_rows.result.reshape(D, B)
-    stage([tokens, qkv, hidden_rows, grads])
-
-    o_block = Flow(
-        column_steps(own_rows(o_rows, y, core, HEADS * HD), own_rows(o_rows, y, 1 - core, HEADS * HD))
-    )
+    scale_one, ff_mine, ff_got, ff_down = stage([tokens, columns], scale_one, ff_mine, ff_got, ff_down)
+
+    hidden_rows = Flow(hidden_steps(ff_mine, ff_got, ff_down))
+    stage([tokens, columns, hidden_rows, grads])
+    stage([columns, hidden_rows])
+
     x_pieces = tokens.result
     ff_all = lax.all_gather(hidden_rows.result, "x", axis=0, tiled=False)
-    query, key_value, scale_all, cosine, sine, qkv_full = project_qkv(place, x_pieces, qkv.result)
-    query, key_value = stage([o_block], query, key_value)
+    query, key_value, scale_all, cosine, sine, qkv_full = project_qkv(place, x_pieces, columns.result)
+    query, key_value = stage([], query, key_value)
 
     earlier = lax.ppermute(key_value, "zlo", [(0, 1)])
-    query, key_value, earlier = stage([grads, o_block], query, key_value, earlier)
+    query, key_value, earlier = stage([grads], query, key_value, earlier)
 
     key_value = jnp.concatenate([earlier, key_value], axis=1)
     mixed, log_total = attention(place, query, key_value)
-    (mixed,) = stage([o_block, grads], mixed)
+    (mixed,) = stage([grads], mixed)
     mixed = mixed.reshape(2 * HALF, HEADS * HD)
-    *parts, o_full = project_out(place, o_block.result, mixed)
+    *parts, o_full = project_out(place, columns.result, mixed)
     sums = Flow(scatter_steps(parts))
     stage([sums, grads])
     grad_pieces = grads.result
@@ -1056,30 +1066,30 @@
     down_parts = stage([hidden_grads], *down_parts)
     result = Flow(scatter_steps(down_parts))
     stage([hidden_grads, result])
-    (down_sum,) = stage([hidden_grads], down_sum)
+    stage([hidden_grads])
 
     hidden_grad_pieces = hidden_grads.result
-    down = Flow(down_steps(down_sum))
     grad_mixed = grad_of_mixed(place, hidden_grad_pieces, o_full)
-    (grad_mixed,) = stage([result, down], grad_mixed)
+    (grad_mixed,) = stage([result], grad_mixed)
     grad_query, grad_earlier, grad_own = attention_back(
         place, query, key_value, grad_mixed.reshape(2, HALF, HEADS * HD), log_total
     )
-    grad_query, grad_earlier, grad_own, mixed = stage([result, down], grad_query, grad_earlier, grad_own, mixed)
+    grad_query, grad_earlier, grad_own, mixed = stage([result], grad_query, grad_earlier, grad_own, mixed)
     later = lax.ppermute(grad_earlier, "zlo", [(1, 0)])
     output_terms = attention_terms(place, hidden_grad_pieces, mixed, "output_terms")
-    later, grad_query, output_terms = stage([result, down], later, grad_query, output_terms)
-    output_sums = Flow(attention_steps(output_terms))
+    later, grad_query, output_terms, down_sum, gate_up_sum = stage(
+        [result], later, grad_query, output_terms, down_sum, gate_up_sum
+    )
+    ff_sums = Flow(ff_steps(jnp.concatenate([gate_up_sum, down_sum], axis=1)))
     *parts, grad_t = qkv_back(grad_query, grad_own, later, cosine, sine, scale_all, qkv_full)
-    *parts, grad_t = stage([output_sums, down], *parts, grad_t)
+    *parts, grad_t = stage([ff_sums], *parts, grad_t)
     sums = Flow(scatter_steps(parts))
-    qkv_term = attention_terms(place, x_pieces, grad_t, "qkv_terms")
-    (qkv_term,) = stage([sums, output_sums, down], qkv_term)
-    qkv_sums = Flow(attention_steps(qkv_term))
-    (gate_up_sum,) = stage([sums, output_sums, qkv_sums], gate_up_sum)
-    gate_up = Flow(gate_up_steps(gate_up_sum))
-    stage([sums, output_sums, qkv_sums, gate_up])
-    stage([sums, output_sums, qkv_sums, gate_up])
+    terms = attention_terms(place, x_pieces, grad_t, "qkv_terms", output_terms)
+    (terms,) = stage([sums, ff_sums], terms)
+    attention_sums = Flow(attention_steps(terms))
+    stage([sums, attention_sums, ff_sums])
+    stage([sums, attention_sums])
+    stage([sums, attention_sums])
     grad_normed = sums.result
     mean_one = jnp.mean(grad_normed * inputs, axis=-1, keepdims=True)
     input_grad = (
@@ -1088,17 +1098,18 @@
         - inputs * (scale_one * scale_one * scale_one) * mean_one
     )
     input_grad = input_grad.astype(BF16)
-    output_grad = lax.all_to_all(output_sums.result.reshape(16, B, B), FSDP, 0, 0, tiled=True)
-    rest = [gate_up, qkv_sums]
-    while any(flow.result is None for flow in rest):
-        stage(rest)
+    while attention_sums.result is None or ff_sums.result is None:
+        stage([attention_sums, ff_sums])
+    output_rows = attention_sums.result[:, :, QKV:].reshape(16, B, B)
+    output_grad = lax.all_to_all(output_rows, FSDP, 0, 0, tiled=True)
+    gate_up, down = ff_sums.result
 
     output_grad = output_grad.transpose(1, 0, 2).reshape(B, D).astype(F32)
-    sums = qkv_sums.result
+    sums = attention_sums.result
     query_grad = sums[:, :, : HEADS * HD].reshape(D, B).T.astype(F32)
     key_grad = jnp.sum(sums[:, :, HEADS * HD : (HEADS + 1) * HD].astype(F32), axis=1)
     key_grad = key_grad.reshape(KV * HD, B).T
-    value_grad = jnp.sum(sums[:, :, (HEADS + 1) * HD :].astype(F32), axis=1)
+    value_grad = jnp.sum(sums[:, :, (HEADS + 1) * HD : QKV].astype(F32), axis=1)
     value_grad = value_grad.reshape(KV * HD, B).T
     attn_gain_grad = (
         jnp.sum(query_grad * w_query.astype(F32), axis=1)
@@ -1106,9 +1117,9 @@
         + jnp.sum(value_grad * w_value.astype(F32), axis=1)
     )
     gain_two = mlp_gain[:, None]
-    gate_grad, gate_gain = finish_hidden(place, [p[0] for p in gate_up.result], w_gate, gain_two)
-    up_grad, up_gain = finish_hidden(place, [p[1] for p in gate_up.result], w_up, gain_two)
-    down_grad = finish_down(place, down.result)
+    gate_grad, gate_gain = finish_hidden(place, [p[0] for p in gate_up], w_gate, gain_two)
+    up_grad, up_gain = finish_hidden(place, [p[1] for p in gate_up], w_up, gain_two)
+    down_grad = finish_down(place, down)
     one = attn_gain[:, None]
     return (
         (hidden + result.result).astype(BF16)[None],

time: 562 us -> 524 us (0.932)
  the two profiles are of different devices: /device:TPU:2 before, /device:TPU:1 now
where the time goes in v5:
time: 524 us; the launch traced here: 513 us
  Pallas kernels  157 us (30%)
  waiting for transfers between devices  152 us (29%)
  starting transfers between devices  107 us (20%)
  local copies, waits for them, and re-layouts  42.9 us (8%)
  other arithmetic  38.3 us (7%)
  between operations  15.5 us (3%)
    ppermute x51, waiting for transfers between devices, shift(): lax.ppermute(value, axis, [(i, (i + by) % size) for i in range(size)])  70.6 us
    ppermute x51, starting transfers between devices, shift(): lax.ppermute(value, axis, [(i, (i + by) % size) for i in range(size)])  59.3 us
    ppermute x16, waiting for transfers between devices, along_y(): return lax.ppermute(value, ('y', 'core'), pairs)  55.6 us
    pallas_call x1, Pallas kernels, feed_forward(): pl.pallas_call(feed_forward_kernel, grid_spec=pltpu.PrefetchScalarGridSpe...  29.1 us
    pallas_call x2, Pallas kernels, ff_terms(): pl.pallas_call(kernel, grid_spec=pltpu.PrefetchScalarGridSpec(num_scalar_...  24.3 us
    ppermute x16, starting transfers between devices, along_y(): return lax.ppermute(value, ('y', 'core'), pairs)  20.7 us
    ppermute x8, waiting for transfers between devices, shift(): lax.ppermute(value, ('zlo', 'zhi'), [(at[z], at[(z + by) % 4]) for z in r...  18.3 us
    unnamed x124, local copies, waits for them, and re-layouts  16.8 us
  transfers between devices with their start and end apart: 84, of which 36 were waited for; matrix products, arithmetic and copies ran while one was open for 10% of the time, Pallas kernels for 25%

profile of v5, /device:TPU:1, one launch (start us, length us, event | category | flops | bytes accessed | tf_op | source)
XLA Modules:
  0.0 513.3 jit_solution(7801107650589996428)
XLA Ops:
  16.5 7.7 %all-to-all-start = ((bf16[16,128,128]{2,1,0:T(8,128)(2,1)}), bf16[16,128,128]{2,1,0:T(8,128)(2,1)S(1)}, u32[]{:S(2)}, u32[]{:S(2)}) async-start(bf16[16,128,128]{2,1,0:T(8,128)(2,1)} %bitcast_bitcast_fusion), calls=%async_computation | async-start | bytes 1048576 | tf_op jit(solution)/shard_map/all_to_all | solution.py:986
  25.6 4.9 prepare_ff.1
  42.0 8.6 %collective-permute-done.6 = bf16[2,640,128]{2,1,0:T(8,128)(2,1)S(1)} collective-permute-done((bf16[2,640,128]{2,1,0:T(8,128)(2,1)S(1)}, bf16[2,640,128]{2,1,0:T(8,128)(2,1)S(1)}, u32[]{:S(2)}, u32[]{:S(2)}) %collective-permute-start.6) | collective-permute-done | bytes 327712 | tf_op jit(solution)/shard_map/ppermute | solution.py:46
  59.8 11.0 %collective-permute-done.10 = bf16[2112,128]{1,0:T(8,128)(2,1)S(1)} collective-permute-done((bf16[2112,128]{1,0:T(8,128)(2,1)S(1)}, bf16[2112,128]{1,0:T(8,128)(2,1)S(1)}, u32[]{:S(2)}, u32[]{:S(2)}) %collective-permute-start.10) | collective-permute-done | bytes 540704 | tf_op jit(solution)/shard_map/ppermute | solution.py:44
  77.5 4.2 collective-permute-done.15
  87.1 9.4 %project_qkv.1 = (bf16[2,4,512,64]{3,2,1,0:T(8,128)(2,1)}, bf16[2,512,128]{2,1,0:T(8,128)(2,1)}, f32[1024,1]{1,0:T(8,128)}, f32[1024,128]{1,0:T(8,128)}, f32[1024,128]{1,0:T(8,128)}, /*index=5*/bf16[384,2048]{1,0:T(8,128)(2,1)}) custom-call(s32[5]{0:T(128)} %stack.197.place.refs_0_.place_ref, bf16[2,128,2176]{2,1,0:T(8,128)(2,1)} %copy-done.4, ...), custom_call_target="tpu_custom_call" | custom-call | flops 1610612736 | bytes 8388608 | tf_op jit(solution)/shard_map/project_qkv/pallas_call | solution.py:293
  109.3 11.0 %attention.1 = (bf16[2,512,256]{2,1,0:T(8,128)(2,1)}, f32[2,4,1,512]{3,2,1,0:T(1,128)}) custom-call(s32[5]{0:T(128)} %stack.197.place.refs_0_.place_ref, bf16[2,4,512,64]{3,2,1,0:T(8,128)(2,1)} %get-tuple-element.203.query_ref, bf16[2,1024,128]{2,1,0:T(8,128)(2,1)} %copy-done.45), custom_call_target="tpu_custom_call" | custom-call | flops 1073741824 | bytes 4194304 | tf_op jit(solution)/shard_map/attention/pallas_call | solution.py:573
  120.4 7.3 %project_out.1 = (bf16[2,128,2048]{2,1,0:T(8,128)(2,1)}, bf16[2,128,2048]{2,1,0:T(8,128)(2,1)}, bf16[2,128,2048]{2,1,0:T(8,128)(2,1)}, bf16[2,64,2048]{2,1,0:T(8...) custom-call(s32[5]{0:T(128)} %stack.197.place.refs_0_.place_ref, ...), custom_call_target="tpu_custom_call" | custom-call | flops 1073741824 | bytes 7340032 | tf_op jit(solution)/shard_map/project_out/pallas_call | solution.py:344
  134.1 7.5 %collective-permute-done.23 = bf16[2,64,2048]{2,1,0:T(8,128)(2,1)S(1)} collective-permute-done((bf16[2,64,2048]{2,1,0:T(8,128)(2,1)S(1)}, bf16[2,64,2048]{2,1,0:T(8,128)(2,1)S(1)}, u32[]{:S(2)}, u32[]{:S(2)}) %collective-permute-start.23) | collective-permute-done | bytes 524320 | tf_op jit(solution)/shard_map/ppermute | solution.py:70
  144.5 11.9 %collective-permute-done.26 = bf16[2,128,2048]{2,1,0:T(8,128)(2,1)S(1)} collective-permute-done((bf16[2,128,2048]{2,1,0:T(8,128)(2,1)S(1)}, bf16[2,128,2048]{2,1,0:T(8,128)(2,1)S(1)}, u32[]{:S(2)}, u32[]{:S(2)}) %collective-permute-start.26) | collective-permute-done | bytes 1048608 | tf_op jit(solution)/shard_map/ppermute | solution.py:70
  156.5 4.1 collective-permute-start.27
  165.1 13.9 %collective-permute-done.29.refs_2_ = bf16[2,128,2048]{2,1,0:T(8,128)(2,1)S(1)} collective-permute-done((bf16[2,128,2048]{2,1,0:T(8,128)(2,1)S(1)}, bf16[2,128,2048]{2,1,0:T(8,128)(2,1)S(1)}, u32[]{:S(2)}, u32[]{:S(2)}) %collective-permute-start.29) | collective-permute-done | bytes 1048608 | tf_op jit(solution)/shard_map/ppermute | solution.py:70
  181.6 8.3 %collective-permute-done.30.refs_4_ = bf16[2,64,2048]{2,1,0:T(8,128)(2,1)S(1)} collective-permute-done((bf16[2,64,2048]{2,1,0:T(8,128)(2,1)S(1)}, bf16[2,64,2048]{2,1,0:T(8,128)(2,1)S(1)}, u32[]{:S(2)}, u32[]{:S(2)}) %collective-permute-start.30) | collective-permute-done | bytes 524320 | tf_op jit(solution)/shard_map/ppermute | solution.py:70
  194.9 29.1 %feed_forward.1 = (bf16[1024,704]{1,0:T(8,128)(2,1)}, bf16[704,1024]{1,0:T(8,128)(2,1)}, bf16[704,1024]{1,0:T(8,128)(2,1)}, bf16[704,1024]{1,0:T(8,128)(2,1)}, b...) custom-call(s32[5]{0:T(128)} %stack.197.place.refs_0_.place_ref, ...), custom_call_target="tpu_custom_call" | custom-call | flops 14763950080 | bytes 33554432 | tf_op jit(solution)/shard_map/feed_forward/pallas_call | solution.py:693
  228.9 9.7 %down_terms.1 = bf16[4,4,704,128]{3,2,1,0:T(8,128)(2,1)} custom-call(s32[5]{0:T(128)} %stack.197.place.refs_0_.place_ref, bf16[2,128,2048]{2,1,0:T(8,128)(2,1)} %copy-done.22, bf16[2,128,2048]{2,1,0:T(8,128)(2,1)} %copy-done.42, bf16[2,128,2048]{2,1,0:T(8,128)(2,1)} %copy-done.49, bf16[2,64,2048]{2,1,0:T(8,128)(2,1)} %copy-done.51, ...), custom_call_target="tpu_custom_call" | custom-call | flops 2952790016 | bytes 12582912 | tf_op jit(solution)/shard_map/down_terms/pallas_call | solution.py:770
  244.2 14.6 %gate_up_terms.1 = bf16[4,4,1408,128]{3,2,1,0:T(8,128)(2,1)} custom-call(s32[5]{0:T(128)} %stack.197.place.refs_0_.place_ref, bf16[2,128,2048]{2,1,0:T(8,128)(2,1)} %copy-done.23, bf16[2,128,2048]{2,1,0:T(8,128)(2,1)} %copy-done.43, bf16[2,128,2048]{2,1,0:T(8,128)(2,1)} %copy-done.50, bf16[2,64,2048]{2,1,0:T(8,128)(2,1)} %copy-done.53, ...), custom_call_target="tpu_custom_call" | custom-call | flops 5905580032 | bytes 16777216 | tf_op jit(solution)/shard_map/gate_up_terms/pallas_call | solution.py:770
  271.4 7.9 %project.1 = (bf16[2,128,2048]{2,1,0:T(8,128)(2,1)}, bf16[2,128,2048]{2,1,0:T(8,128)(2,1)}, bf16[2,128,2048]{2,1,0:T(8,128)(2,1)}, bf16[2,64,2048]{2,1,0:T(8,128)(2,1)}, bf16[2,64,2048]{2,1,0:T(8,128)(2,1)}) custom-call(bf16[1024,704]{1,0:T(8,128)(2,1)} %get-tuple-element.241.left_ref, bf16[704,2048]{1,0:T(8,128)(2,1)} %get-tuple-element.242.weight_ref), custom_call_target="tpu_custom_call" | custom-call | flops 2952790016 | bytes 8388608 | tf_op jit(solution)/shard_map/project/pallas_call | solution.py:366
  279.3 4.3 collective-permute-done.40.refs_2_
  289.2 5.4 %collective-permute-done.41.refs_4_ = bf16[2,64,2048]{2,1,0:T(8,128)(2,1)S(1)} collective-permute-done((bf16[2,64,2048]{2,1,0:T(8,128)(2,1)S(1)}, bf16[2,64,2048]{2,1,0:T(8,128)(2,1)S(1)}, u32[]{:S(2)}, u32[]{:S(2)}) %collective-permute-start.41) | collective-permute-done | bytes 524320 | tf_op jit(solution)/shard_map/ppermute | solution.py:70
  299.0 6.5 %grad_of_mixed.1 = bf16[1024,256]{1,0:T(8,128)(2,1)} custom-call(s32[5]{0:T(128)} %stack.197.place.refs_0_.place_ref, bf16[2,128,2048]{2,1,0:T(8,128)(2,1)} %copy-done.5, bf16[2,128,2048]{2,1,0:T(8,128)(2,1)} %copy-done.6, bf16[2,128,2048]{2,1,0:T(8,128)(2,1)} %copy-done.10, bf16[2,64,2048]{2,1,0:T(8,128)(2,1)} %copy-done.17, ...), custom_call_target="tpu_custom_call" | custom-call | flops 1073741824 | bytes 6291456 | tf_op jit(solution)/shard_map/grad_of_mixed/pallas_call | solution.py:407
  308.4 16.4 %attention_back.1 = (f32[2,512,256]{2,1,0:T(8,128)}, bf16[2,512,128]{2,1,0:T(8,128)(2,1)}, f32[2,512,128]{2,1,0:T(8,128)}) custom-call(s32[5]{0:T(128)} %stack.197.place.refs_0_.place_ref, bf16[2,4,512,64]{3,2,1,0:T(8,128)(2,1)} %get-tuple-element.203.query_ref, bf16[2,1024,128]{2,1,0:T(8,128)(2,1)} %copy-done.45, bf16[2,512,256]{2,1,0:T(8,128)(2,1)} %bitcast.271, ...), custom_call_target="tpu_custom_call" | custom-call | flops 2684354560 | bytes 4194304 | tf_op jit(solution)/shard_map/attention_back/pallas_call | solution.py:584
  328.8 6.8 %output_terms.1.refs_7_ = bf16[4,2,2,256,128]{4,3,2,1,0:T(8,128)(2,1)} custom-call(s32[5]{0:T(128)} %stack.197.place.refs_0_.place_ref, bf16[2,128,2048]{2,1,0:T(8,128)(2,1)} %copy-done.5, bf16[2,128,2048]{2,1,0:T(8,128)(2,1)} %copy-done.6, bf16[2,128,2048]{2,1,0:T(8,128)(2,1)} %copy-done.10, bf16[2,64,2048]{2,1,0:T(8,128)(2,1)} %copy-done.17, ...), custom_call_target="tpu_custom_call" | custom-call | flops 1073741824 | bytes 7340032 | tf_op jit(solution)/shard_map/output_terms/pallas_call | solution.py:476
  344.5 8.3 %qkv_back.1 = (bf16[2,128,2048]{2,1,0:T(8,128)(2,1)}, bf16[2,128,2048]{2,1,0:T(8,128)(2,1)}, bf16[2,128,2048]{2,1,0:T(8,128)(2,1)}, bf16[2,64,2048]{2,1,0:T(8,12...) custom-call(f32[2,512,256]{2,1,0:T(8,128)} %get-tuple-element.276.grad_q_ref, ...), custom_call_target="tpu_custom_call" | custom-call | flops 1610612736 | bytes 9437184 | tf_op jit(solution)/shard_map/qkv_back/pallas_call | solution.py:441
  360.5 8.3 %qkv_terms.1 = bf16[4,2,2,640,128]{4,3,2,1,0:T(8,128)(2,1)} custom-call(s32[5]{0:T(128)} %stack.197.place.refs_0_.place_ref, bf16[2,128,2176]{2,1,0:T(8,128)(2,1)} %copy-done.4, bf16[2,128,2176]{2,1,0:T(8,128)(2,1)} %collective-permute-done.1.refs_2_, bf16[2,128,2176]{2,1,0:T(8,128)(2,1)} %copy-done.8, bf16[2,64,2176]{2,1,0:T(8,128)(2,1)} %copy-done.15, ...), custom_call_target="tpu_custom_call" | custom-call | flops 1610612736 | bytes 7340032 | tf_op jit(solution)/shard_map/qkv_terms/pallas_call | solution.py:476
  401.5 10.4 %collective-permute-done.66 = bf16[2,2,640,128]{3,2,1,0:T(8,128)(2,1)S(1)} collective-permute-done((bf16[2,2,640,128]{3,2,1,0:T(8,128)(2,1)S(1)}, bf16[2,2,640,128]{3,2,1,0:T(8,128)(2,1)S(1)}, u32[]{:S(2)}, u32[]{:S(2)}) %collective-permute-start.66) | collective-permute-done | bytes 655392 | tf_op jit(solution)/shard_map/ppermute | solution.py:46
  419.8 9.1 %collective-permute-done.68 = bf16[2,640,128]{2,1,0:T(8,128)(2,1)S(1)} collective-permute-done((bf16[2,640,128]{2,1,0:T(8,128)(2,1)S(1)}, bf16[2,640,128]{2,1,0:T(8,128)(2,1)S(1)}, u32[]{:S(2)}, u32[]{:S(2)}) %collective-permute-start.68) | collective-permute-done | bytes 327712 | tf_op jit(solution)/shard_map/ppermute | solution.py:46
  433.2 5.8 %collective-permute-done.69 = bf16[640,128]{1,0:T(8,128)(2,1)S(1)} collective-permute-done((bf16[640,128]{1,0:T(8,128)(2,1)S(1)}, bf16[640,128]{1,0:T(8,128)(2,1)S(1)}, u32[]{:S(2)}, u32[]{:S(2)}) %collective-permute-start.69) | collective-permute-done | bytes 163872 | tf_op jit(solution)/shard_map/ppermute | solution.py:46
  451.1 8.0 %collective-permute-done.76 = bf16[2,640,128]{2,1,0:T(8,128)(2,1)S(1)} collective-permute-done((bf16[2,640,128]{2,1,0:T(8,128)(2,1)S(1)}, bf16[2,640,128]{2,1,0:T(8,128)(2,1)S(1)}, u32[]{:S(2)}, u32[]{:S(2)}) %collective-permute-start.76) | collective-permute-done | bytes 327712 | tf_op jit(solution)/shard_map/ppermute | solution.py:46
  459.0 11.6 %collective-permute-done.77 = bf16[1,3,704,128]{3,2,0,1:T(8,128)(2,1)S(1)} collective-permute-done((bf16[1,3,704,128]{3,2,0,1:T(8,128)(2,1)S(1)}, bf16[1,3,704,128]{3,2,0,1:T(8,128)(2,1)S(1)}, u32[]{:S(2)}, u32[]{:S(2)}) %collective-permute-start.77) | collective-permute-done | bytes 540704 | tf_op jit(solution)/shard_map/ppermute | solution.py:46
  480.7 4.2 all-to-all-start.1
  487.6 5.2 %finish_hidden.3 = (f32[128,5632]{1,0:T(8,128)}, f32[128,1]{1,0:T(8,128)}) custom-call(s32[5]{0:T(128)} %stack.197.place.refs_0_.place_ref, bf16[2,704,128]{2,1,0:T(8,128)(2,1)} %get-tuple-element.386.refs_1_, bf16[2,704,128]{2,1,0:T(8,128)(2,1)} %get-tuple-element.382.refs_2_, bf16[2,704,128]{2,1,0:T(8,128)(2,1)} %slice_bitcast_fusion.15.refs_3_, ...), custom_call_target="tpu_custom_call" | custom-call | bytes 6291456 | tf_op jit(solution)/shard_map/finish_hidden/pallas_call | solution.py:808
  492.8 5.4 %finish_hidden.2 = (f32[128,5632]{1,0:T(8,128)}, f32[128,1]{1,0:T(8,128)}) custom-call(s32[5]{0:T(128)} %stack.197.place.refs_0_.place_ref, bf16[2,704,128]{2,1,0:T(8,128)(2,1)} %get-tuple-element.387.refs_1_, bf16[2,704,128]{2,1,0:T(8,128)(2,1)} %get-tuple-element.383.refs_2_, bf16[2,704,128]{2,1,0:T(8,128)(2,1)} %slice_bitcast_fusion.18.refs_3_, ...), custom_call_target="tpu_custom_call" | custom-call | bytes 6291456 | tf_op jit(solution)/shard_map/finish_hidden/pallas_call | solution.py:808
  (399 shorter events, 210.9 us)
Async XLA Ops:
  12.7 23.0 %collective-permute-start.1 = (bf16[2,128,2176]{2,1,0:T(8,128)(2,1)S(1)}, bf16[2,128,2176]{2,1,0:T(8,128)(2,1)}, u32[]{:S(2)}, u32[]{:S(2)}) collective-permute-start(bf16[2,128,2176]{2,1,0:T(8,128)(2,1)S(1)} %pad_maximum_fusion.refs_1_), channel_id=1, source_target_pairs={{0,16},{1,49},{16,32},{17,1},{32,48},{33,17},{48,0},{49,33},{2,18}... | collective-permute-start | bytes 3342344 | tf_op jit(solution)/shard_map/ppermute | solution.py:70
  16.5 19.1 %all-to-all-start = ((bf16[16,128,128]{2,1,0:T(8,128)(2,1)}), bf16[16,128,128]{2,1,0:T(8,128)(2,1)S(1)}, u32[]{:S(2)}, u32[]{:S(2)}) async-start(bf16[16,128,128]{2,1,0:T(8,128)(2,1)} %bitcast_bitcast_fusion), calls=%async_computation | async-start | bytes 1048576 | tf_op jit(solution)/shard_map/all_to_all | solution.py:986
  24.2 170.7 %all-gather.2.cloned.1.call-start = ((), (), s32[]{:S(2)}) async-start(), calls=%async_computation.4 | async-start | bytes 10813440 | tf_op jit(solution)/shard_map/all_gather | solution.py:1021
  30.8 25.7 %collective-permute-start.12 = (bf16[128,2048]{1,0:T(8,128)(2,1)}, bf16[128,2048]{1,0:T(8,128)(2,1)}, u32[]{:S(2)}, u32[]{:S(2)}) collective-permute-start(bf16[128,2048]{1,0:T(8,128)(2,1)} %bitcast.22), channel_id=1, source_target_pairs={{0,1},{1,0},{2,3},{3,2},{4,5},{5,4},{6,7},{7,6},{8,9},{9,8},{10,11... | collective-permute-start | bytes 1572872 | tf_op jit(solution)/shard_map/ppermute | solution.py:46
  35.6 15.0 %collective-permute-start.5 = (bf16[2,128,2176]{2,1,0:T(8,128)(2,1)}, bf16[2,128,2176]{2,1,0:T(8,128)(2,1)S(1)}, u32[]{:S(2)}, u32[]{:S(2)}) collective-permute-start(bf16[2,128,2176]{2,1,0:T(8,128)(2,1)} %collective-permute-done.1.refs_2_), channel_id=1, source_target_pairs={{0,1},{1,0},{2,3},{3,2},{4,5},{5,4},{6,7},{7,6},{8,9},{9,8},{10,11... | collective-permute-start | bytes 3342344 | tf_op jit(solution)/shard_map/ppermute | solution.py:46
  50.7 20.2 %collective-permute-start.8 = (bf16[2,2,640,128]{3,2,1,0:T(8,128)(2,1)S(1)}, bf16[2,2,640,128]{3,2,1,0:T(8,128)(2,1)S(1)}, u32[]{:S(2)}, u32[]{:S(2)}) collective-permute-start(bf16[2,2,640,128]{3,2,1,0:T(8,128)(2,1)S(1)} %maximum_select_fusion.1.refs_6_.refs_1_), channel_id=1, source_target_pairs={{0,2},{2,4},{4,6},{6,0},{1,3},{3,5},{5,7},{7,1},{8,10},{10,12},{12... | collective-permute-start | bytes 1966088 | tf_op jit(solution)/shard_map/ppermute | solution.py:46
  50.8 20.0 %collective-permute-start.9 = (bf16[2,2,640,128]{3,2,1,0:T(8,128)(2,1)S(1)}, bf16[2,2,640,128]{3,2,1,0:T(8,128)(2,1)S(1)}, u32[]{:S(2)}, u32[]{:S(2)}) collective-permute-start(bf16[2,2,640,128]{3,2,1,0:T(8,128)(2,1)S(1)} %maximum_select_fusion.1.refs_6_.refs_1_), channel_id=1, source_target_pairs={{0,6},{2,0},{4,2},{6,4},{1,7},{3,1},{5,3},{7,5},{8,14},{10,8},{12,... | collective-permute-start | bytes 1966088 | tf_op jit(solution)/shard_map/ppermute | solution.py:46
  53.4 17.4 %collective-permute-start.7 = (bf16[2,64,2176]{2,1,0:T(8,128)(2,1)S(1)}, bf16[2,64,2176]{2,1,0:T(8,128)(2,1)S(1)}, u32[]{:S(2)}, u32[]{:S(2)}) collective-permute-start(bf16[2,64,2176]{2,1,0:T(8,128)(2,1)S(1)} %collective-permute-done.4.refs_4_), channel_id=1, source_target_pairs={{0,1},{1,0},{2,3},{3,2},{4,5},{5,4},{6,7},{7,6},{8,9},{9,8},{10,11... | collective-permute-start | bytes 1671176 | tf_op jit(solution)/shard_map/ppermute | solution.py:46
  55.6 15.2 %collective-permute-start.10 = (bf16[2112,128]{1,0:T(8,128)(2,1)S(1)}, bf16[2112,128]{1,0:T(8,128)(2,1)S(1)}, u32[]{:S(2)}, u32[]{:S(2)}) collective-permute-start(bf16[2112,128]{1,0:T(8,128)(2,1)S(1)} %pad_maximum_fusion.7), channel_id=1, source_target_pairs={{0,64},{64,8},{8,72},{72,0},{1,65},{65,9},{9,73},{73,1},{2,66},{66... | collective-permute-start | bytes 1622024 | tf_op jit(solution)/shard_map/ppermute | solution.py:44
  56.5 14.4 %collective-permute-start.11 = (bf16[2112,128]{1,0:T(8,128)(2,1)S(1)}, bf16[2112,128]{1,0:T(8,128)(2,1)S(1)}, u32[]{:S(2)}, u32[]{:S(2)}) collective-permute-start(bf16[2112,128]{1,0:T(8,128)(2,1)S(1)} %pad_maximum_fusion.7), channel_id=1, source_target_pairs={{0,72},{64,0},{8,64},{72,8},{1,73},{65,1},{9,65},{73,9},{2,74},{66... | collective-permute-start | bytes 1622024 | tf_op jit(solution)/shard_map/ppermute | solution.py:44
  84.2 251.5 %reduce-scatter.3.cloned.1.call-start = ((), (), s32[]{:S(2)}) async-start(), calls=%async_computation.5 | async-start | bytes 3604480 | tf_op jit(solution)/shard_map/reduce_scatter | solution.py:1050
  85.5 16.8 %collective-permute-start.17 = (bf16[2,128,2048]{2,1,0:T(8,128)(2,1)S(1)}, bf16[2,128,2048]{2,1,0:T(8,128)(2,1)S(1)}, u32[]{:S(2)}, u32[]{:S(2)}) collective-permute-start(bf16[2,128,2048]{2,1,0:T(8,128)(2,1)S(1)} %pad_maximum_fusion.2.refs_6_.refs_1_), channel_id=1, source_target_pairs={{0,16},{1,49},{16,32},{17,1},{32,48},{33,17},{48,0},{49,33},{2,18}... | collective-permute-start | bytes 3145736 | tf_op jit(solution)/shard_map/ppermute | solution.py:70
  102.3 18.1 %collective-permute-start.20 = (bf16[2,128,2048]{2,1,0:T(8,128)(2,1)S(1)}, bf16[2,128,2048]{2,1,0:T(8,128)(2,1)S(1)}, u32[]{:S(2)}, u32[]{:S(2)}) collective-permute-start(bf16[2,128,2048]{2,1,0:T(8,128)(2,1)S(1)} %collective-permute-done.17.refs_7_.refs_2_), channel_id=1, source_target_pairs={{0,1},{1,0},{2,3},{3,2},{4,5},{5,4},{6,7},{7,6},{8,9},{9,8},{10,11... | collective-permute-start | bytes 3145736 | tf_op jit(solution)/shard_map/ppermute | solution.py:46
  105.5 14.8 %collective-permute-start.19 = (bf16[2,64,2048]{2,1,0:T(8,128)(2,1)S(1)}, bf16[2,64,2048]{2,1,0:T(8,128)(2,1)S(1)}, u32[]{:S(2)}, u32[]{:S(2)}) collective-permute-start(bf16[2,64,2048]{2,1,0:T(8,128)(2,1)S(1)} %constant_dynamic-slice_fusion.4), channel_id=1, source_target_pairs={{0,16},{1,49},{16,32},{17,1},{32,48},{33,17},{48,0},{49,33},{2,18}... | collective-permute-start | bytes 1572872 | tf_op jit(solution)/shard_map/ppermute | solution.py:70
  142.3 14.1 %collective-permute-start.26 = (bf16[2,128,2048]{2,1,0:T(8,128)(2,1)S(1)}, bf16[2,128,2048]{2,1,0:T(8,128)(2,1)S(1)}, u32[]{:S(2)}, u32[]{:S(2)}) collective-permute-start(bf16[2,128,2048]{2,1,0:T(8,128)(2,1)S(1)} %convert_element_type.380), channel_id=1, source_target_pairs={{0,16},{1,49},{16,32},{17,1},{32,48},{33,17},{48,0},{49,33},{2,18}... | collective-permute-start | bytes 3145736 | tf_op jit(solution)/shard_map/ppermute | solution.py:70
  224.5 14.1 %collective-permute-start.35 = (bf16[2,128,2048]{2,1,0:T(8,128)(2,1)}, bf16[2,128,2048]{2,1,0:T(8,128)(2,1)}, u32[]{:S(2)}, u32[]{:S(2)}) collective-permute-start(bf16[2,128,2048]{2,1,0:T(8,128)(2,1)} %get-tuple-element.229), channel_id=1, source_target_pairs={{0,1},{1,0},{2,3},{3,2},{4,5},{5,4},{6,7},{7,6},{8,9},{9,8},{10,11... | collective-permute-start | bytes 3145736 | tf_op jit(solution)/shard_map/ppermute | solution.py:46
  238.7 98.4 %reduce-scatter.5.cloned.1.call-start = ((), (), s32[]{:S(2)}) async-start(), calls=%async_computation.6 | async-start | bytes 7208960 | tf_op jit(solution)/shard_map/reduce_scatter | solution.py:1053
  243.8 15.0 %collective-permute-start.37 = (bf16[2,128,2048]{2,1,0:T(8,128)(2,1)}, bf16[2,128,2048]{2,1,0:T(8,128)(2,1)}, u32[]{:S(2)}, u32[]{:S(2)}) collective-permute-start(bf16[2,128,2048]{2,1,0:T(8,128)(2,1)} %convert_element_type.395), channel_id=1, source_target_pairs={{0,16},{1,49},{16,32},{17,1},{32,48},{33,17},{48,0},{49,33},{2,18}... | collective-permute-start | bytes 3145736 | tf_op jit(solution)/shard_map/ppermute | solution.py:70
  286.7 18.8 %collective-permute-start.45 = (bf16[2,128,2048]{2,1,0:T(8,128)(2,1)}, bf16[2,128,2048]{2,1,0:T(8,128)(2,1)S(1)}, u32[]{:S(2)}, u32[]{:S(2)}) collective-permute-start(bf16[2,128,2048]{2,1,0:T(8,128)(2,1)} %get-tuple-element.253), channel_id=1, source_target_pairs={{0,1},{1,0},{2,3},{3,2},{4,5},{5,4},{6,7},{7,6},{8,9},{9,8},{10,11... | collective-permute-start | bytes 3145736 | tf_op jit(solution)/shard_map/ppermute | solution.py:46
  289.1 16.3 %collective-permute-start.46 = (bf16[128,2048]{1,0:T(8,128)(2,1)}, bf16[128,2048]{1,0:T(8,128)(2,1)S(1)}, u32[]{:S(2)}, u32[]{:S(2)}) collective-permute-start(bf16[128,2048]{1,0:T(8,128)(2,1)} %slice_bitcast_fusion.6), channel_id=1, source_target_pairs={{0,1},{1,0},{2,3},{3,2},{4,5},{5,4},{6,7},{7,6},{8,9},{9,8},{10,11... | collective-permute-start | bytes 1572872 | tf_op jit(solution)/shard_map/ppermute | solution.py:46
  306.9 17.8 %collective-permute-start.48 = (bf16[2,128,2048]{2,1,0:T(8,128)(2,1)S(1)}, bf16[2,128,2048]{2,1,0:T(8,128)(2,1)S(1)}, u32[]{:S(2)}, u32[]{:S(2)}) collective-permute-start(bf16[2,128,2048]{2,1,0:T(8,128)(2,1)S(1)} %convert_element_type.409), channel_id=1, source_target_pairs={{0,16},{1,49},{16,32},{17,1},{32,48},{33,17},{48,0},{49,33},{2,18}... | collective-permute-start | bytes 3145736 | tf_op jit(solution)/shard_map/ppermute | solution.py:70
  358.9 29.8 %collective-permute-start.57 = (bf16[2,128,2048]{2,1,0:T(8,128)(2,1)}, bf16[2,128,2048]{2,1,0:T(8,128)(2,1)}, u32[]{:S(2)}, u32[]{:S(2)}) collective-permute-start(bf16[2,128,2048]{2,1,0:T(8,128)(2,1)} %get-tuple-element.297), channel_id=1, source_target_pairs={{0,1},{1,0},{2,3},{3,2},{4,5},{5,4},{6,7},{7,6},{8,9},{9,8},{10,11... | collective-permute-start | bytes 3145736 | tf_op jit(solution)/shard_map/ppermute | solution.py:46
  359.9 18.0 %collective-permute-start.58 = (bf16[128,2048]{1,0:T(8,128)(2,1)}, bf16[128,2048]{1,0:T(8,128)(2,1)S(1)}, u32[]{:S(2)}, u32[]{:S(2)}) collective-permute-start(bf16[128,2048]{1,0:T(8,128)(2,1)} %slice_bitcast_fusion.4), channel_id=1, source_target_pairs={{0,1},{1,0},{2,3},{3,2},{4,5},{5,4},{6,7},{7,6},{8,9},{9,8},{10,11... | collective-permute-start | bytes 1572872 | tf_op jit(solution)/shard_map/ppermute | solution.py:46
  393.1 21.6 %collective-permute-start.64 = (bf16[2,128,2048]{2,1,0:T(8,128)(2,1)S(1)}, bf16[2,128,2048]{2,1,0:T(8,128)(2,1)S(1)}, u32[]{:S(2)}, u32[]{:S(2)}) collective-permute-start(bf16[2,128,2048]{2,1,0:T(8,128)(2,1)S(1)} %convert_element_type.436), channel_id=1, source_target_pairs={{0,16},{1,49},{16,32},{17,1},{32,48},{33,17},{48,0},{49,33},{2,18}... | collective-permute-start | bytes 3145736 | tf_op jit(solution)/shard_map/ppermute | solution.py:70
  396.5 15.3 %collective-permute-start.66 = (bf16[2,2,640,128]{3,2,1,0:T(8,128)(2,1)S(1)}, bf16[2,2,640,128]{3,2,1,0:T(8,128)(2,1)S(1)}, u32[]{:S(2)}, u32[]{:S(2)}) collective-permute-start(bf16[2,2,640,128]{3,2,1,0:T(8,128)(2,1)S(1)} %pad_maximum_fusion.6), channel_id=1, source_target_pairs={{0,6},{2,0},{4,2},{6,4},{1,7},{3,1},{5,3},{7,5},{8,14},{10,8},{12,... | collective-permute-start | bytes 1966088 | tf_op jit(solution)/shard_map/ppermute | solution.py:46
  397.4 16.3 %collective-permute-start.65 = (bf16[2,2,640,128]{3,2,1,0:T(8,128)(2,1)S(1)}, bf16[2,2,640,128]{3,2,1,0:T(8,128)(2,1)S(1)}, u32[]{:S(2)}, u32[]{:S(2)}) collective-permute-start(bf16[2,2,640,128]{3,2,1,0:T(8,128)(2,1)S(1)} %pad_maximum_fusion.5), channel_id=1, source_target_pairs={{0,2},{2,4},{4,6},{6,0},{1,3},{3,5},{5,7},{7,1},{8,10},{10,12},{12... | collective-permute-start | bytes 1966088 | tf_op jit(solution)/shard_map/ppermute | solution.py:46
  398.6 34.6 %collective-permute-start.72 = (bf16[2,3,704,128]{3,2,0,1:T(8,128)(2,1)S(1)}, bf16[2,3,704,128]{3,2,0,1:T(8,128)(2,1)S(1)}, u32[]{:S(2)}, u32[]{:S(2)}) collective-permute-start(bf16[2,3,704,128]{3,2,0,1:T(8,128)(2,1)S(1)} %pad_maximum_fusion.1), channel_id=1, source_target_pairs={{0,16},{16,32},{32,48},{48,0},{1,17},{17,33},{33,49},{49,1},{2,18}... | collective-permute-start | bytes 3244040 | tf_op jit(solution)/shard_map/ppermute | solution.py:46
  398.7 34.5 %collective-permute-start.73 = (bf16[2,3,704,128]{3,2,0,1:T(8,128)(2,1)S(1)}, bf16[2,3,704,128]{3,2,0,1:T(8,128)(2,1)S(1)}, u32[]{:S(2)}, u32[]{:S(2)}) collective-permute-start(bf16[2,3,704,128]{3,2,0,1:T(8,128)(2,1)S(1)} %pad_maximum_fusion.1), channel_id=1, source_target_pairs={{0,48},{16,0},{32,16},{48,32},{1,49},{17,1},{33,17},{49,33},{2,50}... | collective-permute-start | bytes 3244040 | tf_op jit(solution)/shard_map/ppermute | solution.py:46
  441.5 17.5 %collective-permute-start.76 = (bf16[2,640,128]{2,1,0:T(8,128)(2,1)S(1)}, bf16[2,640,128]{2,1,0:T(8,128)(2,1)S(1)}, u32[]{:S(2)}, u32[]{:S(2)}) collective-permute-start(bf16[2,640,128]{2,1,0:T(8,128)(2,1)S(1)} %fusion.16), channel_id=1, source_target_pairs={{0,16},{16,32},{32,48},{48,0},{1,17},{17,33},{33,49},{49,1},{2,18}... | collective-permute-start | bytes 983048 | tf_op jit(solution)/shard_map/ppermute | solution.py:46
  443.9 26.7 %collective-permute-start.77 = (bf16[1,3,704,128]{3,2,0,1:T(8,128)(2,1)S(1)}, bf16[1,3,704,128]{3,2,0,1:T(8,128)(2,1)S(1)}, u32[]{:S(2)}, u32[]{:S(2)}) collective-permute-start(bf16[1,3,704,128]{3,2,0,1:T(8,128)(2,1)S(1)} %slice.271), channel_id=1, source_target_pairs={{0,16},{16,32},{32,48},{48,0},{1,17},{17,33},{33,49},{49,1},{2,18}... | collective-permute-start | bytes 1622024 | tf_op jit(solution)/shard_map/ppermute | solution.py:46
  445.9 24.7 %collective-permute-start.78 = (bf16[1,3,704,128]{3,2,0,1:T(8,128)(2,1)S(1)}, bf16[1,3,704,128]{3,2,0,1:T(8,128)(2,1)S(1)}, u32[]{:S(2)}, u32[]{:S(2)}) collective-permute-start(bf16[1,3,704,128]{3,2,0,1:T(8,128)(2,1)S(1)} %slice.272), channel_id=1, source_target_pairs={{0,48},{16,0},{32,16},{48,32},{1,49},{17,1},{33,17},{49,33},{2,50}... | collective-permute-start | bytes 1622024 | tf_op jit(solution)/shard_map/ppermute | solution.py:46
  480.7 24.5 %all-to-all-start.1 = ((bf16[16,128,128]{2,1,0:T(8,128)(2,1)}), bf16[16,128,128]{2,1,0:T(8,128)(2,1)S(1)}, u32[]{:S(2)}, u32[]{:S(2)}) async-start(bf16[16,128,128]{2,1,0:T(8,128)(2,1)} %bitcast.95), calls=%async_computation.3 | async-start | bytes 1048576 | tf_op jit(solution)/shard_map/all_to_all | solution.py:1104
  (106 other events, 943.6 us)
Sparse Core Ops, SparseCore 0:
  84.3 84.9 all-gather.1
  238.8 36.4 reduce-scatter.2
  277.7 59.3 reduce-scatter.4

commit v6 on v5

--- a/solution.py
+++ b/solution.py
@@ -318,45 +318,6 @@
     )(place, *x_pieces, *w_pieces)
 
 
-def project_out_kernel(*refs):
-    place, w_refs, left_ref = refs[0], refs[1:6], refs[6]
-    parts, w_out, weights, sems = refs[7:12], refs[12], refs[13], refs[14]
-    step = pl.program_id(0)
-    columns = put_columns(place, w_refs, QKV, weights, sems, 0)
-    back = pltpu.make_async_copy(weights, w_out, sems.at[16])
-
-    @pl.when(step == 0)
-    def _():
-        for copy in columns:
-            copy.start()
-        for copy in columns:
-            copy.wait()
-        back.start()
-
-    put_parts(step, matmul(left_ref[...], weights[...]).astype(BF16), parts)
-
-    @pl.when(step == 3)
-    def _():
-        back.wait()
-
-
-def project_out(place, w_pieces, mixed):
-    return pl.pallas_call(
-        project_out_kernel,
-        grid_spec=pltpu.PrefetchScalarGridSpec(
-            num_scalar_prefetch=1,
-            grid=(4,),
-            in_specs=[ANYWHERE] * 5 + [pl.BlockSpec((TILE, HEADS * HD), lambda i, p: (i, 0))],
-            out_specs=PART_SPECS + [ANYWHERE],
-            scratch_shapes=[pltpu.VMEM((HEADS * HD, D), BF16), pltpu.SemaphoreType.DMA((17,))],
-        ),
-        out_shape=PART_SHAPES + [shaped(HEADS * HD, D)],
-        compiler_params=params("arbitrary"),
-        cost_estimate=cost(2 * 2 * HALF * HEADS * HD * D, 7),
-        name="project_out",
-    )(place, *w_pieces, mixed)
-
-
 def project_kernel(left_ref, weight_ref, *parts):
     put_parts(pl.program_id(0), matmul(left_ref[...], weight_ref[...]).astype(BF16), parts)
 
@@ -375,19 +336,6 @@
     )(left, weight)
 
 
-def grad_mixed_kernel(*refs):
-    grad_refs, weight_ref = refs[1:6], refs[6]
-    grad_mixed_ref, rows, sems = refs[7:]
-    copies = put_tokens(grad_refs, rows, sems, 0)
-    for copy in copies:
-        copy.start()
-    for copy in copies:
-        copy.wait()
-    for i in range(4):
-        tile = rows[i * TILE : (i + 1) * TILE, :]
-        grad_mixed_ref[i * TILE : (i + 1) * TILE, :] = times_transposed(tile, weight_ref[...]).astype(BF16)
-
-
 def put_term(place, left, rows, term_ref):
     def one(i, carry):
         term = matmul(left, rows[:, pl.ds(pl.multiple_of(i * 4 * B, 4 * B), 4 * B)]).astype(BF16)
@@ -399,25 +347,6 @@
         return carry
 
     lax.fori_loop(0, 4, one, 0)
-
-
-def grad_of_mixed(place, grad_pieces, weight):
-    whole = lambda *shape: pl.BlockSpec(shape, lambda i, p: (0,) * len(shape))
-    rows = HEADS * HD
-    return pl.pallas_call(
-        grad_mixed_kernel,
-        grid_spec=pltpu.PrefetchScalarGridSpec(
-            num_scalar_prefetch=1,
-            grid=(1,),
-            in_specs=[ANYWHERE] * 5 + [whole(rows, D)],
-            out_specs=whole(2 * HALF, rows),
-            scratch_shapes=[pltpu.VMEM((2 * HALF, D), BF16), pltpu.SemaphoreType.DMA((10,))],
-        ),
-        out_shape=shaped(2 * HALF, rows),
-        compiler_params=params("arbitrary"),
-        cost_estimate=cost(2 * 2 * HALF * rows * D, 6),
-        name="grad_of_mixed",
-    )(place, *grad_pieces, weight)
 
 
 def qkv_back_kernel(grad_q_ref, own_ref, later_ref, cosine_ref, sine_ref, scale_ref, weight_ref, *outs):
@@ -507,7 +436,9 @@
     bias_ref[HALF:, :] = jnp.where(key_at <= query_at, 0.0, -1e30)
 
 
-def attention_kernel(place_ref, query_ref, kv_ref, mixed_ref, log_ref, bias_ref):
+def attention_kernel(place_ref, query_ref, kv_ref, weight_ref, mixed_ref, log_ref, *rest):
+    parts, bias_ref = rest[:5], rest[5]
+
     @pl.when(pl.program_id(0) == 0)
     def _():
         set_bias(place_ref, bias_ref)
@@ -521,21 +452,38 @@
         low = (weights * (1.0 / total)).astype(BF16)
         mixed_ref[0, :, head * HD : (head + 1) * HD] = outer_sum(value, low).T.astype(BF16)
         log_ref[0, head] = top + jnp.log(total)
-
-
-def attention_back_kernel(
-    place_ref, query_ref, kv_ref, grad_ref, log_ref, grad_query_ref, earlier_ref, own_ref, bias_ref
-):
-    @pl.when(pl.program_id(0) == 0)
-    def _():
+    put_rows(parts, matmul(mixed_ref[0], weight_ref[...]).astype(BF16))
+
+
+def put_rows(parts, rows):
+    row = 0
+    for ref, length in zip(parts, LENGTHS):
+        ref[0] = rows[row : row + length]
+        row += length
+
+
+def attention_back_kernel(place_ref, *refs):
+    grad_refs, query_ref, kv_ref, log_ref, weight_ref = refs[:5], *refs[5:9]
+    grad_query_ref, earlier_ref, own_ref, bias_ref, rows, sems = refs[9:]
+    step = pl.program_id(0)
+    copies = put_tokens(grad_refs, rows, sems, 0)
+
+    @pl.when(step == 0)
+    def _():
+        for copy in copies:
+            copy.start()
         set_bias(place_ref, bias_ref)
-
+        for copy in copies:
+            copy.wait()
+
+    hidden = rows[pl.ds(pl.multiple_of(step * HALF, HALF), HALF), :]
+    grads = times_transposed(hidden, weight_ref[...]).astype(BF16)
     key, value = kv_ref[0, :, :HD], kv_ref[0, :, HD:]
     grad_key = jnp.zeros((2 * HALF, HD), F32)
     grad_value = jnp.zeros((2 * HALF, HD), F32)
     for head in range(HEADS):
         lanes = slice(head * HD, (head + 1) * HD)
-        query, grad = query_ref[0, head], grad_ref[0, :, lanes]
+        query, grad = query_ref[0, head], grads[:, lanes]
         weights = jnp.exp(times_transposed(key, query) + bias_ref[...] - log_ref[0, head])
         grad_weights = times_transposed(value, grad)
         delta = jnp.sum(weights * grad_weights, axis=0, keepdims=True)
@@ -552,7 +500,10 @@
     return pl.BlockSpec((1,) + tail, lambda s, place: (s,) + (0,) * len(tail))
 
 
-def attention_call(kernel, in_specs, out_specs, out_shape, flops, name):
+HEAD_ROWS = pl.BlockSpec((HEADS * HD, D), lambda s, place: (2 * place[1] + place[2], 0))
+
+
+def attention_call(kernel, in_specs, out_specs, out_shape, scratch, flops, name):
     return pl.pallas_call(
         kernel,
         grid_spec=pltpu.PrefetchScalarGridSpec(
@@ -560,32 +511,34 @@
             grid=(2,),
             in_specs=in_specs,
             out_specs=out_specs,
-            scratch_shapes=[pltpu.VMEM((2 * HALF, HALF), F32)],
+            scratch_shapes=[pltpu.VMEM((2 * HALF, HALF), F32)] + scratch,
         ),
         out_shape=out_shape,
         compiler_params=params("arbitrary"),
-        cost_estimate=cost(flops * 8 * 2 * HALF * HALF * HD * 2, 4),
+        cost_estimate=cost(flops * 8 * 2 * HALF * HALF * HD * 2, 8),
         name=name,
     )
 
 
-def attention(place, query, kv):
+def attention(place, query, kv, weight):
     return attention_call(
         attention_kernel,
-        [sequence_block(HEADS, HALF, HD), sequence_block(2 * HALF, 2 * HD)],
-        [sequence_block(HALF, HEADS * HD), sequence_block(HEADS, 1, HALF)],
-        [shaped(2, HALF, HEADS * HD), shaped(2, HEADS, 1, HALF, kind=F32)],
-        2,
+        [sequence_block(HEADS, HALF, HD), sequence_block(2 * HALF, 2 * HD), HEAD_ROWS],
+        [sequence_block(HALF, HEADS * HD), sequence_block(HEADS, 1, HALF)] + [sequence_block(n, D) for n in LENGTHS],
+        [shaped(2, HALF, HEADS * HD), shaped(2, HEADS, 1, HALF, kind=F32)] + PART_SHAPES,
+        [],
+        3,
         "attention",
-    )(place, query, kv)
-
-
-def attention_back(place, query, kv, grad, log_total):
+    )(place, query, kv, weight)
+
+
+def attention_back(place, grad_pieces, query, kv, log_total, weight):
     return attention_call(
         attention_back_kernel,
-        [
+        [ANYWHERE] * 5
+        + [
             sequence_block(HEADS, HALF, HD), sequence_block(2 * HALF, 2 * HD),
-            sequence_block(HALF, HEADS * HD), sequence_block(HEADS, 1, HALF),
+            sequence_block(HEADS, 1, HALF), HEAD_ROWS,
         ],
         [sequence_block(HALF, HEADS * HD), sequence_block(HALF, 2 * HD), sequence_block(HALF, 2 * HD)],
         [
@@ -593,13 +546,74 @@
             shaped(2, HALF, 2 * HD),
             shaped(2, HALF, 2 * HD, kind=F32),
         ],
-        5,
+        [pltpu.VMEM((2 * HALF, D), BF16), pltpu.SemaphoreType.DMA((10,))],
+        6,
         "attention_back",
-    )(place, query, kv, grad, log_total)
-
-
-def own_rows(rows_all, y, core, per):
-    return lax.dynamic_slice_in_dim(rows_all, (2 * y + core) * per, per, 0)
+    )(place, *grad_pieces, query, kv, log_total, weight)
+
+
+def finish_attention_kernel(place, *refs):
+    piece_refs, w_query, w_key, w_value, gain_ref = refs[:4], *refs[4:8]
+    query_out, key_out, value_out, gain_out, send_out, rows = refs[8:]
+    for ref, by in zip(piece_refs, range(4)):
+        at_y = (place[1] + by) % 4
+        for c in range(2):
+            piece = ref[c].astype(F32)
+            rows[pl.ds(pl.multiple_of((2 * at_y + c) * HEADS * HD, HEADS * HD), HEADS * HD)] = piece[: HEADS * HD]
+            for i in range(2):
+                send_out[2 * (2 * at_y + c) + i] = piece[QKV + i * B : QKV + (i + 1) * B].astype(BF16)
+        both = ref[0].astype(F32) + ref[1].astype(F32)
+        at = pl.multiple_of(H * HD + at_y * HD, HD)
+        rows[pl.ds(at, HD)] = both[HEADS * HD : (HEADS + 1) * HD]
+        rows[pl.ds(at + KV * HD, HD)] = both[(HEADS + 1) * HD : QKV]
+    gain = gain_ref[...]
+    total = jnp.zeros((B, 1), F32)
+    row = 0
+    for weight, out in ((w_query, query_out), (w_key, key_out), (w_value, value_out)):
+        for i in range(out.shape[1] // B):
+            lanes = slice(i * B, (i + 1) * B)
+            block = rows[row : row + B].T
+            total = total + jnp.sum(block * weight[:, lanes].astype(F32), axis=1, keepdims=True)
+            out[:, lanes] = block * gain
+            row += B
+    gain_out[...] = total
+
+
+def finish_attention(place, pieces, w_query, w_key, w_value, gain):
+    whole = lambda *shape: pl.BlockSpec(shape, lambda i, p: (0,) * len(shape))
+    kv = KV * HD
+    return pl.pallas_call(
+        finish_attention_kernel,
+        grid_spec=pltpu.PrefetchScalarGridSpec(
+            num_scalar_prefetch=1,
+            grid=(1,),
+            in_specs=[whole(2, QKV + HEADS * HD, B)] * 4 + [whole(B, D), whole(B, kv), whole(B, kv), whole(B, 1)],
+            out_specs=[whole(B, D), whole(B, kv), whole(B, kv), whole(B, 1), whole(16, B, B)],
+            scratch_shapes=[pltpu.VMEM((D + 2 * kv, B), F32)],
+        ),
+        out_shape=[
+            shaped(B, D, kind=F32), shaped(B, kv, kind=F32), shaped(B, kv, kind=F32), shaped(B, 1, kind=F32),
+            shaped(16, B, B),
+        ],
+        compiler_params=params("arbitrary"),
+        cost_estimate=cost(0, 4),
+        name="finish_attention",
+    )(place, *pieces, w_query, w_key, w_value, gain)
+
+
+def finish_output_kernel(blocks, out):
+    for i in range(16):
+        out[:, i * B : (i + 1) * B] = blocks[i].astype(F32)
+
+
+def finish_output(blocks):
+    return pl.pallas_call(
+        finish_output_kernel,
+        out_shape=shaped(B, D, kind=F32),
+        compiler_params=params(),
+        cost_estimate=cost(0, 2),
+        name="finish_output",
+    )(blocks)
 
 
 def feed_forward_kernel(*refs):
@@ -968,8 +982,7 @@
         mine, other = of_core(pair), of_core(pair, True)
         there, here, across = yield trio(mine, other, "zlo")
         own = by_core(add(mine, there), add(here, across)).astype(BF16)
-        ring = yield small_gather(own, "y")
-        return jnp.roll(jnp.stack([own, *ring]), y, axis=0)
+        return whole_ring((yield from ring_gather_steps(own, "y")))
 
     def ff_steps(sums):
         own = yield from ring_scatter_steps([sums[i] for i in range(4)], "z")
@@ -982,10 +995,6 @@
         ring = whole_ring((yield from ring_gather_steps(both, "y")))
         return [piece[:, :2] for piece in ring], [piece[:, 2] for piece in ring]
 
-    def all_to_all_steps(value):
-        (got,) = yield (lax.all_to_all(value, FSDP, 0, 0, tiled=True),)
-        return got
-
     x_low = layer_input[0]
     frequency = theta ** (-jnp.arange(0, HD, 2).astype(F32) / HD)
     angles = positions[0].astype(F32)[:, None] * frequency
@@ -995,45 +1004,35 @@
         tables += [high.astype(BF16), (table - high).astype(BF16)]
     tokens = Flow(gather_steps(jnp.concatenate([x_low, *tables], axis=1)))
     grads = Flow(gather_steps(out_grad[0]))
-    output_rows = Flow(all_to_all_steps(w_output.reshape(B, 16, B).transpose(1, 0, 2)))
-    (gain_one,) = stage([tokens], attn_gain[:, None])
-
-    qkv_mine, qkv_other = prepare_qkv(place, w_query, w_key, w_value, gain_one)
-    ff_mine, ff_other, ff_down = prepare_ff(place, w_gate, w_up, w_down, mlp_gain[:, None])
-    ff_got = swap_core(ff_other)
-    qkv_mine, qkv_other, ff_mine, ff_got, ff_down = stage(
-        [tokens, output_rows], qkv_mine, qkv_other, ff_mine, ff_got, ff_down
-    )
-
-    o_rows = output_rows.result.reshape(D, B)
-    mine = jnp.concatenate([qkv_mine, own_rows(o_rows, y, core, HEADS * HD)], axis=0)
-    other = jnp.concatenate([qkv_other, own_rows(o_rows, y, 1 - core, HEADS * HD)], axis=0)
-    columns = Flow(column_steps(mine, swap_core(other)))
+    o_all = lax.all_gather(w_output, FSDP, axis=0, tiled=True)
+    qkv_mine, qkv_other = prepare_qkv(place, w_query, w_key, w_value, attn_gain[:, None])
+    qkv_mine, qkv_got, gain_two = stage([tokens], qkv_mine, swap_core(qkv_other), mlp_gain[:, None])
+
+    columns = Flow(column_steps(qkv_mine, qkv_got))
+    ff_mine, ff_other, ff_down = prepare_ff(place, w_gate, w_up, w_down, gain_two)
+    ff_mine, ff_got, ff_down, x_low = stage([tokens, columns], ff_mine, swap_core(ff_other), ff_down, x_low)
+
     inputs = x_low.astype(F32)
     scale_one = lax.rsqrt(jnp.mean(inputs * inputs, axis=-1, keepdims=True) + eps)
-    scale_one, ff_mine, ff_got, ff_down = stage([tokens, columns], scale_one, ff_mine, ff_got, ff_down)
+    scale_one, ff_mine, ff_got, ff_down = stage([tokens, columns, grads], scale_one, ff_mine, ff_got, ff_down)
 
     hidden_rows = Flow(hidden_steps(ff_mine, ff_got, ff_down))
-    stage([tokens, columns, hidden_rows, grads])
-    stage([columns, hidden_rows])
+    stage([tokens, columns])
 
     x_pieces = tokens.result
+    query, key_value, scale_all, cosine, sine, qkv_full = project_qkv(place, x_pieces, columns.result)
+    query, key_value = stage([hidden_rows, grads], query, key_value)
+
+    earlier = lax.ppermute(key_value, "zlo", [(0, 1)])
+    query, key_value, earlier = stage([grads, hidden_rows], query, key_value, earlier)
+
     ff_all = lax.all_gather(hidden_rows.result, "x", axis=0, tiled=False)
-    query, key_value, scale_all, cosine, sine, qkv_full = project_qkv(place, x_pieces, columns.result)
-    query, key_value = stage([], query, key_value)
-
-    earlier = lax.ppermute(key_value, "zlo", [(0, 1)])
-    query, key_value, earlier = stage([grads], query, key_value, earlier)
-
     key_value = jnp.concatenate([earlier, key_value], axis=1)
-    mixed, log_total = attention(place, query, key_value)
-    (mixed,) = stage([grads], mixed)
-    mixed = mixed.reshape(2 * HALF, HEADS * HD)
-    *parts, o_full = project_out(place, columns.result, mixed)
+    mixed, log_total, *parts = attention(place, query, key_value, o_all)
+    parts = stage([grads], *parts)
+    grad_pieces = grads.result
     sums = Flow(scatter_steps(parts))
-    stage([sums, grads])
-    grad_pieces = grads.result
-    for _ in range(3):
+    for _ in range(4):
         stage([sums])
     hidden = inputs + sums.result
     scale_two = lax.rsqrt(jnp.mean(hidden * hidden, axis=-1, keepdims=True) + eps)
@@ -1044,13 +1043,13 @@
 
     activation, act_t, gate_t, up_t, *parts, down_full = feed_forward(place, normed_pieces, grad_pieces, ff_all)
     sums = Flow(scatter_steps(parts))
-    (act_t,) = stage([sums], act_t)
+    (gate_t,) = stage([sums], gate_t)
+    gate_up_terms = ff_terms(gate_up_kernel, place, normed_pieces, (gate_t, up_t), 2 * FFL, "gate_up_terms")
+    gate_up_terms, act_t = stage([sums], gate_up_terms, act_t)
+    gate_up_sum = lax.psum_scatter(gate_up_terms, "x", scatter_dimension=0, tiled=True)[0]
     down_terms = ff_terms(down_kernel, place, grad_pieces, (act_t,), FFL, "down_terms")
-    down_terms, gate_t = stage([sums], down_terms, gate_t)
+    (down_terms,) = stage([sums], down_terms)
     down_sum = lax.psum_scatter(down_terms, "x", scatter_dimension=0, tiled=True)[0]
-    gate_up_terms = ff_terms(gate_up_kernel, place, normed_pieces, (gate_t, up_t), 2 * FFL, "gate_up_terms")
-    (gate_up_terms,) = stage([sums], gate_up_terms)
-    gate_up_sum = lax.psum_scatter(gate_up_terms, "x", scatter_dimension=0, tiled=True)[0]
     stage([sums])
 
     grad_normed_two = sums.result
@@ -1069,26 +1068,25 @@
     stage([hidden_grads])
 
     hidden_grad_pieces = hidden_grads.result
-    grad_mixed = grad_of_mixed(place, hidden_grad_pieces, o_full)
-    (grad_mixed,) = stage([result], grad_mixed)
     grad_query, grad_earlier, grad_own = attention_back(
-        place, query, key_value, grad_mixed.reshape(2, HALF, HEADS * HD), log_total
+        place, hidden_grad_pieces, query, key_value, log_total, o_all
     )
     grad_query, grad_earlier, grad_own, mixed = stage([result], grad_query, grad_earlier, grad_own, mixed)
     later = lax.ppermute(grad_earlier, "zlo", [(1, 0)])
-    output_terms = attention_terms(place, hidden_grad_pieces, mixed, "output_terms")
+    output_terms = attention_terms(place, hidden_grad_pieces, mixed.reshape(2 * HALF, HEADS * HD), "output_terms")
     later, grad_query, output_terms, down_sum, gate_up_sum = stage(
         [result], later, grad_query, output_terms, down_sum, gate_up_sum
     )
     ff_sums = Flow(ff_steps(jnp.concatenate([gate_up_sum, down_sum], axis=1)))
     *parts, grad_t = qkv_back(grad_query, grad_own, later, cosine, sine, scale_all, qkv_full)
-    *parts, grad_t = stage([ff_sums], *parts, grad_t)
+    *parts, grad_t = stage([ff_sums, result], *parts, grad_t)
     sums = Flow(scatter_steps(parts))
     terms = attention_terms(place, x_pieces, grad_t, "qkv_terms", output_terms)
     (terms,) = stage([sums, ff_sums], terms)
     attention_sums = Flow(attention_steps(terms))
+    stage([sums, attention_sums])
+    stage([attention_sums])
     stage([sums, attention_sums, ff_sums])
-    stage([sums, attention_sums])
     stage([sums, attention_sums])
     grad_normed = sums.result
     mean_one = jnp.mean(grad_normed * inputs, axis=-1, keepdims=True)
@@ -1098,36 +1096,26 @@
         - inputs * (scale_one * scale_one * scale_one) * mean_one
     )
     input_grad = input_grad.astype(BF16)
-    while attention_sums.result is None or ff_sums.result is None:
-        stage([attention_sums, ff_sums])
-    output_rows = attention_sums.result[:, :, QKV:].reshape(16, B, B)
-    output_grad = lax.all_to_all(output_rows, FSDP, 0, 0, tiled=True)
+    stage([attention_sums, ff_sums])
+    stage([attention_sums, ff_sums])
+
+    query_grad, key_grad, value_grad, attn_gain_grad, output_send = finish_attention(
+        place, attention_sums.result, w_query, w_key, w_value, attn_gain[:, None]
+    )
+    output_grad = finish_output(lax.all_to_all(output_send, FSDP, 0, 0, tiled=True))
     gate_up, down = ff_sums.result
-
-    output_grad = output_grad.transpose(1, 0, 2).reshape(B, D).astype(F32)
-    sums = attention_sums.result
-    query_grad = sums[:, :, : HEADS * HD].reshape(D, B).T.astype(F32)
-    key_grad = jnp.sum(sums[:, :, HEADS * HD : (HEADS + 1) * HD].astype(F32), axis=1)
-    key_grad = key_grad.reshape(KV * HD, B).T
-    value_grad = jnp.sum(sums[:, :, (HEADS + 1) * HD : QKV].astype(F32), axis=1)
-    value_grad = value_grad.reshape(KV * HD, B).T
-    attn_gain_grad = (
-        jnp.sum(query_grad * w_query.astype(F32), axis=1)
-        + jnp.sum(key_grad * w_key.astype(F32), axis=1)
-        + jnp.sum(value_grad * w_value.astype(F32), axis=1)
-    )
     gain_two = mlp_gain[:, None]
     gate_grad, gate_gain = finish_hidden(place, [p[0] for p in gate_up], w_gate, gain_two)
     up_grad, up_gain = finish_hidden(place, [p[1] for p in gate_up], w_up, gain_two)
     down_grad = finish_down(place, down)
-    one = attn_gain[:, None]
+    assert attention_sums.result is not None and ff_sums.result is not None
     return (
         (hidden + result.result).astype(BF16)[None],
         input_grad[None],
-        attn_gain_grad,
-        query_grad * one,
-        key_grad * one,
-        value_grad * one,
+        attn_gain_grad[:, 0],
+        query_grad,
+        key_grad,
+        value_grad,
         output_grad,
         (gate_gain + up_gain)[:, 0],
         gate_grad,

time: 524 us -> 557 us (1.063)
  waiting for transfers between devices: 152 us -> 204 us
  local copies, waits for them, and re-layouts: 42.9 us -> 34.4 us
  other arithmetic: 38.3 us -> 31.6 us
    ppermute x51 -> x52, waiting for transfers between devices: 70.6 us -> 101 us  [shift(): lax.ppermute(value, axis, [(i, (i + by) % size) for i in range(size)])]
    reduce_scatter x1, waiting for transfers between devices: 0.28 us -> 23.1 us  [on_device(): lax.psum_scatter(gate_up_terms, 'x', scatter_dimension=0, tiled=True)[0]]
    ppermute x51 -> x52, starting transfers between devices: 59.3 us -> 68 us  [shift(): lax.ppermute(value, axis, [(i, (i + by) % size) for i in range(size)])]
    ppermute x8, waiting for transfers between devices: 18.3 us -> 9.94 us  [shift(): lax.ppermute(value, ('zlo', 'zhi'), [(at[z], at[(z + by) % 4]) for z in r...]
    unnamed x124 -> x125, local copies, waits for them, and re-layouts: 16.8 us -> 11.7 us
    all_to_all x2 -> x1, starting transfers between devices: 12 us -> 8.87 us  [on_device(): lax.all_to_all(output_send, FSDP, 0, 0, tiled=True)]
  transfers between devices with their start and end apart: 84 -> 85, of which waited for: 36 -> 38; matrix products, arithmetic and copies ran while one was open for 10% -> 9% of each run, Pallas kernels for 25% -> 22%
where the time goes in v6:
time: 557 us; the launch traced here: 550 us
  waiting for transfers between devices  204 us (37%)
  Pallas kernels  156 us (28%)
  starting transfers between devices  109 us (20%)
  local copies, waits for them, and re-layouts  34.4 us (6%)
  other arithmetic  31.6 us (6%)
  between operations  15.2 us (3%)
    ppermute x52, waiting for transfers between devices, shift(): lax.ppermute(value, axis, [(i, (i + by) % size) for i in range(size)])  101 us
    ppermute x52, starting transfers between devices, shift(): lax.ppermute(value, axis, [(i, (i + by) % size) for i in range(size)])  68 us
    ppermute x16, waiting for transfers between devices, along_y(): return lax.ppermute(value, ('y', 'core'), pairs)  61.1 us
    pallas_call x1, Pallas kernels, feed_forward(): pl.pallas_call(feed_forward_kernel, grid_spec=pltpu.PrefetchScalarGridSpe...  28.9 us
    pallas_call x2, Pallas kernels, ff_terms(): pl.pallas_call(kernel, grid_spec=pltpu.PrefetchScalarGridSpec(num_scalar_...  23.9 us
    reduce_scatter x1, waiting for transfers between devices, on_device(): lax.psum_scatter(gate_up_terms, 'x', scatter_dimension=0, tiled=True)[0]  23.1 us
    pallas_call x1, Pallas kernels, attention_back(): attention_call(attention_back_kernel, [ANYWHERE] * 5 + [sequence_block(HE...  20.7 us
    ppermute x16, starting transfers between devices, along_y(): return lax.ppermute(value, ('y', 'core'), pairs)  15.3 us
  transfers between devices with their start and end apart: 85, of which 38 were waited for; matrix products, arithmetic and copies ran while one was open for 9% of the time, Pallas kernels for 22%

profile of v6, /device:TPU:1, one launch (start us, length us, event | category | flops | bytes accessed | tf_op | source)
XLA Modules:
  0.0 549.7 jit_solution(14567665923633720742)
XLA Ops:
  25.2 4.9 prepare_ff.1
  42.5 8.3 %collective-permute-done.7.refs_10_ = bf16[2,2,384,128]{3,2,1,0:T(8,128)(2,1)S(1)} collective-permute-done((bf16[2,2,384,128]{3,2,1,0:T(8,128)(2,1)S(1)}, bf16[2,2,384,128]{3,2,1,0:T(8,128)(2,1)S(1)}, u32[]{:S(2)}, u32[]{:S(2)}) %collective-permute-start.7) | collective-permute-done | bytes 393248 | tf_op jit(solution)/shard_map/ppermute | solution.py:46
  62.6 5.3 collective-permute-done.15.refs_9_
  69.4 9.3 %project_qkv.1 = (bf16[2,4,512,64]{3,2,1,0:T(8,128)(2,1)}, bf16[2,512,128]{2,1,0:T(8,128)(2,1)}, f32[1024,1]{1,0:T(8,128)}, f32[1024,128]{1,0:T(8,128)}, f32[1024,128]{1,0:T(8,128)}, /*index=5*/bf16[384,2048]{1,0:T(8,128)(2,1)}) custom-call(s32[5]{0:T(128)} %stack.179.place.refs_0_.place_ref, bf16[2,128,2176]{2,1,0:T(8,128)(2,1)} %copy-done.2, ...), custom_call_target="tpu_custom_call" | custom-call | flops 1610612736 | bytes 8388608 | tf_op jit(solution)/shard_map/project_qkv/pallas_call | solution.py:293
  78.8 5.9 %collective-permute-done.10 = bf16[2112,128]{1,0:T(8,128)(2,1)S(1)} collective-permute-done((bf16[2112,128]{1,0:T(8,128)(2,1)S(1)}, bf16[2112,128]{1,0:T(8,128)(2,1)S(1)}, u32[]{:S(2)}, u32[]{:S(2)}) %collective-permute-start.10) | collective-permute-done | bytes 540704 | tf_op jit(solution)/shard_map/ppermute | solution.py:44
  95.0 6.4 %collective-permute-done.20 = bf16[2,512,128]{2,1,0:T(8,128)(2,1)S(1)} collective-permute-done((bf16[2,512,128]{2,1,0:T(8,128)(2,1)S(1)}, bf16[2,512,128]{2,1,0:T(8,128)(2,1)S(1)}, u32[]{:S(2)}, u32[]{:S(2)}) %collective-permute-start.20) | collective-permute-done | bytes 262176 | tf_op jit(solution)/shard_map/ppermute | solution.py:1026
  105.8 13.7 %attention.1 = (bf16[2,512,256]{2,1,0:T(8,128)(2,1)}, f32[2,4,1,512]{3,2,1,0:T(1,128)}, bf16[2,128,2048]{2,1,0:T(8,128)(2,1)}, bf16[2,128,2048]{2,1,0:T(8,128)(2...) custom-call(s32[5]{0:T(128)} %stack.179.place.refs_0_.place_ref, ...), custom_call_target="tpu_custom_call" | custom-call | flops 1610612736 | bytes 8388608 | tf_op jit(solution)/shard_map/attention/pallas_call | solution.py:524
  123.7 7.6 %collective-permute-done.23 = bf16[2,64,2048]{2,1,0:T(8,128)(2,1)S(1)} collective-permute-done((bf16[2,64,2048]{2,1,0:T(8,128)(2,1)S(1)}, bf16[2,64,2048]{2,1,0:T(8,128)(2,1)S(1)}, u32[]{:S(2)}, u32[]{:S(2)}) %collective-permute-start.23) | collective-permute-done | bytes 524320 | tf_op jit(solution)/shard_map/ppermute | solution.py:70
  133.4 12.8 %collective-permute-done.26 = bf16[2,128,2048]{2,1,0:T(8,128)(2,1)S(1)} collective-permute-done((bf16[2,128,2048]{2,1,0:T(8,128)(2,1)S(1)}, bf16[2,128,2048]{2,1,0:T(8,128)(2,1)S(1)}, u32[]{:S(2)}, u32[]{:S(2)}) %collective-permute-start.26) | collective-permute-done | bytes 1048608 | tf_op jit(solution)/shard_map/ppermute | solution.py:70
  154.8 14.0 %collective-permute-done.29.refs_2_ = bf16[2,128,2048]{2,1,0:T(8,128)(2,1)S(1)} collective-permute-done((bf16[2,128,2048]{2,1,0:T(8,128)(2,1)S(1)}, bf16[2,128,2048]{2,1,0:T(8,128)(2,1)S(1)}, u32[]{:S(2)}, u32[]{:S(2)}) %collective-permute-start.29) | collective-permute-done | bytes 1048608 | tf_op jit(solution)/shard_map/ppermute | solution.py:70
  171.3 8.4 %collective-permute-done.30.refs_4_ = bf16[2,64,2048]{2,1,0:T(8,128)(2,1)S(1)} collective-permute-done((bf16[2,64,2048]{2,1,0:T(8,128)(2,1)S(1)}, bf16[2,64,2048]{2,1,0:T(8,128)(2,1)S(1)}, u32[]{:S(2)}, u32[]{:S(2)}) %collective-permute-start.30) | collective-permute-done | bytes 524320 | tf_op jit(solution)/shard_map/ppermute | solution.py:70
  180.8 13.9 %collective-permute-start.32 = (bf16[2,64,2048]{2,1,0:T(8,128)(2,1)S(1)}, bf16[2,64,2048]{2,1,0:T(8,128)(2,1)}, u32[]{:S(2)}, u32[]{:S(2)}) collective-permute-start(bf16[2,64,2048]{2,1,0:T(8,128)(2,1)S(1)} %collective-permute-done.30.refs_4_), channel_id=1, source_target_pairs={{0,1},{1,0},{2,3},{3,2},{4,5},{5,4},{6,7},{7,6},{8,9},{9,8},{10,11... | collective-permute-start | bytes 1572872 | tf_op jit(solution)/shard_map/ppermute | solution.py:46
  196.4 28.9 %feed_forward.1 = (bf16[1024,704]{1,0:T(8,128)(2,1)}, bf16[704,1024]{1,0:T(8,128)(2,1)}, bf16[704,1024]{1,0:T(8,128)(2,1)}, bf16[704,1024]{1,0:T(8,128)(2,1)}, b...) custom-call(s32[5]{0:T(128)} %stack.179.place.refs_0_.place_ref, ...), custom_call_target="tpu_custom_call" | custom-call | flops 14763950080 | bytes 33554432 | tf_op jit(solution)/shard_map/feed_forward/pallas_call | solution.py:707
  230.2 14.2 %gate_up_terms.1 = bf16[4,4,1408,128]{3,2,1,0:T(8,128)(2,1)} custom-call(s32[5]{0:T(128)} %stack.179.place.refs_0_.place_ref, bf16[2,128,2048]{2,1,0:T(8,128)(2,1)} %copy-done.23, bf16[2,128,2048]{2,1,0:T(8,128)(2,1)} %copy-done.43, bf16[2,128,2048]{2,1,0:T(8,128)(2,1)} %copy-done.53, bf16[2,64,2048]{2,1,0:T(8,128)(2,1)} %copy-done.56, ...), custom_call_target="tpu_custom_call" | custom-call | flops 5905580032 | bytes 16777216 | tf_op jit(solution)/shard_map/gate_up_terms/pallas_call | solution.py:784
  247.5 9.7 %down_terms.1 = bf16[4,4,704,128]{3,2,1,0:T(8,128)(2,1)} custom-call(s32[5]{0:T(128)} %stack.179.place.refs_0_.place_ref, bf16[2,128,2048]{2,1,0:T(8,128)(2,1)} %copy-done.22, bf16[2,128,2048]{2,1,0:T(8,128)(2,1)} %copy-done.42, bf16[2,128,2048]{2,1,0:T(8,128)(2,1)} %copy-done.52, bf16[2,64,2048]{2,1,0:T(8,128)(2,1)} %copy-done.54, ...), custom_call_target="tpu_custom_call" | custom-call | flops 2952790016 | bytes 12582912 | tf_op jit(solution)/shard_map/down_terms/pallas_call | solution.py:784
  275.0 7.9 %project.1 = (bf16[2,128,2048]{2,1,0:T(8,128)(2,1)}, bf16[2,128,2048]{2,1,0:T(8,128)(2,1)}, bf16[2,128,2048]{2,1,0:T(8,128)(2,1)}, bf16[2,64,2048]{2,1,0:T(8,128)(2,1)}, bf16[2,64,2048]{2,1,0:T(8,128)(2,1)}) custom-call(bf16[1024,704]{1,0:T(8,128)(2,1)} %get-tuple-element.250.left_ref, bf16[704,2048]{1,0:T(8,128)(2,1)} %get-tuple-element.251.weight_ref), custom_call_target="tpu_custom_call" | custom-call | flops 2952790016 | bytes 8388608 | tf_op jit(solution)/shard_map/project/pallas_call | solution.py:327
  292.8 5.4 collective-permute-done.41.refs_3_.refs_4_
  302.6 20.7 %attention_back.1 = (f32[2,512,256]{2,1,0:T(8,128)}, bf16[2,512,128]{2,1,0:T(8,128)(2,1)}, f32[2,512,128]{2,1,0:T(8,128)}) custom-call(s32[5]{0:T(128)} %stack.179.place.refs_0_.place_ref, bf16[2,128,2048]{2,1,0:T(8,128)(2,1)} %copy-done.3, bf16[2,128,2048]{2,1,0:T(8,128)(2,1)} %copy-done.4, bf16[2,128,2048]{2,1,0:T(8,128)(2,1)} %copy-done.7, ...), custom_call_target="tpu_custom_call" | custom-call | flops 3221225472 | bytes 8388608 | tf_op jit(solution)/shard_map/attention_back/pallas_call | solution.py:536
  328.3 6.8 %output_terms.1.refs_7_ = bf16[4,2,2,256,128]{4,3,2,1,0:T(8,128)(2,1)} custom-call(s32[5]{0:T(128)} %stack.179.place.refs_0_.place_ref, bf16[2,128,2048]{2,1,0:T(8,128)(2,1)} %copy-done.3, bf16[2,128,2048]{2,1,0:T(8,128)(2,1)} %copy-done.4, bf16[2,128,2048]{2,1,0:T(8,128)(2,1)} %copy-done.7, bf16[2,64,2048]{2,1,0:T(8,128)(2,1)} %copy-done.14, ...), custom_call_target="tpu_custom_call" | custom-call | flops 1073741824 | bytes 7340032 | tf_op jit(solution)/shard_map/output_terms/pallas_call | solution.py:405
  339.6 23.1 %reduce-scatter.5.cloned.1.call-done = bf16[1,4,1408,128]{3,2,1,0:T(8,128)(2,1)} async-done(((bf16[4,4,1408,128]{3,2,1,0:T(8,128)(2,1)}), bf16[1,4,1408,128]{3,2,1,0:T(8,128)(2,1)}) %reduce-scatter.5.cloned.1.call-update) | async-done | bytes 1441808 | tf_op jit(solution)/shard_map/reduce_scatter | solution.py:1049
  370.5 8.3 %qkv_back.1 = (bf16[2,128,2048]{2,1,0:T(8,128)(2,1)}, bf16[2,128,2048]{2,1,0:T(8,128)(2,1)}, bf16[2,128,2048]{2,1,0:T(8,128)(2,1)}, bf16[2,64,2048]{2,1,0:T(8,12...) custom-call(f32[2,512,256]{2,1,0:T(8,128)} %get-tuple-element.282.grad_q_ref, ...), custom_call_target="tpu_custom_call" | custom-call | flops 1610612736 | bytes 9437184 | tf_op jit(solution)/shard_map/qkv_back/pallas_call | solution.py:370
  386.9 8.3 %qkv_terms.1 = bf16[4,2,2,640,128]{4,3,2,1,0:T(8,128)(2,1)} custom-call(s32[5]{0:T(128)} %stack.179.place.refs_0_.place_ref, bf16[2,128,2176]{2,1,0:T(8,128)(2,1)} %copy-done.2, bf16[2,128,2176]{2,1,0:T(8,128)(2,1)} %collective-permute-done.2.refs_2_, bf16[2,128,2176]{2,1,0:T(8,128)(2,1)} %copy-done.5, bf16[2,64,2176]{2,1,0:T(8,128)(2,1)} %copy-done.12, ...), custom_call_target="tpu_custom_call" | custom-call | flops 1610612736 | bytes 7340032 | tf_op jit(solution)/shard_map/qkv_terms/pallas_call | solution.py:405
  408.0 5.4 collective-permute-done.59
  417.1 11.5 %collective-permute-done.63 = bf16[2,2,640,128]{3,2,1,0:T(8,128)(2,1)S(1)} collective-permute-done((bf16[2,2,640,128]{3,2,1,0:T(8,128)(2,1)S(1)}, bf16[2,2,640,128]{3,2,1,0:T(8,128)(2,1)S(1)}, u32[]{:S(2)}, u32[]{:S(2)}) %collective-permute-start.63) | collective-permute-done | bytes 655392 | tf_op jit(solution)/shard_map/ppermute | solution.py:46
  435.6 6.0 %collective-permute-done.65 = bf16[1408,128]{1,0:T(8,128)(2,1)S(1)} collective-permute-done((bf16[1408,128]{1,0:T(8,128)(2,1)S(1)}, bf16[1408,128]{1,0:T(8,128)(2,1)S(1)}, u32[]{:S(2)}, u32[]{:S(2)}) %collective-permute-start.65) | collective-permute-done | bytes 360480 | tf_op jit(solution)/shard_map/ppermute | solution.py:46
  441.6 6.8 %collective-permute-done.64 = bf16[2,640,128]{2,1,0:T(8,128)(2,1)S(1)} collective-permute-done((bf16[2,640,128]{2,1,0:T(8,128)(2,1)S(1)}, bf16[2,640,128]{2,1,0:T(8,128)(2,1)S(1)}, u32[]{:S(2)}, u32[]{:S(2)}) %collective-permute-start.64) | collective-permute-done | bytes 327712 | tf_op jit(solution)/shard_map/ppermute | solution.py:46
  464.0 20.8 %collective-permute-done.72.refs_3_ = bf16[2,640,128]{2,1,0:T(8,128)(2,1)S(1)} collective-permute-done((bf16[2,640,128]{2,1,0:T(8,128)(2,1)S(1)}, bf16[2,640,128]{2,1,0:T(8,128)(2,1)S(1)}, u32[]{:S(2)}, u32[]{:S(2)}) %collective-permute-start.72) | collective-permute-done | bytes 327712 | tf_op jit(solution)/shard_map/ppermute | solution.py:46
  484.8 5.1 collective-permute-done.73.refs_1_
  499.2 8.5 %collective-permute-done.76 = bf16[1,640,128]{2,1,0:T(8,128)(2,1)S(1)} collective-permute-done((bf16[1,640,128]{2,1,0:T(8,128)(2,1)S(1)}, bf16[1,640,128]{2,1,0:T(8,128)(2,1)S(1)}, u32[]{:S(2)}, u32[]{:S(2)}) %collective-permute-start.76) | collective-permute-done | bytes 163872 | tf_op jit(solution)/shard_map/ppermute | solution.py:46
  512.4 8.9 %all-to-all-start = ((bf16[16,128,128]{2,1,0:T(8,128)(2,1)}), bf16[16,128,128]{2,1,0:T(8,128)(2,1)S(1)}, u32[]{:S(2)}, u32[]{:S(2)}) async-start(bf16[16,128,128]{2,1,0:T(8,128)(2,1)} %get-tuple-element.336), calls=%async_computation.2 | async-start | bytes 1048576 | tf_op jit(solution)/shard_map/all_to_all | solution.py:1105
  527.3 5.2 finish_hidden.3
  533.3 5.2 finish_hidden.2
  (392 shorter events, 207.1 us)
Async XLA Ops:
  7.2 97.8 %all-gather.3.cloned.1.call-start = ((), (), s32[]{:S(2)}) async-start(), calls=%async_computation.3 | async-start | bytes 8912896 | tf_op jit(solution)/shard_map/all_gather | solution.py:1007
  7.9 188.5 %all-gather.5.cloned.1.call-start = ((), (), s32[]{:S(2)}) async-start(), calls=%async_computation.4 | async-start | bytes 10813440 | tf_op jit(solution)/shard_map/all_gather | solution.py:1029
  17.8 15.3 %collective-permute-start.2 = (bf16[2,128,2176]{2,1,0:T(8,128)(2,1)S(1)}, bf16[2,128,2176]{2,1,0:T(8,128)(2,1)}, u32[]{:S(2)}, u32[]{:S(2)}) collective-permute-start(bf16[2,128,2176]{2,1,0:T(8,128)(2,1)S(1)} %pad_maximum_fusion.refs_1_), channel_id=1, source_target_pairs={{0,16},{1,49},{16,32},{17,1},{32,48},{33,17},{48,0},{49,33},{2,18}... | collective-permute-start | bytes 3342344 | tf_op jit(solution)/shard_map/ppermute | solution.py:70
  33.2 19.5 %collective-permute-start.6 = (bf16[2,128,2176]{2,1,0:T(8,128)(2,1)}, bf16[2,128,2176]{2,1,0:T(8,128)(2,1)S(1)}, u32[]{:S(2)}, u32[]{:S(2)}) collective-permute-start(bf16[2,128,2176]{2,1,0:T(8,128)(2,1)} %collective-permute-done.2.refs_2_), channel_id=1, source_target_pairs={{0,1},{1,0},{2,3},{3,2},{4,5},{5,4},{6,7},{7,6},{8,9},{9,8},{10,11... | collective-permute-start | bytes 3342344 | tf_op jit(solution)/shard_map/ppermute | solution.py:46
  36.1 16.6 %collective-permute-start.5 = (bf16[2,64,2176]{2,1,0:T(8,128)(2,1)S(1)}, bf16[2,64,2176]{2,1,0:T(8,128)(2,1)S(1)}, u32[]{:S(2)}, u32[]{:S(2)}) collective-permute-start(bf16[2,64,2176]{2,1,0:T(8,128)(2,1)S(1)} %constant_dynamic-slice_fusion.3), channel_id=1, source_target_pairs={{0,16},{1,49},{16,32},{17,1},{32,48},{33,17},{48,0},{49,33},{2,18}... | collective-permute-start | bytes 1671176 | tf_op jit(solution)/shard_map/ppermute | solution.py:70
  52.8 31.9 %collective-permute-start.12 = (bf16[2,128,2048]{2,1,0:T(8,128)(2,1)S(1)}, bf16[2,128,2048]{2,1,0:T(8,128)(2,1)S(1)}, u32[]{:S(2)}, u32[]{:S(2)}) collective-permute-start(bf16[2,128,2048]{2,1,0:T(8,128)(2,1)S(1)} %pad_maximum_fusion.2.refs_6_.refs_1_), channel_id=1, source_target_pairs={{0,16},{1,49},{16,32},{17,1},{32,48},{33,17},{48,0},{49,33},{2,18}... | collective-permute-start | bytes 3145736 | tf_op jit(solution)/shard_map/ppermute | solution.py:70
  53.9 30.8 %collective-permute-start.10 = (bf16[2112,128]{1,0:T(8,128)(2,1)S(1)}, bf16[2112,128]{1,0:T(8,128)(2,1)S(1)}, u32[]{:S(2)}, u32[]{:S(2)}) collective-permute-start(bf16[2112,128]{1,0:T(8,128)(2,1)S(1)} %pad_maximum_fusion.7), channel_id=1, source_target_pairs={{0,64},{64,8},{8,72},{72,0},{1,65},{65,9},{9,73},{73,1},{2,66},{66... | collective-permute-start | bytes 1622024 | tf_op jit(solution)/shard_map/ppermute | solution.py:44
  55.6 29.0 %collective-permute-start.11 = (bf16[2112,128]{1,0:T(8,128)(2,1)S(1)}, bf16[2112,128]{1,0:T(8,128)(2,1)S(1)}, u32[]{:S(2)}, u32[]{:S(2)}) collective-permute-start(bf16[2112,128]{1,0:T(8,128)(2,1)S(1)} %pad_maximum_fusion.7), channel_id=1, source_target_pairs={{0,72},{64,0},{8,64},{72,8},{1,73},{65,1},{9,65},{73,9},{2,74},{66... | collective-permute-start | bytes 1622024 | tf_op jit(solution)/shard_map/ppermute | solution.py:44
  84.7 16.7 %collective-permute-start.17 = (bf16[2,128,2048]{2,1,0:T(8,128)(2,1)S(1)}, bf16[2,128,2048]{2,1,0:T(8,128)(2,1)S(1)}, u32[]{:S(2)}, u32[]{:S(2)}) collective-permute-start(bf16[2,128,2048]{2,1,0:T(8,128)(2,1)S(1)} %collective-permute-done.12.refs_7_.refs_2_), channel_id=1, source_target_pairs={{0,1},{1,0},{2,3},{3,2},{4,5},{5,4},{6,7},{7,6},{8,9},{9,8},{10,11... | collective-permute-start | bytes 3145736 | tf_op jit(solution)/shard_map/ppermute | solution.py:46
  85.4 16.0 %collective-permute-start.16 = (bf16[2,64,2048]{2,1,0:T(8,128)(2,1)S(1)}, bf16[2,64,2048]{2,1,0:T(8,128)(2,1)S(1)}, u32[]{:S(2)}, u32[]{:S(2)}) collective-permute-start(bf16[2,64,2048]{2,1,0:T(8,128)(2,1)S(1)} %constant_dynamic-slice_fusion.2), channel_id=1, source_target_pairs={{0,16},{1,49},{16,32},{17,1},{32,48},{33,17},{48,0},{49,33},{2,18}... | collective-permute-start | bytes 1572872 | tf_op jit(solution)/shard_map/ppermute | solution.py:70
  103.8 235.8 %reduce-scatter.3.cloned.1.call-start = ((), (), s32[]{:S(2)}) async-start(), calls=%async_computation.5 | async-start | bytes 3604480 | tf_op jit(solution)/shard_map/reduce_scatter | solution.py:1052
  103.9 15.6 %collective-permute-start.21 = (bf16[2,64,2048]{2,1,0:T(8,128)(2,1)S(1)}, bf16[2,64,2048]{2,1,0:T(8,128)(2,1)S(1)}, u32[]{:S(2)}, u32[]{:S(2)}) collective-permute-start(bf16[2,64,2048]{2,1,0:T(8,128)(2,1)S(1)} %collective-permute-done.16.refs_9_.refs_4_), channel_id=1, source_target_pairs={{0,1},{1,0},{2,3},{3,2},{4,5},{5,4},{6,7},{7,6},{8,9},{9,8},{10,11... | collective-permute-start | bytes 1572872 | tf_op jit(solution)/shard_map/ppermute | solution.py:46
  180.8 15.6 %collective-permute-start.32 = (bf16[2,64,2048]{2,1,0:T(8,128)(2,1)S(1)}, bf16[2,64,2048]{2,1,0:T(8,128)(2,1)}, u32[]{:S(2)}, u32[]{:S(2)}) collective-permute-start(bf16[2,64,2048]{2,1,0:T(8,128)(2,1)S(1)} %collective-permute-done.30.refs_4_), channel_id=1, source_target_pairs={{0,1},{1,0},{2,3},{3,2},{4,5},{5,4},{6,7},{7,6},{8,9},{9,8},{10,11... | collective-permute-start | bytes 1572872 | tf_op jit(solution)/shard_map/ppermute | solution.py:46
  225.8 18.7 %collective-permute-start.35 = (bf16[2,128,2048]{2,1,0:T(8,128)(2,1)}, bf16[2,128,2048]{2,1,0:T(8,128)(2,1)}, u32[]{:S(2)}, u32[]{:S(2)}) collective-permute-start(bf16[2,128,2048]{2,1,0:T(8,128)(2,1)} %get-tuple-element.238), channel_id=1, source_target_pairs={{0,1},{1,0},{2,3},{3,2},{4,5},{5,4},{6,7},{7,6},{8,9},{9,8},{10,11... | collective-permute-start | bytes 3145736 | tf_op jit(solution)/shard_map/ppermute | solution.py:46
  227.8 16.6 %collective-permute-start.36 = (bf16[128,2048]{1,0:T(8,128)(2,1)}, bf16[128,2048]{1,0:T(8,128)(2,1)S(1)}, u32[]{:S(2)}, u32[]{:S(2)}) collective-permute-start(bf16[128,2048]{1,0:T(8,128)(2,1)} %slice_bitcast_fusion.8), channel_id=1, source_target_pairs={{0,1},{1,0},{2,3},{3,2},{4,5},{5,4},{6,7},{7,6},{8,9},{9,8},{10,11... | collective-permute-start | bytes 1572872 | tf_op jit(solution)/shard_map/ppermute | solution.py:46
  261.6 101.1 %reduce-scatter.5.cloned.1.call-start = ((), (), s32[]{:S(2)}) async-start(), calls=%async_computation.6 | async-start | bytes 7208960 | tf_op jit(solution)/shard_map/reduce_scatter | solution.py:1049
  290.4 33.0 %collective-permute-start.45 = (bf16[2,128,2048]{2,1,0:T(8,128)(2,1)}, bf16[2,128,2048]{2,1,0:T(8,128)(2,1)S(1)}, u32[]{:S(2)}, u32[]{:S(2)}) collective-permute-start(bf16[2,128,2048]{2,1,0:T(8,128)(2,1)} %get-tuple-element.262), channel_id=1, source_target_pairs={{0,1},{1,0},{2,3},{3,2},{4,5},{5,4},{6,7},{7,6},{8,9},{9,8},{10,11... | collective-permute-start | bytes 3145736 | tf_op jit(solution)/shard_map/ppermute | solution.py:46
  292.8 30.5 %collective-permute-start.46 = (bf16[128,2048]{1,0:T(8,128)(2,1)}, bf16[128,2048]{1,0:T(8,128)(2,1)S(1)}, u32[]{:S(2)}, u32[]{:S(2)}) collective-permute-start(bf16[128,2048]{1,0:T(8,128)(2,1)} %slice_bitcast_fusion.6), channel_id=1, source_target_pairs={{0,1},{1,0},{2,3},{3,2},{4,5},{5,4},{6,7},{7,6},{8,9},{9,8},{10,11... | collective-permute-start | bytes 1572872 | tf_op jit(solution)/shard_map/ppermute | solution.py:46
  300.4 23.0 %collective-permute-start.44 = (bf16[2,64,2048]{2,1,0:T(8,128)(2,1)S(1)}, bf16[2,64,2048]{2,1,0:T(8,128)(2,1)}, u32[]{:S(2)}, u32[]{:S(2)}) collective-permute-start(bf16[2,64,2048]{2,1,0:T(8,128)(2,1)S(1)} %add_convert_fusion.1), channel_id=1, source_target_pairs={{0,16},{1,49},{16,32},{17,1},{32,48},{33,17},{48,0},{49,33},{2,18}... | collective-permute-start | bytes 1572872 | tf_op jit(solution)/shard_map/ppermute | solution.py:70
  385.6 28.0 %collective-permute-start.57 = (bf16[2,128,2048]{2,1,0:T(8,128)(2,1)}, bf16[2,128,2048]{2,1,0:T(8,128)(2,1)S(1)}, u32[]{:S(2)}, u32[]{:S(2)}) collective-permute-start(bf16[2,128,2048]{2,1,0:T(8,128)(2,1)} %get-tuple-element.305), channel_id=1, source_target_pairs={{0,1},{1,0},{2,3},{3,2},{4,5},{5,4},{6,7},{7,6},{8,9},{9,8},{10,11... | collective-permute-start | bytes 3145736 | tf_op jit(solution)/shard_map/ppermute | solution.py:46
  386.5 20.0 %collective-permute-start.58 = (bf16[128,2048]{1,0:T(8,128)(2,1)}, bf16[128,2048]{1,0:T(8,128)(2,1)S(1)}, u32[]{:S(2)}, u32[]{:S(2)}) collective-permute-start(bf16[128,2048]{1,0:T(8,128)(2,1)} %slice_bitcast_fusion.4), channel_id=1, source_target_pairs={{0,1},{1,0},{2,3},{3,2},{4,5},{5,4},{6,7},{7,6},{8,9},{9,8},{10,11... | collective-permute-start | bytes 1572872 | tf_op jit(solution)/shard_map/ppermute | solution.py:46
  406.6 29.0 %collective-permute-start.66 = (bf16[704,128]{1,0:T(8,128)(2,1)S(1)}, bf16[704,128]{1,0:T(8,128)(2,1)S(1)}, u32[]{:S(2)}, u32[]{:S(2)}) collective-permute-start(bf16[704,128]{1,0:T(8,128)(2,1)S(1)} %get-tuple-element.370), channel_id=1, source_target_pairs={{0,1},{1,0},{2,3},{3,2},{4,5},{5,4},{6,7},{7,6},{8,9},{9,8},{10,11... | collective-permute-start | bytes 540680 | tf_op jit(solution)/shard_map/ppermute | solution.py:46
  413.4 22.2 %collective-permute-start.67 = (bf16[704,128]{1,0:T(8,128)(2,1)S(1)}, bf16[704,128]{1,0:T(8,128)(2,1)S(1)}, u32[]{:S(2)}, u32[]{:S(2)}) collective-permute-start(bf16[704,128]{1,0:T(8,128)(2,1)S(1)} %get-tuple-element.370), channel_id=1, source_target_pairs={{0,65},{1,64},{64,1},{65,0},{2,67},{3,66},{66,3},{67,2},{4,69},{5,... | collective-permute-start | bytes 540680 | tf_op jit(solution)/shard_map/ppermute | solution.py:956
  416.2 16.7 %collective-permute-start.62 = (bf16[2,2,640,128]{3,2,1,0:T(8,128)(2,1)S(1)}, bf16[2,2,640,128]{3,2,1,0:T(8,128)(2,1)S(1)}, u32[]{:S(2)}, u32[]{:S(2)}) collective-permute-start(bf16[2,2,640,128]{3,2,1,0:T(8,128)(2,1)S(1)} %pad_maximum_fusion.5), channel_id=1, source_target_pairs={{0,2},{2,4},{4,6},{6,0},{1,3},{3,5},{5,7},{7,1},{8,10},{10,12},{12... | collective-permute-start | bytes 1966088 | tf_op jit(solution)/shard_map/ppermute | solution.py:46
  417.0 31.5 %collective-permute-start.61 = (bf16[2,128,2048]{2,1,0:T(8,128)(2,1)S(1)}, bf16[2,128,2048]{2,1,0:T(8,128)(2,1)S(1)}, u32[]{:S(2)}, u32[]{:S(2)}) collective-permute-start(bf16[2,128,2048]{2,1,0:T(8,128)(2,1)S(1)} %convert_element_type.389), channel_id=1, source_target_pairs={{0,16},{1,49},{16,32},{17,1},{32,48},{33,17},{48,0},{49,33},{2,18}... | collective-permute-start | bytes 3145736 | tf_op jit(solution)/shard_map/ppermute | solution.py:70
  451.1 38.8 %collective-permute-start.74 = (bf16[2,3,704,128]{3,2,0,1:T(8,128)(2,1)S(1)}, bf16[2,3,704,128]{3,2,0,1:T(8,128)(2,1)S(1)}, u32[]{:S(2)}, u32[]{:S(2)}) collective-permute-start(bf16[2,3,704,128]{3,2,0,1:T(8,128)(2,1)S(1)} %pad_maximum_fusion.1), channel_id=1, source_target_pairs={{0,16},{16,32},{32,48},{48,0},{1,17},{17,33},{33,49},{49,1},{2,18}... | collective-permute-start | bytes 3244040 | tf_op jit(solution)/shard_map/ppermute | solution.py:46
  458.5 31.4 %collective-permute-start.75 = (bf16[2,3,704,128]{3,2,0,1:T(8,128)(2,1)S(1)}, bf16[2,3,704,128]{3,2,0,1:T(8,128)(2,1)S(1)}, u32[]{:S(2)}, u32[]{:S(2)}) collective-permute-start(bf16[2,3,704,128]{3,2,0,1:T(8,128)(2,1)S(1)} %pad_maximum_fusion.1), channel_id=1, source_target_pairs={{0,48},{16,0},{32,16},{48,32},{1,49},{17,1},{33,17},{49,33},{2,50}... | collective-permute-start | bytes 3244040 | tf_op jit(solution)/shard_map/ppermute | solution.py:46
  459.5 25.4 %collective-permute-start.72 = (bf16[2,640,128]{2,1,0:T(8,128)(2,1)S(1)}, bf16[2,640,128]{2,1,0:T(8,128)(2,1)S(1)}, u32[]{:S(2)}, u32[]{:S(2)}) collective-permute-start(bf16[2,640,128]{2,1,0:T(8,128)(2,1)S(1)} %fusion.14.refs_0_), channel_id=1, source_target_pairs={{0,16},{16,32},{32,48},{48,0},{1,17},{17,33},{33,49},{49,1},{2,18}... | collective-permute-start | bytes 983048 | tf_op jit(solution)/shard_map/ppermute | solution.py:46
  460.2 29.7 %collective-permute-start.73 = (bf16[2,640,128]{2,1,0:T(8,128)(2,1)S(1)}, bf16[2,640,128]{2,1,0:T(8,128)(2,1)S(1)}, u32[]{:S(2)}, u32[]{:S(2)}) collective-permute-start(bf16[2,640,128]{2,1,0:T(8,128)(2,1)S(1)} %fusion.14.refs_0_), channel_id=1, source_target_pairs={{0,48},{16,0},{32,16},{48,32},{1,49},{17,1},{33,17},{49,33},{2,50}... | collective-permute-start | bytes 983048 | tf_op jit(solution)/shard_map/ppermute | solution.py:46
  490.9 16.8 %collective-permute-start.78 = (bf16[1,3,704,128]{3,2,0,1:T(8,128)(2,1)S(1)}, bf16[1,3,704,128]{3,2,0,1:T(8,128)(2,1)S(1)}, u32[]{:S(2)}, u32[]{:S(2)}) collective-permute-start(bf16[1,3,704,128]{3,2,0,1:T(8,128)(2,1)S(1)} %slice.267), channel_id=1, source_target_pairs={{0,16},{16,32},{32,48},{48,0},{1,17},{17,33},{33,49},{49,1},{2,18}... | collective-permute-start | bytes 1622024 | tf_op jit(solution)/shard_map/ppermute | solution.py:46
  491.1 16.6 %collective-permute-start.79 = (bf16[1,3,704,128]{3,2,0,1:T(8,128)(2,1)S(1)}, bf16[1,3,704,128]{3,2,0,1:T(8,128)(2,1)S(1)}, u32[]{:S(2)}, u32[]{:S(2)}) collective-permute-start(bf16[1,3,704,128]{3,2,0,1:T(8,128)(2,1)S(1)} %slice.268), channel_id=1, source_target_pairs={{0,48},{16,0},{32,16},{48,32},{1,49},{17,1},{33,17},{49,33},{2,50}... | collective-permute-start | bytes 1622024 | tf_op jit(solution)/shard_map/ppermute | solution.py:46
  512.4 27.6 %all-to-all-start = ((bf16[16,128,128]{2,1,0:T(8,128)(2,1)}), bf16[16,128,128]{2,1,0:T(8,128)(2,1)S(1)}, u32[]{:S(2)}, u32[]{:S(2)}) async-start(bf16[16,128,128]{2,1,0:T(8,128)(2,1)} %get-tuple-element.336), calls=%async_computation.2 | async-start | bytes 1048576 | tf_op jit(solution)/shard_map/all_to_all | solution.py:1105
  (112 other events, 1043.7 us)
Sparse Core Ops, SparseCore 0:
  10.5 89.0 all-gather.2
  104.0 86.9 all-gather.4
  261.7 39.2 reduce-scatter.2
  303.2 59.3 reduce-scatter.4
